TPU v7x, 32 devices: a whole 2x2x4 slice. The times are simulated.
32 devices in a mesh: ep: 4 (over z), dp: 8 (over y, x, core).
Axes of the slice: x: 2, y: 2, z: 4, core: 2. Of those that a mesh axis runs over, the one named last changes fastest.
Arguments:
- tokens: bfloat16 [2, 4096, 1024], P(None, ('ep', 'dp')), may hold values from -6 to 6
- segments: int32 [2, 4, 1024], P(None, 'ep', 'dp'), may hold values from 0 to 3, never falling along the last dimension, each value on 1 to 512 neighbouring positions
- routes: int32 [2, 4096, 8], P(None, ('ep', 'dp')), may hold values from 0 to 31, all different within a row; in each aligned block of 128 rows (0 to 127, 128 to 255, ..., all dimensions but the last counted through in order) at most 64 rows name the same one
- first_gain: float32 [1024], replicated, may hold values from 0.1 to 1.9
- w_query: bfloat16 [1024, 1024], replicated, may hold values from -0.1875 to 0.1875
- w_key: bfloat16 [1024, 512], replicated, may hold values from -0.1875 to 0.1875
- w_value: bfloat16 [1024, 512], replicated, may hold values from -0.1875 to 0.1875
- w_out: bfloat16 [1024, 1024], replicated, may hold values from -3 to 3
- second_gain: float32 [1024], replicated, may hold values from 0.1 to 1.9
- w_router: bfloat16 [1024, 32], replicated, may hold values from -0.09375 to 0.09375
- w_gate: bfloat16 [32, 1024, 512], P('ep'), may hold values from -0.1875 to 0.1875
- w_up: bfloat16 [32, 1024, 512], P('ep'), may hold values from -0.1875 to 0.1875
- w_down: bfloat16 [32, 512, 1024], P('ep'), may hold values from -0.75 to 0.75
- cotangent: bfloat16 [2, 4096, 1024], P(None, ('ep', 'dp')), may hold values from -6 to 6
Outputs:
- output: bfloat16 [2, 4096, 1024], P(None, ('ep', 'dp'))
- grad_tokens: float32 [2, 4096, 1024], P(None, ('ep', 'dp'))
- grad_first_gain: float32 [1024], P(('ep', 'dp'))
- grad_w_query: float32 [1024, 1024], P(('ep', 'dp'))
- grad_w_key: float32 [1024, 512], P(('ep', 'dp'))
- grad_w_value: float32 [1024, 512], P(('ep', 'dp'))
- grad_w_out: float32 [1024, 1024], P(('ep', 'dp'))
- grad_second_gain: float32 [1024], P(('ep', 'dp'))
- grad_w_router: float32 [1024, 32], P(('ep', 'dp'))
- grad_w_gate: float32 [32, 1024, 512], P('ep', 'dp')
- grad_w_up: float32 [32, 1024, 512], P('ep', 'dp')
- grad_w_down: float32 [32, 512, 1024], P('ep', 'dp')
Inputs may be any that keep to these rules, and one draw needn't show every extreme that they name: `routes`: the 8 experts of a token are distinct. In the 128 token rows that one device holds in one micro-batch (aligned blocks), no expert is named more than 64 times, and in some blocks one expert is named exactly 64 times. `segments`: along each sequence the ids never fall; every id from 0 to 3 labels a run of consecutive tokens, the longest run being half of the sequence's 1024 tokens.
All inputs are finite; a program needn't handle non-finite values.
Results may differ from a plain program's by a relative error of at most 0.015.
The roundings to bfloat16 on the way count: a program that leaves them out, or rounds other values in their place, can miss the bound.
Values may be sent and summed in bfloat16 or wider, within the bound.
A program may use at most 256 MiB of HBM per device.

v0:
```python
import jax
import jax.numpy as jnp
from jax import lax
from jax.sharding import PartitionSpec as P

HEADS = 16
KV_HEADS = 8
HEAD_DIM = 64
EXPERTS = 32
TOP = 8
CAP = 64


EPSILON = 1e-06
ROPE_BASE = 10000.0
MASKED = -1e30
HIGHEST = lax.Precision.HIGHEST


def rms_scale(values):
    return lax.rsqrt(jnp.mean(values * values, axis=-1, keepdims=True) + EPSILON)


def rope_tables(positions, head_size):
    halfway = head_size // 2
    frequency = ROPE_BASE ** (-(jnp.arange(halfway, dtype=jnp.float32) * 2.0 / head_size))
    angles = positions.astype(jnp.float32)[:, None] * frequency[None, :]
    return (jnp.cos(angles), jnp.sin(angles))


def rotate(values, cosine, sine_table):
    halfway = values.shape[-1] // 2
    first_part = values[..., :halfway]
    second_part = values[..., halfway:]
    cosine_wide = cosine[:, None, :]
    sine_wide = sine_table[:, None, :]
    return jnp.concatenate(
        [
            first_part * cosine_wide - second_part * sine_wide,
            second_part * cosine_wide + first_part * sine_wide,
        ],
        axis=-1,
    )


def unrotate(grads, cosine, sine_table):
    halfway = grads.shape[-1] // 2
    first_part = grads[..., :halfway]
    second_part = grads[..., halfway:]
    cosine_wide = cosine[:, None, :]
    sine_wide = sine_table[:, None, :]
    return jnp.concatenate(
        [
            first_part * cosine_wide + second_part * sine_wide,
            second_part * cosine_wide - first_part * sine_wide,
        ],
        axis=-1,
    )


def allowed_pairs(query_pos, query_seg, key_pos, key_seg):
    return (key_pos[None, :] <= query_pos[:, None]) & (key_seg[None, :] == query_seg[:, None])


def score_block(queries, key_rows, allowed):
    score_scale = queries.shape[-1] ** (-0.5)
    scores = (
        jnp.einsum("qkgd,nkd->kgqn", queries, key_rows, preferred_element_type=jnp.float32)
        * score_scale
    )
    return jnp.where(allowed[None, None], scores, MASKED)


def block_grads(queries, grad_attn, log_total, grad_dot, key_rows, value_rows, allowed):
    score_scale = queries.shape[-1] ** (-0.5)
    scores = score_block(queries, key_rows, allowed)
    weights = jnp.exp(scores - log_total[..., None])
    grad_prob = jnp.einsum(
        "qkgd,nkd->kgqn", grad_attn, value_rows, preferred_element_type=jnp.float32
    )
    grad_score = (weights * (grad_prob - grad_dot[..., None])).astype(jnp.bfloat16)
    grad_query = None
    grad_key = None
    grad_value = None
    grad_query = (
        jnp.einsum("kgqn,nkd->qkgd", grad_score, key_rows, preferred_element_type=jnp.float32)
        * score_scale
    )
    grad_key = (
        jnp.einsum("kgqn,qkgd->nkd", grad_score, queries, preferred_element_type=jnp.float32)
        * score_scale
    )
    grad_value = jnp.einsum(
        "kgqn,qkgd->nkd",
        weights.astype(jnp.bfloat16),
        grad_attn,
        preferred_element_type=jnp.float32,
    )
    return (grad_query, grad_key, grad_value)


def key_blocks(key_all, value_all, key_seg):
    length, kv_heads, head_size = key_all.shape
    block_size = min(1024, length)
    block_count = length // block_size
    return (
        key_all.reshape(block_count, block_size, kv_heads, head_size),
        value_all.reshape(block_count, block_size, kv_heads, head_size),
        jnp.arange(length, dtype=jnp.int32).reshape(block_count, block_size),
        key_seg.reshape(block_count, block_size),
    )


def attend(queries, key_all, value_all, query_pos, query_seg, key_seg):
    blocks = key_blocks(key_all, value_all, key_seg)
    kv_heads, groups = (queries.shape[1], queries.shape[2])
    row_count = queries.shape[0]

    def stats_step(running, block_items):
        run_max, run_sum = running
        key_rows, value_rows, key_pos, key_segs = block_items
        allowed = allowed_pairs(query_pos, query_seg, key_pos, key_segs)
        scores = score_block(queries, key_rows, allowed)
        new_max = jnp.maximum(run_max, jnp.max(scores, axis=-1))
        terms = jnp.where(allowed[None, None], jnp.exp(scores - new_max[..., None]), 0.0)
        run_sum = run_sum * jnp.exp(run_max - new_max) + jnp.sum(terms, axis=-1)
        return ((new_max, run_sum), None)

    start_max = jnp.full((kv_heads, groups, row_count), MASKED, jnp.float32)
    start_sum = jnp.zeros((kv_heads, groups, row_count), jnp.float32)
    (run_max, run_sum), unused = lax.scan(stats_step, (start_max, start_sum), blocks)
    log_total = run_max + jnp.log(run_sum)

    def output_step(total, block_items):
        key_rows, value_rows, key_pos, key_segs = block_items
        allowed = allowed_pairs(query_pos, query_seg, key_pos, key_segs)
        scores = score_block(queries, key_rows, allowed)
        weights = jnp.exp(scores - log_total[..., None]).astype(jnp.bfloat16)
        return (
            total
            + jnp.einsum("kgqn,nkd->qkgd", weights, value_rows, preferred_element_type=jnp.float32),
            None,
        )

    attn_sum, unused = lax.scan(output_step, jnp.zeros(queries.shape, jnp.float32), blocks)
    return (attn_sum, log_total)


def attend_back(
    queries, grad_attn, log_total, grad_dot, key_all, value_all, query_pos, query_seg, key_seg
):
    blocks = key_blocks(key_all, value_all, key_seg)

    def back_step(grad_query, block_items):
        key_rows, value_rows, key_pos, key_segs = block_items
        allowed = allowed_pairs(query_pos, query_seg, key_pos, key_segs)
        part_query, part_key, part_value = block_grads(
            queries, grad_attn, log_total, grad_dot, key_rows, value_rows, allowed
        )
        return (grad_query + part_query, (part_key, part_value))

    return lax.scan(back_step, jnp.zeros(queries.shape, jnp.float32), blocks)


def per_device(
    tokens,
    segments,
    routes,
    first_gain,
    w_query,
    w_key,
    w_value,
    w_out,
    second_gain,
    w_router,
    w_gate,
    w_up,
    w_down,
    cotangent,
):
    micro_count, row_count, model_width = tokens.shape
    head_size = HEAD_DIM
    kv_heads = KV_HEADS
    groups = HEADS // KV_HEADS
    expert_count = EXPERTS
    capacity = CAP
    length = row_count * lax.axis_size("dp")
    query_pos = lax.axis_index("dp") * row_count + jnp.arange(row_count, dtype=jnp.int32)
    seg_all = lax.all_gather(segments, "dp", axis=2, tiled=True)
    expert_ids = jnp.arange(expert_count, dtype=jnp.int32)
    zero_bf16 = jnp.zeros((), jnp.bfloat16)
    router_wide = w_router.astype(jnp.float32)
    grad_norm_one = jnp.zeros((model_width,), jnp.float32)
    grad_norm_two = jnp.zeros((model_width,), jnp.float32)
    grad_w_query = jnp.zeros(w_query.shape, jnp.float32)
    grad_w_key = jnp.zeros(w_key.shape, jnp.float32)
    grad_w_value = jnp.zeros(w_value.shape, jnp.float32)
    grad_w_out = jnp.zeros(w_out.shape, jnp.float32)
    grad_w_router = jnp.zeros(w_router.shape, jnp.float32)
    grad_w_gate = jnp.zeros(w_gate.shape, jnp.float32)
    grad_w_up = jnp.zeros(w_up.shape, jnp.float32)
    grad_w_down = jnp.zeros(w_down.shape, jnp.float32)
    outputs = []
    grad_inputs = []
    for micro_index in range(micro_count):
        inputs = tokens[micro_index].astype(jnp.float32)
        key_seg = seg_all[micro_index, 0]
        query_seg = segments[micro_index, 0]
        seg_start = jnp.searchsorted(key_seg, query_seg, side="left")
        cosine, sine_table = rope_tables(query_pos - seg_start, head_size)
        inv_rms_one = rms_scale(inputs)
        normed_one = (inputs * inv_rms_one * first_gain).astype(jnp.bfloat16)
        query_pre = jnp.dot(normed_one, w_query, preferred_element_type=jnp.float32).reshape(
            row_count, HEADS, head_size
        )
        query_rot = rotate(query_pre, cosine, sine_table).astype(jnp.bfloat16)
        key_pre = jnp.dot(normed_one, w_key, preferred_element_type=jnp.float32).reshape(
            row_count, kv_heads, head_size
        )
        key_rot = (
            rotate(key_pre, cosine, sine_table)
            .astype(jnp.bfloat16)
            .reshape(row_count, kv_heads * head_size)
        )
        value_own = jnp.dot(normed_one, w_value, preferred_element_type=jnp.float32).astype(
            jnp.bfloat16
        )
        key_flat, value_flat = (
            lax.all_gather(key_rot, "dp", axis=0, tiled=True),
            lax.all_gather(value_own, "dp", axis=0, tiled=True),
        )
        key_all = key_flat.reshape(length, kv_heads, head_size)
        value_all = value_flat.reshape(length, kv_heads, head_size)
        queries = query_rot.reshape(row_count, kv_heads, groups, head_size)
        attn_sum, log_total = attend(queries, key_all, value_all, query_pos, query_seg, key_seg)
        attn_low = attn_sum.reshape(row_count, HEADS * head_size).astype(jnp.bfloat16)
        residual = inputs + jnp.dot(attn_low, w_out, preferred_element_type=jnp.float32)
        inv_rms_two = rms_scale(residual)
        normed_two = (residual * inv_rms_two * second_gain).astype(jnp.bfloat16)
        logits = jnp.dot(normed_two, w_router, preferred_element_type=jnp.float32)
        routing = routes[micro_index]
        chosen_mask = (routing[:, :, None] == expert_ids[None, None, :]).astype(jnp.float32)
        chosen = jnp.einsum("te,tke->tk", logits, chosen_mask, precision=HIGHEST)
        gate_probs = jax.nn.softmax(chosen, axis=-1)
        flat_expert = routing.reshape(-1)
        hit_table = (flat_expert[:, None] == expert_ids[None, :]).astype(jnp.int32)
        slot_rank = jnp.sum((jnp.cumsum(hit_table, axis=0) - hit_table) * hit_table, axis=1)
        is_kept = slot_rank < capacity
        slot_index = jnp.where(is_kept, slot_rank, capacity)
        safe_slot = jnp.minimum(slot_index, capacity - 1)
        pair_inputs = jnp.repeat(normed_two, TOP, axis=0)
        outgoing = (
            jnp.zeros((expert_count, capacity, model_width), jnp.bfloat16)
            .at[flat_expert, slot_index]
            .set(pair_inputs, mode="drop")
        )
        incoming = lax.all_to_all(outgoing, "ep", split_axis=0, concat_axis=1, tiled=True)
        gate_pre = jnp.einsum("esd,edf->esf", incoming, w_gate, preferred_element_type=jnp.float32)
        up_pre = jnp.einsum("esd,edf->esf", incoming, w_up, preferred_element_type=jnp.float32)
        gate_sigmoid = jax.nn.sigmoid(gate_pre)
        hidden = (gate_pre * gate_sigmoid * up_pre).astype(jnp.bfloat16)
        expert_out = jnp.einsum(
            "esf,efd->esd", hidden, w_down, preferred_element_type=jnp.float32
        ).astype(jnp.bfloat16)
        returned = lax.all_to_all(expert_out, "ep", split_axis=1, concat_axis=0, tiled=True)
        pair_out = jnp.where(is_kept[:, None], returned[flat_expert, safe_slot], zero_bf16).reshape(
            row_count, TOP, model_width
        )
        expert_mix = jnp.sum(gate_probs[:, :, None] * pair_out, axis=1)
        outputs.append((residual + expert_mix).astype(jnp.bfloat16))
        grad_output = cotangent[micro_index].astype(jnp.float32)
        pair_dot = jnp.sum(grad_output[:, None, :] * pair_out, axis=-1)
        grad_chosen = gate_probs * (
            pair_dot - jnp.sum(gate_probs * pair_dot, axis=-1, keepdims=True)
        )
        grad_logits = jnp.einsum("tk,tke->te", grad_chosen, chosen_mask, precision=HIGHEST)
        grad_w_router = grad_w_router + jnp.einsum(
            "td,te->de", normed_two.astype(jnp.float32), grad_logits, precision=HIGHEST
        )
        grad_normed_two = jnp.einsum("te,de->td", grad_logits, router_wide, precision=HIGHEST)
        grad_pairs = (
            (gate_probs[:, :, None] * grad_output[:, None, :])
            .astype(jnp.bfloat16)
            .reshape(row_count * TOP, model_width)
        )
        grad_outgoing = (
            jnp.zeros((expert_count, capacity, model_width), jnp.bfloat16)
            .at[flat_expert, slot_index]
            .set(grad_pairs, mode="drop")
        )
        grad_incoming = lax.all_to_all(grad_outgoing, "ep", split_axis=0, concat_axis=1, tiled=True)
        grad_hidden = jnp.einsum(
            "esd,efd->esf", grad_incoming, w_down, preferred_element_type=jnp.float32
        )
        grad_w_down = grad_w_down + jnp.einsum(
            "esf,esd->efd", hidden, grad_incoming, preferred_element_type=jnp.float32
        )
        grad_up_pre = (grad_hidden * gate_pre * gate_sigmoid).astype(jnp.bfloat16)
        grad_gate_pre = (
            grad_hidden * up_pre * gate_sigmoid * (1.0 + gate_pre * (1.0 - gate_sigmoid))
        ).astype(jnp.bfloat16)
        grad_w_gate = grad_w_gate + jnp.einsum(
            "esd,esf->edf", incoming, grad_gate_pre, preferred_element_type=jnp.float32
        )
        grad_w_up = grad_w_up + jnp.einsum(
            "esd,esf->edf", incoming, grad_up_pre, preferred_element_type=jnp.float32
        )
        grad_slots = (
            jnp.einsum("esf,edf->esd", grad_gate_pre, w_gate, preferred_element_type=jnp.float32)
            + jnp.einsum("esf,edf->esd", grad_up_pre, w_up, preferred_element_type=jnp.float32)
        ).astype(jnp.bfloat16)
        grad_returned = lax.all_to_all(grad_slots, "ep", split_axis=1, concat_axis=0, tiled=True)
        grad_pair_in = jnp.where(is_kept[:, None], grad_returned[flat_expert, safe_slot], zero_bf16)
        grad_normed_two = grad_normed_two + jnp.sum(
            grad_pair_in.reshape(row_count, TOP, model_width).astype(jnp.float32), axis=1
        )
        scaled_two = grad_normed_two * second_gain
        grad_norm_two = grad_norm_two + jnp.sum(grad_normed_two * residual * inv_rms_two, axis=0)
        grad_residual = (
            grad_output
            + inv_rms_two * scaled_two
            - residual * inv_rms_two**3 * jnp.mean(scaled_two * residual, axis=-1, keepdims=True)
        )
        residual_low = grad_residual.astype(jnp.bfloat16)
        grad_w_out = grad_w_out + jnp.einsum(
            "tf,td->fd", attn_low, residual_low, preferred_element_type=jnp.float32
        )
        grad_attn = jnp.einsum(
            "td,fd->tf", residual_low, w_out, preferred_element_type=jnp.float32
        ).astype(jnp.bfloat16)
        grad_attn = grad_attn.reshape(row_count, kv_heads, groups, head_size)
        grad_dot = jnp.sum(grad_attn.astype(jnp.float32) * attn_sum, axis=-1).transpose(1, 2, 0)
        grad_query_rot, key_parts = attend_back(
            queries,
            grad_attn,
            log_total,
            grad_dot,
            key_all,
            value_all,
            query_pos,
            query_seg,
            key_seg,
        )
        grad_key_flat, grad_value_flat = (
            lax.psum_scatter(
                key_parts[0].reshape(length, kv_heads * head_size).astype(jnp.bfloat16),
                "dp",
                scatter_dimension=0,
                tiled=True,
            ).astype(jnp.float32),
            lax.psum_scatter(
                key_parts[1].reshape(length, kv_heads * head_size).astype(jnp.bfloat16),
                "dp",
                scatter_dimension=0,
                tiled=True,
            ).astype(jnp.float32),
        )
        grad_key_rot = grad_key_flat.reshape(row_count, kv_heads, head_size)
        grad_value_own = grad_value_flat.reshape(row_count, kv_heads, head_size)
        grad_query_pre = (
            unrotate(grad_query_rot.reshape(row_count, HEADS, head_size), cosine, sine_table)
            .astype(jnp.bfloat16)
            .reshape(row_count, HEADS * head_size)
        )
        grad_key_pre = (
            unrotate(grad_key_rot, cosine, sine_table)
            .astype(jnp.bfloat16)
            .reshape(row_count, kv_heads * head_size)
        )
        grad_value_pre = grad_value_own.astype(jnp.bfloat16).reshape(
            row_count, kv_heads * head_size
        )
        grad_w_query = grad_w_query + jnp.einsum(
            "td,tf->df", normed_one, grad_query_pre, preferred_element_type=jnp.float32
        )
        grad_w_key = grad_w_key + jnp.einsum(
            "td,tf->df", normed_one, grad_key_pre, preferred_element_type=jnp.float32
        )
        grad_w_value = grad_w_value + jnp.einsum(
            "td,tf->df", normed_one, grad_value_pre, preferred_element_type=jnp.float32
        )
        grad_normed_one = (
            jnp.einsum("tf,df->td", grad_query_pre, w_query, preferred_element_type=jnp.float32)
            + jnp.einsum("tf,df->td", grad_key_pre, w_key, preferred_element_type=jnp.float32)
            + jnp.einsum("tf,df->td", grad_value_pre, w_value, preferred_element_type=jnp.float32)
        )
        scaled_one = grad_normed_one * first_gain
        grad_norm_one = grad_norm_one + jnp.sum(grad_normed_one * inputs * inv_rms_one, axis=0)
        grad_inputs.append(
            grad_residual
            + inv_rms_one * scaled_one
            - inputs * inv_rms_one**3 * jnp.mean(scaled_one * inputs, axis=-1, keepdims=True)
        )
    dense_sums = (
        lax.psum_scatter(grad_norm_one, ("ep", "dp"), scatter_dimension=0, tiled=True),
        lax.psum_scatter(grad_w_query, ("ep", "dp"), scatter_dimension=0, tiled=True),
        lax.psum_scatter(grad_w_key, ("ep", "dp"), scatter_dimension=0, tiled=True),
        lax.psum_scatter(grad_w_value, ("ep", "dp"), scatter_dimension=0, tiled=True),
        lax.psum_scatter(grad_w_out, ("ep", "dp"), scatter_dimension=0, tiled=True),
        lax.psum_scatter(grad_norm_two, ("ep", "dp"), scatter_dimension=0, tiled=True),
        lax.psum_scatter(grad_w_router, ("ep", "dp"), scatter_dimension=0, tiled=True),
    )
    expert_sums = (
        lax.psum_scatter(
            grad_w_gate.astype(jnp.bfloat16), "dp", scatter_dimension=1, tiled=True
        ).astype(jnp.float32),
        lax.psum_scatter(
            grad_w_up.astype(jnp.bfloat16), "dp", scatter_dimension=1, tiled=True
        ).astype(jnp.float32),
        lax.psum_scatter(
            grad_w_down.astype(jnp.bfloat16), "dp", scatter_dimension=1, tiled=True
        ).astype(jnp.float32),
    )
    return (
        jnp.stack(outputs),
        jnp.stack(grad_inputs),
        dense_sums[0],
        dense_sums[1],
        dense_sums[2],
        dense_sums[3],
        dense_sums[4],
        dense_sums[5],
        dense_sums[6],
        expert_sums[0],
        expert_sums[1],
        expert_sums[2],
    )


def solution(mesh):
    in_specs = (
        P(None, ("ep", "dp"), None),
        P(None, "ep", "dp"),
        P(None, ("ep", "dp"), None),
        P(),
        P(),
        P(),
        P(),
        P(),
        P(),
        P(),
        P("ep", None, None),
        P("ep", None, None),
        P("ep", None, None),
        P(None, ("ep", "dp"), None),
    )
    out_specs = (
        P(None, ("ep", "dp"), None),
        P(None, ("ep", "dp"), None),
        P(("ep", "dp")),
        P(("ep", "dp"), None),
        P(("ep", "dp"), None),
        P(("ep", "dp"), None),
        P(("ep", "dp"), None),
        P(("ep", "dp")),
        P(("ep", "dp"), None),
        P("ep", "dp", None),
        P("ep", "dp", None),
        P("ep", "dp", None),
    )
    return jax.shard_map(
        per_device, mesh=mesh, in_specs=in_specs, out_specs=out_specs, check_vma=False
    )
```

profile of v0, /device:TPU:10, one launch (start us, length us, event | category | flops | bytes accessed | tf_op | source)
XLA Modules:
  0.0 2238.9 jit_solution(1581981547575981231)
XLA Ops:
  115.8 97.2 %all_to_all.144 = bf16[32,64,1024]{2,1,0:T(8,128)(2,1)S(1)} all-to-all(bf16[32,64,1024]{2,1,0:T(8,128)(2,1)} %bitcast.522), channel_id=1, replica_groups=mesh['ep'=4,'dp'=8] {'ep'}, dimensions={0} | all-to-all | bytes 8388608 | tf_op jit(solution)/shard_map/all_to_all | solution.py:257
  247.7 83.9 %all-to-all-done.1 = bf16[8,256,1024]{2,0,1:T(8,128)(2,1)} async-done(((bf16[8,256,1024]{2,0,1:T(8,128)(2,1)}), bf16[8,256,1024]{2,0,1:T(8,128)(2,1)}, u32[]{:S(2)}, u32[]{:S(2)}) %all-to-all-start.1) | async-done | bytes 4194336 | tf_op jit(solution)/shard_map/all_to_all | solution.py:265
  338.2 20.6 gather_fusion.2
  370.5 98.3 %all_to_all.145 = bf16[32,64,1024]{2,1,0:T(8,128)(2,1)S(1)} all-to-all(bf16[32,64,1024]{2,1,0:T(8,128)(2,1)} %bitcast.517), channel_id=1, replica_groups=mesh['ep'=4,'dp'=8] {'ep'}, dimensions={0} | all-to-all | bytes 8388608 | tf_op jit(solution)/shard_map/all_to_all | solution.py:291
  526.3 18.4 all-gather.11.cloned.1.call-done
  550.7 19.8 all-gather.9.cloned.1.call-done
  581.2 25.6 %all-to-all-done.5 = bf16[8,256,1024]{2,0,1:T(8,128)(2,1)} async-done(((bf16[8,256,1024]{2,0,1:T(8,128)(2,1)}), bf16[8,256,1024]{2,0,1:T(8,128)(2,1)}, u32[]{:S(2)}, u32[]{:S(2)}) %all-to-all-start.5) | async-done | bytes 4194336 | tf_op jit(solution)/shard_map/all_to_all | solution.py:312
  613.3 20.6 gather_fusion.4
  649.3 98.4 %all_to_all.146 = bf16[32,64,1024]{2,1,0:T(8,128)(2,1)S(1)} all-to-all(bf16[32,64,1024]{2,1,0:T(8,128)(2,1)} %bitcast.523), channel_id=1, replica_groups=mesh['ep'=4,'dp'=8] {'ep'}, dimensions={0} | all-to-all | bytes 8388608 | tf_op jit(solution)/shard_map/all_to_all | solution.py:257
  780.3 87.0 %all-to-all-done.3 = bf16[8,256,1024]{2,0,1:T(8,128)(2,1)} async-done(((bf16[8,256,1024]{2,0,1:T(8,128)(2,1)}), bf16[8,256,1024]{2,0,1:T(8,128)(2,1)}, u32[]{:S(2)}, u32[]{:S(2)}) %all-to-all-start.3) | async-done | bytes 4194336 | tf_op jit(solution)/shard_map/all_to_all | solution.py:265
  873.8 20.6 gather_fusion.3
  907.8 98.5 %all_to_all.147 = bf16[32,64,1024]{2,1,0:T(8,128)(2,1)S(1)} all-to-all(bf16[32,64,1024]{2,1,0:T(8,128)(2,1)} %bitcast.516), channel_id=1, replica_groups=mesh['ep'=4,'dp'=8] {'ep'}, dimensions={0} | all-to-all | bytes 8388608 | tf_op jit(solution)/shard_map/all_to_all | solution.py:291
  1056.0 87.9 %all-to-all-done.7 = bf16[8,256,1024]{2,0,1:T(8,128)(2,1)} async-done(((bf16[8,256,1024]{2,0,1:T(8,128)(2,1)}), bf16[8,256,1024]{2,0,1:T(8,128)(2,1)}, u32[]{:S(2)}, u32[]{:S(2)}) %all-to-all-start.7) | async-done | bytes 4194336 | tf_op jit(solution)/shard_map/all_to_all | solution.py:312
  1150.4 20.6 gather_fusion.5
  1238.4 13.6 add_convert_fusion
  1311.9 32.5 %reduce-scatter.37.cloned.1.call-done = bf16[128,512]{1,0:T(8,128)(2,1)} async-done(((bf16[1024,512]{1,0:T(8,128)(2,1)}), bf16[128,512]{1,0:T(8,128)(2,1)}) %reduce-scatter.37.cloned.1.call-update) | async-done | bytes 131088
  1376.4 40.9 %all-reduce.2 = (f32[1024]{0:T(1024)S(1)}, f32[1024]{0:T(1024)S(1)}) all-reduce(f32[1024]{0:T(1024)S(1)} %add.382, f32[1024]{0:T(1024)S(1)} %copy-done.94), channel_id=6, replica_groups=mesh['ep'=4,'dp'=8] {'ep','dp'}, use_global_device_ids=true, to_apply=%region_46.47.clone | all-reduce | flops 2048 | bytes 16384
  1424.0 71.4 %reduce-scatter.33.cloned.1.call-done = bf16[8,128,512]{2,1,0:T(8,128)(2,1)} async-done(((bf16[8,1024,512]{2,1,0:T(8,128)(2,1)}), bf16[8,128,512]{2,1,0:T(8,128)(2,1)}) %reduce-scatter.33.cloned.1.call-update) | async-done | bytes 1048592 | tf_op jit(solution)/shard_map/reduce_scatter | solution.py:407
  1498.2 72.0 %reduce-scatter.31.cloned.1.call-done = bf16[8,128,512]{2,1,0:T(8,128)(2,1)} async-done(((bf16[8,1024,512]{2,1,0:T(8,128)(2,1)}), bf16[8,128,512]{2,1,0:T(8,128)(2,1)}) %reduce-scatter.31.cloned.1.call-update) | async-done | bytes 1048592 | tf_op jit(solution)/shard_map/reduce_scatter | solution.py:404
  1573.0 110.0 %reduce-scatter.29.cloned.1.call-done = f32[32,32]{1,0:T(8,128)} async-done(((f32[1024,32]{1,0:T(8,128)}), f32[32,32]{1,0:T(8,128)}) %reduce-scatter.29.cloned.1.call-update) | async-done | bytes 4112 | tf_op jit(solution)/shard_map/reduce_scatter | solution.py:401
  1683.0 135.1 %reduce-scatter.25.cloned.1.call-done = f32[32,512]{1,0:T(8,128)} async-done(((f32[1024,512]{1,0:T(8,128)}), f32[32,512]{1,0:T(8,128)}) %reduce-scatter.25.cloned.1.call-update) | async-done | bytes 65552 | tf_op jit(solution)/shard_map/reduce_scatter | solution.py:398
  1818.1 134.9 %reduce-scatter.23.cloned.1.call-done = f32[32,512]{1,0:T(8,128)} async-done(((f32[1024,512]{1,0:T(8,128)}), f32[32,512]{1,0:T(8,128)}) %reduce-scatter.23.cloned.1.call-update) | async-done | bytes 65552 | tf_op jit(solution)/shard_map/reduce_scatter | solution.py:397
  1953.1 139.3 %reduce-scatter.27.cloned.1.call-done = f32[32,1024]{1,0:T(8,128)} async-done(((f32[1024,1024]{1,0:T(8,128)}), f32[32,1024]{1,0:T(8,128)}) %reduce-scatter.27.cloned.1.call-update) | async-done | bytes 131088 | tf_op jit(solution)/shard_map/reduce_scatter | solution.py:399
  2092.4 139.8 %reduce-scatter.21.cloned.1.call-done = f32[32,1024]{1,0:T(8,128)} async-done(((f32[1024,1024]{1,0:T(8,128)}), f32[32,1024]{1,0:T(8,128)}) %reduce-scatter.21.cloned.1.call-update) | async-done | bytes 131088 | tf_op jit(solution)/shard_map/reduce_scatter | solution.py:396
  (597 shorter events, 557.9 us)
Async XLA Ops:
  7.2 71.3 %all-gather.7.cloned.1.call-start = ((), (), s32[]{:S(2)}) async-start(), calls=%async_computation.21 | async-start | bytes 1179648 | tf_op jit(solution)/shard_map/all_gather | solution.py:229
  47.3 50.1 %all-gather.5.cloned.1.call-start = ((), (), s32[]{:S(2)}) async-start(), calls=%async_computation.20 | async-start | bytes 1179648 | tf_op jit(solution)/shard_map/all_gather | solution.py:230
  71.3 501.5 %copy-start.36 = (pred[128,1024]{0,1:T(8,128)(4,1)}, pred[128,1024]{0,1:T(8,128)(4,1)S(1)}, u32[]{:S(2)}) copy-start(pred[128,1024]{0,1:T(8,128)(4,1)S(1)} %get-tuple-element.474) | copy-start | bytes 393220
  107.5 137.4 %copy-start.28 = (bf16[128,1024]{1,0:T(8,128)(2,1)}, bf16[128,1024]{1,0:T(8,128)(2,1)S(1)}, u32[]{:S(2)}) copy-start(bf16[128,1024]{1,0:T(8,128)(2,1)S(1)} %multiply_convert_fusion.7) | copy-start | bytes 786436
  235.2 96.5 %all-to-all-start.1 = ((bf16[8,256,1024]{2,0,1:T(8,128)(2,1)}), bf16[8,256,1024]{2,0,1:T(8,128)(2,1)}, u32[]{:S(2)}, u32[]{:S(2)}) async-start(bf16[8,256,1024]{2,0,1:T(8,128)(2,1)} %copy.203), calls=%async_computation.1 | async-start | bytes 8388608 | tf_op jit(solution)/shard_map/all_to_all | solution.py:265
  361.3 107.5 %copy-start.57 = (f32[128,8]{1,0:T(8,128)}, f32[128,8]{1,0:T(8,128)S(1)}, u32[]{:S(2)}) copy-start(f32[128,8]{1,0:T(8,128)S(1)} %reduce_sum.277) | copy-start | bytes 12292
  511.1 95.7 %all-to-all-start.5 = ((bf16[8,256,1024]{2,0,1:T(8,128)(2,1)}), bf16[8,256,1024]{2,0,1:T(8,128)(2,1)}, u32[]{:S(2)}, u32[]{:S(2)}) async-start(bf16[8,256,1024]{2,0,1:T(8,128)(2,1)} %copy.221), calls=%async_computation.5 | async-start | bytes 8388608 | tf_op jit(solution)/shard_map/all_to_all | solution.py:312
  517.9 26.8 %all-gather.11.cloned.1.call-start = ((), (), s32[]{:S(2)}) async-start(), calls=%async_computation.23 | async-start | bytes 1179648 | tf_op jit(solution)/shard_map/all_gather | solution.py:229
  520.4 50.2 %all-gather.9.cloned.1.call-start = ((), (), s32[]{:S(2)}) async-start(), calls=%async_computation.22 | async-start | bytes 1179648 | tf_op jit(solution)/shard_map/all_gather | solution.py:230
  771.4 95.9 %all-to-all-start.3 = ((bf16[8,256,1024]{2,0,1:T(8,128)(2,1)}), bf16[8,256,1024]{2,0,1:T(8,128)(2,1)}, u32[]{:S(2)}, u32[]{:S(2)}) async-start(bf16[8,256,1024]{2,0,1:T(8,128)(2,1)} %copy.218), calls=%async_computation.3 | async-start | bytes 8388608 | tf_op jit(solution)/shard_map/all_to_all | solution.py:265
  1048.2 95.7 %all-to-all-start.7 = ((bf16[8,256,1024]{2,0,1:T(8,128)(2,1)}), bf16[8,256,1024]{2,0,1:T(8,128)(2,1)}, u32[]{:S(2)}, u32[]{:S(2)}) async-start(bf16[8,256,1024]{2,0,1:T(8,128)(2,1)} %copy.228), calls=%async_computation.7 | async-start | bytes 8388608 | tf_op jit(solution)/shard_map/all_to_all | solution.py:312
  1055.0 249.4 %reduce-scatter.39.cloned.1.call-start = ((), (), s32[]{:S(2)}) async-start(), calls=%async_computation.33 | async-start | bytes 1179648
  1056.0 119.7 %copy-start.79 = (f32[128,1,32]{2,1,0:T(1,128)}, f32[128,1,32]{2,1,0:T(1,128)S(1)}, u32[]{:S(2)}) copy-start(f32[128,1,32]{2,1,0:T(1,128)S(1)} %fusion.64) | copy-start | bytes 49156
  1189.2 118.0 %reduce-scatter.43.cloned.1.call-start = ((), (), s32[]{:S(2)}) async-start(), calls=%async_computation.35 | async-start | bytes 1179648
  1199.2 111.7 %reduce-scatter.41.cloned.1.call-start = ((), (), s32[]{:S(2)}) async-start(), calls=%async_computation.34 | async-start | bytes 1179648
  1213.0 131.4 %reduce-scatter.37.cloned.1.call-start = ((), (), s32[]{:S(2)}) async-start(), calls=%async_computation.32 | async-start | bytes 1179648
  1226.9 194.3 %reduce-scatter.35.cloned.1.call-start = ((), (), s32[]{:S(2)}) async-start(), calls=%async_computation.31 | async-start | bytes 9437184 | tf_op jit(solution)/shard_map/reduce_scatter | solution.py:410
  1252.1 243.3 %reduce-scatter.33.cloned.1.call-start = ((), (), s32[]{:S(2)}) async-start(), calls=%async_computation.30 | async-start | bytes 9437184 | tf_op jit(solution)/shard_map/reduce_scatter | solution.py:407
  1276.6 293.6 %reduce-scatter.31.cloned.1.call-start = ((), (), s32[]{:S(2)}) async-start(), calls=%async_computation.29 | async-start | bytes 9437184 | tf_op jit(solution)/shard_map/reduce_scatter | solution.py:404
  1301.6 381.3 %reduce-scatter.29.cloned.1.call-start = ((), (), s32[]{:S(2)}) async-start(), calls=%async_computation.28 | async-start | bytes 540672 | tf_op jit(solution)/shard_map/reduce_scatter | solution.py:401
  1304.3 513.8 %reduce-scatter.25.cloned.1.call-start = ((), (), s32[]{:S(2)}) async-start(), calls=%async_computation.26 | async-start | bytes 2162688 | tf_op jit(solution)/shard_map/reduce_scatter | solution.py:398
  1310.8 642.3 %reduce-scatter.23.cloned.1.call-start = ((), (), s32[]{:S(2)}) async-start(), calls=%async_computation.25 | async-start | bytes 2162688 | tf_op jit(solution)/shard_map/reduce_scatter | solution.py:397
  1348.2 744.2 %reduce-scatter.27.cloned.1.call-start = ((), (), s32[]{:S(2)}) async-start(), calls=%async_computation.27 | async-start | bytes 4325376 | tf_op jit(solution)/shard_map/reduce_scatter | solution.py:399
  1352.8 879.3 %reduce-scatter.21.cloned.1.call-start = ((), (), s32[]{:S(2)}) async-start(), calls=%async_computation.24 | async-start | bytes 4325376 | tf_op jit(solution)/shard_map/reduce_scatter | solution.py:396
  (123 other events, 2142.9 us)
Sparse Core Ops, SparseCore 0:
  47.4 23.8 all-gather.6
  73.8 23.4 all-gather.4
  521.1 23.5 all-gather.10
  547.0 23.4 all-gather.8
  1189.3 36.9 reduce-scatter.38
  1229.4 36.0 reduce-scatter.42
  1268.6 35.9 reduce-scatter.40
  1308.4 35.9 reduce-scatter.36
  1347.9 72.4 reduce-scatter.34
  1424.1 71.2 reduce-scatter.32
  1498.9 71.2 reduce-scatter.30
  1572.9 109.9 reduce-scatter.28
  1685.8 132.2 reduce-scatter.24
  1820.9 132.1 reduce-scatter.22
  1955.8 136.5 reduce-scatter.26
  2095.1 137.0 reduce-scatter.20
where the time goes:
time: 2280 us; the launch traced here: 2240 us
  waiting for transfers between devices  1170 us (51%)
  blocking collectives  442 us (19%)
  matrix products  271 us (12%)
  local copies, waits for them, and re-layouts  222 us (10%)
  other arithmetic  86.2 us (4%)
  starting transfers between devices  29.6 us (1%)
    all_to_all x2, blocking collectives, per_device(): lax.all_to_all(grad_outgoing, 'ep', split_axis=0, concat_axis=1, tiled=True)  197 us
    all_to_all x2, blocking collectives, per_device(): lax.all_to_all(outgoing, 'ep', split_axis=0, concat_axis=1, tiled=True)  196 us
    all_to_all x2, waiting for transfers between devices, per_device(): lax.all_to_all(expert_out, 'ep', split_axis=1, concat_axis=0, tiled=True)  171 us
    reduce_scatter x1, waiting for transfers between devices, per_device(): lax.psum_scatter(grad_w_query, ('ep', 'dp'), scatter_dimension=0, tiled=T...  140 us
    reduce_scatter x1, waiting for transfers between devices, per_device(): lax.psum_scatter(grad_w_out, ('ep', 'dp'), scatter_dimension=0, tiled=True)  139 us
    reduce_scatter x1, waiting for transfers between devices, per_device(): lax.psum_scatter(grad_w_value, ('ep', 'dp'), scatter_dimension=0, tiled=T...  135 us
    reduce_scatter x1, waiting for transfers between devices, per_device(): lax.psum_scatter(grad_w_key, ('ep', 'dp'), scatter_dimension=0, tiled=True)  135 us
    all_to_all x2, waiting for transfers between devices, per_device(): lax.all_to_all(grad_slots, 'ep', split_axis=1, concat_axis=0, tiled=True)  113 us
  transfers between devices with their start and end apart: 20, of which 15 were waited for; matrix products, arithmetic and copies ran while one was open for 10% of the time, Pallas kernels for 0%

commit v1 on v0

v1 whole, which is shorter than its diff:
```python
import functools

import jax
import jax.numpy as jnp
from jax import lax
from jax.experimental import pallas as pl
from jax.experimental.pallas import tpu as pltpu
from jax.sharding import PartitionSpec as P

HEADS = 16
KV_HEADS = 8
HEAD_DIM = 64
EXPERTS = 32
CAP = 64
EPSILON = 1e-06
ROPE_BASE = 10000.0
MASKED = -1e30
HIGHEST = lax.Precision.HIGHEST
MESH = pl.DeviceIdType.MESH
BF16 = jnp.bfloat16
F32 = jnp.float32
VMEM = pl.BlockSpec(memory_space=pltpu.VMEM)
ANY = pl.BlockSpec(memory_space=pl.ANY)
DMA = pltpu.SemaphoreType.DMA


def bit_count(n):
    return n.bit_length() - 1


def masks(bits):
    out = [0]
    for b in bits:
        out = out + [m | (1 << b) for m in out]
    return out


def gather_orders(n):
    bits = list(range(bit_count(n)))
    return (bits[1:] + bits[:1], bits[:0:-1] + bits[:1])


def greet(ep, dp, ne, nd):
    barrier = pltpu.get_barrier_semaphore()
    for k in range(1, ne):
        pl.semaphore_signal(
            barrier, inc=1, device_id={"ep": lax.rem(ep + k, ne)}, device_id_type=MESH
        )
    for b in range(bit_count(nd)):
        pl.semaphore_signal(
            barrier, inc=1, device_id={"dp": jnp.bitwise_xor(dp, 1 << b)}, device_id_type=MESH
        )
    pl.semaphore_wait(barrier, ne - 1 + bit_count(nd))


def remote(src, dst, send, recv, where):
    return pltpu.make_async_remote_copy(
        src_ref=src, dst_ref=dst, send_sem=send, recv_sem=recv, device_id=where, device_id_type=MESH
    )


def gather_body(ne, nd, n_dp, n_ep, *refs):
    n_in = n_dp + n_ep
    ins, outs, sems = refs[:n_in], refs[n_in : 2 * n_in], refs[2 * n_in :]
    ep, dp = lax.axis_index("ep"), lax.axis_index("dp")
    own_sem, dp_send, dp_recv, ep_send, ep_recv = sems
    greet(ep, dp, ne, nd)
    own = []
    for a in range(n_in):
        me = dp if a < n_dp else ep
        copy = pltpu.make_async_copy(ins[a], outs[a].at[me], own_sem.at[a])
        copy.start()
        own.append(copy)

    def dp_step(t):
        copies = []
        for a in range(n_dp):
            order = gather_orders(nd)[a % 2]
            for j, m in enumerate(masks(order[:t])):
                block = jnp.bitwise_xor(dp, m)
                src = ins[a] if m == 0 else outs[a].at[block]
                k = (1 << t) - 1 + j
                copies.append(
                    remote(
                        src,
                        outs[a].at[block],
                        dp_send.at[a, k],
                        dp_recv.at[a, k],
                        {"dp": jnp.bitwise_xor(dp, 1 << order[t])},
                    )
                )
        for c in copies:
            c.start()
        return copies

    def ep_copy(a, s, way):
        shard = lax.rem(ep - way * s + ne, ne)
        src = ins[n_dp + a] if s == 0 else outs[n_dp + a].at[shard]
        k = 0 if way == 1 else 1
        return remote(
            src,
            outs[n_dp + a].at[shard],
            ep_send.at[a, k, s],
            ep_recv.at[a, k, s],
            {"ep": lax.rem(ep + way + ne, ne)},
        )

    def sends(s, way):
        if way == 1:
            return (ep >= s) & (ep < ne - 1)
        return (ep + s <= ne - 1) & (ep >= 1)

    def receives(s, way):
        if way == 1:
            return ep >= 1 + s
        return ep + 1 + s <= ne - 1

    def ep_start(s):
        for a in range(n_ep):
            for way in (1, -1):

                @pl.when(sends(s, way))
                def _(a=a, way=way):
                    ep_copy(a, s, way).start()

    def ep_wait(s):
        for a in range(n_ep):
            for way in (1, -1):

                @pl.when(receives(s, way))
                def _(a=a, way=way):
                    ep_copy(a, s, way).wait_recv()

    dp_steps = bit_count(nd) if n_dp else 0
    ep_steps = ne - 1 if n_ep else 0
    started = []
    for t in range(max(dp_steps, ep_steps) + 1):
        if 0 < t <= dp_steps:
            for c in started[-1]:
                c.wait_recv()
        if t < dp_steps:
            started.append(dp_step(t))
        if 0 < t <= ep_steps:
            ep_wait(t - 1)
        if t < ep_steps:
            ep_start(t)
    for group in started:
        for c in group:
            c.wait_send()
    for s in range(ep_steps):
        for a in range(n_ep):
            for way in (1, -1):

                @pl.when(sends(s, way))
                def _(a=a, s=s, way=way):
                    ep_copy(a, s, way).wait_send()

    for c in own:
        c.wait()


def gather(ne, nd, dp_arrays, ep_arrays, collective):
    arrays = list(dp_arrays) + list(ep_arrays)
    counts = [nd] * len(dp_arrays) + [ne] * len(ep_arrays)
    a, b = max(len(dp_arrays), 1), max(len(ep_arrays), 1)
    return pl.pallas_call(
        functools.partial(gather_body, ne, nd, len(dp_arrays), len(ep_arrays)),
        out_shape=[
            jax.ShapeDtypeStruct((n,) + v.shape, v.dtype) for n, v in zip(counts, arrays)
        ],
        in_specs=[ANY] * len(arrays),
        out_specs=[ANY] * len(arrays),
        scratch_shapes=[
            DMA((len(arrays),)),
            DMA((a, nd - 1)),
            DMA((a, nd - 1)),
            DMA((b, 2, ne - 1)),
            DMA((b, 2, ne - 1)),
        ],
        compiler_params=pltpu.CompilerParams(
            collective_id=collective, has_side_effects=True, vmem_limit_bytes=8 * 2**20
        ),
    )(*arrays)


def reduce_body(ne, nd, n_dp, n_ep, n_swap, *refs):
    n_in = n_dp + n_ep + n_swap
    ins, outs = refs[:n_in], refs[n_in : 2 * n_in]
    rest = refs[2 * n_in :]
    n_sum = n_dp + n_ep
    held = rest[:n_sum]
    landing = rest[n_sum : 2 * n_sum]
    in_sem, dp_send, dp_recv, ep_send, ep_recv, swap_send, swap_recv = rest[2 * n_sum :]
    ep, dp = lax.axis_index("ep"), lax.axis_index("dp")
    loads = []
    for a in range(n_sum):
        copy = pltpu.make_async_copy(ins[a], held[a], in_sem.at[a])
        copy.start()
        loads.append(copy)
    greet(ep, dp, ne, nd)
    swaps = []
    for a in range(n_swap):
        src, dst = ins[n_sum + a], outs[n_sum + a]
        copy = pltpu.make_async_copy(src.at[ep], dst.at[ep], in_sem.at[n_sum + a])
        copy.start()
        loads.append(copy)
        for k in range(1, ne):
            to = lax.rem(ep + k, ne)
            copy = remote(
                src.at[to], dst.at[ep], swap_send.at[a, k - 1], swap_recv.at[a, k - 1], {"ep": to}
            )
            copy.start()
            swaps.append(copy)
    for c in loads:
        c.wait()

    def add(a, block, arrived):
        held[a][block] = (held[a][block].astype(F32) + arrived.astype(F32)).astype(held[a].dtype)

    nb = bit_count(nd)

    def dp_parts(a, t):
        order = gather_orders(nd)[a % 2][::-1]
        bit, left = order[t], order[t + 1 :]
        first = sum(1 << (nb - 1 - i) for i in range(t))
        return bit, [(first + j, m) for j, m in enumerate(masks(left))]

    def dp_copies(a, t):
        bit, parts = dp_parts(a, t)
        partner = jnp.bitwise_xor(dp, 1 << bit)
        return [
            (
                m,
                k,
                remote(
                    held[a].at[jnp.bitwise_xor(partner, m)],
                    landing[a].at[k],
                    dp_send.at[a, k],
                    dp_recv.at[a, k],
                    {"dp": partner},
                ),
            )
            for k, m in parts
        ]

    def ep_copy(a, s, way):
        dest = ne - 1 - s if way == 1 else s
        k = 0 if way == 1 else 1
        return remote(
            held[n_dp + a].at[dest],
            landing[n_dp + a].at[k, s],
            ep_send.at[a, k, s],
            ep_recv.at[a, k, s],
            {"ep": lax.rem(ep + way + ne, ne)},
        )

    def ep_sends(s, way):
        return ep < ne - 1 - s if way == 1 else ep > s

    def ep_gets(s, way):
        return (
            (ep >= 1) & (ep <= ne - 1 - s) if way == 1 else (ep <= ne - 2) & (ep >= s)
        )

    dp_steps = nb if n_dp else 0
    ep_steps = ne - 1 if n_ep else 0
    started = []
    for t in range(max(dp_steps + 1, ep_steps)):
        if t < ep_steps:
            for a in range(n_ep):
                for way in (1, -1):

                    @pl.when(ep_gets(t, way))
                    def _(a=a, way=way):
                        ep_copy(a, t, way).wait_recv()
                        dest = ne - 1 - t if way == 1 else t
                        add(n_dp + a, dest, landing[n_dp + a][0 if way == 1 else 1, t])

                    @pl.when(ep_sends(t, way))
                    def _(a=a, way=way):
                        ep_copy(a, t, way).start()

        if 0 < t <= dp_steps:
            for a, group in started[-1]:
                for m, k, c in group:
                    c.wait_recv()
                    add(a, jnp.bitwise_xor(dp, m), landing[a][k])
        if t < dp_steps:
            started.append([(a, dp_copies(a, t)) for a in range(n_dp)])
            for a, group in started[-1]:
                for m, k, c in group:
                    c.start()
    for a in range(n_dp):
        outs[a][...] = held[a][dp]
    for a in range(n_ep):
        outs[n_dp + a][...] = held[n_dp + a][ep]
    for groups in started:
        for a, group in groups:
            for m, k, c in group:
                c.wait_send()
    for s in range(ep_steps):
        for a in range(n_ep):
            for way in (1, -1):

                @pl.when(ep_sends(s, way))
                def _(a=a, s=s, way=way):
                    ep_copy(a, s, way).wait_send()

    for c in swaps:
        c.wait()


def reduce(ne, nd, dp_arrays, ep_arrays, swap_arrays, collective):
    sums = list(dp_arrays) + list(ep_arrays)
    landing = [(nd - 1,) + v.shape[1:] for v in dp_arrays]
    landing += [(2, ne - 1) + v.shape[1:] for v in ep_arrays]
    a, b, c = (max(len(v), 1) for v in (dp_arrays, ep_arrays, swap_arrays))
    return pl.pallas_call(
        functools.partial(
            reduce_body, ne, nd, len(dp_arrays), len(ep_arrays), len(swap_arrays)
        ),
        out_shape=[jax.ShapeDtypeStruct(v.shape[1:], v.dtype) for v in sums]
        + [jax.ShapeDtypeStruct(v.shape, v.dtype) for v in swap_arrays],
        in_specs=[ANY] * (len(sums) + len(swap_arrays)),
        out_specs=[VMEM] * len(sums) + [ANY] * len(swap_arrays),
        scratch_shapes=[pltpu.VMEM(v.shape, v.dtype) for v in sums]
        + [pltpu.VMEM(s, v.dtype) for s, v in zip(landing, sums)]
        + [
            DMA((len(sums) + len(swap_arrays),)),
            DMA((a, nd - 1)),
            DMA((a, nd - 1)),
            DMA((b, 2, ne - 1)),
            DMA((b, 2, ne - 1)),
            DMA((c, ne - 1)),
            DMA((c, ne - 1)),
        ],
        compiler_params=pltpu.CompilerParams(
            collective_id=collective, has_side_effects=True, vmem_limit_bytes=48 * 2**20
        ),
    )(*sums, *swap_arrays)


def dot(a, b, dims=((1,), (0,))):
    return lax.dot_general(a, b, (dims, ((), ())), preferred_element_type=F32)


def expert_body(
    blocks,
    rows,
    half,
    core_ref,
    normed_ref,
    cot_ref,
    probs_ref,
    gate_ref,
    up_ref,
    down_ref,
    mix_ref,
    grad_ref,
    dots_ref,
    keep_gate,
    send_gate,
    keep_up,
    send_up,
    keep_down,
    send_down,
    rows_in,
    cots_in,
    picks,
    weights,
    first,
    second,
    load_sem,
):
    e = pl.program_id(0)
    count = pl.num_programs(0)

    def block_at(s):
        return pl.ds(pl.multiple_of(s * rows, rows), rows)

    def load(s, k):
        src, dst = ((normed_ref, first), (cot_ref, second))[k]
        return pltpu.make_async_copy(src.at[block_at(s)], dst.at[block_at(s)], load_sem.at[k, s])

    def store(s, k):
        src, dst = ((first, mix_ref), (second, grad_ref))[k]
        return pltpu.make_async_copy(src.at[block_at(s)], dst.at[block_at(s)], load_sem.at[k, s])

    @pl.when(e == 0)
    def _():
        before = lax.broadcasted_iota(jnp.int32, (rows, rows), 0)
        after = lax.broadcasted_iota(jnp.int32, (rows, rows), 1)
        earlier = (before < after).astype(BF16)
        n_exp = rows_in.shape[1]
        slot = lax.broadcasted_iota(jnp.int32, (n_exp, CAP, rows), 1)

        @pl.loop(0, blocks)
        def _(s):
            load(s, 0).start()
            load(s, 1).start()

        @pl.loop(0, blocks)
        def _(s):
            at = block_at(s)
            probs = probs_ref[s]
            hit = probs >= 0.0
            rank = dot(hit.astype(BF16), earlier)
            rank = jnp.where(hit, rank, -1.0).astype(jnp.int32)
            pick = jnp.broadcast_to(rank[:, None, :], (n_exp, CAP, rows)) == slot
            pick_f = pick.astype(F32)
            share = jnp.sum(pick_f * probs[:, None, :], axis=2, keepdims=True)
            weights[s] = share
            flat = pick_f.reshape(n_exp * CAP, rows).astype(BF16)
            picks[s] = flat
            load(s, 0).wait()
            load(s, 1).wait()
            rows_in[s] = (
                dot(flat, first[at, :]).astype(BF16).reshape(n_exp, CAP, normed_ref.shape[1])
            )
            cots_in[s] = (
                dot(flat, second[at, :]).astype(BF16).reshape(n_exp, CAP, cot_ref.shape[1])
            )

    width = normed_ref.shape[1]
    x = rows_in[:, e].reshape(blocks * CAP, width)
    c = cots_in[:, e].reshape(blocks * CAP, width)
    p = weights[:, e].reshape(blocks * CAP, 1)
    w_gate, w_up, w_down = gate_ref[0], up_ref[0], down_ref[0]
    gate_pre = dot(x, w_gate)
    up_pre = dot(x, w_up)
    sigma = jax.nn.sigmoid(gate_pre)
    silu = gate_pre * sigma
    hidden = (silu * up_pre).astype(BF16)
    out = dot(hidden, w_down) * p
    back = dot(c, w_down, ((1,), (1,)))
    wide = hidden.astype(F32)
    pair = jnp.sum(wide * back, axis=1, keepdims=True)
    back = back * p
    grad_up = (back * silu).astype(BF16)
    grad_gate = (back * up_pre * (sigma * (1.0 + gate_pre * (1.0 - sigma)))).astype(BF16)
    scaled = (wide * p).astype(BF16)
    grad_x = dot(grad_gate, w_gate, ((1,), (1,))) + dot(grad_up, w_up, ((1,), (1,)))

    flat = picks[:, pl.ds(pl.multiple_of(e * CAP, CAP), CAP), :].astype(F32)
    dots_ref[0] = jnp.sum(flat * pair.reshape(blocks, CAP, 1), axis=1)

    def split(value, keep, send):
        value = value.astype(BF16)
        n, r = half * 2, value.shape[0] // (half * 2)
        value = value.reshape(n, r, value.shape[1])

        @pl.when(core_ref[0] == 0)
        def _():
            for i in range(half):
                keep[i, 0] = value[2 * i]
                send[i, 0] = value[2 * i + 1]

        @pl.when(core_ref[0] == 1)
        def _():
            for i in range(half):
                keep[i, 0] = value[2 * i + 1]
                send[i, 0] = value[2 * i]

    split(dot(scaled, c, ((0,), (0,))), keep_down, send_down)
    split(dot(x, grad_gate, ((0,), (0,))), keep_gate, send_gate)
    split(dot(x, grad_up, ((0,), (0,))), keep_up, send_up)

    rows_in[:, e] = grad_x.astype(BF16).reshape(blocks, CAP, width)
    cots_in[:, e] = out.astype(BF16).reshape(blocks, CAP, width)

    @pl.when(e == count - 1)
    def _():
        n_exp = rows_in.shape[1]

        @pl.loop(0, blocks)
        def _(s):
            at = block_at(s)
            flat = picks[s]
            first[at, :] = dot(
                flat, cots_in[s].reshape(n_exp * CAP, width), ((0,), (0,))
            ).astype(BF16)
            second[at, :] = dot(
                flat, rows_in[s].reshape(n_exp * CAP, width), ((0,), (0,))
            ).astype(BF16)
            store(s, 0).start()
            store(s, 1).start()

        @pl.loop(0, blocks)
        def _(s):
            store(s, 0).wait()
            store(s, 1).wait()


def experts(normed, cot, probs, w_gate, w_up, w_down, rows, nd, core):
    n_exp, width, inner = w_gate.shape
    blocks = normed.shape[0] // rows
    half = nd // 2
    grads = []
    for a, b in ((width, inner), (width, inner), (inner, width)):
        shape = jax.ShapeDtypeStruct((half, n_exp, a // nd, b), BF16)
        spec = pl.BlockSpec((half, 1, a // nd, b), lambda e, *_: (0, e, 0, 0))
        grads += [(shape, spec)] * 2
    one = pl.Buffered(1)
    full = (blocks * rows, width)
    return pl.pallas_call(
        functools.partial(expert_body, blocks, rows, half),
        grid_spec=pltpu.PrefetchScalarGridSpec(
            num_scalar_prefetch=1,
            grid=(n_exp,),
            in_specs=[
                ANY,
                ANY,
                pl.BlockSpec(probs.shape, lambda e, *_: (0, 0, 0), pipeline_mode=one),
                pl.BlockSpec((1, width, inner), lambda e, *_: (e, 0, 0)),
                pl.BlockSpec((1, width, inner), lambda e, *_: (e, 0, 0)),
                pl.BlockSpec((1, inner, width), lambda e, *_: (e, 0, 0)),
            ],
            out_specs=[
                ANY,
                ANY,
                pl.BlockSpec((1, blocks, rows), lambda e, *_: (e, 0, 0)),
            ]
            + [g[1] for g in grads],
            scratch_shapes=[
                pltpu.VMEM((blocks, n_exp, CAP, width), BF16),
                pltpu.VMEM((blocks, n_exp, CAP, width), BF16),
                pltpu.VMEM((blocks, n_exp * CAP, rows), BF16),
                pltpu.VMEM((blocks, n_exp, CAP, 1), F32),
                pltpu.VMEM(full, BF16),
                pltpu.VMEM(full, BF16),
                DMA((2, blocks)),
            ],
        ),
        out_shape=[
            jax.ShapeDtypeStruct(full, BF16),
            jax.ShapeDtypeStruct(full, BF16),
            jax.ShapeDtypeStruct((n_exp, blocks, rows), F32),
        ]
        + [g[0] for g in grads],
        compiler_params=pltpu.CompilerParams(
            vmem_limit_bytes=60 * 2**20, dimension_semantics=("arbitrary",)
        ),
    )(core, normed, cot, probs, w_gate, w_up, w_down)


def rms_scale(values):
    return lax.rsqrt(jnp.mean(values * values, axis=-1, keepdims=True) + EPSILON)


def rotate(values, cosine, sine):
    half = values.shape[-1] // 2
    a, b = values[..., :half], values[..., half:]
    return jnp.concatenate([a * cosine - b * sine, b * cosine + a * sine], axis=-1)


def attend(queries, keys, values, allowed):
    scale = queries.shape[-1] ** (-0.5)
    scores = jnp.einsum("mqkgd,mnkd->mkgqn", queries, keys, preferred_element_type=F32) * scale
    scores = jnp.where(allowed[:, None, None], scores, MASKED)
    top = jnp.max(scores, axis=-1, keepdims=True)
    terms = jnp.exp(scores - top)
    total = jnp.sum(terms, axis=-1, keepdims=True)
    weights = (terms / total).astype(BF16)
    out = jnp.einsum("mkgqn,mnkd->mqkgd", weights, values, preferred_element_type=F32)
    return out, top + jnp.log(total)


def attend_back(queries, grad, log_total, grad_dot, keys, values, allowed):
    scale = queries.shape[-1] ** (-0.5)
    scores = jnp.einsum("mqkgd,mnkd->mkgqn", queries, keys, preferred_element_type=F32) * scale
    scores = jnp.where(allowed[:, None, None], scores, MASKED)
    probs = jnp.exp(scores - log_total)
    grad_prob = jnp.einsum("mqkgd,mnkd->mkgqn", grad, values, preferred_element_type=F32)
    grad_score = (probs * (grad_prob - grad_dot)).astype(BF16)
    grad_query = (
        jnp.einsum("mkgqn,mnkd->mqkgd", grad_score, keys, preferred_element_type=F32) * scale
    )
    grad_key = (
        jnp.einsum("mkgqn,mqkgd->mnkd", grad_score, queries, preferred_element_type=F32) * scale
    )
    grad_value = jnp.einsum(
        "mkgqn,mqkgd->mnkd", probs.astype(BF16), grad, preferred_element_type=F32
    )
    return grad_query, grad_key, grad_value


def halve(values, dp, orders, nb):
    live = list(range(nb - 1, 0, -1))
    for bit in orders:
        axis = live.index(bit)
        mine = jnp.bitwise_and(lax.shift_right_logical(dp, bit), 1)
        kept = lax.dynamic_index_in_dim(values, mine, axis, keepdims=False)
        sent = lax.dynamic_index_in_dim(values, 1 - mine, axis, keepdims=False)
        n = 1 << nb
        arrived = lax.ppermute(sent, "dp", [(i, i ^ (1 << bit)) for i in range(n)])
        values = (kept.astype(F32) + arrived.astype(F32)).astype(BF16)
        live.remove(bit)
    return values


def reduce_expert(keep, send, dp, nd):
    nb = bit_count(nd)
    arrived = lax.ppermute(send, "dp", [(i, i ^ 1) for i in range(nd)])
    values = (keep.astype(F32) + arrived.astype(F32)).astype(BF16)
    values = values.reshape((2,) * (nb - 1) + values.shape[1:])
    half = keep.shape[1] // 2
    first, second = gather_orders(nd)
    out = []
    for part, order in ((0, first), (1, second)):
        piece = lax.slice_in_dim(values, part * half, (part + 1) * half, axis=nb - 1)
        out.append(halve(piece, dp, order[:-1][::-1], nb))
    return jnp.concatenate(out, axis=0).astype(F32)


def per_device(
    tokens,
    segments,
    routes,
    first_gain,
    w_query,
    w_key,
    w_value,
    w_out,
    second_gain,
    w_router,
    w_gate,
    w_up,
    w_down,
    cotangent,
):
    micro, rows, width = tokens.shape
    ne, nd = lax.axis_size("ep"), lax.axis_size("dp")
    ep, dp = lax.axis_index("ep"), lax.axis_index("dp")
    groups = HEADS // KV_HEADS
    length = rows * nd
    kv_width = KV_HEADS * HEAD_DIM
    every = micro * rows
    inputs = tokens.reshape(every, width).astype(F32)
    grad_output = cotangent.reshape(every, width).astype(F32)

    query_pos = dp * rows + jnp.arange(rows, dtype=jnp.int32)
    halfway = HEAD_DIM // 2
    frequency = ROPE_BASE ** (-(jnp.arange(halfway, dtype=F32) * 2.0 / HEAD_DIM))
    angles = query_pos.astype(F32)[:, None] * frequency[None, :]
    cosine = jnp.tile(jnp.cos(angles), (micro, 1))[:, None, :]
    sine = jnp.tile(jnp.sin(angles), (micro, 1))[:, None, :]

    inv_one = rms_scale(inputs)
    normed_one = (inputs * inv_one * first_gain).astype(BF16)
    query_rot = rotate(
        jnp.dot(normed_one, w_query, preferred_element_type=F32).reshape(every, HEADS, HEAD_DIM),
        cosine,
        sine,
    ).astype(BF16)
    key_rot = (
        rotate(
            jnp.dot(normed_one, w_key, preferred_element_type=F32).reshape(
                every, KV_HEADS, HEAD_DIM
            ),
            cosine,
            sine,
        )
        .astype(BF16)
        .reshape(every, kv_width)
    )
    value_own = jnp.dot(normed_one, w_value, preferred_element_type=F32).astype(BF16)

    ids = jnp.arange(128, dtype=jnp.int32)
    counts = jnp.sum((segments[:, 0, :, None] == ids).astype(F32), axis=1)
    counts = jnp.concatenate([counts, jnp.zeros((8 - micro, 128), F32)], axis=0)

    key_all, value_all, count_all, cot_all = gather(
        ne, nd, (key_rot, value_own, counts), (cotangent.reshape(every, width),), 0
    )

    totals = jnp.sum(count_all[:, :micro], axis=0)
    lower = (ids[None, None, :] < segments[:, 0, :, None]).astype(F32)
    starts = jnp.sum(lower * totals[:, None, :], axis=2).astype(jnp.int32)
    key_pos = jnp.arange(length, dtype=jnp.int32)
    allowed = (key_pos[None, None, :] <= query_pos[None, :, None]) & (
        key_pos[None, None, :] >= starts[:, :, None]
    )

    def sequence(gathered):
        return (
            gathered.reshape(nd, micro, rows, kv_width)
            .transpose(1, 0, 2, 3)
            .reshape(micro, length, KV_HEADS, HEAD_DIM)
        )

    keys, values = sequence(key_all), sequence(value_all)
    queries = query_rot.reshape(micro, rows, KV_HEADS, groups, HEAD_DIM)
    attn_sum, log_total = attend(queries, keys, values, allowed)
    attn_low = attn_sum.reshape(every, HEADS * HEAD_DIM).astype(BF16)
    residual = inputs + jnp.dot(attn_low, w_out, preferred_element_type=F32)
    inv_two = rms_scale(residual)
    normed_two = (residual * inv_two * second_gain).astype(BF16)
    logits = jnp.dot(normed_two, w_router, preferred_element_type=F32)
    routing = routes.reshape(every, routes.shape[2])
    chosen = jnp.any(
        routing[:, :, None] == jnp.arange(EXPERTS, dtype=jnp.int32)[None, None, :], axis=1
    )
    masked = jnp.where(chosen, logits, MASKED)
    terms = jnp.where(chosen, jnp.exp(masked - jnp.max(masked, axis=1, keepdims=True)), 0.0)
    gate_probs = terms / jnp.sum(terms, axis=1, keepdims=True)
    marked = jnp.where(chosen, gate_probs, -1.0).T

    normed_all, marked_all = gather(ne, nd, (), (normed_two, marked), 1)
    here = EXPERTS // ne
    probs_here = lax.dynamic_slice_in_dim(marked_all, ep * here, here, axis=1)
    probs_here = (
        probs_here.reshape(ne, here, micro, rows)
        .transpose(0, 2, 1, 3)
        .reshape(ne * micro, here, rows)
    )
    core = jnp.bitwise_and(dp, 1).reshape(1)
    mix, grad_in, pair_dots, *grads = experts(
        normed_all.reshape(ne * every, width),
        cot_all.reshape(ne * every, width),
        probs_here,
        w_gate,
        w_up,
        w_down,
        rows,
        nd,
        core,
    )
    grad_w_gate = reduce_expert(grads[0], grads[1], dp, nd)
    grad_w_up = reduce_expert(grads[2], grads[3], dp, nd)
    grad_w_down = reduce_expert(grads[4], grads[5], dp, nd)

    pair_dots = pair_dots.reshape(here, ne, every).transpose(1, 0, 2)
    grad_back, dots_all = reduce(
        ne, nd, (), (grad_in.reshape(ne, every, width),), (pair_dots,), 2
    )
    pair_dot = dots_all.reshape(EXPERTS, every).T
    grad_logits = gate_probs * (
        pair_dot - jnp.sum(gate_probs * pair_dot, axis=1, keepdims=True)
    )
    grad_w_router = jnp.einsum(
        "td,te->de", normed_two.astype(F32), grad_logits, precision=HIGHEST
    )
    grad_normed_two = (
        jnp.einsum("te,de->td", grad_logits, w_router.astype(F32), precision=HIGHEST)
        + grad_back.astype(F32)
    )
    scaled_two = grad_normed_two * second_gain
    grad_gain_two = jnp.sum(grad_normed_two * residual * inv_two, axis=0)
    grad_residual = (
        grad_output
        + inv_two * scaled_two
        - residual * inv_two**3 * jnp.mean(scaled_two * residual, axis=-1, keepdims=True)
    )
    residual_low = grad_residual.astype(BF16)
    grad_w_out = jnp.einsum("tf,td->fd", attn_low, residual_low, preferred_element_type=F32)
    grad_attn = jnp.einsum("td,fd->tf", residual_low, w_out, preferred_element_type=F32).astype(
        BF16
    )
    grad_attn = grad_attn.reshape(micro, rows, KV_HEADS, groups, HEAD_DIM)
    grad_dot = jnp.sum(grad_attn.astype(F32) * attn_sum, axis=-1).transpose(0, 2, 3, 1)[..., None]
    grad_query_rot, grad_key_all, grad_value_all = attend_back(
        queries, grad_attn, log_total, grad_dot, keys, values, allowed
    )

    def pieces(summed):
        return (
            summed.reshape(micro, nd, rows, kv_width)
            .transpose(1, 0, 2, 3)
            .reshape(nd, every, kv_width)
            .astype(BF16)
        )

    grad_key, grad_value, mix_own = reduce(
        ne,
        nd,
        (pieces(grad_key_all), pieces(grad_value_all)),
        (mix.reshape(ne, every, width),),
        (),
        3,
    )
    output = (residual + mix_own.astype(F32)).astype(BF16).reshape(tokens.shape)
    grad_query_pre = (
        rotate(grad_query_rot.reshape(every, HEADS, HEAD_DIM), cosine, -sine)
        .astype(BF16)
        .reshape(every, HEADS * HEAD_DIM)
    )
    grad_key_pre = (
        rotate(grad_key.astype(F32).reshape(every, KV_HEADS, HEAD_DIM), cosine, -sine)
        .astype(BF16)
        .reshape(every, kv_width)
    )
    grad_value_pre = grad_value

    def weight_grad(grad):
        return jnp.einsum("td,tf->df", normed_one, grad, preferred_element_type=F32)

    grad_w_query = weight_grad(grad_query_pre)
    grad_w_key = weight_grad(grad_key_pre)
    grad_w_value = weight_grad(grad_value_pre)
    grad_normed_one = (
        jnp.einsum("tf,df->td", grad_query_pre, w_query, preferred_element_type=F32)
        + jnp.einsum("tf,df->td", grad_key_pre, w_key, preferred_element_type=F32)
        + jnp.einsum("tf,df->td", grad_value_pre, w_value, preferred_element_type=F32)
    )
    scaled_one = grad_normed_one * first_gain
    grad_gain_one = jnp.sum(grad_normed_one * inputs * inv_one, axis=0)
    grad_tokens = (
        grad_residual
        + inv_one * scaled_one
        - inputs * inv_one**3 * jnp.mean(scaled_one * inputs, axis=-1, keepdims=True)
    )

    small = jnp.concatenate(
        [
            grad_w_router,
            grad_gain_one[:, None],
            grad_gain_two[:, None],
            jnp.zeros((width, 128 - EXPERTS - 2), F32),
        ],
        axis=1,
    )

    def by_owner(grad):
        share = grad.shape[0] // (ne * nd)
        return (
            grad.astype(BF16)
            .reshape(ne, nd, share, grad.shape[1])
            .transpose(1, 0, 2, 3)
            .reshape(nd, ne * share, grad.shape[1])
        )

    dense = reduce(
        ne,
        nd,
        (
            by_owner(jnp.concatenate([grad_w_query, grad_w_key, small], axis=1)),
            by_owner(jnp.concatenate([grad_w_out, grad_w_value], axis=1)),
        ),
        (),
        (),
        4,
    )
    dense = reduce(ne, nd, (), [v.reshape(ne, -1, v.shape[1]) for v in dense], (), 5)
    first, second = (v.astype(F32) for v in dense)
    model = width + kv_width
    return (
        output,
        grad_tokens.reshape(tokens.shape),
        first[:, model + EXPERTS],
        first[:, :width],
        first[:, width:model],
        second[:, width:],
        second[:, :width],
        first[:, model + EXPERTS + 1],
        first[:, model : model + EXPERTS],
        grad_w_gate,
        grad_w_up,
        grad_w_down,
    )


def solution(mesh):
    in_specs = (
        P(None, ("ep", "dp"), None),
        P(None, "ep", "dp"),
        P(None, ("ep", "dp"), None),
        P(),
        P(),
        P(),
        P(),
        P(),
        P(),
        P(),
        P("ep", None, None),
        P("ep", None, None),
        P("ep", None, None),
        P(None, ("ep", "dp"), None),
    )
    out_specs = (
        P(None, ("ep", "dp"), None),
        P(None, ("ep", "dp"), None),
        P(("ep", "dp")),
        P(("ep", "dp"), None),
        P(("ep", "dp"), None),
        P(("ep", "dp"), None),
        P(("ep", "dp"), None),
        P(("ep", "dp")),
        P(("ep", "dp"), None),
        P("ep", "dp", None),
        P("ep", "dp", None),
        P("ep", "dp", None),
    )
    return jax.shard_map(
        per_device, mesh=mesh, in_specs=in_specs, out_specs=out_specs, check_vma=False
    )
```

time: 2280 us -> 735 us (0.32); the launches traced: 2240 us -> 725 us
  waiting for transfers between devices: 1170 us -> 60 us
  Pallas kernels: 0 us -> 448 us
  blocking collectives: 442 us -> 0 us
  matrix products: 271 us -> 66.3 us
  local copies, waits for them, and re-layouts: 222 us -> 86.9 us
  other arithmetic: 86.2 us -> 48.2 us
    reduce_scatter x8 -> x0, waiting for transfers between devices: 802 us -> none  [the longest x1 140 us: per_device(): lax.psum_scatter(grad_w_query, ('ep', 'dp'), scatter_dimension=0, tiled=T...]
    pallas_call x0 -> x7, Pallas kernels: none -> 448 us  [the longest x4 304 us: reduce(): pl.pallas_call(functools.partial(reduce_body, ne, nd, len(dp_arrays), len...]
    all_to_all x4 -> x0, blocking collectives: 392 us -> none  [the longest x2 197 us: per_device(): lax.all_to_all(grad_outgoing, 'ep', split_axis=0, concat_axis=1, tiled=True)]
    all_to_all x4 -> x0, waiting for transfers between devices: 284 us -> none  [the longest x2 171 us: per_device(): lax.all_to_all(expert_out, 'ep', split_axis=1, concat_axis=0, tiled=True)]
    dot_general x64 -> x21, matrix products: 271 us -> 66.3 us  [the longest x1 10.3 us: attend(): jnp.einsum('mqkgd,mnkd->mkgqn', queries, keys, preferred_element_type=F32)]
    gather x26 -> x0, local copies, waits for them, and re-layouts: 104 us -> none  [the longest x2 41.2 us: per_device(): grad_returned[flat_expert, safe_slot]]
    ppermute x0 -> x15, waiting for transfers between devices: none -> 60 us  [the longest x12 60 us: halve(): arrived = lax.ppermute(sent, 'dp', [(i, i ^ 1 << bit) for i in range(n)])]
    all_gather x4 -> x0, waiting for transfers between devices: 51 us -> none  [the longest x2 32.6 us: per_device(): lax.all_gather(value_own, 'dp', axis=0, tiled=True)]
  transfers between devices with their start and end apart: 20 -> 15, of which waited for: 15 -> 6; matrix products, arithmetic and copies ran while one was open for 10% -> 16% of each run, Pallas kernels for 0% -> 42%
where the time goes in v1:
time: 735 us; the launch traced here: 725 us
  Pallas kernels  448 us (61%)
  local copies, waits for them, and re-layouts  86.9 us (12%)
  matrix products  66.3 us (9%)
  waiting for transfers between devices  60 us (8%)
  other arithmetic  48.2 us (7%)
  starting transfers between devices  13.3 us (2%)
    pallas_call x4, Pallas kernels, reduce(): pl.pallas_call(functools.partial(reduce_body, ne, nd, len(dp_arrays), len...  304 us
    pallas_call x2, Pallas kernels, gather(): pl.pallas_call(functools.partial(gather_body, ne, nd, len(dp_arrays), len...  76.5 us
    pallas_call x1, Pallas kernels, experts(): pl.pallas_call(functools.partial(expert_body, blocks, rows, half), grid_s...  68.1 us
    ppermute x12, waiting for transfers between devices, halve(): arrived = lax.ppermute(sent, 'dp', [(i, i ^ 1 << bit) for i in range(n)])  60 us
    unnamed x152, local copies, waits for them, and re-layouts  24.5 us
  transfers between devices with their start and end apart: 15, of which 6 were waited for; matrix products, arithmetic and copies ran while one was open for 16% of the time, Pallas kernels for 42%

profile of v1, /device:TPU:10, one launch (start us, length us, event | category | flops | bytes accessed | tf_op | source)
XLA Modules:
  0.0 725.2 jit_solution(15808826867233176723)
XLA Ops:
  11.2 38.2 %shard_map.229 = (bf16[8,256,512]{2,1,0:T(8,128)(2,1)S(1)}, bf16[8,256,512]{2,1,0:T(8,128)(2,1)S(1)}, f32[8,8,128]{2,1,0:T(8,128)S(1)}, bf16[4,256,1024]{2,1,0:T(8,128)(2,1)S(1)}) custom-call(bf16[256,512]{1,0:T(8,128)(2,1)S(1)} %copy.87.refs_0_, bf16[256,512]{1,0:T(8,128)(2,1)S(1)} %convolution_convert_fusion.5.refs_1_, f32[8,128]{1,0:T(8,128)S(1)} %concatenate.51.refs_2_, ...), custom_call_target="tpu_custom_call" | custom-call | tf_op jit(solution)/shard_map/pallas_call | solution.py:166
  54.4 4.3 copy.89
  58.7 4.2 reshape.460
  71.9 4.4 copy.88
  76.2 4.2 reshape.461
  81.6 10.3 %fusion.4 = (f32[2,8,2,128]{3,2,1,0:T(2,128)S(1)}, f32[2,8,1024,128,2]{3,2,4,1,0:T(8,128)}) fusion(pred[2,128,1024]{1,2,0:T(8,128)(4,1)S(1)} %fusion.49, bf16[2,128,8,2,64]{1,4,3,2,0:T(8,128)(2,1)S(1)} %copy_dynamic-update-slice_fusion, bf16[2,1024,8,64,1]{1,3,2,0,4:T(8,128)(2,1)} %reshape.460), kind=kOutput, calls=%fused_computation.9 | convolution fusion | flops 549449728 | bytes 19677184 | tf_op jit(solution)/shard_map/mqkgd,mnkd->mkgqn/dot_general | solution.py:558
  91.9 9.2 %fusion.2 = f32[2,8,2,128]{3,2,1,0:T(2,128)S(1)} fusion(f32[2,8,1024,128,2]{3,2,4,1,0:T(8,128)} %get-tuple-element.89, f32[2,8,2,128]{3,2,1,0:T(2,128)S(1)} %get-tuple-element.88, pred[2,128,1024]{1,2,0:T(8,128)(4,1)S(1)} %fusion.49), kind=kLoop, calls=%fused_computation.7 | loop fusion | flops 16773120 | bytes 17072128 | tf_op jit(solution)/shard_map/reduce_sum | solution.py:562
  101.8 10.1 %fusion.79 = (bf16[2,128,8,2,64]{1,4,3,2,0:T(8,128)(2,1)S(1)}, f32[2,128,8,2,64]{1,4,3,2,0:T(8,128)}) fusion(f32[2,8,1024,128,2]{3,2,4,1,0:T(8,128)} %get-tuple-element.89, f32[2,8,2,128]{3,2,1,0:T(2,128)S(1)} %fusion.2, f32[2,8,2,128]{3,2,1,0:T(2,128)S(1)} %get-tuple-element.88, pred[2,128,1024]{1,2,0:T(8,128)(4,1)S(1)} %fusion.49, ...), kind=kOutput, calls=%fused_computation.174 | convolution fusion | flops 558104576 | bytes 20742144 | tf_op jit(solution)/shard_map/mkgqn,mnkd->mqkgd/dot_general | solution.py:564
  115.1 38.3 %shard_map.230 = (bf16[4,256,1024]{2,1,0:T(8,128)(2,1)S(1)}, f32[4,32,256]{2,1,0:T(8,128)S(1)}) custom-call(bf16[256,1024]{1,0:T(8,128)(2,1)S(1)} %multiply_convert_fusion.refs_0_, f32[32,256]{1,0:T(8,128)S(1)} %fusion.61.refs_1_), custom_call_target="tpu_custom_call" | custom-call | tf_op jit(solution)/shard_map/pallas_call | solution.py:166
  155.4 68.1 %shard_map.231 = (bf16[1024,1024]{1,0:T(8,128)(2,1)}, bf16[1024,1024]{1,0:T(8,128)(2,1)}, f32[8,8,128]{2,1,0:T(8,128)}, bf16[4,8,128,512]{3,2,1,0:T(8,128)(2,1)}...) custom-call(s32[1]{0:T(128)} %bitcast.21.core_ref, ...), custom_call_target="tpu_custom_call" | custom-call | tf_op jit(solution)/shard_map/pallas_call | solution.py:505
  226.5 104.3 %shard_map.232 = (bf16[256,1024]{1,0:T(8,128)(2,1)S(1)}, f32[4,8,256]{2,1,0:T(8,128)S(1)}) custom-call(bf16[4,256,1024]{2,1,0:T(8,128)(2,1)S(1)} %bitcast.347, f32[4,8,256]{2,1,0:T(8,128)S(1)} %bitcast.352), custom_call_target="tpu_custom_call" | custom-call | tf_op jit(solution)/shard_map/pallas_call | solution.py:318
  337.5 9.8 %bitcast_convert_fusion = bf16[2,8,64,1024]{3,2,1,0:T(8,128)(2,1)S(1)} fusion(bf16[2,128,8,2,64]{1,4,3,2,0:T(8,128)(2,1)S(1)} %copy.97, f32[2,8,1024,128,2]{3,2,4,1,0:T(8,128)} %get-tuple-element.89, f32[2,8,2,128]{3,2,1,0:T(2,128)S(1)} %bitcast.398, pred[2,128,1024]{1,2,0:T(8,128)(4,1)S(1)} %fusion.49), kind=kOutput, calls=%fused_computation.16 | convolution fusion | flops 554696704 | bytes 19677184 | tf_op jit(solution)/shard_map/mkgqn,mqkgd->mnkd/dot_general | solution.py:581
  347.5 9.0 %fusion.1 = bf16[2,8,2,128,1024]{3,4,2,1,0:T(8,128)(2,1)S(1)} fusion(f32[2,8,1024,128,2]{3,2,4,1,0:T(8,128)} %get-tuple-element.89, f32[2,8,2,128]{3,2,1,0:T(2,128)S(1)} %bitcast.397, f32[2,8,2,128]{3,2,1,0:T(2,128)S(1)} %bitcast.399, pred[2,128,1024]{1,2,0:T(8,128)(4,1)S(1)} %fusion.49, bf16[2,128,8,2,64]{1,4,3,2,0:T(8,128)(2,1)S(1)} %copy.97, ...), kind=kOutput, calls=%fused_computation.2 | convolution fusion | flops 562036736 | bytes 28082176 | tf_op jit(solution)/shard_map/mqkgd,mnkd->mkgqn/dot_general | solution.py:573
  371.6 4.3 copy.100
  378.5 96.1 %shard_map.233 = (bf16[256,512]{1,0:T(8,128)(2,1)S(1)}, bf16[256,512]{1,0:T(8,128)(2,1)S(1)}, bf16[256,1024]{1,0:T(8,128)(2,1)S(1)}) custom-call(bf16[8,256,512]{2,1,0:T(8,128)(2,1)S(1)} %bitcast.343, bf16[8,256,512]{2,1,0:T(8,128)(2,1)S(1)} %bitcast.342, bf16[4,256,1024]{2,1,0:T(8,128)(2,1)} %bitcast.376), custom_call_target="tpu_custom_call" | custom-call | tf_op jit(solution)/shard_map/pallas_call | solution.py:318
  504.8 6.7 concatenate.61
  515.6 38.5 %shard_map.234 = (bf16[128,1664]{1,0:T(8,128)(2,1)S(1)}, bf16[128,1536]{1,0:T(8,128)(2,1)S(1)}) custom-call(bf16[8,128,1664]{2,1,0:T(8,128)(2,1)} %bitcast.357, bf16[8,128,1536]{2,1,0:T(8,128)(2,1)S(1)} %bitcast.341), custom_call_target="tpu_custom_call" | custom-call | tf_op jit(solution)/shard_map/pallas_call | solution.py:318
  554.2 65.0 %shard_map.235 = (bf16[32,1664]{1,0:T(8,128)(2,1)S(1)}, bf16[32,1536]{1,0:T(8,128)(2,1)S(1)}) custom-call(bf16[4,32,1664]{2,1,0:T(8,128)(2,1)S(1)} %bitcast.350, bf16[4,32,1536]{2,1,0:T(8,128)(2,1)S(1)} %bitcast.351), custom_call_target="tpu_custom_call" | custom-call | tf_op jit(solution)/shard_map/pallas_call | solution.py:318
  627.1 4.3 add_convert_fusion
  646.7 11.7 %collective-permute-done.11 = bf16[2,4,64,1024]{3,2,1,0:T(8,128)(2,1)} collective-permute-done((bf16[2,4,64,1024]{3,2,1,0:T(8,128)(2,1)S(1)}, bf16[2,4,64,1024]{3,2,1,0:T(8,128)(2,1)}, u32[]{:S(2)}, u32[]{:S(2)}) %collective-permute-start.11) | collective-permute-done | bytes 1048608 | tf_op jit(solution)/shard_map/ppermute | solution.py:595
  663.9 17.0 %collective-permute-done.6 = bf16[2,4,128,512]{3,2,1,0:T(8,128)(2,1)} collective-permute-done((bf16[2,4,128,512]{3,2,1,0:T(8,128)(2,1)S(1)}, bf16[2,4,128,512]{3,2,1,0:T(8,128)(2,1)}, u32[]{:S(2)}, u32[]{:S(2)}) %collective-permute-start.6) | collective-permute-done | bytes 1048608 | tf_op jit(solution)/shard_map/ppermute | solution.py:595
  685.0 18.3 %collective-permute-done.1 = bf16[2,4,128,512]{3,2,1,0:T(8,128)(2,1)S(1)} collective-permute-done((bf16[2,4,128,512]{3,2,1,0:T(8,128)(2,1)S(1)}, bf16[2,4,128,512]{3,2,1,0:T(8,128)(2,1)S(1)}, u32[]{:S(2)}, u32[]{:S(2)}) %collective-permute-start.1) | collective-permute-done | bytes 1048608 | tf_op jit(solution)/shard_map/ppermute | solution.py:595
  706.1 5.9 collective-permute-done.12
  713.0 4.6 collective-permute-done.7
  (295 shorter events, 136.4 us)
Async XLA Ops:
  0.6 111.8 %copy-start = (bf16[1024,1024]{1,0:T(8,128)(2,1)S(1)}, bf16[1024,1024]{1,0:T(8,128)(2,1)}, u32[]{:S(2)}) copy-start(bf16[1024,1024]{1,0:T(8,128)(2,1)} %param.21) | copy-start | bytes 6291460
  155.4 175.5 %copy-start.38 = (f32[256,32]{0,1:T(8,128)S(1)}, f32[256,32]{0,1:T(8,128)}, u32[]{:S(2)}) copy-start(f32[256,32]{0,1:T(8,128)} %copy-done.37) | copy-start | bytes 98308
  155.4 175.5 %copy-start.55 = (f32[256]{0:T(256)S(1)}, f32[256]{0:T(256)}, u32[]{:S(2)}) copy-start(f32[256]{0:T(256)} %copy-done.54) | copy-start | bytes 3076
  155.4 175.5 %copy-start.58 = (f32[256]{0:T(256)S(1)}, f32[256]{0:T(256)}, u32[]{:S(2)}) copy-start(f32[256]{0:T(256)} %copy-done.57) | copy-start | bytes 3076
  155.4 175.6 %copy-start.61 = (f32[256]{0:T(256)S(1)}, f32[256]{0:T(256)}, u32[]{:S(2)}) copy-start(f32[256]{0:T(256)} %copy-done.60) | copy-start | bytes 3076
  223.5 110.3 %copy-start.70 = (f32[256]{0:T(256)S(1)}, f32[256]{0:T(256)}, u32[]{:S(2)}) copy-start(f32[256]{0:T(256)} %get-tuple-element.82) | copy-start | bytes 3076
  223.5 403.6 %collective-permute-start.10 = (bf16[4,8,64,1024]{3,2,1,0:T(8,128)(2,1)}, bf16[4,8,64,1024]{3,2,1,0:T(8,128)(2,1)}, u32[]{:S(2)}, u32[]{:S(2)}) collective-permute-start(bf16[4,8,64,1024]{3,2,1,0:T(8,128)(2,1)} %get-tuple-element.59), channel_id=1, source_target_pairs={{0,1},{1,0},{2,3},{3,2},{4,5},{5,4},{6,7},{7,6},{8,9},{9,8},{10,11... | collective-permute-start | bytes 12582920 | tf_op jit(solution)/shard_map/ppermute | solution.py:603
  223.5 410.9 %collective-permute-start.5 = (bf16[4,8,128,512]{3,2,1,0:T(8,128)(2,1)}, bf16[4,8,128,512]{3,2,1,0:T(8,128)(2,1)}, u32[]{:S(2)}, u32[]{:S(2)}) collective-permute-start(bf16[4,8,128,512]{3,2,1,0:T(8,128)(2,1)} %get-tuple-element.57), channel_id=1, source_target_pairs={{0,1},{1,0},{2,3},{3,2},{4,5},{5,4},{6,7},{7,6},{8,9},{9,8},{10,11... | collective-permute-start | bytes 12582920 | tf_op jit(solution)/shard_map/ppermute | solution.py:603
  224.0 416.9 %collective-permute-start = (bf16[4,8,128,512]{3,2,1,0:T(8,128)(2,1)}, bf16[4,8,128,512]{3,2,1,0:T(8,128)(2,1)}, u32[]{:S(2)}, u32[]{:S(2)}) collective-permute-start(bf16[4,8,128,512]{3,2,1,0:T(8,128)(2,1)} %get-tuple-element.55), channel_id=1, source_target_pairs={{0,1},{1,0},{2,3},{3,2},{4,5},{5,4},{6,7},{7,6},{8,9},{9,8},{10,11... | collective-permute-start | bytes 12582920 | tf_op jit(solution)/shard_map/ppermute | solution.py:603
  224.1 258.4 %copy-start.46 = (f32[256,32]{0,1:T(8,128)}, f32[256,32]{0,1:T(8,128)S(1)}, u32[]{:S(2)}) copy-start(f32[256,32]{0,1:T(8,128)S(1)} %fusion.73) | copy-start | bytes 98308
  226.5 107.2 %copy-start.11 = (f32[256,1024]{1,0:T(8,128)S(1)}, f32[256,1024]{1,0:T(8,128)}, u32[]{:S(2)}) copy-start(f32[256,1024]{1,0:T(8,128)} %copy-done.10) | copy-start | bytes 3145732
  515.6 107.5 %copy-start.67 = (f32[2,128]{1,0:T(2,128)S(1)}, f32[2,128]{1,0:T(2,128)}, u32[]{:S(2)}) copy-start(f32[2,128]{1,0:T(2,128)} %copy-done.66) | copy-start | bytes 3076
  632.2 26.3 %collective-permute-start.11 = (bf16[2,4,64,1024]{3,2,1,0:T(8,128)(2,1)S(1)}, bf16[2,4,64,1024]{3,2,1,0:T(8,128)(2,1)}, u32[]{:S(2)}, u32[]{:S(2)}) collective-permute-start(bf16[2,4,64,1024]{3,2,1,0:T(8,128)(2,1)S(1)} %dynamic-slice_bitcast_fusion.1), channel_id=1, source_target_pairs={{0,4},{1,5},{2,6},{3,7},{4,0},{5,1},{6,2},{7,3},{8,12},{9,13},{10,... | collective-permute-start | bytes 3145736 | tf_op jit(solution)/shard_map/ppermute | solution.py:595
  633.8 27.8 %collective-permute-start.13 = (bf16[2,4,64,1024]{3,2,1,0:T(8,128)(2,1)S(1)}, bf16[2,4,64,1024]{3,2,1,0:T(8,128)(2,1)}, u32[]{:S(2)}, u32[]{:S(2)}) collective-permute-start(bf16[2,4,64,1024]{3,2,1,0:T(8,128)(2,1)S(1)} %dynamic-slice_bitcast_fusion), channel_id=1, source_target_pairs={{0,2},{1,3},{2,0},{3,1},{4,6},{5,7},{6,4},{7,5},{8,10},{9,11},{10,... | collective-permute-start | bytes 3145736 | tf_op jit(solution)/shard_map/ppermute | solution.py:595
  638.6 42.3 %collective-permute-start.6 = (bf16[2,4,128,512]{3,2,1,0:T(8,128)(2,1)S(1)}, bf16[2,4,128,512]{3,2,1,0:T(8,128)(2,1)}, u32[]{:S(2)}, u32[]{:S(2)}) collective-permute-start(bf16[2,4,128,512]{3,2,1,0:T(8,128)(2,1)S(1)} %dynamic-slice_bitcast_fusion.3), channel_id=1, source_target_pairs={{0,4},{1,5},{2,6},{3,7},{4,0},{5,1},{6,2},{7,3},{8,12},{9,13},{10,... | collective-permute-start | bytes 3145736 | tf_op jit(solution)/shard_map/ppermute | solution.py:595
  640.2 43.8 %collective-permute-start.8 = (bf16[2,4,128,512]{3,2,1,0:T(8,128)(2,1)S(1)}, bf16[2,4,128,512]{3,2,1,0:T(8,128)(2,1)S(1)}, u32[]{:S(2)}, u32[]{:S(2)}) collective-permute-start(bf16[2,4,128,512]{3,2,1,0:T(8,128)(2,1)S(1)} %dynamic-slice_bitcast_fusion.2), channel_id=1, source_target_pairs={{0,2},{1,3},{2,0},{3,1},{4,6},{5,7},{6,4},{7,5},{8,10},{9,11},{10,... | collective-permute-start | bytes 3145736 | tf_op jit(solution)/shard_map/ppermute | solution.py:595
  645.1 58.2 %collective-permute-start.1 = (bf16[2,4,128,512]{3,2,1,0:T(8,128)(2,1)S(1)}, bf16[2,4,128,512]{3,2,1,0:T(8,128)(2,1)S(1)}, u32[]{:S(2)}, u32[]{:S(2)}) collective-permute-start(bf16[2,4,128,512]{3,2,1,0:T(8,128)(2,1)S(1)} %dynamic-slice_bitcast_fusion.5), channel_id=1, source_target_pairs={{0,4},{1,5},{2,6},{3,7},{4,0},{5,1},{6,2},{7,3},{8,12},{9,13},{10,... | collective-permute-start | bytes 3145736 | tf_op jit(solution)/shard_map/ppermute | solution.py:595
  658.5 46.7 %collective-permute-start.3 = (bf16[2,4,128,512]{3,2,1,0:T(8,128)(2,1)S(1)}, bf16[2,4,128,512]{3,2,1,0:T(8,128)(2,1)S(1)}, u32[]{:S(2)}, u32[]{:S(2)}) collective-permute-start(bf16[2,4,128,512]{3,2,1,0:T(8,128)(2,1)S(1)} %dynamic-slice_bitcast_fusion.4), channel_id=1, source_target_pairs={{0,2},{1,3},{2,0},{3,1},{4,6},{5,7},{6,4},{7,5},{8,10},{9,11},{10,... | collective-permute-start | bytes 3145736 | tf_op jit(solution)/shard_map/ppermute | solution.py:595
  661.6 50.5 %collective-permute-start.12 = (bf16[4,64,1024]{2,1,0:T(8,128)(2,1)S(1)}, bf16[4,64,1024]{2,1,0:T(8,128)(2,1)S(1)}, u32[]{:S(2)}, u32[]{:S(2)}) collective-permute-start(bf16[4,64,1024]{2,1,0:T(8,128)(2,1)S(1)} %dynamic-slice_bitcast_fusion.7), channel_id=1, source_target_pairs={{0,2},{1,3},{2,0},{3,1},{4,6},{5,7},{6,4},{7,5},{8,10},{9,11},{10,... | collective-permute-start | bytes 1572872 | tf_op jit(solution)/shard_map/ppermute | solution.py:595
  680.9 31.9 %collective-permute-start.14 = (bf16[4,64,1024]{2,1,0:T(8,128)(2,1)S(1)}, bf16[4,64,1024]{2,1,0:T(8,128)(2,1)S(1)}, u32[]{:S(2)}, u32[]{:S(2)}) collective-permute-start(bf16[4,64,1024]{2,1,0:T(8,128)(2,1)S(1)} %dynamic-slice_bitcast_fusion.6), channel_id=1, source_target_pairs={{0,4},{1,5},{2,6},{3,7},{4,0},{5,1},{6,2},{7,3},{8,12},{9,13},{10,... | collective-permute-start | bytes 1572872 | tf_op jit(solution)/shard_map/ppermute | solution.py:595
  684.0 33.6 %collective-permute-start.7 = (bf16[4,128,512]{2,1,0:T(8,128)(2,1)S(1)}, bf16[4,128,512]{2,1,0:T(8,128)(2,1)S(1)}, u32[]{:S(2)}, u32[]{:S(2)}) collective-permute-start(bf16[4,128,512]{2,1,0:T(8,128)(2,1)S(1)} %dynamic-slice_bitcast_fusion.9), channel_id=1, source_target_pairs={{0,2},{1,3},{2,0},{3,1},{4,6},{5,7},{6,4},{7,5},{8,10},{9,11},{10,... | collective-permute-start | bytes 1572872 | tf_op jit(solution)/shard_map/ppermute | solution.py:595
  703.3 14.5 %collective-permute-start.9 = (bf16[4,128,512]{2,1,0:T(8,128)(2,1)S(1)}, bf16[4,128,512]{2,1,0:T(8,128)(2,1)S(1)}, u32[]{:S(2)}, u32[]{:S(2)}) collective-permute-start(bf16[4,128,512]{2,1,0:T(8,128)(2,1)S(1)} %dynamic-slice_bitcast_fusion.8), channel_id=1, source_target_pairs={{0,4},{1,5},{2,6},{3,7},{4,0},{5,1},{6,2},{7,3},{8,12},{9,13},{10,... | collective-permute-start | bytes 1572872 | tf_op jit(solution)/shard_map/ppermute | solution.py:595
  705.2 18.1 %collective-permute-start.2 = (bf16[4,128,512]{2,1,0:T(8,128)(2,1)S(1)}, bf16[4,128,512]{2,1,0:T(8,128)(2,1)S(1)}, u32[]{:S(2)}, u32[]{:S(2)}) collective-permute-start(bf16[4,128,512]{2,1,0:T(8,128)(2,1)S(1)} %dynamic-slice_bitcast_fusion.11), channel_id=1, source_target_pairs={{0,2},{1,3},{2,0},{3,1},{4,6},{5,7},{6,4},{7,5},{8,10},{9,11},{10,... | collective-permute-start | bytes 1572872 | tf_op jit(solution)/shard_map/ppermute | solution.py:595
  712.0 11.4 %collective-permute-start.4 = (bf16[4,128,512]{2,1,0:T(8,128)(2,1)S(1)}, bf16[4,128,512]{2,1,0:T(8,128)(2,1)S(1)}, u32[]{:S(2)}, u32[]{:S(2)}) collective-permute-start(bf16[4,128,512]{2,1,0:T(8,128)(2,1)S(1)} %dynamic-slice_bitcast_fusion.10), channel_id=1, source_target_pairs={{0,4},{1,5},{2,6},{3,7},{4,0},{5,1},{6,2},{7,3},{8,12},{9,13},{10,... | collective-permute-start | bytes 1572872 | tf_op jit(solution)/shard_map/ppermute | solution.py:595
  (63 other events, 676.7 us)

commit v2 on v1

--- a/solution.py
+++ b/solution.py
@@ -159,7 +159,11 @@
         c.wait()
 
 
-def gather(ne, nd, dp_arrays, ep_arrays, collective):
+def cost(us):
+    return pl.CostEstimate(flops=0, bytes_accessed=int(us * 3.0e6), transcendentals=0)
+
+
+def gather(ne, nd, dp_arrays, ep_arrays, collective, us):
     arrays = list(dp_arrays) + list(ep_arrays)
     counts = [nd] * len(dp_arrays) + [ne] * len(ep_arrays)
     a, b = max(len(dp_arrays), 1), max(len(ep_arrays), 1)
@@ -180,6 +184,7 @@
         compiler_params=pltpu.CompilerParams(
             collective_id=collective, has_side_effects=True, vmem_limit_bytes=8 * 2**20
         ),
+        cost_estimate=cost(us),
     )(*arrays)
 
 
@@ -243,42 +248,47 @@
             for k, m in parts
         ]
 
-    def ep_copy(a, s, way):
-        dest = ne - 1 - s if way == 1 else s
+    def ep_copy(a, dest, way):
         k = 0 if way == 1 else 1
         return remote(
             held[n_dp + a].at[dest],
-            landing[n_dp + a].at[k, s],
-            ep_send.at[a, k, s],
-            ep_recv.at[a, k, s],
+            landing[n_dp + a].at[k, dest],
+            ep_send.at[a, k, dest],
+            ep_recv.at[a, k, dest],
             {"ep": lax.rem(ep + way + ne, ne)},
         )
 
-    def ep_sends(s, way):
-        return ep < ne - 1 - s if way == 1 else ep > s
-
-    def ep_gets(s, way):
-        return (
-            (ep >= 1) & (ep <= ne - 1 - s) if way == 1 else (ep <= ne - 2) & (ep >= s)
-        )
+    def ep_turn(t, way):
+        return ep + ne - 1 - t if way == 1 else ep + t - (ne - 1)
+
+    def ep_has(t, way):
+        return ep_turn(t, way) <= ne - 1 if way == 1 else ep_turn(t, way) >= 0
+
+    def ep_inner(way):
+        return ep >= 1 if way == 1 else ep <= ne - 2
+
+    def ep_go(t):
+        for a in range(n_ep):
+            for way in (1, -1):
+                dest = ep_turn(t, way)
+
+                @pl.when(ep_has(t, way) & ep_inner(way))
+                def _(a=a, way=way, dest=dest):
+                    ep_copy(a, dest, way).wait_recv()
+                    add(n_dp + a, dest, landing[n_dp + a][0 if way == 1 else 1, dest])
+
+                if t < ne - 1:
+
+                    @pl.when(ep_has(t, way))
+                    def _(a=a, way=way, dest=dest):
+                        ep_copy(a, dest, way).start()
 
     dp_steps = nb if n_dp else 0
-    ep_steps = ne - 1 if n_ep else 0
+    ep_steps = ne if n_ep else 0
     started = []
     for t in range(max(dp_steps + 1, ep_steps)):
         if t < ep_steps:
-            for a in range(n_ep):
-                for way in (1, -1):
-
-                    @pl.when(ep_gets(t, way))
-                    def _(a=a, way=way):
-                        ep_copy(a, t, way).wait_recv()
-                        dest = ne - 1 - t if way == 1 else t
-                        add(n_dp + a, dest, landing[n_dp + a][0 if way == 1 else 1, t])
-
-                    @pl.when(ep_sends(t, way))
-                    def _(a=a, way=way):
-                        ep_copy(a, t, way).start()
+            ep_go(t)
 
         if 0 < t <= dp_steps:
             for a, group in started[-1]:
@@ -298,22 +308,23 @@
         for a, group in groups:
             for m, k, c in group:
                 c.wait_send()
-    for s in range(ep_steps):
+    for t in range(ep_steps - 1):
         for a in range(n_ep):
             for way in (1, -1):
-
-                @pl.when(ep_sends(s, way))
-                def _(a=a, s=s, way=way):
-                    ep_copy(a, s, way).wait_send()
+                dest = ep_turn(t, way)
+
+                @pl.when(ep_has(t, way))
+                def _(a=a, way=way, dest=dest):
+                    ep_copy(a, dest, way).wait_send()
 
     for c in swaps:
         c.wait()
 
 
-def reduce(ne, nd, dp_arrays, ep_arrays, swap_arrays, collective):
+def reduce(ne, nd, dp_arrays, ep_arrays, swap_arrays, collective, us):
     sums = list(dp_arrays) + list(ep_arrays)
     landing = [(nd - 1,) + v.shape[1:] for v in dp_arrays]
-    landing += [(2, ne - 1) + v.shape[1:] for v in ep_arrays]
+    landing += [(2, ne) + v.shape[1:] for v in ep_arrays]
     a, b, c = (max(len(v), 1) for v in (dp_arrays, ep_arrays, swap_arrays))
     return pl.pallas_call(
         functools.partial(
@@ -329,14 +340,15 @@
             DMA((len(sums) + len(swap_arrays),)),
             DMA((a, nd - 1)),
             DMA((a, nd - 1)),
-            DMA((b, 2, ne - 1)),
-            DMA((b, 2, ne - 1)),
+            DMA((b, 2, ne)),
+            DMA((b, 2, ne)),
             DMA((c, ne - 1)),
             DMA((c, ne - 1)),
         ],
         compiler_params=pltpu.CompilerParams(
             collective_id=collective, has_side_effects=True, vmem_limit_bytes=48 * 2**20
         ),
+        cost_estimate=cost(us),
     )(*sums, *swap_arrays)
 
 
@@ -540,6 +552,7 @@
         compiler_params=pltpu.CompilerParams(
             vmem_limit_bytes=60 * 2**20, dimension_semantics=("arbitrary",)
         ),
+        cost_estimate=cost(65),
     )(core, normed, cot, probs, w_gate, w_up, w_down)
 
 
@@ -547,41 +560,252 @@
     return lax.rsqrt(jnp.mean(values * values, axis=-1, keepdims=True) + EPSILON)
 
 
-def rotate(values, cosine, sine):
-    half = values.shape[-1] // 2
-    a, b = values[..., :half], values[..., half:]
-    return jnp.concatenate([a * cosine - b * sine, b * cosine + a * sine], axis=-1)
-
-
-def attend(queries, keys, values, allowed):
-    scale = queries.shape[-1] ** (-0.5)
-    scores = jnp.einsum("mqkgd,mnkd->mkgqn", queries, keys, preferred_element_type=F32) * scale
-    scores = jnp.where(allowed[:, None, None], scores, MASKED)
-    top = jnp.max(scores, axis=-1, keepdims=True)
+def partner(x):
+    lane = lax.broadcasted_iota(jnp.int32, x.shape, 1)
+    half = HEAD_DIM // 2
+    low = lax.rem(lane, HEAD_DIM) < half
+    return jnp.where(low, pltpu.roll(x, x.shape[1] - half, 1), pltpu.roll(x, half, 1))
+
+
+def turn(x, cosine, sine):
+    return x * cosine + partner(x) * sine
+
+
+def project_body(
+    tokens_ref, gain_ref, cos_ref, sin_ref, wq_ref, wk_ref, wv_ref, n_ref, q_ref, k_ref, v_ref
+):
+    x = tokens_ref[...].astype(F32)
+    n_ref[...] = (x * rms_scale(x) * gain_ref[...]).astype(BF16)
+    normed = n_ref[...]
+    cosine, sine = cos_ref[...], sin_ref[...]
+    tile = 256
+    for w, out, turned in ((wk_ref, k_ref, True), (wv_ref, v_ref, False), (wq_ref, q_ref, True)):
+        for c in range(0, w.shape[1], tile):
+            y = dot(normed, w[:, c : c + tile])
+            if turned:
+                for i in range(0, tile, 128):
+                    out[:, c + i : c + i + 128] = turn(y[:, i : i + 128], cosine, sine).astype(BF16)
+            else:
+                out[:, c : c + tile] = y.astype(BF16)
+
+
+def project(tokens, gain, cosine, sine, w_query, w_key, w_value):
+    rows, width = tokens.shape
+    shapes = [width, w_query.shape[1], w_key.shape[1], w_value.shape[1]]
+    return pl.pallas_call(
+        project_body,
+        out_shape=[jax.ShapeDtypeStruct((rows, n), BF16) for n in shapes],
+        in_specs=[VMEM] * 7,
+        out_specs=[VMEM] * 4,
+        compiler_params=pltpu.CompilerParams(vmem_limit_bytes=32 * 2**20),
+        cost_estimate=cost(5),
+    )(tokens, gain, cosine, sine, w_query, w_key, w_value)
+
+
+def spread(x):
+    lane = lax.broadcasted_iota(jnp.int32, (x.shape[0], 128), 1)
+    low = lane < HEAD_DIM
+    zero = jnp.zeros((), x.dtype)
+    first, second = x[:, :128], x[:, 128:]
+    return jnp.concatenate(
+        [
+            jnp.where(low, first, zero),
+            jnp.where(low, pltpu.roll(first, HEAD_DIM, 1), zero),
+            jnp.where(low, zero, pltpu.roll(second, HEAD_DIM, 1)),
+            jnp.where(low, zero, second),
+        ],
+        axis=0,
+    )
+
+
+def gathered(x, rows):
+    lane = lax.broadcasted_iota(jnp.int32, (rows, 128), 1)
+    low = lane < HEAD_DIM
+    h = [x[i * rows : (i + 1) * rows] for i in range(4)]
+    return jnp.concatenate(
+        [
+            jnp.where(low, h[0], pltpu.roll(h[1], HEAD_DIM, 1)),
+            jnp.where(low, pltpu.roll(h[2], HEAD_DIM, 1), h[3]),
+        ],
+        axis=1,
+    )
+
+
+def window_of(dp, span):
+    return jnp.maximum(dp - (span - 1), 0)
+
+
+def window_scores(dp, span, rows, starts_ref, q, k):
+    keys = k.shape[0]
+    scores = dot(q, k, ((1,), (1,))).reshape(4, rows, keys)
+    key_pos = window_of(dp, span) * rows + lax.broadcasted_iota(jnp.int32, (rows, keys), 1)
+    query_pos = dp * rows + lax.broadcasted_iota(jnp.int32, (rows, keys), 0)
+    allowed = (key_pos <= query_pos) & (key_pos >= starts_ref[...])
+    return jnp.where(allowed[None], scores, MASKED).reshape(4 * rows, keys)
+
+
+def in_window(ref, dp, span):
+    block = ref[pl.ds(window_of(dp, span), span)]
+    return block.reshape(span * block.shape[1], block.shape[2])
+
+
+SCALE = HEAD_DIM ** (-0.5)
+
+
+def attend_body(span, dp_ref, starts_ref, q_ref, k_ref, v_ref, out_ref, log_ref):
+    dp = dp_ref[0]
+    rows = q_ref.shape[0]
+    q = spread(q_ref[...].astype(F32) * SCALE).astype(BF16)
+    scores = window_scores(dp, span, rows, starts_ref, q, in_window(k_ref, dp, span))
+    top = jnp.max(scores, axis=1, keepdims=True)
     terms = jnp.exp(scores - top)
-    total = jnp.sum(terms, axis=-1, keepdims=True)
-    weights = (terms / total).astype(BF16)
-    out = jnp.einsum("mkgqn,mnkd->mqkgd", weights, values, preferred_element_type=F32)
-    return out, top + jnp.log(total)
-
-
-def attend_back(queries, grad, log_total, grad_dot, keys, values, allowed):
-    scale = queries.shape[-1] ** (-0.5)
-    scores = jnp.einsum("mqkgd,mnkd->mkgqn", queries, keys, preferred_element_type=F32) * scale
-    scores = jnp.where(allowed[:, None, None], scores, MASKED)
-    probs = jnp.exp(scores - log_total)
-    grad_prob = jnp.einsum("mqkgd,mnkd->mkgqn", grad, values, preferred_element_type=F32)
-    grad_score = (probs * (grad_prob - grad_dot)).astype(BF16)
-    grad_query = (
-        jnp.einsum("mkgqn,mnkd->mqkgd", grad_score, keys, preferred_element_type=F32) * scale
-    )
-    grad_key = (
-        jnp.einsum("mkgqn,mqkgd->mnkd", grad_score, queries, preferred_element_type=F32) * scale
-    )
-    grad_value = jnp.einsum(
-        "mkgqn,mqkgd->mnkd", probs.astype(BF16), grad, preferred_element_type=F32
-    )
-    return grad_query, grad_key, grad_value
+    total = jnp.sum(terms, axis=1, keepdims=True)
+    log_ref[0, 0] = top + jnp.log(total)
+    weights = (terms * (1.0 / total)).astype(BF16)
+    out = dot(weights, in_window(v_ref, dp, span))
+    out_ref[...] = gathered(out, rows).astype(BF16)
+
+
+def attention_specs(micro, rows, nd):
+    pairs = KV_HEADS // 2
+    mine = pl.BlockSpec((rows, 4 * HEAD_DIM), lambda m, h, *_: (m, h))
+    theirs = pl.BlockSpec((nd, rows, 2 * HEAD_DIM), lambda m, h, *_: (0, m, h))
+    column = pl.BlockSpec((rows, 1), lambda m, h, *_: (m, 0))
+    logs = pl.BlockSpec((1, 1, 4 * rows, 1), lambda m, h, *_: (m, h, 0, 0))
+    log_shape = jax.ShapeDtypeStruct((micro, pairs, 4 * rows, 1), F32)
+    return (micro, pairs), mine, theirs, column, logs, log_shape
+
+
+def attend(dp, starts, queries, keys, values, micro, rows, nd):
+    grid, mine, theirs, column, logs, log_shape = attention_specs(micro, rows, nd)
+    return pl.pallas_call(
+        functools.partial(attend_body, nd // 2 + 1),
+        grid_spec=pltpu.PrefetchScalarGridSpec(
+            num_scalar_prefetch=1,
+            grid=grid,
+            in_specs=[column, mine, theirs, theirs],
+            out_specs=[mine, logs],
+        ),
+        out_shape=[jax.ShapeDtypeStruct(queries.shape, BF16), log_shape],
+        compiler_params=pltpu.CompilerParams(vmem_limit_bytes=40 * 2**20),
+        cost_estimate=cost(15),
+    )(dp.reshape(1), starts, queries, keys, values)
+
+
+def attend_back_body(
+    span, dp_ref, starts_ref, q_ref, k_ref, v_ref, log_ref, g_ref, cos_ref, sin_ref, *outs
+):
+    dq_ref, dk_ref, dv_ref = outs
+    dp = dp_ref[0]
+    rows = q_ref.shape[0]
+    q = spread(q_ref[...].astype(F32) * SCALE).astype(BF16)
+    g = spread(g_ref[...].astype(F32)).astype(BF16)
+    k, v = in_window(k_ref, dp, span), in_window(v_ref, dp, span)
+    scores = window_scores(dp, span, rows, starts_ref, q, k)
+    probs = jnp.exp(scores - log_ref[0, 0])
+    grad_probs = dot(g, v, ((1,), (1,)))
+    total = jnp.sum(probs * grad_probs, axis=1, keepdims=True)
+    grad_scores = (probs * (grad_probs - total)).astype(BF16)
+    dq = gathered(dot(grad_scores, k) * SCALE, rows)
+    cosine, sine = cos_ref[...], -sin_ref[...]
+    for i in range(0, dq.shape[1], 128):
+        dq_ref[:, i : i + 128] = turn(dq[:, i : i + 128], cosine, sine).astype(BF16)
+    dk_ref[...] = jnp.zeros_like(dk_ref)
+    dv_ref[...] = jnp.zeros_like(dv_ref)
+    here = pl.ds(window_of(dp, span), span)
+    dk = dot(grad_scores, q, ((0,), (0,))).astype(BF16)
+    dk_ref[here] = dk.reshape(span, rows, dk.shape[1])
+    dv = dot(probs.astype(BF16), g, ((0,), (0,))).astype(BF16)
+    dv_ref[here] = dv.reshape(span, rows, dv.shape[1])
+
+
+def attend_back(dp, starts, queries, keys, values, logs_in, grad, cosine, sine, micro, rows, nd):
+    grid, mine, theirs, column, logs, _ = attention_specs(micro, rows, nd)
+    table = pl.BlockSpec((rows, 128), lambda m, h, *_: (0, 0))
+    return pl.pallas_call(
+        functools.partial(attend_back_body, nd // 2 + 1),
+        grid_spec=pltpu.PrefetchScalarGridSpec(
+            num_scalar_prefetch=1,
+            grid=grid,
+            in_specs=[column, mine, theirs, theirs, logs, mine, table, table],
+            out_specs=[mine, theirs, theirs],
+        ),
+        out_shape=[
+            jax.ShapeDtypeStruct(queries.shape, BF16),
+            jax.ShapeDtypeStruct(keys.shape, BF16),
+            jax.ShapeDtypeStruct(values.shape, BF16),
+        ],
+        compiler_params=pltpu.CompilerParams(vmem_limit_bytes=48 * 2**20),
+        cost_estimate=cost(25),
+    )(dp.reshape(1), starts, queries, keys, values, logs_in, grad, cosine, sine)
+
+
+def input_body(
+    ne,
+    nd,
+    n_ref,
+    dq_ref,
+    dk_ref,
+    dv_ref,
+    cos_ref,
+    sin_ref,
+    wq_ref,
+    wk_ref,
+    wv_ref,
+    tokens_ref,
+    gain_ref,
+    res_ref,
+    wq_out,
+    wk_out,
+    wv_out,
+    tok_out,
+    gain_out,
+    dk_turned,
+):
+    normed = n_ref[...]
+    cosine, sine = cos_ref[...], -sin_ref[...]
+    for i in range(0, dk_ref.shape[1], 128):
+        part = dk_ref[:, i : i + 128].astype(F32)
+        dk_turned[:, i : i + 128] = turn(part, cosine, sine).astype(BF16)
+    tile = 256
+    for grad, out in ((dq_ref, wq_out), (dk_turned, wk_out), (dv_ref, wv_out)):
+        share = out.shape[1] // ne
+        for c in range(0, grad.shape[1], tile):
+            y = dot(normed, grad[:, c : c + tile], ((0,), (0,))).astype(BF16)
+            for e in range(ne):
+                for d in range(nd):
+                    r = (e * nd + d) * share
+                    out[d, e * share : (e + 1) * share, c : c + tile] = y[r : r + share]
+    back = (
+        dot(dq_ref[...], wq_ref[...], ((1,), (1,)))
+        + dot(dk_turned[...], wk_ref[...], ((1,), (1,)))
+        + dot(dv_ref[...], wv_ref[...], ((1,), (1,)))
+    )
+    x = tokens_ref[...].astype(F32)
+    r = rms_scale(x)
+    scaled = back * gain_ref[...]
+    gain_out[...] = jnp.sum(back * x * r, axis=0, keepdims=True)
+    tok_out[...] = (
+        res_ref[...] + r * scaled - x * (r * r * r) * jnp.mean(scaled * x, axis=1, keepdims=True)
+    )
+
+
+def input_grads(ne, nd, normed, dq, dk, dv, cosine, sine, weights, tokens, gain, grad_residual):
+    rows, width = tokens.shape
+    share = width // (ne * nd)
+    return pl.pallas_call(
+        functools.partial(input_body, ne, nd),
+        out_shape=[jax.ShapeDtypeStruct((nd, ne * share, w.shape[1]), BF16) for w in weights]
+        + [
+            jax.ShapeDtypeStruct((rows, width), F32),
+            jax.ShapeDtypeStruct((1, width), F32),
+        ],
+        in_specs=[VMEM] * 12,
+        out_specs=[VMEM] * 5,
+        scratch_shapes=[pltpu.VMEM(dk.shape, BF16)],
+        compiler_params=pltpu.CompilerParams(vmem_limit_bytes=48 * 2**20),
+        cost_estimate=cost(10),
+    )(normed, dq, dk, dv, cosine, sine, *weights, tokens, gain, grad_residual)
 
 
 def halve(values, dp, orders, nb):
@@ -632,7 +856,6 @@
     ne, nd = lax.axis_size("ep"), lax.axis_size("dp")
     ep, dp = lax.axis_index("ep"), lax.axis_index("dp")
     groups = HEADS // KV_HEADS
-    length = rows * nd
     kv_width = KV_HEADS * HEAD_DIM
     every = micro * rows
     inputs = tokens.reshape(every, width).astype(F32)
@@ -642,56 +865,30 @@
     halfway = HEAD_DIM // 2
     frequency = ROPE_BASE ** (-(jnp.arange(halfway, dtype=F32) * 2.0 / HEAD_DIM))
     angles = query_pos.astype(F32)[:, None] * frequency[None, :]
-    cosine = jnp.tile(jnp.cos(angles), (micro, 1))[:, None, :]
-    sine = jnp.tile(jnp.sin(angles), (micro, 1))[:, None, :]
-
-    inv_one = rms_scale(inputs)
-    normed_one = (inputs * inv_one * first_gain).astype(BF16)
-    query_rot = rotate(
-        jnp.dot(normed_one, w_query, preferred_element_type=F32).reshape(every, HEADS, HEAD_DIM),
-        cosine,
-        sine,
-    ).astype(BF16)
-    key_rot = (
-        rotate(
-            jnp.dot(normed_one, w_key, preferred_element_type=F32).reshape(
-                every, KV_HEADS, HEAD_DIM
-            ),
-            cosine,
-            sine,
-        )
-        .astype(BF16)
-        .reshape(every, kv_width)
-    )
-    value_own = jnp.dot(normed_one, w_value, preferred_element_type=F32).astype(BF16)
+    lanes = 2 * HEAD_DIM // halfway
+    sign = jnp.where(jnp.arange(2 * HEAD_DIM) % HEAD_DIM < halfway, -1.0, 1.0).astype(F32)
+    cosine = jnp.tile(jnp.cos(angles), (micro, lanes))
+    sine = jnp.tile(jnp.sin(angles), (micro, lanes)) * sign
+
+    tokens_flat = tokens.reshape(every, width)
+    gain_one = first_gain.reshape(1, width)
+    normed_one, query_rot, key_rot, value_own = project(
+        tokens_flat, gain_one, cosine, sine, w_query, w_key, w_value
+    )
 
     ids = jnp.arange(128, dtype=jnp.int32)
     counts = jnp.sum((segments[:, 0, :, None] == ids).astype(F32), axis=1)
     counts = jnp.concatenate([counts, jnp.zeros((8 - micro, 128), F32)], axis=0)
 
     key_all, value_all, count_all, cot_all = gather(
-        ne, nd, (key_rot, value_own, counts), (cotangent.reshape(every, width),), 0
+        ne, nd, (key_rot, value_own, counts), (cotangent.reshape(every, width),), 0, 40
     )
 
     totals = jnp.sum(count_all[:, :micro], axis=0)
     lower = (ids[None, None, :] < segments[:, 0, :, None]).astype(F32)
     starts = jnp.sum(lower * totals[:, None, :], axis=2).astype(jnp.int32)
-    key_pos = jnp.arange(length, dtype=jnp.int32)
-    allowed = (key_pos[None, None, :] <= query_pos[None, :, None]) & (
-        key_pos[None, None, :] >= starts[:, :, None]
-    )
-
-    def sequence(gathered):
-        return (
-            gathered.reshape(nd, micro, rows, kv_width)
-            .transpose(1, 0, 2, 3)
-            .reshape(micro, length, KV_HEADS, HEAD_DIM)
-        )
-
-    keys, values = sequence(key_all), sequence(value_all)
-    queries = query_rot.reshape(micro, rows, KV_HEADS, groups, HEAD_DIM)
-    attn_sum, log_total = attend(queries, keys, values, allowed)
-    attn_low = attn_sum.reshape(every, HEADS * HEAD_DIM).astype(BF16)
+    starts = starts.reshape(every, 1)
+    attn_low, logs = attend(dp, starts, query_rot, key_all, value_all, micro, rows, nd)
     residual = inputs + jnp.dot(attn_low, w_out, preferred_element_type=F32)
     inv_two = rms_scale(residual)
     normed_two = (residual * inv_two * second_gain).astype(BF16)
@@ -705,7 +902,7 @@
     gate_probs = terms / jnp.sum(terms, axis=1, keepdims=True)
     marked = jnp.where(chosen, gate_probs, -1.0).T
 
-    normed_all, marked_all = gather(ne, nd, (), (normed_two, marked), 1)
+    normed_all, marked_all = gather(ne, nd, (), (normed_two, marked), 1, 38)
     here = EXPERTS // ne
     probs_here = lax.dynamic_slice_in_dim(marked_all, ep * here, here, axis=1)
     probs_here = (
@@ -731,7 +928,7 @@
 
     pair_dots = pair_dots.reshape(here, ne, every).transpose(1, 0, 2)
     grad_back, dots_all = reduce(
-        ne, nd, (), (grad_in.reshape(ne, every, width),), (pair_dots,), 2
+        ne, nd, (), (grad_in.reshape(ne, every, width),), (pair_dots,), 2, 40
     )
     pair_dot = dots_all.reshape(EXPERTS, every).T
     grad_logits = gate_probs * (
@@ -756,64 +953,49 @@
     grad_attn = jnp.einsum("td,fd->tf", residual_low, w_out, preferred_element_type=F32).astype(
         BF16
     )
-    grad_attn = grad_attn.reshape(micro, rows, KV_HEADS, groups, HEAD_DIM)
-    grad_dot = jnp.sum(grad_attn.astype(F32) * attn_sum, axis=-1).transpose(0, 2, 3, 1)[..., None]
-    grad_query_rot, grad_key_all, grad_value_all = attend_back(
-        queries, grad_attn, log_total, grad_dot, keys, values, allowed
-    )
-
-    def pieces(summed):
-        return (
-            summed.reshape(micro, nd, rows, kv_width)
-            .transpose(1, 0, 2, 3)
-            .reshape(nd, every, kv_width)
-            .astype(BF16)
-        )
-
+    grad_query, grad_key_all, grad_value_all = attend_back(
+        dp,
+        starts,
+        query_rot,
+        key_all,
+        value_all,
+        logs,
+        grad_attn,
+        cosine,
+        sine,
+        micro,
+        rows,
+        nd,
+    )
     grad_key, grad_value, mix_own = reduce(
         ne,
         nd,
-        (pieces(grad_key_all), pieces(grad_value_all)),
+        (grad_key_all, grad_value_all),
         (mix.reshape(ne, every, width),),
         (),
         3,
+        40,
     )
     output = (residual + mix_own.astype(F32)).astype(BF16).reshape(tokens.shape)
-    grad_query_pre = (
-        rotate(grad_query_rot.reshape(every, HEADS, HEAD_DIM), cosine, -sine)
-        .astype(BF16)
-        .reshape(every, HEADS * HEAD_DIM)
-    )
-    grad_key_pre = (
-        rotate(grad_key.astype(F32).reshape(every, KV_HEADS, HEAD_DIM), cosine, -sine)
-        .astype(BF16)
-        .reshape(every, kv_width)
-    )
-    grad_value_pre = grad_value
-
-    def weight_grad(grad):
-        return jnp.einsum("td,tf->df", normed_one, grad, preferred_element_type=F32)
-
-    grad_w_query = weight_grad(grad_query_pre)
-    grad_w_key = weight_grad(grad_key_pre)
-    grad_w_value = weight_grad(grad_value_pre)
-    grad_normed_one = (
-        jnp.einsum("tf,df->td", grad_query_pre, w_query, preferred_element_type=F32)
-        + jnp.einsum("tf,df->td", grad_key_pre, w_key, preferred_element_type=F32)
-        + jnp.einsum("tf,df->td", grad_value_pre, w_value, preferred_element_type=F32)
-    )
-    scaled_one = grad_normed_one * first_gain
-    grad_gain_one = jnp.sum(grad_normed_one * inputs * inv_one, axis=0)
-    grad_tokens = (
-        grad_residual
-        + inv_one * scaled_one
-        - inputs * inv_one**3 * jnp.mean(scaled_one * inputs, axis=-1, keepdims=True)
+    grad_w_query, grad_w_key, grad_w_value, grad_tokens, grad_gain_one = input_grads(
+        ne,
+        nd,
+        normed_one,
+        grad_query,
+        grad_key,
+        grad_value,
+        cosine,
+        sine,
+        (w_query, w_key, w_value),
+        tokens_flat,
+        gain_one,
+        grad_residual,
     )
 
     small = jnp.concatenate(
         [
             grad_w_router,
-            grad_gain_one[:, None],
+            grad_gain_one.reshape(width, 1),
             grad_gain_two[:, None],
             jnp.zeros((width, 128 - EXPERTS - 2), F32),
         ],
@@ -832,27 +1014,24 @@
     dense = reduce(
         ne,
         nd,
-        (
-            by_owner(jnp.concatenate([grad_w_query, grad_w_key, small], axis=1)),
-            by_owner(jnp.concatenate([grad_w_out, grad_w_value], axis=1)),
-        ),
+        (grad_w_query, by_owner(grad_w_out), grad_w_key, grad_w_value, by_owner(small)),
         (),
         (),
         4,
-    )
-    dense = reduce(ne, nd, (), [v.reshape(ne, -1, v.shape[1]) for v in dense], (), 5)
-    first, second = (v.astype(F32) for v in dense)
-    model = width + kv_width
+        45,
+    )
+    dense = reduce(ne, nd, (), [v.reshape(ne, -1, v.shape[1]) for v in dense], (), 5, 18)
+    d_query, d_out, d_key, d_value, d_small = (v.astype(F32) for v in dense)
     return (
         output,
         grad_tokens.reshape(tokens.shape),
-        first[:, model + EXPERTS],
-        first[:, :width],
-        first[:, width:model],
-        second[:, width:],
-        second[:, :width],
-        first[:, model + EXPERTS + 1],
-        first[:, model : model + EXPERTS],
+        d_small[:, EXPERTS],
+        d_query,
+        d_key,
+        d_value,
+        d_out,
+        d_small[:, EXPERTS + 1],
+        d_small[:, :EXPERTS],
         grad_w_gate,
         grad_w_up,
         grad_w_down,

time: 735 us -> 495 us (0.67)
  Pallas kernels: 448 us -> 323 us
  matrix products: 66.3 us -> 9.13 us
  local copies, waits for them, and re-layouts: 86.9 us -> 36 us
  other arithmetic: 48.2 us -> 33.8 us
  waiting for transfers between devices: 60 us -> 72.2 us
    pallas_call x4, Pallas kernels: 304 us -> 145 us  [reduce(): pl.pallas_call(functools.partial(reduce_body, ne, nd, len(dp_arrays), len...]
    dot_general x15 -> x0, matrix products: 60.6 us -> none  [the longest x1 10.3 us: attend(): jnp.einsum('mqkgd,mnkd->mkgqn', queries, keys, preferred_element_type=F32)]
    pallas_call x0 -> x4, Pallas kernels: none -> 33.4 us  [the longest x1 15.1 us: attend_back(): pl.pallas_call(functools.partial(attend_back_body, nd // 2 + 1), grid_spe...]
    transpose x4 -> x0, local copies, waits for them, and re-layouts: 14.9 us -> none  [the longest x2 8.67 us: sequence(): return gathered.reshape(nd, micro, rows, kv_width).transpose(1, 0, 2, 3)....]
    reshape x6 -> x1, local copies, waits for them, and re-layouts: 13.9 us -> 1.64 us  [by_owner(): return grad.astype(BF16).reshape(ne, nd, share, grad.shape[1]).transpose(...]
    ppermute x12, waiting for transfers between devices: 60 us -> 72.2 us  [halve(): arrived = lax.ppermute(sent, 'dp', [(i, i ^ 1 << bit) for i in range(n)])]
    reduce_sum x3 -> x0, other arithmetic: 10.8 us -> none  [the longest x1 9.24 us: attend(): total = jnp.sum(terms, axis=-1, keepdims=True)]
    concatenate x6 -> x7, local copies, waits for them, and re-layouts: 11.5 us -> 3.35 us  [per_device(): jnp.concatenate([grad_w_router, grad_gain_one.reshape(width, 1), grad_gai...]
  transfers between devices with their start and end apart: 15 -> 15, of which waited for: 6 -> 6; matrix products, arithmetic and copies ran while one was open for 16% -> 9% of each run, Pallas kernels for 42% -> 34%
where the time goes in v2:
time: 495 us; the launch traced here: 489 us
  Pallas kernels  323 us (65%)
  waiting for transfers between devices  72.2 us (15%)
  local copies, waits for them, and re-layouts  36 us (7%)
  other arithmetic  33.8 us (7%)
  starting transfers between devices  13.4 us (3%)
  matrix products  9.13 us (2%)
    pallas_call x4, Pallas kernels, reduce(): pl.pallas_call(functools.partial(reduce_body, ne, nd, len(dp_arrays), len...  145 us
    pallas_call x2, Pallas kernels, gather(): pl.pallas_call(functools.partial(gather_body, ne, nd, len(dp_arrays), len...  76.5 us
    ppermute x12, waiting for transfers between devices, halve(): arrived = lax.ppermute(sent, 'dp', [(i, i ^ 1 << bit) for i in range(n)])  72.2 us
    pallas_call x1, Pallas kernels, experts(): pl.pallas_call(functools.partial(expert_body, blocks, rows, half), grid_s...  68 us
    unnamed x114, local copies, waits for them, and re-layouts  24.2 us
    pallas_call x1, Pallas kernels, attend_back(): pl.pallas_call(functools.partial(attend_back_body, nd // 2 + 1), grid_spe...  15.1 us
    convert_element_type x3, other arithmetic, reduce_expert(): values = (keep.astype(F32) + arrived.astype(F32)).astype(BF16)  13 us
    ppermute x12, starting transfers between devices, halve(): arrived = lax.ppermute(sent, 'dp', [(i, i ^ 1 << bit) for i in range(n)])  12.7 us
  transfers between devices with their start and end apart: 15, of which 6 were waited for; matrix products, arithmetic and copies ran while one was open for 9% of the time, Pallas kernels for 34%

profile of v2, /device:TPU:10, one launch (start us, length us, event | category | flops | bytes accessed | tf_op | source)
XLA Modules:
  0.0 489.5 jit_solution(14468009578045307224)
XLA Ops:
  6.6 1.7 shard_map.229
  8.3 38.1 %shard_map.230 = (bf16[8,256,512]{2,1,0:T(8,128)(2,1)S(1)}, bf16[8,256,512]{2,1,0:T(8,128)(2,1)S(1)}, f32[8,8,128]{2,1,0:T(8,128)S(1)}, bf16[4,256,1024]{2,1,0:T(8,128)(2,1)S(1)}) custom-call(bf16[256,512]{1,0:T(8,128)(2,1)S(1)} %get-tuple-element.56.refs_0_, bf16[256,512]{1,0:T(8,128)(2,1)S(1)} %get-tuple-element.57.refs_1_, ...), custom_call_target="tpu_custom_call" | custom-call | bytes 120000000 | tf_op jit(solution)/shard_map/pallas_call | solution.py:170
  55.0 10.2 %shard_map.231 = (bf16[256,1024]{1,0:T(8,128)(2,1)S(1)}, f32[2,4,512,1]{3,2,1,0:T(8,128)S(1)}) custom-call(s32[1]{0:T(128)} %bitcast.1.dp_ref, s32[256,1]{1,0:T(8,128)S(1)} %copy.49.starts_ref, bf16[256,1024]{1,0:T(8,128)(2,1)S(1)} %copy-done.22, bf16[8,256,512]{2,1,0:T(8,128)(2,1)S(1)} %copy-done.4, bf16[8,256,512]{2,1,0:T(8,128)(2,1)S(1)} %copy-done.6), custom_call_target="tpu_custom_call" | custom-call | bytes 45000000 | tf_op jit(solution)/shard_map/pallas_call | solution.py:681
  65.3 1.8 multiply_reduce_fusion.2
  72.0 38.3 %shard_map.232 = (bf16[4,256,1024]{2,1,0:T(8,128)(2,1)S(1)}, f32[4,32,256]{2,1,0:T(8,128)S(1)}) custom-call(bf16[256,1024]{1,0:T(8,128)(2,1)S(1)} %multiply_convert_fusion.refs_0_, f32[32,256]{1,0:T(8,128)S(1)} %fusion.21.refs_1_), custom_call_target="tpu_custom_call" | custom-call | bytes 114000000 | tf_op jit(solution)/shard_map/pallas_call | solution.py:170
  113.7 68.0 %shard_map.233 = (bf16[1024,1024]{1,0:T(8,128)(2,1)}, bf16[1024,1024]{1,0:T(8,128)(2,1)}, f32[8,8,128]{2,1,0:T(8,128)}, bf16[4,8,128,512]{3,2,1,0:T(8,128)(2,1)}...) custom-call(s32[1]{0:T(128)} %bitcast.7.core_ref, ...), custom_call_target="tpu_custom_call" | custom-call | bytes 195000000 | tf_op jit(solution)/shard_map/pallas_call | solution.py:517
  186.2 43.1 %shard_map.234 = (bf16[256,1024]{1,0:T(8,128)(2,1)S(1)}, f32[4,8,256]{2,1,0:T(8,128)S(1)}) custom-call(bf16[4,256,1024]{2,1,0:T(8,128)(2,1)S(1)} %bitcast.162, f32[4,8,256]{2,1,0:T(8,128)S(1)} %bitcast.167), custom_call_target="tpu_custom_call" | custom-call | bytes 120000000 | tf_op jit(solution)/shard_map/pallas_call | solution.py:329
  230.1 2.2 multiply_reduce_fusion
  236.6 1.7 copy.57
  238.3 2.0 convolution_convert_fusion.1.g_ref
  240.3 15.1 %shard_map.235 = (bf16[256,1024]{1,0:T(8,128)(2,1)S(1)}, bf16[8,256,512]{2,1,0:T(8,128)(2,1)S(1)}, bf16[8,256,512]{2,1,0:T(8,128)(2,1)S(1)}) custom-call(s32[1]{0:T(128)} %bitcast.1.dp_ref, s32[256,1]{1,0:T(8,128)S(1)} %copy.49.starts_ref, bf16[256,1024]{1,0:T(8,128)(2,1)S(1)} %copy-done.23, bf16[8,256,512]{2,1,0:T(8,128)(2,1)} %copy-done.3, ...), custom_call_target="tpu_custom_call" | custom-call | bytes 75000000 | tf_op jit(solution)/shard_map/pallas_call | solution.py:725
  255.5 37.2 %shard_map.236 = (bf16[256,512]{1,0:T(8,128)(2,1)S(1)}, bf16[256,512]{1,0:T(8,128)(2,1)S(1)}, bf16[256,1024]{1,0:T(8,128)(2,1)S(1)}) custom-call(bf16[8,256,512]{2,1,0:T(8,128)(2,1)S(1)} %get-tuple-element.71.refs_0_, bf16[8,256,512]{2,1,0:T(8,128)(2,1)S(1)} %get-tuple-element.72.refs_1_, bf16[4,256,1024]{2,1,0:T(8,128)(2,1)} %bitcast.178), custom_call_target="tpu_custom_call" | custom-call | bytes 120000000 | tf_op jit(solution)/shard_map/pallas_call | solution.py:329
  293.6 6.4 %shard_map.237 = (bf16[8,128,1024]{2,1,0:T(8,128)(2,1)}, bf16[8,128,512]{2,1,0:T(8,128)(2,1)S(1)}, bf16[8,128,512]{2,1,0:T(8,128)(2,1)S(1)}, f32[256,1024]{1,0:T(8,128)}, f32[1,1024]{1,0:T(1,128)S(1)}) custom-call(bf16[256,1024]{1,0:T(8,128)(2,1)S(1)} %copy-done.29, bf16[256,1024]{1,0:T(8,128)(2,1)S(1)} %get-tuple-element.76.dq_ref, ...), custom_call_target="tpu_custom_call" | custom-call | bytes 30000000 | tf_op jit(solution)/shard_map/pallas_call | solution.py:796
  307.9 38.8 %shard_map.238 = (bf16[128,1024]{1,0:T(8,128)(2,1)S(1)}, bf16[128,1024]{1,0:T(8,128)(2,1)S(1)}, bf16[128,512]{1,0:T(8,128)(2,1)S(1)}, bf16[128,512]{1,0:T(8,128)(2,1)S(1)}, bf16[128,128]{1,0:T(8,128)(2,1)S(1)}) custom-call(bf16[8,128,1024]{2,1,0:T(8,128)(2,1)S(1)} %copy-done.13, bf16[8,128,1024]{2,1,0:T(8,128)(2,1)} %bitcast.176, ...), custom_call_target="tpu_custom_call" | custom-call | bytes 135000000 | tf_op jit(solution)/shard_map/pallas_call | solution.py:329
  346.7 26.2 %shard_map.239 = (bf16[32,1024]{1,0:T(8,128)(2,1)S(1)}, bf16[32,1024]{1,0:T(8,128)(2,1)S(1)}, bf16[32,512]{1,0:T(8,128)(2,1)S(1)}, bf16[32,512]{1,0:T(8,128)(2,1)S(1)}, bf16[32,128]{1,0:T(8,128)(2,1)S(1)}) custom-call(bf16[4,32,1024]{2,1,0:T(8,128)(2,1)S(1)} %bitcast.165, bf16[4,32,1024]{2,1,0:T(8,128)(2,1)S(1)} %bitcast.166, ...), custom_call_target="tpu_custom_call" | custom-call | bytes 54000000 | tf_op jit(solution)/shard_map/pallas_call | solution.py:329
  377.7 5.0 %add_convert_fusion.2 = bf16[4,8,128,512]{3,2,1,0:T(8,128)(2,1)S(1)} fusion(bf16[4,8,128,512]{3,2,1,0:T(8,128)(2,1)} %collective-permute-done, bf16[4,8,128,512]{3,2,1,0:T(8,128)(2,1)} %get-tuple-element.94), kind=kLoop, calls=%fused_computation.2 | loop fusion | flops 8388608 | bytes 12582912 | tf_op jit(solution)/shard_map/convert_element_type | solution.py:828
  385.5 3.7 add_convert_fusion.1
  392.0 4.3 add_convert_fusion
  398.6 11.0 %collective-permute-done.3 = bf16[2,4,128,512]{3,2,1,0:T(8,128)(2,1)} collective-permute-done((bf16[2,4,128,512]{3,2,1,0:T(8,128)(2,1)S(1)}, bf16[2,4,128,512]{3,2,1,0:T(8,128)(2,1)}, u32[]{:S(2)}, u32[]{:S(2)}) %collective-permute-start.3) | collective-permute-done | bytes 1048608 | tf_op jit(solution)/shard_map/ppermute | solution.py:819
  414.8 17.2 %collective-permute-done.8 = bf16[2,4,128,512]{3,2,1,0:T(8,128)(2,1)} collective-permute-done((bf16[2,4,128,512]{3,2,1,0:T(8,128)(2,1)S(1)}, bf16[2,4,128,512]{3,2,1,0:T(8,128)(2,1)}, u32[]{:S(2)}, u32[]{:S(2)}) %collective-permute-start.8) | collective-permute-done | bytes 1048608 | tf_op jit(solution)/shard_map/ppermute | solution.py:819
  436.1 18.3 %collective-permute-done.13 = bf16[2,4,64,1024]{3,2,1,0:T(8,128)(2,1)S(1)} collective-permute-done((bf16[2,4,64,1024]{3,2,1,0:T(8,128)(2,1)S(1)}, bf16[2,4,64,1024]{3,2,1,0:T(8,128)(2,1)S(1)}, u32[]{:S(2)}, u32[]{:S(2)}) %collective-permute-start.13) | collective-permute-done | bytes 1048608 | tf_op jit(solution)/shard_map/ppermute | solution.py:819
  457.5 9.7 %collective-permute-done.4 = bf16[4,128,512]{2,1,0:T(8,128)(2,1)S(1)} collective-permute-done((bf16[4,128,512]{2,1,0:T(8,128)(2,1)S(1)}, bf16[4,128,512]{2,1,0:T(8,128)(2,1)S(1)}, u32[]{:S(2)}, u32[]{:S(2)}) %collective-permute-start.4) | collective-permute-done | bytes 524320 | tf_op jit(solution)/shard_map/ppermute | solution.py:819
  468.1 10.3 %collective-permute-done.9 = bf16[4,128,512]{2,1,0:T(8,128)(2,1)S(1)} collective-permute-done((bf16[4,128,512]{2,1,0:T(8,128)(2,1)S(1)}, bf16[4,128,512]{2,1,0:T(8,128)(2,1)S(1)}, u32[]{:S(2)}, u32[]{:S(2)}) %collective-permute-start.9) | collective-permute-done | bytes 524320 | tf_op jit(solution)/shard_map/ppermute | solution.py:819
  481.7 5.7 %collective-permute-done.14 = bf16[4,64,1024]{2,1,0:T(8,128)(2,1)S(1)} collective-permute-done((bf16[4,64,1024]{2,1,0:T(8,128)(2,1)S(1)}, bf16[4,64,1024]{2,1,0:T(8,128)(2,1)S(1)}, u32[]{:S(2)}, u32[]{:S(2)}) %collective-permute-start.14) | collective-permute-done | bytes 524320 | tf_op jit(solution)/shard_map/ppermute | solution.py:819
  (216 shorter events, 71.6 us)
Async XLA Ops:
  0.6 64.6 %copy-start = (bf16[1024,1024]{1,0:T(8,128)(2,1)S(1)}, bf16[1024,1024]{1,0:T(8,128)(2,1)}, u32[]{:S(2)}) copy-start(bf16[1024,1024]{1,0:T(8,128)(2,1)} %param.21) | copy-start | bytes 6291460
  6.6 43.9 %copy-start.55 = (s32[2,1,128]{2,1,0:T(1,128)S(1)}, s32[2,1,128]{2,1,0:T(1,128)}, u32[]{:S(2)}) copy-start(s32[2,1,128]{2,1,0:T(1,128)} %param.15) | copy-start | bytes 3076
  181.7 196.0 %collective-permute-start = (bf16[4,8,128,512]{3,2,1,0:T(8,128)(2,1)}, bf16[4,8,128,512]{3,2,1,0:T(8,128)(2,1)}, u32[]{:S(2)}, u32[]{:S(2)}) collective-permute-start(bf16[4,8,128,512]{3,2,1,0:T(8,128)(2,1)} %get-tuple-element.95), channel_id=1, source_target_pairs={{0,1},{1,0},{2,3},{3,2},{4,5},{5,4},{6,7},{7,6},{8,9},{9,8},{10,11... | collective-permute-start | bytes 12582920 | tf_op jit(solution)/shard_map/ppermute | solution.py:827
  181.8 203.7 %collective-permute-start.5 = (bf16[4,8,128,512]{3,2,1,0:T(8,128)(2,1)}, bf16[4,8,128,512]{3,2,1,0:T(8,128)(2,1)}, u32[]{:S(2)}, u32[]{:S(2)}) collective-permute-start(bf16[4,8,128,512]{3,2,1,0:T(8,128)(2,1)} %get-tuple-element.97), channel_id=1, source_target_pairs={{0,1},{1,0},{2,3},{3,2},{4,5},{5,4},{6,7},{7,6},{8,9},{9,8},{10,11... | collective-permute-start | bytes 12582920 | tf_op jit(solution)/shard_map/ppermute | solution.py:827
  182.3 209.7 %collective-permute-start.10 = (bf16[4,8,64,1024]{3,2,1,0:T(8,128)(2,1)}, bf16[4,8,64,1024]{3,2,1,0:T(8,128)(2,1)}, u32[]{:S(2)}, u32[]{:S(2)}) collective-permute-start(bf16[4,8,64,1024]{3,2,1,0:T(8,128)(2,1)} %get-tuple-element.99), channel_id=1, source_target_pairs={{0,1},{1,0},{2,3},{3,2},{4,5},{5,4},{6,7},{7,6},{8,9},{9,8},{10,11... | collective-permute-start | bytes 12582920 | tf_op jit(solution)/shard_map/ppermute | solution.py:827
  183.8 45.5 %copy-start.43 = (f32[256,32]{0,1:T(8,128)S(1)}, f32[256,32]{0,1:T(8,128)}, u32[]{:S(2)}) copy-start(f32[256,32]{0,1:T(8,128)} %copy-done.42) | copy-start | bytes 98308
  186.1 43.9 %copy-start.37 = (f32[256,1024]{1,0:T(8,128)S(1)}, f32[256,1024]{1,0:T(8,128)}, u32[]{:S(2)}) copy-start(f32[256,1024]{1,0:T(8,128)} %get-tuple-element.117) | copy-start | bytes 3145732
  186.1 43.9 %copy-start.45 = (bf16[1024,32]{0,1:T(8,128)(2,1)S(1)}, bf16[1024,32]{0,1:T(8,128)(2,1)}, u32[]{:S(2)}) copy-start(bf16[1024,32]{0,1:T(8,128)(2,1)} %param.23) | copy-start | bytes 196612
  186.1 46.1 %copy-start.19 = (bf16[2,128,1024]{2,1,0:T(8,128)(2,1)S(1)}, bf16[2,128,1024]{2,1,0:T(8,128)(2,1)}, u32[]{:S(2)}) copy-start(bf16[2,128,1024]{2,1,0:T(8,128)(2,1)} %param.27) | copy-start | bytes 1572868
  186.1 46.1 %copy-start.50 = (f32[256]{0:T(256)S(1)}, f32[256]{0:T(256)}, u32[]{:S(2)}) copy-start(f32[256]{0:T(256)} %copy-done.49) | copy-start | bytes 3076
  186.2 46.1 %copy-start.54 = (f32[256]{0:T(256)S(1)}, f32[256]{0:T(256)}, u32[]{:S(2)}) copy-start(f32[256]{0:T(256)} %get-tuple-element.112) | copy-start | bytes 3076
  307.9 68.9 %copy-start.31 = (bf16[256,1024]{1,0:T(8,128)(2,1)S(1)}, bf16[256,1024]{1,0:T(8,128)(2,1)}, u32[]{:S(2)}) copy-start(bf16[256,1024]{1,0:T(8,128)(2,1)} %copy-done.30) | copy-start | bytes 1572868
  383.3 26.3 %collective-permute-start.3 = (bf16[2,4,128,512]{3,2,1,0:T(8,128)(2,1)S(1)}, bf16[2,4,128,512]{3,2,1,0:T(8,128)(2,1)}, u32[]{:S(2)}, u32[]{:S(2)}) collective-permute-start(bf16[2,4,128,512]{3,2,1,0:T(8,128)(2,1)S(1)} %dynamic-slice_bitcast_fusion.4), channel_id=1, source_target_pairs={{0,2},{1,3},{2,0},{3,1},{4,6},{5,7},{6,4},{7,5},{8,10},{9,11},{10,... | collective-permute-start | bytes 3145736 | tf_op jit(solution)/shard_map/ppermute | solution.py:819
  384.9 27.1 %collective-permute-start.1 = (bf16[2,4,128,512]{3,2,1,0:T(8,128)(2,1)S(1)}, bf16[2,4,128,512]{3,2,1,0:T(8,128)(2,1)}, u32[]{:S(2)}, u32[]{:S(2)}) collective-permute-start(bf16[2,4,128,512]{3,2,1,0:T(8,128)(2,1)S(1)} %dynamic-slice_bitcast_fusion.5), channel_id=1, source_target_pairs={{0,4},{1,5},{2,6},{3,7},{4,0},{5,1},{6,2},{7,3},{8,12},{9,13},{10,... | collective-permute-start | bytes 3145736 | tf_op jit(solution)/shard_map/ppermute | solution.py:819
  389.8 42.2 %collective-permute-start.8 = (bf16[2,4,128,512]{3,2,1,0:T(8,128)(2,1)S(1)}, bf16[2,4,128,512]{3,2,1,0:T(8,128)(2,1)}, u32[]{:S(2)}, u32[]{:S(2)}) collective-permute-start(bf16[2,4,128,512]{3,2,1,0:T(8,128)(2,1)S(1)} %dynamic-slice_bitcast_fusion.2), channel_id=1, source_target_pairs={{0,2},{1,3},{2,0},{3,1},{4,6},{5,7},{6,4},{7,5},{8,10},{9,11},{10,... | collective-permute-start | bytes 3145736 | tf_op jit(solution)/shard_map/ppermute | solution.py:819
  391.2 43.8 %collective-permute-start.6 = (bf16[2,4,128,512]{3,2,1,0:T(8,128)(2,1)S(1)}, bf16[2,4,128,512]{3,2,1,0:T(8,128)(2,1)S(1)}, u32[]{:S(2)}, u32[]{:S(2)}) collective-permute-start(bf16[2,4,128,512]{3,2,1,0:T(8,128)(2,1)S(1)} %dynamic-slice_bitcast_fusion.3), channel_id=1, source_target_pairs={{0,4},{1,5},{2,6},{3,7},{4,0},{5,1},{6,2},{7,3},{8,12},{9,13},{10,... | collective-permute-start | bytes 3145736 | tf_op jit(solution)/shard_map/ppermute | solution.py:819
  397.0 57.4 %collective-permute-start.13 = (bf16[2,4,64,1024]{3,2,1,0:T(8,128)(2,1)S(1)}, bf16[2,4,64,1024]{3,2,1,0:T(8,128)(2,1)S(1)}, u32[]{:S(2)}, u32[]{:S(2)}) collective-permute-start(bf16[2,4,64,1024]{3,2,1,0:T(8,128)(2,1)S(1)} %dynamic-slice_bitcast_fusion), channel_id=1, source_target_pairs={{0,2},{1,3},{2,0},{3,1},{4,6},{5,7},{6,4},{7,5},{8,10},{9,11},{10,... | collective-permute-start | bytes 3145736 | tf_op jit(solution)/shard_map/ppermute | solution.py:819
  409.6 46.7 %collective-permute-start.11 = (bf16[2,4,64,1024]{3,2,1,0:T(8,128)(2,1)S(1)}, bf16[2,4,64,1024]{3,2,1,0:T(8,128)(2,1)S(1)}, u32[]{:S(2)}, u32[]{:S(2)}) collective-permute-start(bf16[2,4,64,1024]{3,2,1,0:T(8,128)(2,1)S(1)} %dynamic-slice_bitcast_fusion.1), channel_id=1, source_target_pairs={{0,4},{1,5},{2,6},{3,7},{4,0},{5,1},{6,2},{7,3},{8,12},{9,13},{10,... | collective-permute-start | bytes 3145736 | tf_op jit(solution)/shard_map/ppermute | solution.py:819
  411.9 55.3 %collective-permute-start.4 = (bf16[4,128,512]{2,1,0:T(8,128)(2,1)S(1)}, bf16[4,128,512]{2,1,0:T(8,128)(2,1)S(1)}, u32[]{:S(2)}, u32[]{:S(2)}) collective-permute-start(bf16[4,128,512]{2,1,0:T(8,128)(2,1)S(1)} %dynamic-slice_bitcast_fusion.10), channel_id=1, source_target_pairs={{0,4},{1,5},{2,6},{3,7},{4,0},{5,1},{6,2},{7,3},{8,12},{9,13},{10,... | collective-permute-start | bytes 1572872 | tf_op jit(solution)/shard_map/ppermute | solution.py:819
  432.0 35.9 %collective-permute-start.2 = (bf16[4,128,512]{2,1,0:T(8,128)(2,1)S(1)}, bf16[4,128,512]{2,1,0:T(8,128)(2,1)S(1)}, u32[]{:S(2)}, u32[]{:S(2)}) collective-permute-start(bf16[4,128,512]{2,1,0:T(8,128)(2,1)S(1)} %dynamic-slice_bitcast_fusion.11), channel_id=1, source_target_pairs={{0,2},{1,3},{2,0},{3,1},{4,6},{5,7},{6,4},{7,5},{8,10},{9,11},{10,... | collective-permute-start | bytes 1572872 | tf_op jit(solution)/shard_map/ppermute | solution.py:819
  435.1 43.4 %collective-permute-start.9 = (bf16[4,128,512]{2,1,0:T(8,128)(2,1)S(1)}, bf16[4,128,512]{2,1,0:T(8,128)(2,1)S(1)}, u32[]{:S(2)}, u32[]{:S(2)}) collective-permute-start(bf16[4,128,512]{2,1,0:T(8,128)(2,1)S(1)} %dynamic-slice_bitcast_fusion.8), channel_id=1, source_target_pairs={{0,4},{1,5},{2,6},{3,7},{4,0},{5,1},{6,2},{7,3},{8,12},{9,13},{10,... | collective-permute-start | bytes 1572872 | tf_op jit(solution)/shard_map/ppermute | solution.py:819
  454.4 24.2 %collective-permute-start.7 = (bf16[4,128,512]{2,1,0:T(8,128)(2,1)S(1)}, bf16[4,128,512]{2,1,0:T(8,128)(2,1)S(1)}, u32[]{:S(2)}, u32[]{:S(2)}) collective-permute-start(bf16[4,128,512]{2,1,0:T(8,128)(2,1)S(1)} %dynamic-slice_bitcast_fusion.9), channel_id=1, source_target_pairs={{0,2},{1,3},{2,0},{3,1},{4,6},{5,7},{6,4},{7,5},{8,10},{9,11},{10,... | collective-permute-start | bytes 1572872 | tf_op jit(solution)/shard_map/ppermute | solution.py:819
  456.3 31.1 %collective-permute-start.14 = (bf16[4,64,1024]{2,1,0:T(8,128)(2,1)S(1)}, bf16[4,64,1024]{2,1,0:T(8,128)(2,1)S(1)}, u32[]{:S(2)}, u32[]{:S(2)}) collective-permute-start(bf16[4,64,1024]{2,1,0:T(8,128)(2,1)S(1)} %dynamic-slice_bitcast_fusion.6), channel_id=1, source_target_pairs={{0,4},{1,5},{2,6},{3,7},{4,0},{5,1},{6,2},{7,3},{8,12},{9,13},{10,... | collective-permute-start | bytes 1572872 | tf_op jit(solution)/shard_map/ppermute | solution.py:819
  467.2 20.4 %collective-permute-start.12 = (bf16[4,64,1024]{2,1,0:T(8,128)(2,1)S(1)}, bf16[4,64,1024]{2,1,0:T(8,128)(2,1)S(1)}, u32[]{:S(2)}, u32[]{:S(2)}) collective-permute-start(bf16[4,64,1024]{2,1,0:T(8,128)(2,1)S(1)} %dynamic-slice_bitcast_fusion.7), channel_id=1, source_target_pairs={{0,2},{1,3},{2,0},{3,1},{4,6},{5,7},{6,4},{7,5},{8,10},{9,11},{10,... | collective-permute-start | bytes 1572872 | tf_op jit(solution)/shard_map/ppermute | solution.py:819
  (47 other events, 318.3 us)

commit v3 on v2

--- a/solution.py
+++ b/solution.py
@@ -356,60 +356,68 @@
     return lax.dot_general(a, b, (dims, ((), ())), preferred_element_type=F32)
 
 
-def expert_body(
-    blocks,
-    rows,
-    half,
-    core_ref,
-    normed_ref,
-    cot_ref,
-    probs_ref,
-    gate_ref,
-    up_ref,
-    down_ref,
-    mix_ref,
-    grad_ref,
-    dots_ref,
-    keep_gate,
-    send_gate,
-    keep_up,
-    send_up,
-    keep_down,
-    send_down,
-    rows_in,
-    cots_in,
-    picks,
-    weights,
-    first,
-    second,
-    load_sem,
-):
+def expert_body(ne, nd, micro, rows, *refs):
+    cots = refs[:ne]
+    normed_ref, probs_ref, gate_ref, up_ref, down_ref = refs[ne : ne + 5]
+    mix_ref, grad_ref, dots_ref, sums_ref = refs[ne + 5 : ne + 9]
+    rows_in, cots_in, picks, weights, first, second, keep, send, arrived = refs[ne + 9 : ne + 18]
+    load_sem, store_sem, send_sem, recv_sem, free_sem = refs[ne + 18 :]
     e = pl.program_id(0)
-    count = pl.num_programs(0)
+    last = pl.num_programs(0) - 1
+    ep, dp = lax.axis_index("ep"), lax.axis_index("dp")
+    other = {"dp": jnp.bitwise_xor(dp, 1)}
+    every = micro * rows
+    blocks = ne * micro
+    width = first.shape[1]
+    n_exp = rows_in.shape[1]
+
+    def exchange():
+        return remote(send, arrived, send_sem, recv_sem, other)
+
+    def loads():
+        out = [pltpu.make_async_copy(normed_ref, first, load_sem.at[ne])]
+        for k in range(ne):
+            at = pl.multiple_of(lax.rem(ep - k + ne, ne) * every, every)
+            out.append(
+                pltpu.make_async_copy(cots[k], second.at[pl.ds(at, every)], load_sem.at[k])
+            )
+        return out
 
     def block_at(s):
         return pl.ds(pl.multiple_of(s * rows, rows), rows)
 
-    def load(s, k):
-        src, dst = ((normed_ref, first), (cot_ref, second))[k]
-        return pltpu.make_async_copy(src.at[block_at(s)], dst.at[block_at(s)], load_sem.at[k, s])
-
-    def store(s, k):
-        src, dst = ((first, mix_ref), (second, grad_ref))[k]
-        return pltpu.make_async_copy(src.at[block_at(s)], dst.at[block_at(s)], load_sem.at[k, s])
+    def returned(t):
+        k, m = t // micro, lax.rem(t, micro)
+        return lax.rem(ep + k, ne) * micro + m
+
+    def stores(t):
+        s = returned(t)
+        return (
+            pltpu.make_async_copy(
+                first.at[block_at(s)], mix_ref.at[block_at(t)], store_sem.at[0, t]
+            ),
+            pltpu.make_async_copy(
+                second.at[block_at(s)], grad_ref.at[block_at(s)], store_sem.at[1, t]
+            ),
+        )
+
+    def collect():
+        exchange().wait_recv()
+        sums_ref[:, 0] = (keep[...].astype(F32) + arrived[...].astype(F32)).astype(BF16)
 
     @pl.when(e == 0)
     def _():
+        for copy in loads():
+            copy.start()
+        barrier = pltpu.get_barrier_semaphore()
+        pl.semaphore_signal(barrier, inc=1, device_id=other, device_id_type=MESH)
+        pl.semaphore_wait(barrier, 1)
         before = lax.broadcasted_iota(jnp.int32, (rows, rows), 0)
         after = lax.broadcasted_iota(jnp.int32, (rows, rows), 1)
         earlier = (before < after).astype(BF16)
-        n_exp = rows_in.shape[1]
         slot = lax.broadcasted_iota(jnp.int32, (n_exp, CAP, rows), 1)
-
-        @pl.loop(0, blocks)
-        def _(s):
-            load(s, 0).start()
-            load(s, 1).start()
+        for copy in loads():
+            copy.wait()
 
         @pl.loop(0, blocks)
         def _(s):
@@ -424,68 +432,75 @@
             weights[s] = share
             flat = pick_f.reshape(n_exp * CAP, rows).astype(BF16)
             picks[s] = flat
-            load(s, 0).wait()
-            load(s, 1).wait()
-            rows_in[s] = (
-                dot(flat, first[at, :]).astype(BF16).reshape(n_exp, CAP, normed_ref.shape[1])
-            )
-            cots_in[s] = (
-                dot(flat, second[at, :]).astype(BF16).reshape(n_exp, CAP, cot_ref.shape[1])
-            )
-
-    width = normed_ref.shape[1]
-    x = rows_in[:, e].reshape(blocks * CAP, width)
-    c = cots_in[:, e].reshape(blocks * CAP, width)
-    p = weights[:, e].reshape(blocks * CAP, 1)
-    w_gate, w_up, w_down = gate_ref[0], up_ref[0], down_ref[0]
-    gate_pre = dot(x, w_gate)
-    up_pre = dot(x, w_up)
-    sigma = jax.nn.sigmoid(gate_pre)
-    silu = gate_pre * sigma
-    hidden = (silu * up_pre).astype(BF16)
-    out = dot(hidden, w_down) * p
-    back = dot(c, w_down, ((1,), (1,)))
-    wide = hidden.astype(F32)
-    pair = jnp.sum(wide * back, axis=1, keepdims=True)
-    back = back * p
-    grad_up = (back * silu).astype(BF16)
-    grad_gate = (back * up_pre * (sigma * (1.0 + gate_pre * (1.0 - sigma)))).astype(BF16)
-    scaled = (wide * p).astype(BF16)
-    grad_x = dot(grad_gate, w_gate, ((1,), (1,))) + dot(grad_up, w_up, ((1,), (1,)))
-
-    flat = picks[:, pl.ds(pl.multiple_of(e * CAP, CAP), CAP), :].astype(F32)
-    dots_ref[0] = jnp.sum(flat * pair.reshape(blocks, CAP, 1), axis=1)
-
-    def split(value, keep, send):
-        value = value.astype(BF16)
-        n, r = half * 2, value.shape[0] // (half * 2)
-        value = value.reshape(n, r, value.shape[1])
-
-        @pl.when(core_ref[0] == 0)
+            rows_in[s] = dot(flat, first[at, :]).astype(BF16).reshape(n_exp, CAP, width)
+            cots_in[s] = dot(flat, second[at, :]).astype(BF16).reshape(n_exp, CAP, width)
+
+    @pl.when(e < last)
+    def _():
+        x = rows_in[:, e].reshape(blocks * CAP, width)
+        c = cots_in[:, e].reshape(blocks * CAP, width)
+        p = weights[:, e].reshape(blocks * CAP, 1)
+        w_gate, w_up, w_down = gate_ref[0], up_ref[0], down_ref[0]
+        gate_pre = dot(x, w_gate)
+        up_pre = dot(x, w_up)
+        sigma = jax.nn.sigmoid(gate_pre)
+        silu = gate_pre * sigma
+        hidden = (silu * up_pre).astype(BF16)
+        out = dot(hidden, w_down) * p
+        back = dot(c, w_down, ((1,), (1,)))
+        wide = hidden.astype(F32)
+        pair = jnp.sum(wide * back, axis=1, keepdims=True)
+        back = back * p
+        grad_up = (back * silu).astype(BF16)
+        grad_gate = (back * up_pre * (sigma * (1.0 + gate_pre * (1.0 - sigma)))).astype(BF16)
+        scaled = (wide * p).astype(BF16)
+        grad_x = dot(grad_gate, w_gate, ((1,), (1,))) + dot(grad_up, w_up, ((1,), (1,)))
+
+        flat = picks[:, pl.ds(pl.multiple_of(e * CAP, CAP), CAP), :].astype(F32)
+        dots_ref[0] = jnp.sum(flat * pair.reshape(blocks, CAP, 1), axis=1)
+
+        @pl.when(e > 0)
         def _():
-            for i in range(half):
-                keep[i, 0] = value[2 * i]
-                send[i, 0] = value[2 * i + 1]
-
-        @pl.when(core_ref[0] == 1)
-        def _():
-            for i in range(half):
-                keep[i, 0] = value[2 * i + 1]
-                send[i, 0] = value[2 * i]
-
-    split(dot(scaled, c, ((0,), (0,))), keep_down, send_down)
-    split(dot(x, grad_gate, ((0,), (0,))), keep_gate, send_gate)
-    split(dot(x, grad_up, ((0,), (0,))), keep_up, send_up)
-
-    rows_in[:, e] = grad_x.astype(BF16).reshape(blocks, CAP, width)
-    cots_in[:, e] = out.astype(BF16).reshape(blocks, CAP, width)
-
-    @pl.when(e == count - 1)
+            collect()
+            pl.semaphore_signal(free_sem, inc=1, device_id=other, device_id_type=MESH)
+            exchange().wait_send()
+            pl.semaphore_wait(free_sem, 1)
+
+        def split(value, offset):
+            value = value.astype(BF16)
+            piece, columns = value.shape[0] // nd, keep.shape[2]
+
+            def put(even, odd):
+                for i in range(nd):
+                    ref = odd if i % 2 else even
+                    for j in range(value.shape[1] // columns):
+                        at = offset + j * piece
+                        ref[i // 2, at : at + piece] = value[
+                            i * piece : (i + 1) * piece, j * columns : (j + 1) * columns
+                        ]
+
+            @pl.when(jnp.bitwise_and(dp, 1) == 0)
+            def _():
+                put(keep, send)
+
+            @pl.when(jnp.bitwise_and(dp, 1) == 1)
+            def _():
+                put(send, keep)
+
+        share = width // nd
+        split(dot(scaled, c, ((0,), (0,))), 2 * share)
+        split(dot(x, grad_gate, ((0,), (0,))), 0)
+        split(dot(x, grad_up, ((0,), (0,))), share)
+        exchange().start()
+
+        rows_in[:, e] = grad_x.astype(BF16).reshape(blocks, CAP, width)
+        cots_in[:, e] = out.astype(BF16).reshape(blocks, CAP, width)
+
+    @pl.when(e == last)
     def _():
-        n_exp = rows_in.shape[1]
-
         @pl.loop(0, blocks)
-        def _(s):
+        def _(t):
+            s = returned(t)
             at = block_at(s)
             flat = picks[s]
             first[at, :] = dot(
@@ -494,66 +509,72 @@
             second[at, :] = dot(
                 flat, rows_in[s].reshape(n_exp * CAP, width), ((0,), (0,))
             ).astype(BF16)
-            store(s, 0).start()
-            store(s, 1).start()
+            for copy in stores(t):
+                copy.start()
+
+        collect()
+        exchange().wait_send()
 
         @pl.loop(0, blocks)
-        def _(s):
-            store(s, 0).wait()
-            store(s, 1).wait()
-
-
-def experts(normed, cot, probs, w_gate, w_up, w_down, rows, nd, core):
+        def _(t):
+            for copy in stores(t):
+                copy.wait()
+
+
+def experts(normed, cots, probs, w_gate, w_up, w_down, micro, rows, ne, nd, collective):
     n_exp, width, inner = w_gate.shape
-    blocks = normed.shape[0] // rows
+    blocks = ne * micro
     half = nd // 2
-    grads = []
-    for a, b in ((width, inner), (width, inner), (inner, width)):
-        shape = jax.ShapeDtypeStruct((half, n_exp, a // nd, b), BF16)
-        spec = pl.BlockSpec((half, 1, a // nd, b), lambda e, *_: (0, e, 0, 0))
-        grads += [(shape, spec)] * 2
+    packed = 2 * width // nd + (inner // nd) * (width // inner)
+    full = (blocks * rows, width)
     one = pl.Buffered(1)
-    full = (blocks * rows, width)
+    weight = lambda e: (jnp.minimum(e, n_exp - 1), 0, 0)
     return pl.pallas_call(
-        functools.partial(expert_body, blocks, rows, half),
-        grid_spec=pltpu.PrefetchScalarGridSpec(
-            num_scalar_prefetch=1,
-            grid=(n_exp,),
-            in_specs=[
-                ANY,
-                ANY,
-                pl.BlockSpec(probs.shape, lambda e, *_: (0, 0, 0), pipeline_mode=one),
-                pl.BlockSpec((1, width, inner), lambda e, *_: (e, 0, 0)),
-                pl.BlockSpec((1, width, inner), lambda e, *_: (e, 0, 0)),
-                pl.BlockSpec((1, inner, width), lambda e, *_: (e, 0, 0)),
-            ],
-            out_specs=[
-                ANY,
-                ANY,
-                pl.BlockSpec((1, blocks, rows), lambda e, *_: (e, 0, 0)),
-            ]
-            + [g[1] for g in grads],
-            scratch_shapes=[
-                pltpu.VMEM((blocks, n_exp, CAP, width), BF16),
-                pltpu.VMEM((blocks, n_exp, CAP, width), BF16),
-                pltpu.VMEM((blocks, n_exp * CAP, rows), BF16),
-                pltpu.VMEM((blocks, n_exp, CAP, 1), F32),
-                pltpu.VMEM(full, BF16),
-                pltpu.VMEM(full, BF16),
-                DMA((2, blocks)),
-            ],
-        ),
+        functools.partial(expert_body, ne, nd, micro, rows),
+        grid=(n_exp + 1,),
+        in_specs=[ANY] * (ne + 1)
+        + [
+            pl.BlockSpec(probs.shape, lambda e: (0, 0, 0), pipeline_mode=one),
+            pl.BlockSpec((1, width, inner), weight),
+            pl.BlockSpec((1, width, inner), weight),
+            pl.BlockSpec((1, inner, width), weight),
+        ],
+        out_specs=[
+            ANY,
+            ANY,
+            pl.BlockSpec((1, blocks, rows), weight),
+            pl.BlockSpec((half, 1, packed, inner), lambda e: (0, jnp.maximum(e - 1, 0), 0, 0)),
+        ],
+        scratch_shapes=[
+            pltpu.VMEM((blocks, n_exp, CAP, width), BF16),
+            pltpu.VMEM((blocks, n_exp, CAP, width), BF16),
+            pltpu.VMEM((blocks, n_exp * CAP, rows), BF16),
+            pltpu.VMEM((blocks, n_exp, CAP, 1), F32),
+            pltpu.VMEM(full, BF16),
+            pltpu.VMEM(full, BF16),
+            pltpu.VMEM((half, packed, inner), BF16),
+            pltpu.VMEM((half, packed, inner), BF16),
+            pltpu.VMEM((half, packed, inner), BF16),
+            DMA((ne + 1,)),
+            DMA((2, blocks)),
+            DMA,
+            DMA,
+            pltpu.SemaphoreType.REGULAR,
+        ],
         out_shape=[
             jax.ShapeDtypeStruct(full, BF16),
             jax.ShapeDtypeStruct(full, BF16),
             jax.ShapeDtypeStruct((n_exp, blocks, rows), F32),
-        ]
-        + [g[0] for g in grads],
+            jax.ShapeDtypeStruct((half, n_exp, packed, inner), BF16),
+        ],
         compiler_params=pltpu.CompilerParams(
-            vmem_limit_bytes=60 * 2**20, dimension_semantics=("arbitrary",)
+            vmem_limit_bytes=62 * 2**20,
+            dimension_semantics=("arbitrary",),
+            collective_id=collective,
+            has_side_effects=True,
         ),
         cost_estimate=cost(65),
-    )(core, normed, cot, probs, w_gate, w_up, w_down)
+    )(*cots, normed, probs, w_gate, w_up, w_down)
 
 
 def rms_scale(values):
@@ -808,32 +829,25 @@
     )(normed, dq, dk, dv, cosine, sine, *weights, tokens, gain, grad_residual)
 
 
-def halve(values, dp, orders, nb):
-    live = list(range(nb - 1, 0, -1))
-    for bit in orders:
-        axis = live.index(bit)
-        mine = jnp.bitwise_and(lax.shift_right_logical(dp, bit), 1)
-        kept = lax.dynamic_index_in_dim(values, mine, axis, keepdims=False)
-        sent = lax.dynamic_index_in_dim(values, 1 - mine, axis, keepdims=False)
-        n = 1 << nb
-        arrived = lax.ppermute(sent, "dp", [(i, i ^ (1 << bit)) for i in range(n)])
-        values = (kept.astype(F32) + arrived.astype(F32)).astype(BF16)
-        live.remove(bit)
-    return values
-
-
-def reduce_expert(keep, send, dp, nd):
-    nb = bit_count(nd)
-    arrived = lax.ppermute(send, "dp", [(i, i ^ 1) for i in range(nd)])
-    values = (keep.astype(F32) + arrived.astype(F32)).astype(BF16)
-    values = values.reshape((2,) * (nb - 1) + values.shape[1:])
-    half = keep.shape[1] // 2
-    first, second = gather_orders(nd)
-    out = []
-    for part, order in ((0, first), (1, second)):
-        piece = lax.slice_in_dim(values, part * half, (part + 1) * half, axis=nb - 1)
-        out.append(halve(piece, dp, order[:-1][::-1], nb))
-    return jnp.concatenate(out, axis=0).astype(F32)
+def halves(values, dp, axis, bit, part, parts_axis):
+    count = values.shape[parts_axis] // 2
+    values = lax.slice_in_dim(values, part * count, (part + 1) * count, axis=parts_axis)
+    mine = jnp.bitwise_and(lax.shift_right_logical(dp, bit), 1)
+    kept = lax.dynamic_index_in_dim(values, mine, axis, keepdims=False)
+    sent = lax.dynamic_index_in_dim(values, 1 - mine, axis, keepdims=False)
+    return kept, sent
+
+
+def swap_bit(sent, bit, nd):
+    return lax.ppermute(sent, "dp", [(i, i ^ (1 << bit)) for i in range(nd)])
+
+
+def plus(a, b):
+    return (a.astype(F32) + b.astype(F32)).astype(BF16)
+
+
+def tie(value, *others):
+    return lax.optimization_barrier((value,) + others)
 
 
 def per_device(
@@ -880,9 +894,13 @@
     counts = jnp.sum((segments[:, 0, :, None] == ids).astype(F32), axis=1)
     counts = jnp.concatenate([counts, jnp.zeros((8 - micro, 128), F32)], axis=0)
 
-    key_all, value_all, count_all, cot_all = gather(
-        ne, nd, (key_rot, value_own, counts), (cotangent.reshape(every, width),), 0, 40
-    )
+    cot_own = cotangent.reshape(every, width)
+
+    def around(value, k):
+        return lax.ppermute(value, "ep", [(i, (i + k) % ne) for i in range(ne)])
+
+    cots = [cot_own] + [around(cot_own, k) for k in range(1, ne)]
+    key_all, value_all, count_all = gather(ne, nd, (key_rot, value_own, counts), (), 0, 25)
 
     totals = jnp.sum(count_all[:, :micro], axis=0)
     lower = (ids[None, None, :] < segments[:, 0, :, None]).astype(F32)
@@ -910,21 +928,27 @@
         .transpose(0, 2, 1, 3)
         .reshape(ne * micro, here, rows)
     )
-    core = jnp.bitwise_and(dp, 1).reshape(1)
-    mix, grad_in, pair_dots, *grads = experts(
+    mix, grad_in, pair_dots, sums = experts(
         normed_all.reshape(ne * every, width),
-        cot_all.reshape(ne * every, width),
+        cots,
         probs_here,
         w_gate,
         w_up,
         w_down,
+        micro,
         rows,
+        ne,
         nd,
-        core,
-    )
-    grad_w_gate = reduce_expert(grads[0], grads[1], dp, nd)
-    grad_w_up = reduce_expert(grads[2], grads[3], dp, nd)
-    grad_w_down = reduce_expert(grads[4], grads[5], dp, nd)
+        6,
+    )
+    nb = bit_count(nd)
+    sums = sums.reshape((2,) * (nb - 1) + sums.shape[1:])
+    orders = [order[:-1][::-1] for order in gather_orders(nd)]
+    first_kept, first_sent = zip(
+        *[halves(sums, dp, nb - 1 - orders[i][0], orders[i][0], i, nb - 1) for i in range(2)]
+    )
+    grad_in, *first_sent = tie(grad_in, *first_sent)
+    first_arrived = [swap_bit(v, orders[i][0], nd) for i, v in enumerate(first_sent)]
 
     pair_dots = pair_dots.reshape(here, ne, every).transpose(1, 0, 2)
     grad_back, dots_all = reduce(
@@ -967,16 +991,35 @@
         rows,
         nd,
     )
-    grad_key, grad_value, mix_own = reduce(
-        ne,
-        nd,
-        (grad_key_all, grad_value_all),
-        (mix.reshape(ne, every, width),),
-        (),
-        3,
-        40,
-    )
-    output = (residual + mix_own.astype(F32)).astype(BF16).reshape(tokens.shape)
+    mix = mix.reshape(ne, every, width)
+    mix_parts = [mix[0]] + [around(mix[k], k) for k in range(1, ne)]
+    grad_key, grad_value = reduce(ne, nd, (grad_key_all, grad_value_all), (), (), 3, 25)
+
+    grads = []
+    for i in range(2):
+        value, bits = plus(first_kept[i], first_arrived[i]), orders[i]
+        live = [b for b in range(nb - 1, 0, -1) if b != bits[0]]
+        for bit in bits[1:]:
+            axis = live.index(bit)
+            mine = jnp.bitwise_and(lax.shift_right_logical(dp, bit), 1)
+            kept = lax.dynamic_index_in_dim(value, mine, axis, keepdims=False)
+            sent = lax.dynamic_index_in_dim(value, 1 - mine, axis, keepdims=False)
+            grad_key, sent = tie(grad_key, sent)
+            value = plus(kept, swap_bit(sent, bit, nd))
+            live.remove(bit)
+        grads.append(value)
+    grads = jnp.concatenate(grads, axis=0).astype(F32)
+    share = width // nd
+    grad_w_gate, grad_w_up = grads[:, :share], grads[:, share : 2 * share]
+    grad_w_down = jnp.concatenate(
+        [
+            grads[:, at : at + w_down.shape[1] // nd]
+            for at in range(2 * share, grads.shape[1], w_down.shape[1] // nd)
+        ],
+        axis=2,
+    )
+    output = residual + sum(v.astype(F32) for v in mix_parts)
+    output = output.astype(BF16).reshape(tokens.shape)
     grad_w_query, grad_w_key, grad_w_value, grad_tokens, grad_gain_one = input_grads(
         ne,
         nd,

time: 495 us -> 422 us (0.85)
  waiting for transfers between devices: 72.2 us -> 0.03 us
  Pallas kernels: 323 us -> 336 us
  other arithmetic: 33.8 us -> 21 us
  local copies, waits for them, and re-layouts: 36 us -> 42.7 us
  matrix products: 9.13 us -> 3.88 us
    ppermute x15 -> x10, waiting for transfers between devices: 72.2 us -> 0.03 us  [the longest x6 0.02 us: around(): return lax.ppermute(value, 'ep', [(i, (i + k) % ne) for i in range(ne)])]
    pallas_call x4, Pallas kernels: 145 us -> 163 us  [reduce(): pl.pallas_call(functools.partial(reduce_body, ne, nd, len(dp_arrays), len...]
    convert_element_type x19 -> x5, other arithmetic: 25.1 us -> 10 us  [the longest x4 9.64 us: plus(): return (a.astype(F32) + b.astype(F32)).astype(BF16)]
    pallas_call x2, Pallas kernels: 76.5 us -> 65.8 us  [gather(): pl.pallas_call(functools.partial(gather_body, ne, nd, len(dp_arrays), len...]
    slice x4, local copies, waits for them, and re-layouts: 2.16 us -> 9.47 us  [the longest x1 5.35 us: halves(): lax.slice_in_dim(values, part * count, (part + 1) * count, axis=parts_axis)]
    squeeze x12 -> x4, local copies, waits for them, and re-layouts: 0.76 us -> 6.62 us  [the longest x2 3.89 us: halves(): sent = lax.dynamic_index_in_dim(values, 1 - mine, axis, keepdims=False)]
    pallas_call x1, Pallas kernels: 68 us -> 73.5 us  [experts(): pl.pallas_call(functools.partial(expert_body, ne, nd, micro, rows), grid=...]
    unnamed x114 -> x124, local copies, waits for them, and re-layouts: 24.2 us -> 20.5 us
  transfers between devices with their start and end apart: 15 -> 10, of which waited for: 6 -> 0; matrix products, arithmetic and copies ran while one was open for 9% -> 7% of each run, Pallas kernels for 34% -> 63%
where the time goes in v3:
time: 422 us; the launch traced here: 420 us
  Pallas kernels  336 us (80%)
  local copies, waits for them, and re-layouts  42.7 us (10%)
  other arithmetic  21 us (5%)
  starting transfers between devices  14.3 us (3%)
    pallas_call x4, Pallas kernels, reduce(): pl.pallas_call(functools.partial(reduce_body, ne, nd, len(dp_arrays), len...  163 us
    pallas_call x1, Pallas kernels, experts(): pl.pallas_call(functools.partial(expert_body, ne, nd, micro, rows), grid=...  73.5 us
    pallas_call x2, Pallas kernels, gather(): pl.pallas_call(functools.partial(gather_body, ne, nd, len(dp_arrays), len...  65.8 us
    unnamed x124, local copies, waits for them, and re-layouts  20.5 us
    pallas_call x1, Pallas kernels, attend_back(): pl.pallas_call(functools.partial(attend_back_body, nd // 2 + 1), grid_spe...  15.3 us
    pallas_call x1, Pallas kernels, attend(): pl.pallas_call(functools.partial(attend_body, nd // 2 + 1), grid_spec=plt...  10.2 us
    ppermute x6, starting transfers between devices, around(): return lax.ppermute(value, 'ep', [(i, (i + k) % ne) for i in range(ne)])  9.72 us
    convert_element_type x4, other arithmetic, plus(): return (a.astype(F32) + b.astype(F32)).astype(BF16)  9.64 us
  transfers between devices with their start and end apart: 10, of which 0 were waited for; matrix products, arithmetic and copies ran while one was open for 7% of the time, Pallas kernels for 63%

profile of v3, /device:TPU:10, one launch (start us, length us, event | category | flops | bytes accessed | tf_op | source)
XLA Modules:
  0.0 419.7 jit_solution(7059323187391435645)
XLA Ops:
  3.5 1.8 collective-permute-start.2
  14.9 24.3 %shard_map.230 = (bf16[8,256,512]{2,1,0:T(8,128)(2,1)S(1)}, bf16[8,256,512]{2,1,0:T(8,128)(2,1)S(1)}, f32[8,8,128]{2,1,0:T(8,128)S(1)}) custom-call(bf16[256,512]{1,0:T(8,128)(2,1)S(1)} %get-tuple-element.56.refs_0_, bf16[256,512]{1,0:T(8,128)(2,1)S(1)} %get-tuple-element.57.refs_1_, f32[8,128]{1,0:T(8,128)S(1)} %concatenate.23.refs_2_), custom_call_target="tpu_custom_call" | custom-call | bytes 75000000 | tf_op jit(solution)/shard_map/pallas_call | solution.py:170
  45.4 10.2 %shard_map.231 = (bf16[256,1024]{1,0:T(8,128)(2,1)S(1)}, f32[2,4,512,1]{3,2,1,0:T(8,128)S(1)}) custom-call(s32[1]{0:T(128)} %bitcast.1.dp_ref, s32[256,1]{1,0:T(8,128)S(1)} %copy.45.starts_ref, bf16[256,1024]{1,0:T(8,128)(2,1)S(1)} %get-tuple-element.59.q_ref, bf16[8,256,512]{2,1,0:T(8,128)(2,1)S(1)} %copy-done.4, bf16[8,256,512]{2,1,0:T(8,128)(2,1)S(1)} %copy-done.6), custom_call_target="tpu_custom_call" | custom-call | bytes 45000000 | tf_op jit(solution)/shard_map/pallas_call | solution.py:702
  57.8 41.5 %shard_map.232 = (bf16[4,256,1024]{2,1,0:T(8,128)(2,1)S(1)}, f32[4,32,256]{2,1,0:T(8,128)S(1)}) custom-call(bf16[256,1024]{1,0:T(8,128)(2,1)S(1)} %multiply_convert_fusion.refs_0_, f32[32,256]{1,0:T(8,128)S(1)} %fusion.13.refs_1_), custom_call_target="tpu_custom_call" | custom-call | bytes 114000000 | tf_op jit(solution)/shard_map/pallas_call | solution.py:170
  101.2 73.5 %shard_map.233 = (bf16[1024,1024]{1,0:T(8,128)(2,1)}, bf16[1024,1024]{1,0:T(8,128)(2,1)}, f32[8,8,128]{2,1,0:T(8,128)}, bf16[4,8,384,512]{3,2,1,0:T(8,128)(2,1)}) custom-call(bf16[256,1024]{1,0:T(8,128)(2,1)} %bitcast.128, bf16[256,1024]{1,0:T(8,128)(2,1)} %collective-permute-done.refs_1_, bf16[256,1024]{1,0:T(8,128)(2,1)} %collective-permute-done.1.refs_2_, ...), custom_call_target="tpu_custom_call" | custom-call | bytes 195000000 | tf_op jit(solution)/shard_map/pallas_call | solution.py:532
  174.8 5.4 %fusion.21 = (bf16[2,2,4,384,512]{4,3,2,1,0:T(8,128)(2,1)S(1)}, bf16[2,2,4,384,512]{4,3,2,1,0:T(8,128)(2,1)S(1)}) fusion(bf16[2,2,8,384,512]{4,3,2,1,0:T(8,128)(2,1)} %bitcast.122), kind=kLoop, calls=%fused_computation.71 | loop fusion | bytes 25165824 | tf_op jit(solution)/shard_map/slice | solution.py:834
  180.2 2.0 dynamic-slice_bitcast_fusion
  183.8 1.8 copy-done.29
  185.6 1.9 dynamic-slice_bitcast_fusion.1
  187.6 2.3 collective-permute-start.6
  192.9 3.8 collective-permute-start.4
  196.8 70.2 %shard_map.234 = (bf16[256,1024]{1,0:T(8,128)(2,1)S(1)}, f32[4,8,256]{2,1,0:T(8,128)S(1)}) custom-call(bf16[4,256,1024]{2,1,0:T(8,128)(2,1)S(1)} %bitcast.108, f32[4,8,256]{2,1,0:T(8,128)S(1)} %bitcast.112), custom_call_target="tpu_custom_call" | custom-call | bytes 120000000 | tf_op jit(solution)/shard_map/pallas_call | solution.py:329
  268.2 2.6 multiply_subtract_fusion
  272.1 15.3 %shard_map.235 = (bf16[256,1024]{1,0:T(8,128)(2,1)S(1)}, bf16[8,256,512]{2,1,0:T(8,128)(2,1)S(1)}, bf16[8,256,512]{2,1,0:T(8,128)(2,1)S(1)}) custom-call(s32[1]{0:T(128)} %bitcast.1.dp_ref, s32[256,1]{1,0:T(8,128)S(1)} %copy.45.starts_ref, bf16[256,1024]{1,0:T(8,128)(2,1)S(1)} %copy-done.17, bf16[8,256,512]{2,1,0:T(8,128)(2,1)} %copy-done.3, ...), custom_call_target="tpu_custom_call" | custom-call | bytes 75000000 | tf_op jit(solution)/shard_map/pallas_call | solution.py:746
  287.4 26.4 %shard_map.236 = (bf16[256,512]{1,0:T(8,128)(2,1)S(1)}, bf16[256,512]{1,0:T(8,128)(2,1)S(1)}) custom-call(bf16[8,256,512]{2,1,0:T(8,128)(2,1)S(1)} %get-tuple-element.75.refs_0_, bf16[8,256,512]{2,1,0:T(8,128)(2,1)S(1)} %get-tuple-element.76.refs_1_), custom_call_target="tpu_custom_call" | custom-call | bytes 75000000 | tf_op jit(solution)/shard_map/pallas_call | solution.py:329
  314.0 3.1 fusion.1
  318.6 1.7 collective-permute-start.8
  320.3 2.9 fusion
  330.9 6.4 %shard_map.237 = (bf16[8,128,1024]{2,1,0:T(8,128)(2,1)}, bf16[8,128,512]{2,1,0:T(8,128)(2,1)S(1)}, bf16[8,128,512]{2,1,0:T(8,128)(2,1)S(1)}, f32[256,1024]{1,0:T(8,128)}, f32[1,1024]{1,0:T(1,128)S(1)}) custom-call(bf16[256,1024]{1,0:T(8,128)(2,1)S(1)} %copy-done.19, bf16[256,1024]{1,0:T(8,128)(2,1)S(1)} %copy-done.21, bf16[256,512]{1,0:T(8,128)(2,1)S(1)} %copy-done.23, ...), custom_call_target="tpu_custom_call" | custom-call | bytes 30000000 | tf_op jit(solution)/shard_map/pallas_call | solution.py:817
  340.5 49.3 %shard_map.238 = (bf16[128,1024]{1,0:T(8,128)(2,1)S(1)}, bf16[128,1024]{1,0:T(8,128)(2,1)S(1)}, bf16[128,512]{1,0:T(8,128)(2,1)S(1)}, bf16[128,512]{1,0:T(8,128)(2,1)S(1)}, bf16[128,128]{1,0:T(8,128)(2,1)S(1)}) custom-call(bf16[8,128,1024]{2,1,0:T(8,128)(2,1)S(1)} %copy-done.13, bf16[8,128,1024]{2,1,0:T(8,128)(2,1)} %bitcast.123, ...), custom_call_target="tpu_custom_call" | custom-call | bytes 135000000 | tf_op jit(solution)/shard_map/pallas_call | solution.py:329
  389.8 17.5 %shard_map.239 = (bf16[32,1024]{1,0:T(8,128)(2,1)S(1)}, bf16[32,1024]{1,0:T(8,128)(2,1)S(1)}, bf16[32,512]{1,0:T(8,128)(2,1)S(1)}, bf16[32,512]{1,0:T(8,128)(2,1)S(1)}, bf16[32,128]{1,0:T(8,128)(2,1)S(1)}) custom-call(bf16[4,32,1024]{2,1,0:T(8,128)(2,1)S(1)} %bitcast.110, bf16[4,32,1024]{2,1,0:T(8,128)(2,1)S(1)} %bitcast.111, ...), custom_call_target="tpu_custom_call" | custom-call | bytes 54000000 | tf_op jit(solution)/shard_map/pallas_call | solution.py:329
  411.2 1.8 fusion.3
  413.1 1.9 fusion.2
  415.7 2.5 fusion.22
  (198 shorter events, 48.1 us)
Async XLA Ops:
  0.6 56.7 %copy-start = (bf16[1024,32]{0,1:T(8,128)(2,1)S(1)}, bf16[1024,32]{0,1:T(8,128)(2,1)}, u32[]{:S(2)}) copy-start(bf16[1024,32]{0,1:T(8,128)(2,1)} %param.23) | copy-start | bytes 196612
  0.7 100.6 %collective-permute-start = (bf16[256,1024]{1,0:T(8,128)(2,1)}, bf16[256,1024]{1,0:T(8,128)(2,1)}, u32[]{:S(2)}, u32[]{:S(2)}) collective-permute-start(bf16[256,1024]{1,0:T(8,128)(2,1)} %bitcast.125), channel_id=1, source_target_pairs={{0,8},{8,16},{16,24},{24,0},{1,9},{9,17},{17,25},{25,1},{2,10},{10... | collective-permute-start | bytes 1572872 | tf_op jit(solution)/shard_map/ppermute | solution.py:900
  2.3 99.0 %collective-permute-start.1 = (bf16[256,1024]{1,0:T(8,128)(2,1)}, bf16[256,1024]{1,0:T(8,128)(2,1)}, u32[]{:S(2)}, u32[]{:S(2)}) collective-permute-start(bf16[256,1024]{1,0:T(8,128)(2,1)} %bitcast.126), channel_id=1, source_target_pairs={{0,16},{8,24},{16,0},{24,8},{1,17},{9,25},{17,1},{25,9},{2,18},{10... | collective-permute-start | bytes 1572872 | tf_op jit(solution)/shard_map/ppermute | solution.py:900
  3.5 97.7 %collective-permute-start.2 = (bf16[256,1024]{1,0:T(8,128)(2,1)}, bf16[256,1024]{1,0:T(8,128)(2,1)}, u32[]{:S(2)}, u32[]{:S(2)}) collective-permute-start(bf16[256,1024]{1,0:T(8,128)(2,1)} %bitcast.127), channel_id=1, source_target_pairs={{0,24},{8,0},{16,8},{24,16},{1,25},{9,1},{17,9},{25,17},{2,26},{10... | collective-permute-start | bytes 1572872 | tf_op jit(solution)/shard_map/ppermute | solution.py:900
  57.1 43.5 %copy-start.43 = (pred[256,32]{0,1:T(8,128)(4,1)}, pred[256,32]{0,1:T(8,128)(4,1)S(1)}, u32[]{:S(2)}) copy-start(pred[256,32]{0,1:T(8,128)(4,1)S(1)} %fusion.6) | copy-start | bytes 24580
  57.6 42.9 %copy-start.45 = (f32[256]{0:T(256)}, f32[256]{0:T(256)S(1)}, u32[]{:S(2)}) copy-start(f32[256]{0:T(256)S(1)} %get-tuple-element.123) | copy-start | bytes 3076
  57.6 42.9 %copy-start.41 = (f32[256,32]{0,1:T(8,128)}, f32[256,32]{0,1:T(8,128)S(1)}, u32[]{:S(2)}) copy-start(f32[256,32]{0,1:T(8,128)S(1)} %get-tuple-element.124) | copy-start | bytes 98308
  187.5 79.5 %copy-start.42 = (f32[256,32]{0,1:T(8,128)S(1)}, f32[256,32]{0,1:T(8,128)}, u32[]{:S(2)}) copy-start(f32[256,32]{0,1:T(8,128)} %copy-done.41) | copy-start | bytes 98308
  187.5 79.5 %copy-start.44 = (pred[256,32]{0,1:T(8,128)(4,1)S(1)}, pred[256,32]{0,1:T(8,128)(4,1)}, u32[]{:S(2)}) copy-start(pred[256,32]{0,1:T(8,128)(4,1)} %copy-done.43) | copy-start | bytes 24580
  187.5 79.5 %copy-start.46 = (f32[256]{0:T(256)S(1)}, f32[256]{0:T(256)}, u32[]{:S(2)}) copy-start(f32[256]{0:T(256)} %copy-done.45) | copy-start | bytes 3076
  187.5 79.5 %copy-start.51 = (f32[256]{0:T(256)S(1)}, f32[256]{0:T(256)}, u32[]{:S(2)}) copy-start(f32[256]{0:T(256)} %copy-done.50) | copy-start | bytes 3076
  187.5 79.6 %copy-start.33 = (f32[256,1024]{1,0:T(8,128)S(1)}, f32[256,1024]{1,0:T(8,128)}, u32[]{:S(2)}) copy-start(f32[256,1024]{1,0:T(8,128)} %copy-done.32) | copy-start | bytes 3145732
  187.5 79.6 %copy-start.48 = (f32[1024]{0:T(1024)S(1)}, f32[1024]{0:T(1024)}, u32[]{:S(2)}) copy-start(f32[1024]{0:T(1024)} %param.22) | copy-start | bytes 12292
  187.6 79.6 %copy-start.53 = (f32[256]{0:T(256)S(1)}, f32[256]{0:T(256)}, u32[]{:S(2)}) copy-start(f32[256]{0:T(256)} %copy-done.52) | copy-start | bytes 3076
  187.6 126.4 %collective-permute-start.6 = (bf16[2,4,384,512]{3,2,1,0:T(8,128)(2,1)}, bf16[2,4,384,512]{3,2,1,0:T(8,128)(2,1)}, u32[]{:S(2)}, u32[]{:S(2)}) collective-permute-start(bf16[2,4,384,512]{3,2,1,0:T(8,128)(2,1)} %dynamic-slice_bitcast_fusion.1), channel_id=1, source_target_pairs={{0,4},{1,5},{2,6},{3,7},{4,0},{5,1},{6,2},{7,3},{8,12},{9,13},{10,... | collective-permute-start | bytes 9437192 | tf_op jit(solution)/shard_map/ppermute | solution.py:842
  189.9 130.4 %collective-permute-start.7 = (bf16[2,4,384,512]{3,2,1,0:T(8,128)(2,1)}, bf16[2,4,384,512]{3,2,1,0:T(8,128)(2,1)}, u32[]{:S(2)}, u32[]{:S(2)}) collective-permute-start(bf16[2,4,384,512]{3,2,1,0:T(8,128)(2,1)} %dynamic-slice_bitcast_fusion), channel_id=1, source_target_pairs={{0,2},{1,3},{2,0},{3,1},{4,6},{5,7},{6,4},{7,5},{8,10},{9,11},{10,... | collective-permute-start | bytes 9437192 | tf_op jit(solution)/shard_map/ppermute | solution.py:842
  191.7 76.4 %copy-start.40 = (bf16[2,128,1024]{2,1,0:T(8,128)(2,1)S(1)}, bf16[2,128,1024]{2,1,0:T(8,128)(2,1)}, u32[]{:S(2)}) copy-start(bf16[2,128,1024]{2,1,0:T(8,128)(2,1)} %param.27) | copy-start | bytes 1572868
  191.7 76.4 %copy-start.56 = (f32[256]{0:T(256)S(1)}, f32[256]{0:T(256)}, u32[]{:S(2)}) copy-start(f32[256]{0:T(256)} %get-tuple-element.117) | copy-start | bytes 3076
  191.7 76.3 %collective-permute-start.3 = (bf16[256,1024]{1,0:T(8,128)(2,1)S(1)}, bf16[256,1024]{1,0:T(8,128)(2,1)S(1)}, u32[]{:S(2)}, u32[]{:S(2)}) collective-permute-start(bf16[256,1024]{1,0:T(8,128)(2,1)S(1)} %get-tuple-element.110), channel_id=1, source_target_pairs={{0,8},{8,16},{16,24},{24,0},{1,9},{9,17},{17,25},{25,1},{2,10},{10... | collective-permute-start | bytes 1572872 | tf_op jit(solution)/shard_map/ppermute | solution.py:900
  192.9 75.2 %collective-permute-start.4 = (bf16[256,1024]{1,0:T(8,128)(2,1)S(1)}, bf16[256,1024]{1,0:T(8,128)(2,1)S(1)}, u32[]{:S(2)}, u32[]{:S(2)}) collective-permute-start(bf16[256,1024]{1,0:T(8,128)(2,1)S(1)} %get-tuple-element.112), channel_id=1, source_target_pairs={{0,16},{8,24},{16,0},{24,8},{1,17},{9,25},{17,1},{25,9},{2,18},{10... | collective-permute-start | bytes 1572872 | tf_op jit(solution)/shard_map/ppermute | solution.py:900
  196.7 71.5 %collective-permute-start.5 = (bf16[256,1024]{1,0:T(8,128)(2,1)S(1)}, bf16[256,1024]{1,0:T(8,128)(2,1)S(1)}, u32[]{:S(2)}, u32[]{:S(2)}) collective-permute-start(bf16[256,1024]{1,0:T(8,128)(2,1)S(1)} %get-tuple-element.111), channel_id=1, source_target_pairs={{0,24},{8,0},{16,8},{24,16},{1,25},{9,1},{17,9},{25,17},{2,26},{10... | collective-permute-start | bytes 1572872 | tf_op jit(solution)/shard_map/ppermute | solution.py:900
  318.6 92.7 %collective-permute-start.8 = (bf16[4,384,512]{2,1,0:T(8,128)(2,1)}, bf16[4,384,512]{2,1,0:T(8,128)(2,1)}, u32[]{:S(2)}, u32[]{:S(2)}) collective-permute-start(bf16[4,384,512]{2,1,0:T(8,128)(2,1)} %dynamic-slice_bitcast_fusion.3), channel_id=1, source_target_pairs={{0,2},{1,3},{2,0},{3,1},{4,6},{5,7},{6,4},{7,5},{8,10},{9,11},{10,... | collective-permute-start | bytes 4718600 | tf_op jit(solution)/shard_map/ppermute | solution.py:842
  325.3 87.8 %collective-permute-start.9 = (bf16[4,384,512]{2,1,0:T(8,128)(2,1)}, bf16[4,384,512]{2,1,0:T(8,128)(2,1)}, u32[]{:S(2)}, u32[]{:S(2)}) collective-permute-start(bf16[4,384,512]{2,1,0:T(8,128)(2,1)} %dynamic-slice_bitcast_fusion.2), channel_id=1, source_target_pairs={{0,4},{1,5},{2,6},{3,7},{4,0},{5,1},{6,2},{7,3},{8,12},{9,13},{10,... | collective-permute-start | bytes 4718600 | tf_op jit(solution)/shard_map/ppermute | solution.py:842
  340.5 70.7 %copy-start.35 = (bf16[2,4,384,512]{3,2,1,0:T(8,128)(2,1)S(1)}, bf16[2,4,384,512]{3,2,1,0:T(8,128)(2,1)}, u32[]{:S(2)}) copy-start(bf16[2,4,384,512]{3,2,1,0:T(8,128)(2,1)} %copy-done.34) | copy-start | bytes 9437188
  (47 other events, 433.5 us)

commit v4 on v3

--- a/solution.py
+++ b/solution.py
@@ -72,26 +72,17 @@
         copy.start()
         own.append(copy)
 
-    def dp_step(t):
-        copies = []
-        for a in range(n_dp):
-            order = gather_orders(nd)[a % 2]
-            for j, m in enumerate(masks(order[:t])):
-                block = jnp.bitwise_xor(dp, m)
-                src = ins[a] if m == 0 else outs[a].at[block]
-                k = (1 << t) - 1 + j
-                copies.append(
-                    remote(
-                        src,
-                        outs[a].at[block],
-                        dp_send.at[a, k],
-                        dp_recv.at[a, k],
-                        {"dp": jnp.bitwise_xor(dp, 1 << order[t])},
-                    )
-                )
-        for c in copies:
-            c.start()
-        return copies
+    def dp_copy(a, t, m):
+        order = gather_orders(nd)[a % 2]
+        block = jnp.bitwise_xor(dp, m)
+        k = (1 << t) - 1 + masks(order[:t]).index(m)
+        return remote(
+            ins[a] if m == 0 else outs[a].at[block],
+            outs[a].at[block],
+            dp_send.at[a, k],
+            dp_recv.at[a, k],
+            {"dp": jnp.bitwise_xor(dp, 1 << order[t])},
+        )
 
     def ep_copy(a, s, way):
         shard = lax.rem(ep - way * s + ne, ne)
@@ -133,20 +124,25 @@
 
     dp_steps = bit_count(nd) if n_dp else 0
     ep_steps = ne - 1 if n_ep else 0
-    started = []
+    for t in range(dp_steps):
+        for a in range(n_dp):
+            dp_copy(a, t, 0).start()
     for t in range(max(dp_steps, ep_steps) + 1):
         if 0 < t <= dp_steps:
-            for c in started[-1]:
-                c.wait_recv()
-        if t < dp_steps:
-            started.append(dp_step(t))
+            for a in range(n_dp):
+                order = gather_orders(nd)[a % 2]
+                for m in masks(order[: t - 1]):
+                    dp_copy(a, t - 1, m).wait_recv()
+                    for later in range(t, dp_steps):
+                        dp_copy(a, later, m | (1 << order[t - 1])).start()
         if 0 < t <= ep_steps:
             ep_wait(t - 1)
         if t < ep_steps:
             ep_start(t)
-    for group in started:
-        for c in group:
-            c.wait_send()
+    for t in range(dp_steps):
+        for a in range(n_dp):
+            for m in masks(gather_orders(nd)[a % 2][:t]):
+                dp_copy(a, t, m).wait_send()
     for s in range(ep_steps):
         for a in range(n_ep):
             for way in (1, -1):
@@ -182,7 +178,7 @@
             DMA((b, 2, ne - 1)),
         ],
         compiler_params=pltpu.CompilerParams(
-            collective_id=collective, has_side_effects=True, vmem_limit_bytes=8 * 2**20
+            collective_id=collective, has_side_effects=True, vmem_limit_bytes=60 * 2**20
         ),
         cost_estimate=cost(us),
     )(*arrays)
@@ -290,16 +286,16 @@
         if t < ep_steps:
             ep_go(t)
 
-        if 0 < t <= dp_steps:
-            for a, group in started[-1]:
-                for m, k, c in group:
+        groups = [(a, dp_copies(a, t)) for a in range(n_dp)] if t < dp_steps else []
+        for a in range(n_dp):
+            if 0 < t <= dp_steps:
+                for m, k, c in started[-1][a][1]:
                     c.wait_recv()
                     add(a, jnp.bitwise_xor(dp, m), landing[a][k])
-        if t < dp_steps:
-            started.append([(a, dp_copies(a, t)) for a in range(n_dp)])
-            for a, group in started[-1]:
-                for m, k, c in group:
+            if t < dp_steps:
+                for m, k, c in groups[a][1]:
                     c.start()
+        started.append(groups)
     for a in range(n_dp):
         outs[a][...] = held[a][dp]
     for a in range(n_ep):
@@ -352,16 +348,139 @@
     )(*sums, *swap_arrays)
 
 
+def reduce_all_body(ne, nd, count, *refs):
+    ins, outs, held = refs[:count], refs[count : 2 * count], refs[2 * count : 3 * count]
+    pair_in, line_in = refs[3 * count : 4 * count], refs[4 * count : 5 * count]
+    in_sem, dp_send, dp_recv, ep_send, ep_recv = refs[5 * count :]
+    ep, dp = lax.axis_index("ep"), lax.axis_index("dp")
+    nb = bit_count(nd)
+
+    def load(a):
+        return pltpu.make_async_copy(ins[a], held[a], in_sem.at[a])
+
+    for a in range(count):
+        load(a).start()
+    greet(ep, dp, ne, nd)
+
+    def total(x, y):
+        return (x.astype(F32) + y.astype(F32)).astype(BF16)
+
+    def pair_copies(a, t):
+        order = gather_orders(nd)[a % 2][::-1]
+        partner = jnp.bitwise_xor(dp, 1 << order[t])
+        first = sum(1 << (nb - 1 - i) for i in range(t))
+        return [
+            (
+                m,
+                first + j,
+                remote(
+                    held[a].at[jnp.bitwise_xor(partner, m)],
+                    pair_in[a].at[first + j],
+                    dp_send.at[a, first + j],
+                    dp_recv.at[a, first + j],
+                    {"dp": partner},
+                ),
+            )
+            for j, m in enumerate(masks(order[t + 1 :]))
+        ]
+
+    for t in range(nb + 1):
+        for a in range(count):
+            if t == 0:
+                load(a).wait()
+            else:
+                for m, k, copy in pair_copies(a, t - 1):
+                    copy.wait_recv()
+                    block = jnp.bitwise_xor(dp, m)
+                    held[a][block] = total(held[a][block], pair_in[a][k])
+            if t < nb:
+                for m, k, copy in pair_copies(a, t):
+                    copy.start()
+
+    def line_copy(a, dest, way):
+        k = 0 if way == 1 else 1
+        return remote(
+            held[a].at[dp, dest],
+            line_in[a].at[k, dest],
+            ep_send.at[a, k, dest],
+            ep_recv.at[a, k, dest],
+            {"ep": lax.rem(ep + way + ne, ne)},
+        )
+
+    def line_turn(t, way):
+        dest = ep + ne - 1 - t if way == 1 else ep + t - (ne - 1)
+        has = dest <= ne - 1 if way == 1 else dest >= 0
+        inner = ep >= 1 if way == 1 else ep <= ne - 2
+        return dest, has, inner
+
+    for t in range(ne):
+        for a in range(count):
+            for way in (1, -1):
+                dest, has, inner = line_turn(t, way)
+
+                @pl.when(has & inner)
+                def _(a=a, way=way, dest=dest):
+                    line_copy(a, dest, way).wait_recv()
+                    held[a][dp, dest] = total(
+                        held[a][dp, dest], line_in[a][0 if way == 1 else 1, dest]
+                    )
+
+                if t < ne - 1:
+
+                    @pl.when(has)
+                    def _(a=a, way=way, dest=dest):
+                        line_copy(a, dest, way).start()
+
+    for a in range(count):
+        outs[a][...] = held[a][dp, ep]
+        for t in range(nb):
+            for m, k, copy in pair_copies(a, t):
+                copy.wait_send()
+        for t in range(ne - 1):
+            for way in (1, -1):
+                dest, has, inner = line_turn(t, way)
+
+                @pl.when(has)
+                def _(a=a, way=way, dest=dest):
+                    line_copy(a, dest, way).wait_send()
+
+
+def reduce_all(ne, nd, arrays, collective, us):
+    n = len(arrays)
+    tails = [v.shape[2:] for v in arrays]
+    return pl.pallas_call(
+        functools.partial(reduce_all_body, ne, nd, n),
+        out_shape=[jax.ShapeDtypeStruct(s, BF16) for s in tails],
+        in_specs=[ANY] * n,
+        out_specs=[VMEM] * n,
+        scratch_shapes=[pltpu.VMEM(v.shape, BF16) for v in arrays]
+        + [pltpu.VMEM((nd - 1, ne) + s, BF16) for s in tails]
+        + [pltpu.VMEM((2, ne) + s, BF16) for s in tails]
+        + [
+            DMA((n,)),
+            DMA((n, nd - 1)),
+            DMA((n, nd - 1)),
+            DMA((n, 2, ne)),
+            DMA((n, 2, ne)),
+        ],
+        compiler_params=pltpu.CompilerParams(
+            collective_id=collective, has_side_effects=True, vmem_limit_bytes=48 * 2**20
+        ),
+        cost_estimate=cost(us),
+    )(*arrays)
+
+
 def dot(a, b, dims=((1,), (0,))):
     return lax.dot_general(a, b, (dims, ((), ())), preferred_element_type=F32)
 
 
-def expert_body(ne, nd, micro, rows, *refs):
-    cots = refs[:ne]
-    normed_ref, probs_ref, gate_ref, up_ref, down_ref = refs[ne : ne + 5]
-    mix_ref, grad_ref, dots_ref, sums_ref = refs[ne + 5 : ne + 9]
-    rows_in, cots_in, picks, weights, first, second, keep, send, arrived = refs[ne + 9 : ne + 18]
-    load_sem, store_sem, send_sem, recv_sem, free_sem = refs[ne + 18 :]
+def expert_body(ne, nd, micro, rows, n_prior, *refs):
+    cots, prior, refs = refs[:ne], refs[ne : ne + n_prior], refs[ne + n_prior :]
+    normed_ref, probs_ref, gate_ref, up_ref, down_ref = refs[:5]
+    mix_ref, grad_ref, dots_ref = refs[5:8]
+    kept, sent = refs[8:10], refs[10:12]
+    rows_in, cots_in, picks, weights, first, second, keep, send, arrived = refs[12:21]
+    load_sem, store_sem, send_sem, recv_sem, free_sem = refs[21:]
     e = pl.program_id(0)
     last = pl.num_programs(0) - 1
     ep, dp = lax.axis_index("ep"), lax.axis_index("dp")
@@ -401,9 +520,39 @@
             ),
         )
 
+    def prior_loads(t):
+        at = block_at(returned(t))
+        out = []
+        for k, (src, dst) in enumerate(zip(prior, (first, second))):
+            out.append(
+                pltpu.make_async_copy(
+                    src.at[block_at(t) if k == 0 else at], dst.at[at], store_sem.at[k, t]
+                )
+            )
+        return out
+
     def collect():
         exchange().wait_recv()
-        sums_ref[:, 0] = (keep[...].astype(F32) + arrived[...].astype(F32)).astype(BF16)
+        pieces = keep.shape[0]
+        for i, bit in enumerate(first_bits(nd)):
+
+            def put(low, high, bit=bit):
+                for j in range(pieces):
+                    value = (keep[j].astype(F32) + arrived[j].astype(F32)).astype(BF16)
+                    at = (j >> bit << (bit - 1)) | (j & ((1 << (bit - 1)) - 1))
+                    ref = high if (j >> (bit - 1)) & 1 else low
+                    ref[at, 0] = value
+
+            here = (e - 1 < n_exp // 2) if i == 0 else (e - 1 >= n_exp // 2)
+            mine = jnp.bitwise_and(lax.shift_right_logical(dp, bit), 1)
+
+            @pl.when(here & (mine == 0))
+            def _(i=i, put=put):
+                put(kept[i], sent[i])
+
+            @pl.when(here & (mine == 1))
+            def _(i=i, put=put):
+                put(sent[i], kept[i])
 
     @pl.when(e == 0)
     def _():
@@ -434,6 +583,15 @@
             picks[s] = flat
             rows_in[s] = dot(flat, first[at, :]).astype(BF16).reshape(n_exp, CAP, width)
             cots_in[s] = dot(flat, second[at, :]).astype(BF16).reshape(n_exp, CAP, width)
+
+    if n_prior:
+
+        @pl.when(e == 1)
+        def _():
+            @pl.loop(0, blocks)
+            def _(t):
+                for copy in prior_loads(t):
+                    copy.start()
 
     @pl.when(e < last)
     def _():
@@ -503,12 +661,13 @@
             s = returned(t)
             at = block_at(s)
             flat = picks[s]
-            first[at, :] = dot(
-                flat, cots_in[s].reshape(n_exp * CAP, width), ((0,), (0,))
-            ).astype(BF16)
-            second[at, :] = dot(
-                flat, rows_in[s].reshape(n_exp * CAP, width), ((0,), (0,))
-            ).astype(BF16)
+            for copy in prior_loads(t):
+                copy.wait()
+            for done, slots in ((first, cots_in), (second, rows_in)):
+                value = dot(flat, slots[s].reshape(n_exp * CAP, width), ((0,), (0,)))
+                if n_prior:
+                    value = value + done[at, :].astype(F32)
+                done[at, :] = value.astype(BF16)
             for copy in stores(t):
                 copy.start()
 
@@ -521,18 +680,32 @@
                 copy.wait()
 
 
-def experts(normed, cots, probs, w_gate, w_up, w_down, micro, rows, ne, nd, collective):
-    n_exp, width, inner = w_gate.shape
+def first_bits(nd):
+    return [order[-2] for order in gather_orders(nd)]
+
+
+def experts(
+    normed, cots, probs, prior, start, w_gate, w_up, w_down, micro, rows, ne, nd, collective
+):
+    n_exp, (width, inner) = probs.shape[1], w_gate.shape[1:]
     blocks = ne * micro
     half = nd // 2
     packed = 2 * width // nd + (inner // nd) * (width // inner)
     full = (blocks * rows, width)
     one = pl.Buffered(1)
-    weight = lambda e: (jnp.minimum(e, n_exp - 1), 0, 0)
+    weight = lambda e: (start + jnp.minimum(e, n_exp - 1), 0, 0)
+    part = (half // 2, n_exp // 2, packed, inner)
+    parts = [
+        pl.BlockSpec(
+            (half // 2, 1, packed, inner),
+            lambda e, i=i: (0, jnp.clip(e - 1 - i * (n_exp // 2), 0, n_exp // 2 - 1), 0, 0),
+        )
+        for i in range(2)
+    ]
     return pl.pallas_call(
-        functools.partial(expert_body, ne, nd, micro, rows),
+        functools.partial(expert_body, ne, nd, micro, rows, len(prior)),
         grid=(n_exp + 1,),
-        in_specs=[ANY] * (ne + 1)
+        in_specs=[ANY] * (ne + 1 + len(prior))
         + [
             pl.BlockSpec(probs.shape, lambda e: (0, 0, 0), pipeline_mode=one),
             pl.BlockSpec((1, width, inner), weight),
@@ -542,9 +715,10 @@
         out_specs=[
             ANY,
             ANY,
-            pl.BlockSpec((1, blocks, rows), weight),
-            pl.BlockSpec((half, 1, packed, inner), lambda e: (0, jnp.maximum(e - 1, 0), 0, 0)),
-        ],
+            pl.BlockSpec((1, blocks, rows), lambda e: (jnp.minimum(e, n_exp - 1), 0, 0)),
+        ]
+        + parts
+        + parts,
         scratch_shapes=[
             pltpu.VMEM((blocks, n_exp, CAP, width), BF16),
             pltpu.VMEM((blocks, n_exp, CAP, width), BF16),
@@ -565,16 +739,16 @@
             jax.ShapeDtypeStruct(full, BF16),
             jax.ShapeDtypeStruct(full, BF16),
             jax.ShapeDtypeStruct((n_exp, blocks, rows), F32),
-            jax.ShapeDtypeStruct((half, n_exp, packed, inner), BF16),
-        ],
+        ]
+        + [jax.ShapeDtypeStruct(part, BF16)] * 4,
         compiler_params=pltpu.CompilerParams(
-            vmem_limit_bytes=62 * 2**20,
+            vmem_limit_bytes=60 * 2**20,
             dimension_semantics=("arbitrary",),
             collective_id=collective,
             has_side_effects=True,
         ),
-        cost_estimate=cost(65),
-    )(*cots, normed, probs, w_gate, w_up, w_down)
+        cost_estimate=cost(35),
+    )(*cots, *prior, normed, probs, w_gate, w_up, w_down)
 
 
 def rms_scale(values):
@@ -593,14 +767,24 @@
 
 
 def project_body(
-    tokens_ref, gain_ref, cos_ref, sin_ref, wq_ref, wk_ref, wv_ref, n_ref, q_ref, k_ref, v_ref
+    tokens_ref, gain_ref, cos_ref, sin_ref, wq_ref, wk_ref, wv_ref, n_ref, q_ref, k_ref, v_ref, *rest
 ):
+    wq, wk, wv, sem = rest
+    loads = [
+        pltpu.make_async_copy(src, dst, sem.at[i])
+        for i, (src, dst) in enumerate(((wk_ref, wk), (wv_ref, wv), (wq_ref, wq)))
+    ]
+    for copy in loads:
+        copy.start()
     x = tokens_ref[...].astype(F32)
     n_ref[...] = (x * rms_scale(x) * gain_ref[...]).astype(BF16)
     normed = n_ref[...]
     cosine, sine = cos_ref[...], sin_ref[...]
     tile = 256
-    for w, out, turned in ((wk_ref, k_ref, True), (wv_ref, v_ref, False), (wq_ref, q_ref, True)):
+    for copy, (w, out, turned) in zip(
+        loads, ((wk, k_ref, True), (wv, v_ref, False), (wq, q_ref, True))
+    ):
+        copy.wait()
         for c in range(0, w.shape[1], tile):
             y = dot(normed, w[:, c : c + tile])
             if turned:
@@ -616,9 +800,10 @@
     return pl.pallas_call(
         project_body,
         out_shape=[jax.ShapeDtypeStruct((rows, n), BF16) for n in shapes],
-        in_specs=[VMEM] * 7,
+        in_specs=[VMEM] * 4 + [ANY] * 3,
         out_specs=[VMEM] * 4,
-        compiler_params=pltpu.CompilerParams(vmem_limit_bytes=32 * 2**20),
+        scratch_shapes=[pltpu.VMEM(w.shape, BF16) for w in (w_query, w_key, w_value)] + [DMA((3,))],
+        compiler_params=pltpu.CompilerParams(vmem_limit_bytes=60 * 2**20),
         cost_estimate=cost(5),
     )(tokens, gain, cosine, sine, w_query, w_key, w_value)
 
@@ -829,15 +1014,6 @@
     )(normed, dq, dk, dv, cosine, sine, *weights, tokens, gain, grad_residual)
 
 
-def halves(values, dp, axis, bit, part, parts_axis):
-    count = values.shape[parts_axis] // 2
-    values = lax.slice_in_dim(values, part * count, (part + 1) * count, axis=parts_axis)
-    mine = jnp.bitwise_and(lax.shift_right_logical(dp, bit), 1)
-    kept = lax.dynamic_index_in_dim(values, mine, axis, keepdims=False)
-    sent = lax.dynamic_index_in_dim(values, 1 - mine, axis, keepdims=False)
-    return kept, sent
-
-
 def swap_bit(sent, bit, nd):
     return lax.ppermute(sent, "dp", [(i, i ^ (1 << bit)) for i in range(nd)])
 
@@ -928,32 +1104,58 @@
         .transpose(0, 2, 1, 3)
         .reshape(ne * micro, here, rows)
     )
-    mix, grad_in, pair_dots, sums = experts(
-        normed_all.reshape(ne * every, width),
-        cots,
-        probs_here,
-        w_gate,
-        w_up,
-        w_down,
-        micro,
-        rows,
-        ne,
-        nd,
-        6,
-    )
     nb = bit_count(nd)
-    sums = sums.reshape((2,) * (nb - 1) + sums.shape[1:])
     orders = [order[:-1][::-1] for order in gather_orders(nd)]
-    first_kept, first_sent = zip(
-        *[halves(sums, dp, nb - 1 - orders[i][0], orders[i][0], i, nb - 1) for i in range(2)]
-    )
-    grad_in, *first_sent = tie(grad_in, *first_sent)
-    first_arrived = [swap_bit(v, orders[i][0], nd) for i, v in enumerate(first_sent)]
+    prior, dots, kept, arrived = (), [], [], []
+    for h in range(2):
+        count = here // 2
+        *prior, dot_part, kept_a, kept_b, sent_a, sent_b = experts(
+            normed_all.reshape(ne * every, width),
+            cots,
+            probs_here[:, h * count : (h + 1) * count],
+            prior,
+            h * count,
+            w_gate,
+            w_up,
+            w_down,
+            micro,
+            rows,
+            ne,
+            nd,
+            6 + h,
+        )
+        dots.append(dot_part)
+        kept.append((kept_a, kept_b))
+        arrived.append(
+            [swap_bit(v, orders[i][0], nd) for i, v in enumerate((sent_a, sent_b))]
+        )
+    mix, grad_in = prior
+    pair_dots = jnp.concatenate(dots, axis=0)
+
+    def finish(h, i, after):
+        value, bits = plus(kept[h][i], arrived[h][i]), orders[i]
+        value = value.reshape((2,) * (nb - 2) + value.shape[1:])
+        live = [b for b in range(nb - 1, 0, -1) if b != bits[0]]
+        for n, bit in enumerate(bits[1:]):
+            axis = live.index(bit)
+            mine = jnp.bitwise_and(lax.shift_right_logical(dp, bit), 1)
+            keeps = lax.dynamic_index_in_dim(value, mine, axis, keepdims=False)
+            sends = lax.dynamic_index_in_dim(value, 1 - mine, axis, keepdims=False)
+            if n == 0:
+                after, sends = tie(after, sends)
+            value = plus(keeps, swap_bit(sends, bit, nd))
+            live.remove(bit)
+        return value, after
+
+    grads = {}
+    for i in range(2):
+        grads[0, i], grad_in = finish(0, i, grad_in)
 
     pair_dots = pair_dots.reshape(here, ne, every).transpose(1, 0, 2)
     grad_back, dots_all = reduce(
         ne, nd, (), (grad_in.reshape(ne, every, width),), (pair_dots,), 2, 40
     )
+    grad_back, mix = tie(grad_back, mix)
     pair_dot = dots_all.reshape(EXPERTS, every).T
     grad_logits = gate_probs * (
         pair_dot - jnp.sum(gate_probs * pair_dot, axis=1, keepdims=True)
@@ -977,6 +1179,8 @@
     grad_attn = jnp.einsum("td,fd->tf", residual_low, w_out, preferred_element_type=F32).astype(
         BF16
     )
+    for i in range(2):
+        grads[1, i], grad_attn = finish(1, i, grad_attn)
     grad_query, grad_key_all, grad_value_all = attend_back(
         dp,
         starts,
@@ -995,20 +1199,7 @@
     mix_parts = [mix[0]] + [around(mix[k], k) for k in range(1, ne)]
     grad_key, grad_value = reduce(ne, nd, (grad_key_all, grad_value_all), (), (), 3, 25)
 
-    grads = []
-    for i in range(2):
-        value, bits = plus(first_kept[i], first_arrived[i]), orders[i]
-        live = [b for b in range(nb - 1, 0, -1) if b != bits[0]]
-        for bit in bits[1:]:
-            axis = live.index(bit)
-            mine = jnp.bitwise_and(lax.shift_right_logical(dp, bit), 1)
-            kept = lax.dynamic_index_in_dim(value, mine, axis, keepdims=False)
-            sent = lax.dynamic_index_in_dim(value, 1 - mine, axis, keepdims=False)
-            grad_key, sent = tie(grad_key, sent)
-            value = plus(kept, swap_bit(sent, bit, nd))
-            live.remove(bit)
-        grads.append(value)
-    grads = jnp.concatenate(grads, axis=0).astype(F32)
+    grads = jnp.concatenate([grads[h, i] for h in range(2) for i in range(2)], axis=0).astype(F32)
     share = width // nd
     grad_w_gate, grad_w_up = grads[:, :share], grads[:, share : 2 * share]
     grad_w_down = jnp.concatenate(
@@ -1047,23 +1238,24 @@
 
     def by_owner(grad):
         share = grad.shape[0] // (ne * nd)
-        return (
-            grad.astype(BF16)
-            .reshape(ne, nd, share, grad.shape[1])
-            .transpose(1, 0, 2, 3)
-            .reshape(nd, ne * share, grad.shape[1])
-        )
-
-    dense = reduce(
+        return grad.astype(BF16).reshape(ne, nd, share, grad.shape[1]).transpose(1, 0, 2, 3)
+
+    def blocks_of(grad):
+        return grad.reshape(nd, ne, -1, grad.shape[2])
+
+    dense = reduce_all(
         ne,
         nd,
-        (grad_w_query, by_owner(grad_w_out), grad_w_key, grad_w_value, by_owner(small)),
-        (),
-        (),
+        (
+            blocks_of(grad_w_query),
+            by_owner(grad_w_out),
+            blocks_of(grad_w_key),
+            blocks_of(grad_w_value),
+            by_owner(small),
+        ),
         4,
-        45,
-    )
-    dense = reduce(ne, nd, (), [v.reshape(ne, -1, v.shape[1]) for v in dense], (), 5, 18)
+        60,
+    )
     d_query, d_out, d_key, d_value, d_small = (v.astype(F32) for v in dense)
     return (
         output,

time: 422 us -> 496 us (1.18)
  waiting for transfers between devices: 0.03 us -> 103 us
  Pallas kernels: 336 us -> 306 us
  local copies, waits for them, and re-layouts: 42.7 us -> 32.1 us
  other arithmetic: 21 us -> 27.3 us
    pallas_call x4 -> x2, Pallas kernels: 163 us -> 67.2 us  [reduce(): pl.pallas_call(functools.partial(reduce_body, ne, nd, len(dp_arrays), len...]
    ppermute x4 -> x8, waiting for transfers between devices: 0.01 us -> 70.5 us  [swap_bit(): return lax.ppermute(sent, 'dp', [(i, i ^ 1 << bit) for i in range(nd)])]
    pallas_call x1 -> x3, Pallas kernels: 73.5 us -> 137 us  [the longest x2 85.3 us: experts(): pl.pallas_call(functools.partial(expert_body, ne, nd, micro, rows, len(pr...]
    ppermute x6, waiting for transfers between devices: 0.02 us -> 32.5 us  [around(): return lax.ppermute(value, 'ep', [(i, (i + k) % ne) for i in range(ne)])]
    unnamed x124 -> x84, local copies, waits for them, and re-layouts: 20.5 us -> 15.3 us
    convert_element_type x4 -> x8, other arithmetic: 9.64 us -> 12.6 us  [plus(): return (a.astype(F32) + b.astype(F32)).astype(BF16)]
  transfers between devices with their start and end apart: 10 -> 14, of which waited for: 0 -> 5; matrix products, arithmetic and copies ran while one was open for 7% -> 9% of each run, Pallas kernels for 63% -> 54%
where the time goes in v4:
time: 496 us; the launch traced here: 492 us
  Pallas kernels  306 us (62%)
  waiting for transfers between devices  103 us (21%)
  local copies, waits for them, and re-layouts  32.1 us (6%)
  other arithmetic  27.3 us (6%)
  starting transfers between devices  15.5 us (3%)
  matrix products  6.16 us (1%)
    pallas_call x2, Pallas kernels, experts(): pl.pallas_call(functools.partial(expert_body, ne, nd, micro, rows, len(pr...  85.3 us
    ppermute x8, waiting for transfers between devices, swap_bit(): return lax.ppermute(sent, 'dp', [(i, i ^ 1 << bit) for i in range(nd)])  70.5 us
    pallas_call x2, Pallas kernels, reduce(): pl.pallas_call(functools.partial(reduce_body, ne, nd, len(dp_arrays), len...  67.2 us
    pallas_call x2, Pallas kernels, gather(): pl.pallas_call(functools.partial(gather_body, ne, nd, len(dp_arrays), len...  64.8 us
    pallas_call x1, Pallas kernels, reduce_all(): pl.pallas_call(functools.partial(reduce_all_body, ne, nd, n), out_shape=[...  51.5 us
    ppermute x6, waiting for transfers between devices, around(): return lax.ppermute(value, 'ep', [(i, (i + k) % ne) for i in range(ne)])  32.5 us
    unnamed x84, local copies, waits for them, and re-layouts  15.3 us
    pallas_call x1, Pallas kernels, attend_back(): pl.pallas_call(functools.partial(attend_back_body, nd // 2 + 1), grid_spe...  15.1 us
  transfers between devices with their start and end apart: 14, of which 5 were waited for; matrix products, arithmetic and copies ran while one was open for 9% of the time, Pallas kernels for 54%

profile of v4, /device:TPU:10, one launch (start us, length us, event | category | flops | bytes accessed | tf_op | source)
XLA Modules:
  0.0 491.8 jit_solution(3375857551883223770)
XLA Ops:
  1.2 2.6 collective-permute-start.1
  3.8 2.5 collective-permute-start
  10.2 5.4 %shard_map.229 = (bf16[256,1024]{1,0:T(8,128)(2,1)}, bf16[256,1024]{1,0:T(8,128)(2,1)}, bf16[256,512]{1,0:T(8,128)(2,1)}, bf16[256,512]{1,0:T(8,128)(2,1)}) custom-call(bf16[256,1024]{1,0:T(8,128)(2,1)} %bitcast.96, f32[1,1024]{1,0:T(1,128)} %bitcast.104, f32[256,128]{1,0:T(8,128)} %copy.39.cos_ref, f32[256,128]{1,0:T(8,128)} %broadcast_multiply_fusion.sin_ref, ...), custom_call_target="tpu_custom_call" | custom-call | bytes 15000000 | tf_op jit(solution)/shard_map/pallas_call | solution.py:800
  15.6 23.0 %shard_map.230 = (bf16[8,256,512]{2,1,0:T(8,128)(2,1)}, bf16[8,256,512]{2,1,0:T(8,128)(2,1)}, f32[8,8,128]{2,1,0:T(8,128)}) custom-call(bf16[256,512]{1,0:T(8,128)(2,1)} %get-tuple-element.64.refs_0_, bf16[256,512]{1,0:T(8,128)(2,1)} %get-tuple-element.65.refs_1_, f32[8,128]{1,0:T(8,128)} %concatenate.26.refs_2_), custom_call_target="tpu_custom_call" | custom-call | bytes 75000000 | tf_op jit(solution)/shard_map/pallas_call | solution.py:166
  43.9 10.4 %shard_map.231 = (bf16[256,1024]{1,0:T(8,128)(2,1)S(1)}, f32[2,4,512,1]{3,2,1,0:T(8,128)S(1)}) custom-call(s32[1]{0:T(128)} %bitcast.1.dp_ref, s32[256,1]{1,0:T(8,128)S(1)} %copy.40.starts_ref, bf16[256,1024]{1,0:T(8,128)(2,1)S(1)} %copy-done.10, bf16[8,256,512]{2,1,0:T(8,128)(2,1)S(1)} %copy-done.1, bf16[8,256,512]{2,1,0:T(8,128)(2,1)S(1)} %copy-done.2), custom_call_target="tpu_custom_call" | custom-call | bytes 45000000 | tf_op jit(solution)/shard_map/pallas_call | solution.py:887
  58.5 41.8 %shard_map.232 = (bf16[4,256,1024]{2,1,0:T(8,128)(2,1)}, f32[4,32,256]{2,1,0:T(8,128)}) custom-call(bf16[256,1024]{1,0:T(8,128)(2,1)} %copy-done.21, f32[32,256]{1,0:T(8,128)} %fusion.13.refs_1_), custom_call_target="tpu_custom_call" | custom-call | bytes 114000000 | tf_op jit(solution)/shard_map/pallas_call | solution.py:166
  101.7 42.4 %shard_map.233 = (bf16[1024,1024]{1,0:T(8,128)(2,1)}, bf16[1024,1024]{1,0:T(8,128)(2,1)}, f32[4,8,128]{2,1,0:T(8,128)}, bf16[2,2,384,512]{3,2,1,0:T(8,128)(2,1)}...) custom-call(bf16[256,1024]{1,0:T(8,128)(2,1)} %bitcast.113, ...), custom_call_target="tpu_custom_call" | custom-call | bytes 105000000 | tf_op jit(solution)/shard_map/pallas_call | solution.py:705
  144.7 42.9 %shard_map.234 = (bf16[1024,1024]{1,0:T(8,128)(2,1)}, bf16[1024,1024]{1,0:T(8,128)(2,1)}, f32[4,8,128]{2,1,0:T(8,128)}, bf16[2,2,384,512]{3,2,1,0:T(8,128)(2,1)}...) custom-call(bf16[256,1024]{1,0:T(8,128)(2,1)} %bitcast.114, ...), custom_call_target="tpu_custom_call" | custom-call | bytes 105000000 | tf_op jit(solution)/shard_map/pallas_call | solution.py:705
  192.1 2.5 add_convert_fusion.3
  194.6 30.1 %collective-permute-done.8 = bf16[2,2,384,512]{3,2,1,0:T(8,128)(2,1)} collective-permute-done((bf16[2,2,384,512]{3,2,1,0:T(8,128)(2,1)}, bf16[2,2,384,512]{3,2,1,0:T(8,128)(2,1)}, u32[]{:S(2)}, u32[]{:S(2)}) %collective-permute-start.8) | collective-permute-done | bytes 1572896 | tf_op jit(solution)/shard_map/ppermute | solution.py:1018
  229.1 2.0 add_convert_fusion.2
  231.1 29.4 %collective-permute-done.9 = bf16[2,2,384,512]{3,2,1,0:T(8,128)(2,1)} collective-permute-done((bf16[2,2,384,512]{3,2,1,0:T(8,128)(2,1)}, bf16[2,2,384,512]{3,2,1,0:T(8,128)(2,1)}, u32[]{:S(2)}, u32[]{:S(2)}) %collective-permute-start.9) | collective-permute-done | bytes 1572896 | tf_op jit(solution)/shard_map/ppermute | solution.py:1018
  265.1 38.9 %shard_map.235 = (bf16[256,1024]{1,0:T(8,128)(2,1)S(1)}, f32[4,8,256]{2,1,0:T(8,128)S(1)}) custom-call(bf16[4,256,1024]{2,1,0:T(8,128)(2,1)S(1)} %bitcast.100, f32[4,8,256]{2,1,0:T(8,128)S(1)} %bitcast.103), custom_call_target="tpu_custom_call" | custom-call | bytes 120000000 | tf_op jit(solution)/shard_map/pallas_call | solution.py:325
  310.8 2.0 copy.46
  312.7 3.2 multiply_reduce_fusion
  317.5 24.8 %collective-permute-done.5 = bf16[256,1024]{1,0:T(8,128)(2,1)} collective-permute-done((bf16[256,1024]{1,0:T(8,128)(2,1)}, bf16[256,1024]{1,0:T(8,128)(2,1)}, u32[]{:S(2)}, u32[]{:S(2)}) %collective-permute-start.5) | collective-permute-done | bytes 524320 | tf_op jit(solution)/shard_map/ppermute | solution.py:1076
  342.3 7.7 %collective-permute-done.6 = bf16[256,1024]{1,0:T(8,128)(2,1)} collective-permute-done((bf16[256,1024]{1,0:T(8,128)(2,1)}, bf16[256,1024]{1,0:T(8,128)(2,1)}, u32[]{:S(2)}, u32[]{:S(2)}) %collective-permute-start.6) | collective-permute-done | bytes 524320 | tf_op jit(solution)/shard_map/ppermute | solution.py:1076
  350.0 3.7 multiply_subtract_fusion
  357.3 15.1 %shard_map.236 = (bf16[256,1024]{1,0:T(8,128)(2,1)S(1)}, bf16[8,256,512]{2,1,0:T(8,128)(2,1)S(1)}, bf16[8,256,512]{2,1,0:T(8,128)(2,1)S(1)}) custom-call(s32[1]{0:T(128)} %bitcast.1.dp_ref, s32[256,1]{1,0:T(8,128)S(1)} %copy.40.starts_ref, bf16[256,1024]{1,0:T(8,128)(2,1)S(1)} %copy-done.11, bf16[8,256,512]{2,1,0:T(8,128)(2,1)} %get-tuple-element.68.k_ref, ...), custom_call_target="tpu_custom_call" | custom-call | bytes 75000000 | tf_op jit(solution)/shard_map/pallas_call | solution.py:931
  372.4 28.3 %shard_map.237 = (bf16[256,512]{1,0:T(8,128)(2,1)S(1)}, bf16[256,512]{1,0:T(8,128)(2,1)S(1)}) custom-call(bf16[8,256,512]{2,1,0:T(8,128)(2,1)S(1)} %get-tuple-element.98.refs_0_, bf16[8,256,512]{2,1,0:T(8,128)(2,1)S(1)} %get-tuple-element.99.refs_1_), custom_call_target="tpu_custom_call" | custom-call | bytes 75000000 | tf_op jit(solution)/shard_map/pallas_call | solution.py:325
  400.8 6.4 %shard_map.238 = (bf16[8,128,1024]{2,1,0:T(8,128)(2,1)}, bf16[8,128,512]{2,1,0:T(8,128)(2,1)S(1)}, bf16[8,128,512]{2,1,0:T(8,128)(2,1)S(1)}, f32[256,1024]{1,0:T(8,128)}, f32[1,1024]{1,0:T(1,128)S(1)}) custom-call(bf16[256,1024]{1,0:T(8,128)(2,1)S(1)} %copy-done.16, bf16[256,1024]{1,0:T(8,128)(2,1)S(1)} %get-tuple-element.97.dq_ref, ...), custom_call_target="tpu_custom_call" | custom-call | bytes 30000000 | tf_op jit(solution)/shard_map/pallas_call | solution.py:1002
  414.8 51.5 %shard_map.239 = (bf16[32,1024]{1,0:T(8,128)(2,1)S(1)}, bf16[32,1024]{1,0:T(8,128)(2,1)S(1)}, bf16[32,512]{1,0:T(8,128)(2,1)S(1)}, bf16[32,512]{1,0:T(8,128)(2,1)S(1)}, bf16[32,128]{1,0:T(8,128)(2,1)S(1)}) custom-call(bf16[8,4,32,1024]{3,2,1,0:T(8,128)(2,1)S(1)} %bitcast.99, bf16[8,4,32,1024]{3,2,1,0:T(8,128)(2,1)} %bitcast.106, ...), custom_call_target="tpu_custom_call" | custom-call | bytes 180000000 | tf_op jit(solution)/shard_map/pallas_call | solution.py:451
  475.2 11.0 %collective-permute-done.12 = bf16[2,384,512]{2,1,0:T(8,128)(2,1)S(1)} collective-permute-done((bf16[2,384,512]{2,1,0:T(8,128)(2,1)S(1)}, bf16[2,384,512]{2,1,0:T(8,128)(2,1)S(1)}, u32[]{:S(2)}, u32[]{:S(2)}) %collective-permute-start.12) | collective-permute-done | bytes 786464 | tf_op jit(solution)/shard_map/ppermute | solution.py:1018
  487.3 2.7 fusion.21
  (167 shorter events, 60.1 us)
Async XLA Ops:
  0.6 53.7 %copy-start = (bf16[1024,1024]{1,0:T(8,128)(2,1)S(1)}, bf16[1024,1024]{1,0:T(8,128)(2,1)}, u32[]{:S(2)}) copy-start(bf16[1024,1024]{1,0:T(8,128)(2,1)} %param.21) | copy-start | bytes 6291460
  0.7 101.1 %collective-permute-start.2 = (bf16[256,1024]{1,0:T(8,128)(2,1)}, bf16[256,1024]{1,0:T(8,128)(2,1)}, u32[]{:S(2)}, u32[]{:S(2)}) collective-permute-start(bf16[256,1024]{1,0:T(8,128)(2,1)} %bitcast.110), channel_id=1, source_target_pairs={{0,24},{8,0},{16,8},{24,16},{1,25},{9,1},{17,9},{25,17},{2,26},{10... | collective-permute-start | bytes 1572872 | tf_op jit(solution)/shard_map/ppermute | solution.py:1076
  1.2 100.6 %collective-permute-start.1 = (bf16[256,1024]{1,0:T(8,128)(2,1)}, bf16[256,1024]{1,0:T(8,128)(2,1)}, u32[]{:S(2)}, u32[]{:S(2)}) collective-permute-start(bf16[256,1024]{1,0:T(8,128)(2,1)} %bitcast.111), channel_id=1, source_target_pairs={{0,16},{8,24},{16,0},{24,8},{1,17},{9,25},{17,1},{25,9},{2,18},{10... | collective-permute-start | bytes 1572872 | tf_op jit(solution)/shard_map/ppermute | solution.py:1076
  3.8 98.0 %collective-permute-start = (bf16[256,1024]{1,0:T(8,128)(2,1)}, bf16[256,1024]{1,0:T(8,128)(2,1)}, u32[]{:S(2)}, u32[]{:S(2)}) collective-permute-start(bf16[256,1024]{1,0:T(8,128)(2,1)} %bitcast.112), channel_id=1, source_target_pairs={{0,8},{8,16},{16,24},{24,0},{1,9},{9,17},{17,25},{25,1},{2,10},{10... | collective-permute-start | bytes 1572872 | tf_op jit(solution)/shard_map/ppermute | solution.py:1076
  10.2 29.2 %copy-start.40 = (s32[2,1,128]{2,1,0:T(1,128)S(1)}, s32[2,1,128]{2,1,0:T(1,128)}, u32[]{:S(2)}) copy-start(s32[2,1,128]{2,1,0:T(1,128)} %param.15) | copy-start | bytes 3076
  144.1 47.9 %collective-permute-start.3 = (bf16[2,2,384,512]{3,2,1,0:T(8,128)(2,1)}, bf16[2,2,384,512]{3,2,1,0:T(8,128)(2,1)}, u32[]{:S(2)}, u32[]{:S(2)}) collective-permute-start(bf16[2,2,384,512]{3,2,1,0:T(8,128)(2,1)} %get-tuple-element.77), channel_id=1, source_target_pairs={{0,4},{1,5},{2,6},{3,7},{4,0},{5,1},{6,2},{7,3},{8,12},{9,13},{10,... | collective-permute-start | bytes 4718600 | tf_op jit(solution)/shard_map/ppermute | solution.py:1018
  144.7 46.6 %copy-start.39 = (f32[4,8,128]{2,1,0:T(8,128)S(1)}, f32[4,8,128]{2,1,0:T(8,128)}, u32[]{:S(2)}) copy-start(f32[4,8,128]{2,1,0:T(8,128)} %get-tuple-element.82) | copy-start | bytes 49156
  187.6 37.0 %collective-permute-start.8 = (bf16[2,2,384,512]{3,2,1,0:T(8,128)(2,1)}, bf16[2,2,384,512]{3,2,1,0:T(8,128)(2,1)}, u32[]{:S(2)}, u32[]{:S(2)}) collective-permute-start(bf16[2,2,384,512]{3,2,1,0:T(8,128)(2,1)} %get-tuple-element.92), channel_id=1, source_target_pairs={{0,4},{1,5},{2,6},{3,7},{4,0},{5,1},{6,2},{7,3},{8,12},{9,13},{10,... | collective-permute-start | bytes 4718600 | tf_op jit(solution)/shard_map/ppermute | solution.py:1018
  189.2 39.3 %collective-permute-start.4 = (bf16[2,2,384,512]{3,2,1,0:T(8,128)(2,1)}, bf16[2,2,384,512]{3,2,1,0:T(8,128)(2,1)}, u32[]{:S(2)}, u32[]{:S(2)}) collective-permute-start(bf16[2,2,384,512]{3,2,1,0:T(8,128)(2,1)} %get-tuple-element.80), channel_id=1, source_target_pairs={{0,2},{1,3},{2,0},{3,1},{4,6},{5,7},{6,4},{7,5},{8,10},{9,11},{10,... | collective-permute-start | bytes 4718600 | tf_op jit(solution)/shard_map/ppermute | solution.py:1018
  189.8 70.7 %collective-permute-start.9 = (bf16[2,2,384,512]{3,2,1,0:T(8,128)(2,1)}, bf16[2,2,384,512]{3,2,1,0:T(8,128)(2,1)}, u32[]{:S(2)}, u32[]{:S(2)}) collective-permute-start(bf16[2,2,384,512]{3,2,1,0:T(8,128)(2,1)} %get-tuple-element.95), channel_id=1, source_target_pairs={{0,2},{1,3},{2,0},{3,1},{4,6},{5,7},{6,4},{7,5},{8,10},{9,11},{10,... | collective-permute-start | bytes 4718600 | tf_op jit(solution)/shard_map/ppermute | solution.py:1018
  192.1 32.6 %copy-start.34 = (bf16[2,2,384,512]{3,2,1,0:T(8,128)(2,1)S(1)}, bf16[2,2,384,512]{3,2,1,0:T(8,128)(2,1)}, u32[]{:S(2)}) copy-start(bf16[2,2,384,512]{3,2,1,0:T(8,128)(2,1)} %get-tuple-element.91) | copy-start | bytes 4718596
  194.6 31.9 %copy-start.25 = (bf16[2,2,384,512]{3,2,1,0:T(8,128)(2,1)}, bf16[2,2,384,512]{3,2,1,0:T(8,128)(2,1)S(1)}, u32[]{:S(2)}) copy-start(bf16[2,2,384,512]{3,2,1,0:T(8,128)(2,1)S(1)} %add_convert_fusion.3) | copy-start | bytes 4718596
  227.8 243.0 %collective-permute-start.10 = (bf16[2,384,512]{2,1,0:T(8,128)(2,1)}, bf16[2,384,512]{2,1,0:T(8,128)(2,1)}, u32[]{:S(2)}, u32[]{:S(2)}) collective-permute-start(bf16[2,384,512]{2,1,0:T(8,128)(2,1)} %get-tuple-element.112), channel_id=1, source_target_pairs={{0,2},{1,3},{2,0},{3,1},{4,6},{5,7},{6,4},{7,5},{8,10},{9,11},{10,... | collective-permute-start | bytes 2359304 | tf_op jit(solution)/shard_map/ppermute | solution.py:1018
  229.1 31.4 %copy-start.33 = (bf16[2,2,384,512]{3,2,1,0:T(8,128)(2,1)S(1)}, bf16[2,2,384,512]{3,2,1,0:T(8,128)(2,1)}, u32[]{:S(2)}) copy-start(bf16[2,2,384,512]{3,2,1,0:T(8,128)(2,1)} %get-tuple-element.94) | copy-start | bytes 4718596
  231.1 31.3 %copy-start.29 = (bf16[2,2,384,512]{3,2,1,0:T(8,128)(2,1)}, bf16[2,2,384,512]{3,2,1,0:T(8,128)(2,1)S(1)}, u32[]{:S(2)}) copy-start(bf16[2,2,384,512]{3,2,1,0:T(8,128)(2,1)S(1)} %add_convert_fusion.2) | copy-start | bytes 4718596
  262.4 42.4 %copy-start.31 = (bf16[1024,1024]{1,0:T(8,128)(2,1)S(1)}, bf16[1024,1024]{1,0:T(8,128)(2,1)}, u32[]{:S(2)}) copy-start(bf16[1024,1024]{1,0:T(8,128)(2,1)} %get-tuple-element.86) | copy-start | bytes 6291460
  306.1 36.3 %collective-permute-start.5 = (bf16[256,1024]{1,0:T(8,128)(2,1)}, bf16[256,1024]{1,0:T(8,128)(2,1)}, u32[]{:S(2)}, u32[]{:S(2)}) collective-permute-start(bf16[256,1024]{1,0:T(8,128)(2,1)} %get-tuple-element.124), channel_id=1, source_target_pairs={{0,8},{8,16},{16,24},{24,0},{1,9},{9,17},{17,25},{25,1},{2,10},{10... | collective-permute-start | bytes 1572872 | tf_op jit(solution)/shard_map/ppermute | solution.py:1076
  307.1 35.2 %collective-permute-start.7 = (bf16[256,1024]{1,0:T(8,128)(2,1)}, bf16[256,1024]{1,0:T(8,128)(2,1)}, u32[]{:S(2)}, u32[]{:S(2)}) collective-permute-start(bf16[256,1024]{1,0:T(8,128)(2,1)} %get-tuple-element.125), channel_id=1, source_target_pairs={{0,24},{8,0},{16,8},{24,16},{1,25},{9,1},{17,9},{25,17},{2,26},{10... | collective-permute-start | bytes 1572872 | tf_op jit(solution)/shard_map/ppermute | solution.py:1076
  308.1 41.9 %collective-permute-start.6 = (bf16[256,1024]{1,0:T(8,128)(2,1)}, bf16[256,1024]{1,0:T(8,128)(2,1)}, u32[]{:S(2)}, u32[]{:S(2)}) collective-permute-start(bf16[256,1024]{1,0:T(8,128)(2,1)} %get-tuple-element.126), channel_id=1, source_target_pairs={{0,16},{8,24},{16,0},{24,8},{1,17},{9,25},{17,1},{25,9},{2,18},{10... | collective-permute-start | bytes 1572872 | tf_op jit(solution)/shard_map/ppermute | solution.py:1076
  317.0 155.3 %collective-permute-start.11 = (bf16[2,384,512]{2,1,0:T(8,128)(2,1)}, bf16[2,384,512]{2,1,0:T(8,128)(2,1)}, u32[]{:S(2)}, u32[]{:S(2)}) collective-permute-start(bf16[2,384,512]{2,1,0:T(8,128)(2,1)} %get-tuple-element.113), channel_id=1, source_target_pairs={{0,4},{1,5},{2,6},{3,7},{4,0},{5,1},{6,2},{7,3},{8,12},{9,13},{10,... | collective-permute-start | bytes 2359304 | tf_op jit(solution)/shard_map/ppermute | solution.py:1018
  355.2 118.6 %collective-permute-start.13 = (bf16[2,384,512]{2,1,0:T(8,128)(2,1)}, bf16[2,384,512]{2,1,0:T(8,128)(2,1)}, u32[]{:S(2)}, u32[]{:S(2)}) collective-permute-start(bf16[2,384,512]{2,1,0:T(8,128)(2,1)} %get-tuple-element.115), channel_id=1, source_target_pairs={{0,4},{1,5},{2,6},{3,7},{4,0},{5,1},{6,2},{7,3},{8,12},{9,13},{10,... | collective-permute-start | bytes 2359304 | tf_op jit(solution)/shard_map/ppermute | solution.py:1018
  414.8 52.2 %copy-start.36 = (bf16[2,384,512]{2,1,0:T(8,128)(2,1)S(1)}, bf16[2,384,512]{2,1,0:T(8,128)(2,1)}, u32[]{:S(2)}) copy-start(bf16[2,384,512]{2,1,0:T(8,128)(2,1)} %get-tuple-element.114) | copy-start | bytes 2359300
  414.8 56.0 %copy-start.26 = (bf16[2,2,384,512]{3,2,1,0:T(8,128)(2,1)S(1)}, bf16[2,2,384,512]{3,2,1,0:T(8,128)(2,1)}, u32[]{:S(2)}) copy-start(bf16[2,2,384,512]{3,2,1,0:T(8,128)(2,1)} %copy-done.25) | copy-start | bytes 4718596
  467.0 19.2 %collective-permute-start.12 = (bf16[2,384,512]{2,1,0:T(8,128)(2,1)S(1)}, bf16[2,384,512]{2,1,0:T(8,128)(2,1)S(1)}, u32[]{:S(2)}, u32[]{:S(2)}) collective-permute-start(bf16[2,384,512]{2,1,0:T(8,128)(2,1)S(1)} %copy-done.36), channel_id=1, source_target_pairs={{0,2},{1,3},{2,0},{3,1},{4,6},{5,7},{6,4},{7,5},{8,10},{9,11},{10,... | collective-permute-start | bytes 2359304 | tf_op jit(solution)/shard_map/ppermute | solution.py:1018
  (31 other events, 168.9 us)

commit v5 on v3

--- a/solution.py
+++ b/solution.py
@@ -72,26 +72,17 @@
         copy.start()
         own.append(copy)
 
-    def dp_step(t):
-        copies = []
-        for a in range(n_dp):
-            order = gather_orders(nd)[a % 2]
-            for j, m in enumerate(masks(order[:t])):
-                block = jnp.bitwise_xor(dp, m)
-                src = ins[a] if m == 0 else outs[a].at[block]
-                k = (1 << t) - 1 + j
-                copies.append(
-                    remote(
-                        src,
-                        outs[a].at[block],
-                        dp_send.at[a, k],
-                        dp_recv.at[a, k],
-                        {"dp": jnp.bitwise_xor(dp, 1 << order[t])},
-                    )
-                )
-        for c in copies:
-            c.start()
-        return copies
+    def dp_copy(a, t, m):
+        order = gather_orders(nd)[a % 2]
+        block = jnp.bitwise_xor(dp, m)
+        k = (1 << t) - 1 + masks(order[:t]).index(m)
+        return remote(
+            ins[a] if m == 0 else outs[a].at[block],
+            outs[a].at[block],
+            dp_send.at[a, k],
+            dp_recv.at[a, k],
+            {"dp": jnp.bitwise_xor(dp, 1 << order[t])},
+        )
 
     def ep_copy(a, s, way):
         shard = lax.rem(ep - way * s + ne, ne)
@@ -133,20 +124,25 @@
 
     dp_steps = bit_count(nd) if n_dp else 0
     ep_steps = ne - 1 if n_ep else 0
-    started = []
+    for t in range(dp_steps):
+        for a in range(n_dp):
+            dp_copy(a, t, 0).start()
     for t in range(max(dp_steps, ep_steps) + 1):
         if 0 < t <= dp_steps:
-            for c in started[-1]:
-                c.wait_recv()
-        if t < dp_steps:
-            started.append(dp_step(t))
+            for a in range(n_dp):
+                order = gather_orders(nd)[a % 2]
+                for m in masks(order[: t - 1]):
+                    dp_copy(a, t - 1, m).wait_recv()
+                    for later in range(t, dp_steps):
+                        dp_copy(a, later, m | (1 << order[t - 1])).start()
         if 0 < t <= ep_steps:
             ep_wait(t - 1)
         if t < ep_steps:
             ep_start(t)
-    for group in started:
-        for c in group:
-            c.wait_send()
+    for t in range(dp_steps):
+        for a in range(n_dp):
+            for m in masks(gather_orders(nd)[a % 2][:t]):
+                dp_copy(a, t, m).wait_send()
     for s in range(ep_steps):
         for a in range(n_ep):
             for way in (1, -1):
@@ -182,33 +178,59 @@
             DMA((b, 2, ne - 1)),
         ],
         compiler_params=pltpu.CompilerParams(
-            collective_id=collective, has_side_effects=True, vmem_limit_bytes=8 * 2**20
+            collective_id=collective, has_side_effects=True, vmem_limit_bytes=60 * 2**20
         ),
         cost_estimate=cost(us),
     )(*arrays)
 
 
-def reduce_body(ne, nd, n_dp, n_ep, n_swap, *refs):
-    n_in = n_dp + n_ep + n_swap
-    ins, outs = refs[:n_in], refs[n_in : 2 * n_in]
-    rest = refs[2 * n_in :]
-    n_sum = n_dp + n_ep
-    held = rest[:n_sum]
-    landing = rest[n_sum : 2 * n_sum]
-    in_sem, dp_send, dp_recv, ep_send, ep_recv, swap_send, swap_recv = rest[2 * n_sum :]
+def add_into(ref, arrived):
+    if len(ref.shape) > 2:
+
+        @pl.loop(0, ref.shape[0])
+        def _(i):
+            add_into(ref.at[i], arrived.at[i])
+
+    else:
+        ref[...] = (ref[...].astype(F32) + arrived[...].astype(F32)).astype(ref.dtype)
+
+
+def reduce_body(ne, nd, pairs, n_line, n_swap, *refs):
+    n_pair = len(pairs)
+    n_extra = sum(extra for _, extra, _ in pairs)
+    n_sum = n_pair + n_line
+    sizes = (n_sum, n_extra, n_swap, n_sum, n_swap, n_sum, n_extra, n_pair)
+    groups, at = [], 0
+    for size in sizes:
+        groups.append(refs[at : at + size])
+        at += size
+    ins, extra_ins, swap_ins, outs, swap_outs, held, extras, pair_in = groups
+    lined = [a for a in range(n_pair) if pairs[a][2]] + list(range(n_pair, n_sum))
+    line_in = dict(zip(lined, refs[at : at + len(lined)]))
+    in_sem, extra_sem, out_sem, dp_send, dp_recv, ep_send, ep_recv, swap_send, swap_recv = refs[
+        at + len(lined) :
+    ]
     ep, dp = lax.axis_index("ep"), lax.axis_index("dp")
-    loads = []
+    extra_of = [sum(extra for _, extra, _ in pairs[:a]) for a in range(n_pair)]
+
+    def load(a):
+        return pltpu.make_async_copy(ins[a], held[a], in_sem.at[a])
+
+    def load_extra(a):
+        i = extra_of[a]
+        return pltpu.make_async_copy(extra_ins[i], extras[i], extra_sem.at[i])
+
     for a in range(n_sum):
-        copy = pltpu.make_async_copy(ins[a], held[a], in_sem.at[a])
-        copy.start()
-        loads.append(copy)
+        load(a).start()
+        if a < n_pair and pairs[a][1]:
+            load_extra(a).start()
     greet(ep, dp, ne, nd)
     swaps = []
     for a in range(n_swap):
-        src, dst = ins[n_sum + a], outs[n_sum + a]
-        copy = pltpu.make_async_copy(src.at[ep], dst.at[ep], in_sem.at[n_sum + a])
-        copy.start()
-        loads.append(copy)
+        src, dst = swap_ins[a], swap_outs[a]
+        own = pltpu.make_async_copy(src.at[ep], dst.at[ep], in_sem.at[n_sum + a])
+        own.start()
+        swaps.append(own)
         for k in range(1, ne):
             to = lax.rem(ep + k, ne)
             copy = remote(
@@ -216,140 +238,163 @@
             )
             copy.start()
             swaps.append(copy)
-    for c in loads:
-        c.wait()
-
-    def add(a, block, arrived):
-        held[a][block] = (held[a][block].astype(F32) + arrived.astype(F32)).astype(held[a].dtype)
-
-    nb = bit_count(nd)
-
-    def dp_parts(a, t):
-        order = gather_orders(nd)[a % 2][::-1]
-        bit, left = order[t], order[t + 1 :]
-        first = sum(1 << (nb - 1 - i) for i in range(t))
-        return bit, [(first + j, m) for j, m in enumerate(masks(left))]
-
-    def dp_copies(a, t):
-        bit, parts = dp_parts(a, t)
-        partner = jnp.bitwise_xor(dp, 1 << bit)
+
+    def place(order, bit):
+        return sorted(order).index(bit)
+
+    def index_of(order):
+        index = 0
+        for b in order:
+            side = jnp.bitwise_and(lax.shift_right_logical(dp, b), 1)
+            index = index + (side << place(order, b))
+        return index
+
+    def pair_copies(a, t):
+        order = pairs[a][0]
+        side = 1 << place(order, order[t])
+        partner = jnp.bitwise_xor(index_of(order), side)
+        first = sum(1 << (len(order) - 1 - i) for i in range(t))
         return [
             (
                 m,
-                k,
+                first + j,
                 remote(
                     held[a].at[jnp.bitwise_xor(partner, m)],
-                    landing[a].at[k],
-                    dp_send.at[a, k],
-                    dp_recv.at[a, k],
-                    {"dp": partner},
+                    pair_in[a].at[first + j],
+                    dp_send.at[a, first + j],
+                    dp_recv.at[a, first + j],
+                    {"dp": jnp.bitwise_xor(dp, 1 << order[t])},
                 ),
             )
-            for k, m in parts
+            for j, m in enumerate(masks([place(order, b) for b in order[t + 1 :]]))
         ]
 
-    def ep_copy(a, dest, way):
+    def pair_step(a, t):
+        order = pairs[a][0]
+        if t == 0:
+            load(a).wait()
+            if pairs[a][1]:
+                load_extra(a).wait()
+                add_into(held[a], extras[extra_of[a]])
+        elif t <= len(order):
+            for m, k, copy in pair_copies(a, t - 1):
+                copy.wait_recv()
+                add_into(held[a].at[jnp.bitwise_xor(index_of(order), m)], pair_in[a].at[k])
+        if t < len(order):
+            for m, k, copy in pair_copies(a, t):
+                copy.start()
+
+    def line_block(a, dest):
+        return held[a].at[index_of(pairs[a][0]), dest] if a < n_pair else held[a].at[dest]
+
+    def line_copy(a, dest, way):
         k = 0 if way == 1 else 1
+        i = lined.index(a)
         return remote(
-            held[n_dp + a].at[dest],
-            landing[n_dp + a].at[k, dest],
-            ep_send.at[a, k, dest],
-            ep_recv.at[a, k, dest],
+            line_block(a, dest),
+            line_in[a].at[k, dest],
+            ep_send.at[i, k, dest],
+            ep_recv.at[i, k, dest],
             {"ep": lax.rem(ep + way + ne, ne)},
         )
 
-    def ep_turn(t, way):
-        return ep + ne - 1 - t if way == 1 else ep + t - (ne - 1)
-
-    def ep_has(t, way):
-        return ep_turn(t, way) <= ne - 1 if way == 1 else ep_turn(t, way) >= 0
-
-    def ep_inner(way):
-        return ep >= 1 if way == 1 else ep <= ne - 2
-
-    def ep_go(t):
-        for a in range(n_ep):
+    def line_turn(t, way):
+        dest = ep + ne - 1 - t if way == 1 else ep + t - (ne - 1)
+        has = dest <= ne - 1 if way == 1 else dest >= 0
+        inner = ep >= 1 if way == 1 else ep <= ne - 2
+        return dest, has, inner
+
+    def line_step(a, t):
+        if t == 0 and a >= n_pair:
+            load(a).wait()
+        for way in (1, -1):
+            dest, has, inner = line_turn(t, way)
+
+            @pl.when(has & inner)
+            def _(way=way, dest=dest):
+                line_copy(a, dest, way).wait_recv()
+                add_into(line_block(a, dest), line_in[a].at[0 if way == 1 else 1, dest])
+
+            if t < ne - 1:
+
+                @pl.when(has)
+                def _(way=way, dest=dest):
+                    line_copy(a, dest, way).start()
+
+    steps = max([len(order) + 1 for order, _, _ in pairs] + [ne if n_line else 0])
+    for t in range(steps):
+        for a in range(n_pair, n_sum):
+            if t < ne:
+                line_step(a, t)
+        for a in range(n_pair):
+            pair_step(a, t)
+    for t in range(ne):
+        for a in lined:
+            if a < n_pair:
+                line_step(a, t)
+
+    results = []
+    for a in range(n_sum):
+        if a >= n_pair:
+            src = held[a].at[ep]
+        else:
+            src = line_block(a, ep) if pairs[a][2] else held[a].at[index_of(pairs[a][0])]
+        copy = pltpu.make_async_copy(src, outs[a], out_sem.at[a])
+        copy.start()
+        results.append(copy)
+    for a in range(n_pair):
+        for t in range(len(pairs[a][0])):
+            for m, k, copy in pair_copies(a, t):
+                copy.wait_send()
+    for a in lined:
+        for t in range(ne - 1):
             for way in (1, -1):
-                dest = ep_turn(t, way)
-
-                @pl.when(ep_has(t, way) & ep_inner(way))
+                dest, has, inner = line_turn(t, way)
+
+                @pl.when(has)
                 def _(a=a, way=way, dest=dest):
-                    ep_copy(a, dest, way).wait_recv()
-                    add(n_dp + a, dest, landing[n_dp + a][0 if way == 1 else 1, dest])
-
-                if t < ne - 1:
-
-                    @pl.when(ep_has(t, way))
-                    def _(a=a, way=way, dest=dest):
-                        ep_copy(a, dest, way).start()
-
-    dp_steps = nb if n_dp else 0
-    ep_steps = ne if n_ep else 0
-    started = []
-    for t in range(max(dp_steps + 1, ep_steps)):
-        if t < ep_steps:
-            ep_go(t)
-
-        if 0 < t <= dp_steps:
-            for a, group in started[-1]:
-                for m, k, c in group:
-                    c.wait_recv()
-                    add(a, jnp.bitwise_xor(dp, m), landing[a][k])
-        if t < dp_steps:
-            started.append([(a, dp_copies(a, t)) for a in range(n_dp)])
-            for a, group in started[-1]:
-                for m, k, c in group:
-                    c.start()
-    for a in range(n_dp):
-        outs[a][...] = held[a][dp]
-    for a in range(n_ep):
-        outs[n_dp + a][...] = held[n_dp + a][ep]
-    for groups in started:
-        for a, group in groups:
-            for m, k, c in group:
-                c.wait_send()
-    for t in range(ep_steps - 1):
-        for a in range(n_ep):
-            for way in (1, -1):
-                dest = ep_turn(t, way)
-
-                @pl.when(ep_has(t, way))
-                def _(a=a, way=way, dest=dest):
-                    ep_copy(a, dest, way).wait_send()
-
-    for c in swaps:
-        c.wait()
-
-
-def reduce(ne, nd, dp_arrays, ep_arrays, swap_arrays, collective, us):
-    sums = list(dp_arrays) + list(ep_arrays)
-    landing = [(nd - 1,) + v.shape[1:] for v in dp_arrays]
-    landing += [(2, ne) + v.shape[1:] for v in ep_arrays]
-    a, b, c = (max(len(v), 1) for v in (dp_arrays, ep_arrays, swap_arrays))
+                    line_copy(a, dest, way).wait_send()
+
+    for copy in swaps + results:
+        copy.wait()
+
+
+def reduce(ne, nd, pairs, lines, swaps, collective, us):
+    arrays = [p[0] for p in pairs] + list(lines)
+    extras = [p[2] for p in pairs if p[2] is not None]
+    kinds = tuple((tuple(order), extra is not None, both) for _, order, extra, both in pairs)
+    results = [v.shape[2:] if both else v.shape[1:] for v, _, _, both in pairs]
+    results += [v.shape[1:] for v in lines]
+    landing = [(v.shape[0] - 1,) + v.shape[1:] for v, _, _, _ in pairs]
+    landing += [(2,) + v.shape[1:] for v, _, _, both in pairs if both]
+    landing += [(2,) + v.shape for v in lines]
+    some = lambda v: max(len(v), 1)
+    line_count = max(len(lines) + sum(both for _, _, _, both in pairs), 1)
+    deep = max([v.shape[0] - 1 for v, _, _, _ in pairs] + [1])
     return pl.pallas_call(
-        functools.partial(
-            reduce_body, ne, nd, len(dp_arrays), len(ep_arrays), len(swap_arrays)
-        ),
-        out_shape=[jax.ShapeDtypeStruct(v.shape[1:], v.dtype) for v in sums]
-        + [jax.ShapeDtypeStruct(v.shape, v.dtype) for v in swap_arrays],
-        in_specs=[ANY] * (len(sums) + len(swap_arrays)),
-        out_specs=[VMEM] * len(sums) + [ANY] * len(swap_arrays),
-        scratch_shapes=[pltpu.VMEM(v.shape, v.dtype) for v in sums]
-        + [pltpu.VMEM(s, v.dtype) for s, v in zip(landing, sums)]
+        functools.partial(reduce_body, ne, nd, kinds, len(lines), len(swaps)),
+        out_shape=[jax.ShapeDtypeStruct(s, BF16) for s in results]
+        + [jax.ShapeDtypeStruct(v.shape, v.dtype) for v in swaps],
+        in_specs=[ANY] * (len(arrays) + len(extras) + len(swaps)),
+        out_specs=[ANY] * (len(arrays) + len(swaps)),
+        scratch_shapes=[pltpu.VMEM(v.shape, BF16) for v in arrays + extras]
+        + [pltpu.VMEM(s, BF16) for s in landing]
         + [
-            DMA((len(sums) + len(swap_arrays),)),
-            DMA((a, nd - 1)),
-            DMA((a, nd - 1)),
-            DMA((b, 2, ne)),
-            DMA((b, 2, ne)),
-            DMA((c, ne - 1)),
-            DMA((c, ne - 1)),
+            DMA((len(arrays) + len(swaps),)),
+            DMA((some(extras),)),
+            DMA((len(arrays),)),
+            DMA((some(pairs), deep)),
+            DMA((some(pairs), deep)),
+            DMA((line_count, 2, ne)),
+            DMA((line_count, 2, ne)),
+            DMA((some(swaps), ne - 1)),
+            DMA((some(swaps), ne - 1)),
         ],
         compiler_params=pltpu.CompilerParams(
-            collective_id=collective, has_side_effects=True, vmem_limit_bytes=48 * 2**20
+            collective_id=collective, has_side_effects=True, vmem_limit_bytes=56 * 2**20
         ),
         cost_estimate=cost(us),
-    )(*sums, *swap_arrays)
+    )(*arrays, *extras, *swaps)
 
 
 def dot(a, b, dims=((1,), (0,))):
@@ -357,11 +402,12 @@
 
 
 def expert_body(ne, nd, micro, rows, *refs):
-    cots = refs[:ne]
-    normed_ref, probs_ref, gate_ref, up_ref, down_ref = refs[ne : ne + 5]
-    mix_ref, grad_ref, dots_ref, sums_ref = refs[ne + 5 : ne + 9]
-    rows_in, cots_in, picks, weights, first, second, keep, send, arrived = refs[ne + 9 : ne + 18]
-    load_sem, store_sem, send_sem, recv_sem, free_sem = refs[ne + 18 :]
+    cots, refs = refs[:ne], refs[ne:]
+    normed_ref, probs_ref, gate_ref, up_ref, down_ref = refs[:5]
+    mix_ref, grad_ref, dots_ref = refs[5:8]
+    kept, landed = refs[8:10], refs[10:12]
+    rows_in, cots_in, picks, weights, first, second, keep, send, arrived, leaving = refs[12:22]
+    load_sem, store_sem, send_sem, recv_sem, free_sem, far_send, far_recv = refs[22:]
     e = pl.program_id(0)
     last = pl.num_programs(0) - 1
     ep, dp = lax.axis_index("ep"), lax.axis_index("dp")
@@ -394,24 +440,69 @@
         s = returned(t)
         return (
             pltpu.make_async_copy(
-                first.at[block_at(s)], mix_ref.at[block_at(t)], store_sem.at[0, t]
+                first.at[block_at(s)], mix_ref.at[block_at(s)], store_sem.at[0, t]
             ),
             pltpu.make_async_copy(
                 second.at[block_at(s)], grad_ref.at[block_at(s)], store_sem.at[1, t]
             ),
         )
 
+    def far(i, n):
+        return remote(
+            leaving.at[i],
+            landed[i].at[:, n],
+            far_send.at[i],
+            far_recv.at[i, n],
+            {"dp": jnp.bitwise_xor(dp, 1 << first_bits(nd)[i])},
+        )
+
     def collect():
         exchange().wait_recv()
-        sums_ref[:, 0] = (keep[...].astype(F32) + arrived[...].astype(F32)).astype(BF16)
+        pieces = keep.shape[0]
+        n = (e - 1) // 2
+        for i, bit in enumerate(first_bits(nd)):
+
+            def put(side, i=i, bit=bit):
+                for j in range(pieces):
+                    value = (keep[j].astype(F32) + arrived[j].astype(F32)).astype(BF16)
+                    at = (j >> bit << (bit - 1)) | (j & ((1 << (bit - 1)) - 1))
+                    if (j >> (bit - 1)) & 1 == side:
+                        kept[i][at, 0] = value
+                    else:
+                        leaving[i, at] = value
+
+            @pl.when(lax.rem(e - 1, 2) == i)
+            def _(i=i, bit=bit, put=put):
+                @pl.when(n > 0)
+                def _():
+                    far(i, n - 1).wait_send()
+
+                mine = jnp.bitwise_and(lax.shift_right_logical(dp, bit), 1)
+
+                @pl.when(mine == 0)
+                def _():
+                    put(0)
+
+                @pl.when(mine == 1)
+                def _():
+                    put(1)
+
+                far(i, n).start()
 
     @pl.when(e == 0)
     def _():
         for copy in loads():
             copy.start()
         barrier = pltpu.get_barrier_semaphore()
-        pl.semaphore_signal(barrier, inc=1, device_id=other, device_id_type=MESH)
-        pl.semaphore_wait(barrier, 1)
+        met = [0] + sorted(set(first_bits(nd)))
+        for bit in met:
+            pl.semaphore_signal(
+                barrier,
+                inc=1,
+                device_id={"dp": jnp.bitwise_xor(dp, 1 << bit)},
+                device_id_type=MESH,
+            )
+        pl.semaphore_wait(barrier, len(met))
         before = lax.broadcasted_iota(jnp.int32, (rows, rows), 0)
         after = lax.broadcasted_iota(jnp.int32, (rows, rows), 1)
         earlier = (before < after).astype(BF16)
@@ -503,22 +594,32 @@
             s = returned(t)
             at = block_at(s)
             flat = picks[s]
-            first[at, :] = dot(
-                flat, cots_in[s].reshape(n_exp * CAP, width), ((0,), (0,))
-            ).astype(BF16)
-            second[at, :] = dot(
-                flat, rows_in[s].reshape(n_exp * CAP, width), ((0,), (0,))
-            ).astype(BF16)
+            for done, slots in ((first, cots_in), (second, rows_in)):
+                value = dot(flat, slots[s].reshape(n_exp * CAP, width), ((0,), (0,)))
+                done[at, :] = value.astype(BF16)
             for copy in stores(t):
                 copy.start()
 
-        collect()
-        exchange().wait_send()
+            @pl.when(t == 1)
+            def _():
+                collect()
+                exchange().wait_send()
 
         @pl.loop(0, blocks)
         def _(t):
             for copy in stores(t):
                 copy.wait()
+
+        for i in range(2):
+            far(i, n_exp // 2 - 1).wait_send()
+
+            @pl.loop(0, n_exp // 2)
+            def _(n, i=i):
+                far(i, n).wait_recv()
+
+
+def first_bits(nd):
+    return [order[-2] for order in gather_orders(nd)]
 
 
 def experts(normed, cots, probs, w_gate, w_up, w_down, micro, rows, ne, nd, collective):
@@ -529,6 +630,10 @@
     full = (blocks * rows, width)
     one = pl.Buffered(1)
     weight = lambda e: (jnp.minimum(e, n_exp - 1), 0, 0)
+    part = (half // 2, n_exp // 2, packed, inner)
+    kept = pl.BlockSpec(
+        (half // 2, 1, packed, inner), lambda e: (0, jnp.maximum(e - 1, 0) // 2, 0, 0)
+    )
     return pl.pallas_call(
         functools.partial(expert_body, ne, nd, micro, rows),
         grid=(n_exp + 1,),
@@ -539,12 +644,7 @@
             pl.BlockSpec((1, width, inner), weight),
             pl.BlockSpec((1, inner, width), weight),
         ],
-        out_specs=[
-            ANY,
-            ANY,
-            pl.BlockSpec((1, blocks, rows), weight),
-            pl.BlockSpec((half, 1, packed, inner), lambda e: (0, jnp.maximum(e - 1, 0), 0, 0)),
-        ],
+        out_specs=[ANY, ANY, pl.BlockSpec((1, blocks, rows), weight), kept, kept, ANY, ANY],
         scratch_shapes=[
             pltpu.VMEM((blocks, n_exp, CAP, width), BF16),
             pltpu.VMEM((blocks, n_exp, CAP, width), BF16),
@@ -555,25 +655,28 @@
             pltpu.VMEM((half, packed, inner), BF16),
             pltpu.VMEM((half, packed, inner), BF16),
             pltpu.VMEM((half, packed, inner), BF16),
+            pltpu.VMEM((2, half // 2, packed, inner), BF16),
             DMA((ne + 1,)),
             DMA((2, blocks)),
             DMA,
             DMA,
             pltpu.SemaphoreType.REGULAR,
+            DMA((2,)),
+            DMA((2, n_exp // 2)),
         ],
         out_shape=[
             jax.ShapeDtypeStruct(full, BF16),
             jax.ShapeDtypeStruct(full, BF16),
             jax.ShapeDtypeStruct((n_exp, blocks, rows), F32),
-            jax.ShapeDtypeStruct((half, n_exp, packed, inner), BF16),
-        ],
+        ]
+        + [jax.ShapeDtypeStruct(part, BF16)] * 4,
         compiler_params=pltpu.CompilerParams(
             vmem_limit_bytes=62 * 2**20,
             dimension_semantics=("arbitrary",),
             collective_id=collective,
             has_side_effects=True,
         ),
-        cost_estimate=cost(65),
+        cost_estimate=cost(75),
     )(*cots, normed, probs, w_gate, w_up, w_down)
 
 
@@ -593,14 +696,24 @@
 
 
 def project_body(
-    tokens_ref, gain_ref, cos_ref, sin_ref, wq_ref, wk_ref, wv_ref, n_ref, q_ref, k_ref, v_ref
+    tokens_ref, gain_ref, cos_ref, sin_ref, wq_ref, wk_ref, wv_ref, n_ref, q_ref, k_ref, v_ref, *rest
 ):
+    wq, wk, wv, sem = rest
+    loads = [
+        pltpu.make_async_copy(src, dst, sem.at[i])
+        for i, (src, dst) in enumerate(((wk_ref, wk), (wv_ref, wv), (wq_ref, wq)))
+    ]
+    for copy in loads:
+        copy.start()
     x = tokens_ref[...].astype(F32)
     n_ref[...] = (x * rms_scale(x) * gain_ref[...]).astype(BF16)
     normed = n_ref[...]
     cosine, sine = cos_ref[...], sin_ref[...]
     tile = 256
-    for w, out, turned in ((wk_ref, k_ref, True), (wv_ref, v_ref, False), (wq_ref, q_ref, True)):
+    for copy, (w, out, turned) in zip(
+        loads, ((wk, k_ref, True), (wv, v_ref, False), (wq, q_ref, True))
+    ):
+        copy.wait()
         for c in range(0, w.shape[1], tile):
             y = dot(normed, w[:, c : c + tile])
             if turned:
@@ -616,9 +729,10 @@
     return pl.pallas_call(
         project_body,
         out_shape=[jax.ShapeDtypeStruct((rows, n), BF16) for n in shapes],
-        in_specs=[VMEM] * 7,
+        in_specs=[VMEM] * 4 + [ANY] * 3,
         out_specs=[VMEM] * 4,
-        compiler_params=pltpu.CompilerParams(vmem_limit_bytes=32 * 2**20),
+        scratch_shapes=[pltpu.VMEM(w.shape, BF16) for w in (w_query, w_key, w_value)] + [DMA((3,))],
+        compiler_params=pltpu.CompilerParams(vmem_limit_bytes=60 * 2**20),
         cost_estimate=cost(5),
     )(tokens, gain, cosine, sine, w_query, w_key, w_value)
 
@@ -829,27 +943,6 @@
     )(normed, dq, dk, dv, cosine, sine, *weights, tokens, gain, grad_residual)
 
 
-def halves(values, dp, axis, bit, part, parts_axis):
-    count = values.shape[parts_axis] // 2
-    values = lax.slice_in_dim(values, part * count, (part + 1) * count, axis=parts_axis)
-    mine = jnp.bitwise_and(lax.shift_right_logical(dp, bit), 1)
-    kept = lax.dynamic_index_in_dim(values, mine, axis, keepdims=False)
-    sent = lax.dynamic_index_in_dim(values, 1 - mine, axis, keepdims=False)
-    return kept, sent
-
-
-def swap_bit(sent, bit, nd):
-    return lax.ppermute(sent, "dp", [(i, i ^ (1 << bit)) for i in range(nd)])
-
-
-def plus(a, b):
-    return (a.astype(F32) + b.astype(F32)).astype(BF16)
-
-
-def tie(value, *others):
-    return lax.optimization_barrier((value,) + others)
-
-
 def per_device(
     tokens,
     segments,
@@ -928,7 +1021,9 @@
         .transpose(0, 2, 1, 3)
         .reshape(ne * micro, here, rows)
     )
-    mix, grad_in, pair_dots, sums = experts(
+    nb = bit_count(nd)
+    orders = [order[:-1][::-1] for order in gather_orders(nd)]
+    mix, grad_in, pair_dots, kept_a, kept_b, landed_a, landed_b = experts(
         normed_all.reshape(ne * every, width),
         cots,
         probs_here,
@@ -941,18 +1036,22 @@
         nd,
         6,
     )
-    nb = bit_count(nd)
-    sums = sums.reshape((2,) * (nb - 1) + sums.shape[1:])
-    orders = [order[:-1][::-1] for order in gather_orders(nd)]
-    first_kept, first_sent = zip(
-        *[halves(sums, dp, nb - 1 - orders[i][0], orders[i][0], i, nb - 1) for i in range(2)]
-    )
-    grad_in, *first_sent = tie(grad_in, *first_sent)
-    first_arrived = [swap_bit(v, orders[i][0], nd) for i, v in enumerate(first_sent)]
-
     pair_dots = pair_dots.reshape(here, ne, every).transpose(1, 0, 2)
-    grad_back, dots_all = reduce(
-        ne, nd, (), (grad_in.reshape(ne, every, width),), (pair_dots,), 2, 40
+
+    grads_a, grads_b, grad_back, dots_all = reduce(
+        ne,
+        nd,
+        [
+            (kept, order[1:], landed, False)
+            for kept, landed, order in (
+                (kept_a, landed_a, orders[0]),
+                (kept_b, landed_b, orders[1]),
+            )
+        ],
+        (grad_in.reshape(ne, every, width),),
+        (pair_dots,),
+        2,
+        40,
     )
     pair_dot = dots_all.reshape(EXPERTS, every).T
     grad_logits = gate_probs * (
@@ -991,24 +1090,19 @@
         rows,
         nd,
     )
-    mix = mix.reshape(ne, every, width)
-    mix_parts = [mix[0]] + [around(mix[k], k) for k in range(1, ne)]
-    grad_key, grad_value = reduce(ne, nd, (grad_key_all, grad_value_all), (), (), 3, 25)
-
-    grads = []
-    for i in range(2):
-        value, bits = plus(first_kept[i], first_arrived[i]), orders[i]
-        live = [b for b in range(nb - 1, 0, -1) if b != bits[0]]
-        for bit in bits[1:]:
-            axis = live.index(bit)
-            mine = jnp.bitwise_and(lax.shift_right_logical(dp, bit), 1)
-            kept = lax.dynamic_index_in_dim(value, mine, axis, keepdims=False)
-            sent = lax.dynamic_index_in_dim(value, 1 - mine, axis, keepdims=False)
-            grad_key, sent = tie(grad_key, sent)
-            value = plus(kept, swap_bit(sent, bit, nd))
-            live.remove(bit)
-        grads.append(value)
-    grads = jnp.concatenate(grads, axis=0).astype(F32)
+    whole = [[0] + order for order in orders]
+    grad_key, grad_value = reduce(
+        ne,
+        nd,
+        [(grad_key_all, whole[0], None, False), (grad_value_all, whole[1], None, False)],
+        (),
+        (),
+        3,
+        25,
+    )
+
+    grads = jnp.stack([grads_a, grads_b], axis=1)
+    grads = grads.reshape((here,) + grads.shape[2:]).astype(F32)
     share = width // nd
     grad_w_gate, grad_w_up = grads[:, :share], grads[:, share : 2 * share]
     grad_w_down = jnp.concatenate(
@@ -1018,8 +1112,6 @@
         ],
         axis=2,
     )
-    output = residual + sum(v.astype(F32) for v in mix_parts)
-    output = output.astype(BF16).reshape(tokens.shape)
     grad_w_query, grad_w_key, grad_w_value, grad_tokens, grad_gain_one = input_grads(
         ne,
         nd,
@@ -1047,24 +1139,29 @@
 
     def by_owner(grad):
         share = grad.shape[0] // (ne * nd)
-        return (
-            grad.astype(BF16)
-            .reshape(ne, nd, share, grad.shape[1])
-            .transpose(1, 0, 2, 3)
-            .reshape(nd, ne * share, grad.shape[1])
-        )
-
-    dense = reduce(
+        return grad.astype(BF16).reshape(ne, nd, share, grad.shape[1]).transpose(1, 0, 2, 3)
+
+    def blocks_of(grad):
+        return grad.reshape(nd, ne, -1, grad.shape[2])
+
+    dense = [
+        blocks_of(grad_w_query),
+        by_owner(grad_w_out),
+        blocks_of(grad_w_key),
+        blocks_of(grad_w_value),
+        by_owner(small),
+    ]
+    *dense, mix_own = reduce(
         ne,
         nd,
-        (grad_w_query, by_owner(grad_w_out), grad_w_key, grad_w_value, by_owner(small)),
-        (),
+        [(v, whole[i % 2], None, True) for i, v in enumerate(dense)],
+        (mix.reshape(ne, every, width),),
         (),
         4,
-        45,
-    )
-    dense = reduce(ne, nd, (), [v.reshape(ne, -1, v.shape[1]) for v in dense], (), 5, 18)
+        60,
+    )
     d_query, d_out, d_key, d_value, d_small = (v.astype(F32) for v in dense)
+    output = (residual + mix_own.astype(F32)).astype(BF16).reshape(tokens.shape)
     return (
         output,
         grad_tokens.reshape(tokens.shape),

time: 422 us -> 394 us (0.934)
  local copies, waits for them, and re-layouts: 42.7 us -> 27 us
  starting transfers between devices: 14.3 us -> 4.67 us
  other arithmetic: 21 us -> 12.4 us
  Pallas kernels: 336 us -> 342 us
    pallas_call x1, Pallas kernels: 73.5 us -> 101 us  [experts(): pl.pallas_call(functools.partial(expert_body, ne, nd, micro, rows), grid=...]
    pallas_call x4 -> x3, Pallas kernels: 163 us -> 139 us  [reduce(): pl.pallas_call(functools.partial(reduce_body, ne, nd, kinds, len(lines),...]
    convert_element_type x5 -> x2, other arithmetic: 10 us -> 1.35 us  [the longest x1 0.95 us: per_device(): output = (residual + mix_own.astype(F32)).astype(BF16).reshape(tokens.shape)]
    squeeze x4 -> x0, local copies, waits for them, and re-layouts: 6.62 us -> none  [the longest x2 3.89 us: halves(): sent = lax.dynamic_index_in_dim(values, 1 - mine, axis, keepdims=False)]
    slice x3 -> x2, local copies, waits for them, and re-layouts: 6.98 us -> 0.96 us  [the longest x1 5.35 us: halves(): lax.slice_in_dim(values, part * count, (part + 1) * count, axis=parts_axis)]
    unnamed x124 -> x82, local copies, waits for them, and re-layouts: 20.5 us -> 14.8 us
    ppermute x6 -> x3, starting transfers between devices: 9.72 us -> 4.67 us  [around(): return lax.ppermute(value, 'ep', [(i, (i + k) % ne) for i in range(ne)])]
    ppermute x4 -> x0, starting transfers between devices: 4.57 us -> none  [swap_bit(): return lax.ppermute(sent, 'dp', [(i, i ^ 1 << bit) for i in range(nd)])]
  transfers between devices with their start and end apart: 10 -> 3, of which waited for: 0 -> 0; matrix products, arithmetic and copies ran while one was open for 7% -> 2% of each run, Pallas kernels for 63% -> 21%
where the time goes in v5:
time: 394 us; the launch traced here: 392 us
  Pallas kernels  342 us (87%)
  local copies, waits for them, and re-layouts  27 us (7%)
  other arithmetic  12.4 us (3%)
  matrix products  4.95 us (1%)
  starting transfers between devices  4.67 us (1%)
    pallas_call x3, Pallas kernels, reduce(): pl.pallas_call(functools.partial(reduce_body, ne, nd, kinds, len(lines),...  139 us
    pallas_call x1, Pallas kernels, experts(): pl.pallas_call(functools.partial(expert_body, ne, nd, micro, rows), grid=...  101 us
    pallas_call x2, Pallas kernels, gather(): pl.pallas_call(functools.partial(gather_body, ne, nd, len(dp_arrays), len...  65.3 us
    pallas_call x1, Pallas kernels, attend_back(): pl.pallas_call(functools.partial(attend_back_body, nd // 2 + 1), grid_spe...  15.1 us
    unnamed x82, local copies, waits for them, and re-layouts  14.8 us
    pallas_call x1, Pallas kernels, attend(): pl.pallas_call(functools.partial(attend_body, nd // 2 + 1), grid_spec=plt...  10.2 us
  transfers between devices with their start and end apart: 3, of which 0 were waited for; matrix products, arithmetic and copies ran while one was open for 2% of the time, Pallas kernels for 21%

profile of v5, /device:TPU:10, one launch (start us, length us, event | category | flops | bytes accessed | tf_op | source)
XLA Modules:
  0.0 392.2 jit_solution(11458724483402598953)
XLA Ops:
  0.7 1.6 collective-permute-start
  2.3 1.2 collective-permute-start.1
  3.5 1.8 collective-permute-start.2
  8.5 5.4 %shard_map.229 = (bf16[256,1024]{1,0:T(8,128)(2,1)}, bf16[256,1024]{1,0:T(8,128)(2,1)}, bf16[256,512]{1,0:T(8,128)(2,1)}, bf16[256,512]{1,0:T(8,128)(2,1)}) custom-call(bf16[256,1024]{1,0:T(8,128)(2,1)} %bitcast.80, f32[1,1024]{1,0:T(1,128)} %bitcast.85, f32[256,128]{1,0:T(8,128)} %copy.40.cos_ref, f32[256,128]{1,0:T(8,128)} %broadcast_multiply_fusion.sin_ref, ...), custom_call_target="tpu_custom_call" | custom-call | bytes 15000000 | tf_op jit(solution)/shard_map/pallas_call | solution.py:729
  13.9 23.0 %shard_map.230 = (bf16[8,256,512]{2,1,0:T(8,128)(2,1)}, bf16[8,256,512]{2,1,0:T(8,128)(2,1)}, f32[8,8,128]{2,1,0:T(8,128)}) custom-call(bf16[256,512]{1,0:T(8,128)(2,1)} %get-tuple-element.50.refs_0_, bf16[256,512]{1,0:T(8,128)(2,1)} %get-tuple-element.51.refs_1_, f32[8,128]{1,0:T(8,128)} %concatenate.20.refs_2_), custom_call_target="tpu_custom_call" | custom-call | bytes 75000000 | tf_op jit(solution)/shard_map/pallas_call | solution.py:166
  38.1 1.6 copy-done.2
  39.7 1.6 copy-done.3
  41.2 1.0 copy-done.11
  42.3 10.2 %shard_map.231 = (bf16[256,1024]{1,0:T(8,128)(2,1)S(1)}, f32[2,4,512,1]{3,2,1,0:T(8,128)S(1)}) custom-call(s32[1]{0:T(128)} %bitcast.1.dp_ref, s32[256,1]{1,0:T(8,128)S(1)} %copy.41.starts_ref, bf16[256,1024]{1,0:T(8,128)(2,1)S(1)} %copy-done.11, bf16[8,256,512]{2,1,0:T(8,128)(2,1)S(1)} %copy-done.2, bf16[8,256,512]{2,1,0:T(8,128)(2,1)S(1)} %copy-done.3), custom_call_target="tpu_custom_call" | custom-call | bytes 45000000 | tf_op jit(solution)/shard_map/pallas_call | solution.py:816
  56.1 42.3 %shard_map.232 = (bf16[4,256,1024]{2,1,0:T(8,128)(2,1)}, f32[4,32,256]{2,1,0:T(8,128)}) custom-call(bf16[256,1024]{1,0:T(8,128)(2,1)} %copy-done.25, f32[32,256]{1,0:T(8,128)} %fusion.9.refs_1_), custom_call_target="tpu_custom_call" | custom-call | bytes 114000000 | tf_op jit(solution)/shard_map/pallas_call | solution.py:166
  99.9 100.7 %shard_map.233 = (bf16[1024,1024]{1,0:T(8,128)(2,1)}, bf16[1024,1024]{1,0:T(8,128)(2,1)}, f32[8,8,128]{2,1,0:T(8,128)}, bf16[2,4,384,512]{3,2,1,0:T(8,128)(2,1)}...) custom-call(bf16[256,1024]{1,0:T(8,128)(2,1)} %bitcast.94, ...), custom_call_target="tpu_custom_call" | custom-call | bytes 225000000 | tf_op jit(solution)/shard_map/pallas_call | solution.py:637
  202.0 55.6 %shard_map.234 = (bf16[4,384,512]{2,1,0:T(8,128)(2,1)}, bf16[4,384,512]{2,1,0:T(8,128)(2,1)}, bf16[256,1024]{1,0:T(8,128)(2,1)}, f32[4,8,256]{2,1,0:T(8,128)}) custom-call(bf16[2,4,384,512]{3,2,1,0:T(8,128)(2,1)} %get-tuple-element.61.refs_0_, bf16[2,4,384,512]{3,2,1,0:T(8,128)(2,1)} %get-tuple-element.62.refs_1_, bf16[4,256,1024]{2,1,0:T(8,128)(2,1)} %bitcast.96, ...), custom_call_target="tpu_custom_call" | custom-call | bytes 120000000 | tf_op jit(solution)/shard_map/pallas_call | solution.py:374
  258.5 2.0 multiply_reduce_fusion
  260.9 1.2 copy-done.24
  264.3 1.6 copy.57
  266.3 15.1 %shard_map.235 = (bf16[256,1024]{1,0:T(8,128)(2,1)S(1)}, bf16[8,256,512]{2,1,0:T(8,128)(2,1)S(1)}, bf16[8,256,512]{2,1,0:T(8,128)(2,1)S(1)}) custom-call(s32[1]{0:T(128)} %bitcast.1.dp_ref, s32[256,1]{1,0:T(8,128)S(1)} %copy.41.starts_ref, bf16[256,1024]{1,0:T(8,128)(2,1)S(1)} %copy-done.12, bf16[8,256,512]{2,1,0:T(8,128)(2,1)} %get-tuple-element.54.k_ref, ...), custom_call_target="tpu_custom_call" | custom-call | bytes 75000000 | tf_op jit(solution)/shard_map/pallas_call | solution.py:860
  281.4 1.3 copy-done.8
  282.7 1.3 copy-done.9
  284.0 26.2 %shard_map.236 = (bf16[256,512]{1,0:T(8,128)(2,1)}, bf16[256,512]{1,0:T(8,128)(2,1)}) custom-call(bf16[8,256,512]{2,1,0:T(8,128)(2,1)} %copy-done.8, bf16[8,256,512]{2,1,0:T(8,128)(2,1)} %copy-done.9), custom_call_target="tpu_custom_call" | custom-call | bytes 75000000 | tf_op jit(solution)/shard_map/pallas_call | solution.py:374
  312.2 6.4 %shard_map.237 = (bf16[8,128,1024]{2,1,0:T(8,128)(2,1)}, bf16[8,128,512]{2,1,0:T(8,128)(2,1)S(1)}, bf16[8,128,512]{2,1,0:T(8,128)(2,1)S(1)}, f32[256,1024]{1,0:T(8,128)}, f32[1,1024]{1,0:T(1,128)S(1)}) custom-call(bf16[256,1024]{1,0:T(8,128)(2,1)S(1)} %copy-done.15, bf16[256,1024]{1,0:T(8,128)(2,1)S(1)} %get-tuple-element.69.dq_ref, ...), custom_call_target="tpu_custom_call" | custom-call | bytes 30000000 | tf_op jit(solution)/shard_map/pallas_call | solution.py:931
  322.4 57.1 %shard_map.238 = (bf16[32,1024]{1,0:T(8,128)(2,1)}, bf16[32,1024]{1,0:T(8,128)(2,1)}, bf16[32,512]{1,0:T(8,128)(2,1)}, bf16[32,512]{1,0:T(8,128)(2,1)}, bf16[32,...) custom-call(bf16[8,4,32,1024]{3,2,1,0:T(8,128)(2,1)} %bitcast.98, bf16[8,4,32,1024]{3,2,1,0:T(8,128)(2,1)} %bitcast.90, ...), custom_call_target="tpu_custom_call" | custom-call | bytes 180000000 | tf_op jit(solution)/shard_map/pallas_call | solution.py:374
  380.2 1.3 slice.42
  382.6 2.4 fusion.19
  390.7 1.5 pad_maximum_fusion
  (131 shorter events, 27.5 us)
Async XLA Ops:
  0.6 54.4 %copy-start = (bf16[1024,32]{0,1:T(8,128)(2,1)S(1)}, bf16[1024,32]{0,1:T(8,128)(2,1)}, u32[]{:S(2)}) copy-start(bf16[1024,32]{0,1:T(8,128)(2,1)} %param.23) | copy-start | bytes 196612
  0.7 99.2 %collective-permute-start = (bf16[256,1024]{1,0:T(8,128)(2,1)}, bf16[256,1024]{1,0:T(8,128)(2,1)}, u32[]{:S(2)}, u32[]{:S(2)}) collective-permute-start(bf16[256,1024]{1,0:T(8,128)(2,1)} %bitcast.91), channel_id=1, source_target_pairs={{0,8},{8,16},{16,24},{24,0},{1,9},{9,17},{17,25},{25,1},{2,10},{10... | collective-permute-start | bytes 1572872 | tf_op jit(solution)/shard_map/ppermute | solution.py:993
  2.3 97.6 %collective-permute-start.1 = (bf16[256,1024]{1,0:T(8,128)(2,1)}, bf16[256,1024]{1,0:T(8,128)(2,1)}, u32[]{:S(2)}, u32[]{:S(2)}) collective-permute-start(bf16[256,1024]{1,0:T(8,128)(2,1)} %bitcast.92), channel_id=1, source_target_pairs={{0,16},{8,24},{16,0},{24,8},{1,17},{9,25},{17,1},{25,9},{2,18},{10... | collective-permute-start | bytes 1572872 | tf_op jit(solution)/shard_map/ppermute | solution.py:993
  3.5 96.3 %collective-permute-start.2 = (bf16[256,1024]{1,0:T(8,128)(2,1)}, bf16[256,1024]{1,0:T(8,128)(2,1)}, u32[]{:S(2)}, u32[]{:S(2)}) collective-permute-start(bf16[256,1024]{1,0:T(8,128)(2,1)} %bitcast.93), channel_id=1, source_target_pairs={{0,24},{8,0},{16,8},{24,16},{1,25},{9,1},{17,9},{25,17},{2,26},{10... | collective-permute-start | bytes 1572872 | tf_op jit(solution)/shard_map/ppermute | solution.py:993
  8.5 29.2 %copy-start.39 = (s32[2,1,128]{2,1,0:T(1,128)S(1)}, s32[2,1,128]{2,1,0:T(1,128)}, u32[]{:S(2)}) copy-start(s32[2,1,128]{2,1,0:T(1,128)} %param.15) | copy-start | bytes 3076
  38.1 1.6 copy-start.2
  42.3 10.3 %copy-start.4 = (bf16[2,128,1024]{2,1,0:T(8,128)(2,1)S(1)}, bf16[2,128,1024]{2,1,0:T(8,128)(2,1)}, u32[]{:S(2)}) copy-start(bf16[2,128,1024]{2,1,0:T(8,128)(2,1)} %param.14) | copy-start | bytes 1572868
  42.3 10.3 %copy-start.23 = (bf16[1024,1024]{1,0:T(8,128)(2,1)S(1)}, bf16[1024,1024]{1,0:T(8,128)(2,1)}, u32[]{:S(2)}) copy-start(bf16[1024,1024]{1,0:T(8,128)(2,1)} %param.21) | copy-start | bytes 6291460
  52.6 2.3 copy-start.35
  202.0 56.5 %copy-start.20 = (f32[256,1024]{1,0:T(8,128)S(1)}, f32[256,1024]{1,0:T(8,128)}, u32[]{:S(2)}) copy-start(f32[256,1024]{1,0:T(8,128)} %copy-done.19) | copy-start | bytes 3145732
  257.6 2.9 copy-start.27
  257.6 2.9 copy-start.28
  264.2 2.0 copy-start.6
  264.3 2.0 copy-start.7
  264.3 2.0 copy-start.12
  284.0 26.2 %copy-start.5 = (bf16[1024,512]{1,0:T(8,128)(2,1)S(1)}, bf16[1024,512]{1,0:T(8,128)(2,1)}, u32[]{:S(2)}) copy-start(bf16[1024,512]{1,0:T(8,128)(2,1)} %wk_ref.3) | copy-start | bytes 3145732
  284.0 26.2 %copy-start.15 = (bf16[256,1024]{1,0:T(8,128)(2,1)S(1)}, bf16[256,1024]{1,0:T(8,128)(2,1)}, u32[]{:S(2)}) copy-start(bf16[256,1024]{1,0:T(8,128)(2,1)} %get-tuple-element.57.n_ref) | copy-start | bytes 1572868
  284.0 26.2 %copy-start.18 = (f32[1024]{0:T(1024)S(1)}, f32[1024]{0:T(1024)}, u32[]{:S(2)}) copy-start(f32[1024]{0:T(1024)} %param.17) | copy-start | bytes 12292
  322.4 59.1 %copy-start.29 = (bf16[4,384,512]{2,1,0:T(8,128)(2,1)S(1)}, bf16[4,384,512]{2,1,0:T(8,128)(2,1)}, u32[]{:S(2)}) copy-start(bf16[4,384,512]{2,1,0:T(8,128)(2,1)} %get-tuple-element.86) | copy-start | bytes 4718596
  322.4 59.1 %copy-start.30 = (bf16[4,384,512]{2,1,0:T(8,128)(2,1)S(1)}, bf16[4,384,512]{2,1,0:T(8,128)(2,1)}, u32[]{:S(2)}) copy-start(bf16[4,384,512]{2,1,0:T(8,128)(2,1)} %get-tuple-element.87) | copy-start | bytes 4718596
  385.3 2.8 copy-start.34
  385.3 3.4 copy-start.37
  385.4 4.1 %copy-start.36 = (bf16[32,512]{1,0:T(8,128)(2,1)S(1)}, bf16[32,512]{1,0:T(8,128)(2,1)}, u32[]{:S(2)}) copy-start(bf16[32,512]{1,0:T(8,128)(2,1)} %get-tuple-element.84) | copy-start | bytes 98308
  385.4 4.7 %copy-start.33 = (bf16[32,1024]{1,0:T(8,128)(2,1)S(1)}, bf16[32,1024]{1,0:T(8,128)(2,1)}, u32[]{:S(2)}) copy-start(bf16[32,1024]{1,0:T(8,128)(2,1)} %get-tuple-element.85) | copy-start | bytes 196612
  (19 other events, 23.0 us)

commit v6 on v5

--- a/solution.py
+++ b/solution.py
@@ -195,40 +195,182 @@
         ref[...] = (ref[...].astype(F32) + arrived[...].astype(F32)).astype(ref.dtype)
 
 
+class PairSum:
+    def __init__(self, dp, order, sources, held, extra, landing, load_sem, send_sem, recv_sem):
+        self.dp, self.order, self.held, self.landing = dp, order, held, landing
+        self.send_sem, self.recv_sem = send_sem, recv_sem
+        self.extra = extra
+        self.loads = [
+            pltpu.make_async_copy(src, dst, load_sem.at[i])
+            for i, (src, dst) in enumerate(zip(sources, (held, extra)))
+        ]
+        self.index = 0
+        for b in order:
+            side = jnp.bitwise_and(lax.shift_right_logical(dp, b), 1)
+            self.index = self.index + (side << self.place(b))
+
+    def place(self, bit):
+        return sorted(self.order).index(bit)
+
+    def copies(self, t):
+        order = self.order
+        partner = jnp.bitwise_xor(self.index, 1 << self.place(order[t]))
+        first = sum(1 << (len(order) - 1 - i) for i in range(t))
+        return [
+            (
+                m,
+                first + j,
+                remote(
+                    self.held.at[jnp.bitwise_xor(partner, m)],
+                    self.landing.at[first + j],
+                    self.send_sem.at[first + j],
+                    self.recv_sem.at[first + j],
+                    {"dp": jnp.bitwise_xor(self.dp, 1 << order[t])},
+                ),
+            )
+            for j, m in enumerate(masks([self.place(b) for b in order[t + 1 :]]))
+        ]
+
+    def load(self):
+        for copy in self.loads:
+            copy.start()
+
+    def step(self, t):
+        if t == 0:
+            for copy in self.loads:
+                copy.wait()
+            if len(self.loads) > 1:
+                add_into(self.held, self.extra)
+        elif t <= len(self.order):
+            for m, k, copy in self.copies(t - 1):
+                copy.wait_recv()
+                add_into(self.held.at[jnp.bitwise_xor(self.index, m)], self.landing.at[k])
+        if t < len(self.order):
+            for m, k, copy in self.copies(t):
+                copy.start()
+
+    def own(self):
+        return self.held.at[self.index]
+
+    def wait_sends(self):
+        for t in range(len(self.order)):
+            for m, k, copy in self.copies(t):
+                copy.wait_send()
+
+
+class LineSum:
+    def __init__(self, ep, ne, blocks, landing, send_sem, recv_sem):
+        self.ep, self.ne, self.blocks, self.landing = ep, ne, blocks, landing
+        self.send_sem, self.recv_sem = send_sem, recv_sem
+
+    def copy(self, dest, way):
+        k = 0 if way == 1 else 1
+        return remote(
+            self.blocks.at[dest],
+            self.landing.at[k, dest],
+            self.send_sem.at[k, dest],
+            self.recv_sem.at[k, dest],
+            {"ep": lax.rem(self.ep + way + self.ne, self.ne)},
+        )
+
+    def turn(self, t, way):
+        ep, ne = self.ep, self.ne
+        dest = ep + ne - 1 - t if way == 1 else ep + t - (ne - 1)
+        has = dest <= ne - 1 if way == 1 else dest >= 0
+        inner = ep >= 1 if way == 1 else ep <= ne - 2
+        return dest, has, inner
+
+    def step(self, t):
+        for way in (1, -1):
+            dest, has, inner = self.turn(t, way)
+
+            @pl.when(has & inner)
+            def _(way=way, dest=dest):
+                self.copy(dest, way).wait_recv()
+                add_into(self.blocks.at[dest], self.landing.at[0 if way == 1 else 1, dest])
+
+            if t < self.ne - 1:
+
+                @pl.when(has)
+                def _(way=way, dest=dest):
+                    self.copy(dest, way).start()
+
+    def own(self):
+        return self.blocks.at[self.ep]
+
+    def wait_sends(self):
+        for t in range(self.ne - 1):
+            for way in (1, -1):
+                dest, has, inner = self.turn(t, way)
+
+                @pl.when(has)
+                def _(way=way, dest=dest):
+                    self.copy(dest, way).wait_send()
+
+
+def shape_at(array, where):
+    return tuple(len(range(*w.indices(n))) for w, n in zip(where, array.shape)) + array.shape[len(where) :]
+
+
 def reduce_body(ne, nd, pairs, n_line, n_swap, *refs):
+    refs = list(refs)
+
+    def take(n):
+        return [refs.pop(0) for _ in range(n)]
+
     n_pair = len(pairs)
-    n_extra = sum(extra for _, extra, _ in pairs)
+    n_extra = sum(p[2] for p in pairs)
+    n_both = sum(p[3] for p in pairs)
     n_sum = n_pair + n_line
-    sizes = (n_sum, n_extra, n_swap, n_sum, n_swap, n_sum, n_extra, n_pair)
-    groups, at = [], 0
-    for size in sizes:
-        groups.append(refs[at : at + size])
-        at += size
-    ins, extra_ins, swap_ins, outs, swap_outs, held, extras, pair_in = groups
-    lined = [a for a in range(n_pair) if pairs[a][2]] + list(range(n_pair, n_sum))
-    line_in = dict(zip(lined, refs[at : at + len(lined)]))
-    in_sem, extra_sem, out_sem, dp_send, dp_recv, ep_send, ep_recv, swap_send, swap_recv = refs[
-        at + len(lined) :
-    ]
+    ins, extra_ins, swap_ins = take(n_sum), take(n_extra), take(n_swap)
+    outs, swap_outs = take(n_sum), take(n_swap)
+    held, extras, pair_in = take(n_sum), take(n_extra), take(n_pair)
+    both_in, line_in = take(n_both), take(n_line)
+    load_sem, out_sem, dp_send, dp_recv, ep_send, ep_recv, swap_send, swap_recv = refs
     ep, dp = lax.axis_index("ep"), lax.axis_index("dp")
-    extra_of = [sum(extra for _, extra, _ in pairs[:a]) for a in range(n_pair)]
-
-    def load(a):
-        return pltpu.make_async_copy(ins[a], held[a], in_sem.at[a])
-
-    def load_extra(a):
-        i = extra_of[a]
-        return pltpu.make_async_copy(extra_ins[i], extras[i], extra_sem.at[i])
-
-    for a in range(n_sum):
-        load(a).start()
-        if a < n_pair and pairs[a][1]:
-            load_extra(a).start()
+    sums, then = [], []
+    for a, (order, where, has_extra, both) in enumerate(pairs):
+        sources = [ins[a].at[where] if where else ins[a]]
+        extra = extras.pop(0) if has_extra else None
+        if has_extra:
+            source = extra_ins.pop(0)
+            sources.append(source.at[where] if where else source)
+        sums.append(
+            PairSum(
+                dp,
+                order,
+                sources,
+                held[a],
+                extra,
+                pair_in[a],
+                load_sem.at[a],
+                dp_send.at[a],
+                dp_recv.at[a],
+            )
+        )
+        if both:
+            i = len(then)
+            then.append(
+                LineSum(ep, ne, sums[a].own(), both_in[i], ep_send.at[i], ep_recv.at[i])
+            )
+    lines, line_loads = [], []
+    for i in range(n_line):
+        a = n_pair + i
+        line_loads.append(pltpu.make_async_copy(ins[a], held[a], load_sem.at[a, 0]))
+        lines.append(
+            LineSum(
+                ep, ne, held[a], line_in[i], ep_send.at[n_both + i], ep_recv.at[n_both + i]
+            )
+        )
+    for copy in line_loads:
+        copy.start()
+    for each in sums:
+        each.load()
     greet(ep, dp, ne, nd)
     swaps = []
     for a in range(n_swap):
         src, dst = swap_ins[a], swap_outs[a]
-        own = pltpu.make_async_copy(src.at[ep], dst.at[ep], in_sem.at[n_sum + a])
+        own = pltpu.make_async_copy(src.at[ep], dst.at[ep], load_sem.at[n_sum + a, 0])
         own.start()
         swaps.append(own)
         for k in range(1, ne):
@@ -238,160 +380,67 @@
             )
             copy.start()
             swaps.append(copy)
-
-    def place(order, bit):
-        return sorted(order).index(bit)
-
-    def index_of(order):
-        index = 0
-        for b in order:
-            side = jnp.bitwise_and(lax.shift_right_logical(dp, b), 1)
-            index = index + (side << place(order, b))
-        return index
-
-    def pair_copies(a, t):
-        order = pairs[a][0]
-        side = 1 << place(order, order[t])
-        partner = jnp.bitwise_xor(index_of(order), side)
-        first = sum(1 << (len(order) - 1 - i) for i in range(t))
-        return [
-            (
-                m,
-                first + j,
-                remote(
-                    held[a].at[jnp.bitwise_xor(partner, m)],
-                    pair_in[a].at[first + j],
-                    dp_send.at[a, first + j],
-                    dp_recv.at[a, first + j],
-                    {"dp": jnp.bitwise_xor(dp, 1 << order[t])},
-                ),
-            )
-            for j, m in enumerate(masks([place(order, b) for b in order[t + 1 :]]))
-        ]
-
-    def pair_step(a, t):
-        order = pairs[a][0]
-        if t == 0:
-            load(a).wait()
-            if pairs[a][1]:
-                load_extra(a).wait()
-                add_into(held[a], extras[extra_of[a]])
-        elif t <= len(order):
-            for m, k, copy in pair_copies(a, t - 1):
-                copy.wait_recv()
-                add_into(held[a].at[jnp.bitwise_xor(index_of(order), m)], pair_in[a].at[k])
-        if t < len(order):
-            for m, k, copy in pair_copies(a, t):
-                copy.start()
-
-    def line_block(a, dest):
-        return held[a].at[index_of(pairs[a][0]), dest] if a < n_pair else held[a].at[dest]
-
-    def line_copy(a, dest, way):
-        k = 0 if way == 1 else 1
-        i = lined.index(a)
-        return remote(
-            line_block(a, dest),
-            line_in[a].at[k, dest],
-            ep_send.at[i, k, dest],
-            ep_recv.at[i, k, dest],
-            {"ep": lax.rem(ep + way + ne, ne)},
-        )
-
-    def line_turn(t, way):
-        dest = ep + ne - 1 - t if way == 1 else ep + t - (ne - 1)
-        has = dest <= ne - 1 if way == 1 else dest >= 0
-        inner = ep >= 1 if way == 1 else ep <= ne - 2
-        return dest, has, inner
-
-    def line_step(a, t):
-        if t == 0 and a >= n_pair:
-            load(a).wait()
-        for way in (1, -1):
-            dest, has, inner = line_turn(t, way)
-
-            @pl.when(has & inner)
-            def _(way=way, dest=dest):
-                line_copy(a, dest, way).wait_recv()
-                add_into(line_block(a, dest), line_in[a].at[0 if way == 1 else 1, dest])
-
-            if t < ne - 1:
-
-                @pl.when(has)
-                def _(way=way, dest=dest):
-                    line_copy(a, dest, way).start()
-
-    steps = max([len(order) + 1 for order, _, _ in pairs] + [ne if n_line else 0])
+    for copy in line_loads:
+        copy.wait()
+    steps = max([len(p[0]) + 1 for p in pairs] + [ne if n_line else 0])
     for t in range(steps):
-        for a in range(n_pair, n_sum):
-            if t < ne:
-                line_step(a, t)
-        for a in range(n_pair):
-            pair_step(a, t)
+        if t < ne:
+            for each in lines:
+                each.step(t)
+        for each in sums:
+            each.step(t)
     for t in range(ne):
-        for a in lined:
-            if a < n_pair:
-                line_step(a, t)
-
-    results = []
+        for each in then:
+            each.step(t)
+    results, after = [], iter(then)
     for a in range(n_sum):
         if a >= n_pair:
-            src = held[a].at[ep]
+            src = lines[a - n_pair].own()
         else:
-            src = line_block(a, ep) if pairs[a][2] else held[a].at[index_of(pairs[a][0])]
+            src = next(after).own() if pairs[a][3] else sums[a].own()
         copy = pltpu.make_async_copy(src, outs[a], out_sem.at[a])
         copy.start()
         results.append(copy)
-    for a in range(n_pair):
-        for t in range(len(pairs[a][0])):
-            for m, k, copy in pair_copies(a, t):
-                copy.wait_send()
-    for a in lined:
-        for t in range(ne - 1):
-            for way in (1, -1):
-                dest, has, inner = line_turn(t, way)
-
-                @pl.when(has)
-                def _(a=a, way=way, dest=dest):
-                    line_copy(a, dest, way).wait_send()
-
+    for each in sums + then + lines:
+        each.wait_sends()
     for copy in swaps + results:
         copy.wait()
 
 
 def reduce(ne, nd, pairs, lines, swaps, collective, us):
     arrays = [p[0] for p in pairs] + list(lines)
-    extras = [p[2] for p in pairs if p[2] is not None]
-    kinds = tuple((tuple(order), extra is not None, both) for _, order, extra, both in pairs)
-    results = [v.shape[2:] if both else v.shape[1:] for v, _, _, both in pairs]
+    extras = [p[3] for p in pairs if p[3] is not None]
+    kinds = tuple((tuple(p[1]), p[2], p[3] is not None, p[4]) for p in pairs)
+    shapes = [shape_at(p[0], p[2]) if p[2] else p[0].shape for p in pairs]
+    boths = [s for s, p in zip(shapes, pairs) if p[4]]
+    results = [s[2:] if p[4] else s[1:] for s, p in zip(shapes, pairs)]
     results += [v.shape[1:] for v in lines]
-    landing = [(v.shape[0] - 1,) + v.shape[1:] for v, _, _, _ in pairs]
-    landing += [(2,) + v.shape[1:] for v, _, _, both in pairs if both]
-    landing += [(2,) + v.shape for v in lines]
-    some = lambda v: max(len(v), 1)
-    line_count = max(len(lines) + sum(both for _, _, _, both in pairs), 1)
-    deep = max([v.shape[0] - 1 for v, _, _, _ in pairs] + [1])
+    scratch = shapes + [v.shape for v in lines]
+    scratch += [s for s, p in zip(shapes, pairs) if p[3] is not None]
+    scratch += [(s[0] - 1,) + s[1:] for s in shapes]
+    scratch += [(2,) + s[1:] for s in boths] + [(2,) + v.shape for v in lines]
+    some = lambda n: max(n, 1)
+    line_count = some(len(lines) + len(boths))
+    deep = max([s[0] - 1 for s in shapes] + [1])
     return pl.pallas_call(
         functools.partial(reduce_body, ne, nd, kinds, len(lines), len(swaps)),
         out_shape=[jax.ShapeDtypeStruct(s, BF16) for s in results]
         + [jax.ShapeDtypeStruct(v.shape, v.dtype) for v in swaps],
         in_specs=[ANY] * (len(arrays) + len(extras) + len(swaps)),
         out_specs=[ANY] * (len(arrays) + len(swaps)),
-        scratch_shapes=[pltpu.VMEM(v.shape, BF16) for v in arrays + extras]
-        + [pltpu.VMEM(s, BF16) for s in landing]
+        scratch_shapes=[pltpu.VMEM(s, BF16) for s in scratch]
         + [
-            DMA((len(arrays) + len(swaps),)),
-            DMA((some(extras),)),
+            DMA((len(arrays) + len(swaps), 2)),
             DMA((len(arrays),)),
-            DMA((some(pairs), deep)),
-            DMA((some(pairs), deep)),
+            DMA((some(len(pairs)), deep)),
+            DMA((some(len(pairs)), deep)),
             DMA((line_count, 2, ne)),
             DMA((line_count, 2, ne)),
-            DMA((some(swaps), ne - 1)),
-            DMA((some(swaps), ne - 1)),
+            DMA((some(len(swaps)), ne - 1)),
+            DMA((some(len(swaps)), ne - 1)),
         ],
         compiler_params=pltpu.CompilerParams(
-            collective_id=collective, has_side_effects=True, vmem_limit_bytes=56 * 2**20
+            collective_id=collective, has_side_effects=True, vmem_limit_bytes=60 * 2**20
         ),
         cost_estimate=cost(us),
     )(*arrays, *extras, *swaps)
@@ -405,9 +454,9 @@
     cots, refs = refs[:ne], refs[ne:]
     normed_ref, probs_ref, gate_ref, up_ref, down_ref = refs[:5]
     mix_ref, grad_ref, dots_ref = refs[5:8]
-    kept, landed = refs[8:10], refs[10:12]
-    rows_in, cots_in, picks, weights, first, second, keep, send, arrived, leaving = refs[12:22]
-    load_sem, store_sem, send_sem, recv_sem, free_sem, far_send, far_recv = refs[22:]
+    kept, landed, whole = refs[8:10], refs[10:12], refs[12:14]
+    rows_in, cots_in, picks, first, second, keep, send, arrived, leaving = refs[14:23]
+    load_sem, store_sem, send_sem, recv_sem, free_sem, far_send, far_recv = refs[23:]
     e = pl.program_id(0)
     last = pl.num_programs(0) - 1
     ep, dp = lax.axis_index("ep"), lax.axis_index("dp")
@@ -456,6 +505,9 @@
             {"dp": jnp.bitwise_xor(dp, 1 << first_bits(nd)[i])},
         )
 
+    def last_copy():
+        return pltpu.make_async_copy(keep, whole[1], load_sem.at[0])
+
     def collect():
         exchange().wait_recv()
         pieces = keep.shape[0]
@@ -471,7 +523,7 @@
                     else:
                         leaving[i, at] = value
 
-            @pl.when(lax.rem(e - 1, 2) == i)
+            @pl.when((lax.rem(e - 1, 2) == i) & (n < n_exp // 2 - 1))
             def _(i=i, bit=bit, put=put):
                 @pl.when(n > 0)
                 def _():
@@ -488,6 +540,14 @@
                     put(1)
 
                 far(i, n).start()
+
+            @pl.when((lax.rem(e - 1, 2) == i) & (n == n_exp // 2 - 1))
+            def _(i=i):
+                add_into(keep, arrived)
+                if i == 0:
+                    whole[0][...] = keep[...]
+                else:
+                    last_copy().start()
 
     @pl.when(e == 0)
     def _():
@@ -519,8 +579,6 @@
             rank = jnp.where(hit, rank, -1.0).astype(jnp.int32)
             pick = jnp.broadcast_to(rank[:, None, :], (n_exp, CAP, rows)) == slot
             pick_f = pick.astype(F32)
-            share = jnp.sum(pick_f * probs[:, None, :], axis=2, keepdims=True)
-            weights[s] = share
             flat = pick_f.reshape(n_exp * CAP, rows).astype(BF16)
             picks[s] = flat
             rows_in[s] = dot(flat, first[at, :]).astype(BF16).reshape(n_exp, CAP, width)
@@ -530,7 +588,9 @@
     def _():
         x = rows_in[:, e].reshape(blocks * CAP, width)
         c = cots_in[:, e].reshape(blocks * CAP, width)
-        p = weights[:, e].reshape(blocks * CAP, 1)
+        flat = picks[:, pl.ds(pl.multiple_of(e * CAP, CAP), CAP), :].astype(F32)
+        p = jnp.sum(flat * probs_ref[:, pl.ds(e, 1), :], axis=2, keepdims=True)
+        p = p.reshape(blocks * CAP, 1)
         w_gate, w_up, w_down = gate_ref[0], up_ref[0], down_ref[0]
         gate_pre = dot(x, w_gate)
         up_pre = dot(x, w_up)
@@ -547,7 +607,6 @@
         scaled = (wide * p).astype(BF16)
         grad_x = dot(grad_gate, w_gate, ((1,), (1,))) + dot(grad_up, w_up, ((1,), (1,)))
 
-        flat = picks[:, pl.ds(pl.multiple_of(e * CAP, CAP), CAP), :].astype(F32)
         dots_ref[0] = jnp.sum(flat * pair.reshape(blocks, CAP, 1), axis=1)
 
         @pl.when(e > 0)
@@ -610,10 +669,11 @@
             for copy in stores(t):
                 copy.wait()
 
+        last_copy().wait()
         for i in range(2):
-            far(i, n_exp // 2 - 1).wait_send()
-
-            @pl.loop(0, n_exp // 2)
+            far(i, n_exp // 2 - 2).wait_send()
+
+            @pl.loop(0, n_exp // 2 - 1)
             def _(n, i=i):
                 far(i, n).wait_recv()
 
@@ -630,10 +690,13 @@
     full = (blocks * rows, width)
     one = pl.Buffered(1)
     weight = lambda e: (jnp.minimum(e, n_exp - 1), 0, 0)
-    part = (half // 2, n_exp // 2, packed, inner)
+    early = n_exp // 2 - 1
+    part = (half // 2, early, packed, inner)
     kept = pl.BlockSpec(
-        (half // 2, 1, packed, inner), lambda e: (0, jnp.maximum(e - 1, 0) // 2, 0, 0)
-    )
+        (half // 2, 1, packed, inner),
+        lambda e: (0, jnp.minimum(jnp.maximum(e - 1, 0) // 2, early - 1), 0, 0),
+    )
+    last = (half, packed, inner)
     return pl.pallas_call(
         functools.partial(expert_body, ne, nd, micro, rows),
         grid=(n_exp + 1,),
@@ -644,12 +707,12 @@
             pl.BlockSpec((1, width, inner), weight),
             pl.BlockSpec((1, inner, width), weight),
         ],
-        out_specs=[ANY, ANY, pl.BlockSpec((1, blocks, rows), weight), kept, kept, ANY, ANY],
+        out_specs=[ANY, ANY, pl.BlockSpec((1, blocks, rows), weight), kept, kept, ANY, ANY]
+        + [pl.BlockSpec(last, lambda e: (0, 0, 0), pipeline_mode=one), ANY],
         scratch_shapes=[
             pltpu.VMEM((blocks, n_exp, CAP, width), BF16),
             pltpu.VMEM((blocks, n_exp, CAP, width), BF16),
             pltpu.VMEM((blocks, n_exp * CAP, rows), BF16),
-            pltpu.VMEM((blocks, n_exp, CAP, 1), F32),
             pltpu.VMEM(full, BF16),
             pltpu.VMEM(full, BF16),
             pltpu.VMEM((half, packed, inner), BF16),
@@ -662,14 +725,15 @@
             DMA,
             pltpu.SemaphoreType.REGULAR,
             DMA((2,)),
-            DMA((2, n_exp // 2)),
+            DMA((2, early)),
         ],
         out_shape=[
             jax.ShapeDtypeStruct(full, BF16),
             jax.ShapeDtypeStruct(full, BF16),
             jax.ShapeDtypeStruct((n_exp, blocks, rows), F32),
         ]
-        + [jax.ShapeDtypeStruct(part, BF16)] * 4,
+        + [jax.ShapeDtypeStruct(part, BF16)] * 4
+        + [jax.ShapeDtypeStruct(last, BF16)] * 2,
         compiler_params=pltpu.CompilerParams(
             vmem_limit_bytes=62 * 2**20,
             dimension_semantics=("arbitrary",),
@@ -822,16 +886,59 @@
             out_specs=[mine, logs],
         ),
         out_shape=[jax.ShapeDtypeStruct(queries.shape, BF16), log_shape],
-        compiler_params=pltpu.CompilerParams(vmem_limit_bytes=40 * 2**20),
+        compiler_params=pltpu.CompilerParams(vmem_limit_bytes=60 * 2**20),
         cost_estimate=cost(15),
     )(dp.reshape(1), starts, queries, keys, values)
 
 
-def attend_back_body(
-    span, dp_ref, starts_ref, q_ref, k_ref, v_ref, log_ref, g_ref, cos_ref, sin_ref, *outs
-):
-    dq_ref, dk_ref, dv_ref = outs
-    dp = dp_ref[0]
+def attend_back_body(span, nd, orders, *refs):
+    starts_ref, q_ref, k_ref, v_ref, log_ref, g_ref, cos_ref, sin_ref = refs[:8]
+    n = len(orders)
+    sources, extras = refs[8 : 8 + n], refs[8 + n : 8 + 2 * n]
+    dq_ref, dk_ref, dv_ref = refs[8 + 2 * n : 11 + 2 * n]
+    outs, rest = refs[11 + 2 * n : 11 + 3 * n], refs[11 + 3 * n :]
+    dp = lax.axis_index("dp")
+    step = pl.program_id(0) * pl.num_programs(1) + pl.program_id(1)
+    final = pl.num_programs(0) * pl.num_programs(1) - 1
+    if n:
+        held, more, landing, (load_sem, out_sem, send_sem, recv_sem) = (
+            rest[:n],
+            rest[n : 2 * n],
+            rest[2 * n : 3 * n],
+            rest[3 * n :],
+        )
+        sums = [
+            PairSum(
+                dp,
+                orders[a],
+                (sources[a].at[:, 1:], extras[a].at[:, 1:]),
+                held[a],
+                more[a],
+                landing[a],
+                load_sem.at[a],
+                send_sem.at[a],
+                recv_sem.at[a],
+            )
+            for a in range(n)
+        ]
+
+        @pl.when(step == 0)
+        def _():
+            for each in sums:
+                each.load()
+            barrier = pltpu.get_barrier_semaphore()
+            met = sorted(set(b for order in orders for b in order))
+            for bit in met:
+                pl.semaphore_signal(
+                    barrier,
+                    inc=1,
+                    device_id={"dp": jnp.bitwise_xor(dp, 1 << bit)},
+                    device_id_type=MESH,
+                )
+            pl.semaphore_wait(barrier, len(met))
+            for each in sums:
+                each.step(0)
+
     rows = q_ref.shape[0]
     q = spread(q_ref[...].astype(F32) * SCALE).astype(BF16)
     g = spread(g_ref[...].astype(F32)).astype(BF16)
@@ -853,26 +960,63 @@
     dv = dot(probs.astype(BF16), g, ((0,), (0,))).astype(BF16)
     dv_ref[here] = dv.reshape(span, rows, dv.shape[1])
 
-
-def attend_back(dp, starts, queries, keys, values, logs_in, grad, cosine, sine, micro, rows, nd):
+    if n:
+
+        @pl.when(step == final)
+        def _():
+            copies = []
+            for t in range(1, max(len(order) for order in orders) + 1):
+                for each in sums:
+                    each.step(t)
+            for a, each in enumerate(sums):
+                copies.append(pltpu.make_async_copy(each.own(), outs[a], out_sem.at[a]))
+                copies[a].start()
+            for each in sums:
+                each.wait_sends()
+            for copy in copies:
+                copy.wait()
+
+
+def attend_back(
+    starts, queries, keys, values, logs_in, grad, cosine, sine, sums, micro, rows, nd, collective
+):
     grid, mine, theirs, column, logs, _ = attention_specs(micro, rows, nd)
     table = pl.BlockSpec((rows, 128), lambda m, h, *_: (0, 0))
+    n = len(sums)
+    shapes = [(v.shape[0], v.shape[1] - 1) + v.shape[2:] for v, _, _ in sums]
+    deep = max([s[0] - 1 for s in shapes] + [1])
+    scratch = [pltpu.VMEM(s, BF16) for s in shapes] * 2
+    scratch += [pltpu.VMEM((s[0] - 1,) + s[1:], BF16) for s in shapes]
+    scratch += [DMA((n, 2)), DMA((n,)), DMA((n, deep)), DMA((n, deep))] if n else []
+    remote_params = dict(collective_id=collective, has_side_effects=True) if n else {}
     return pl.pallas_call(
-        functools.partial(attend_back_body, nd // 2 + 1),
-        grid_spec=pltpu.PrefetchScalarGridSpec(
-            num_scalar_prefetch=1,
-            grid=grid,
-            in_specs=[column, mine, theirs, theirs, logs, mine, table, table],
-            out_specs=[mine, theirs, theirs],
+        functools.partial(
+            attend_back_body, nd // 2 + 1, nd, tuple(tuple(order) for _, order, _ in sums)
         ),
+        grid=grid,
+        in_specs=[column, mine, theirs, theirs, logs, mine, table, table] + [ANY] * (2 * n),
+        out_specs=[mine, theirs, theirs] + [ANY] * n,
         out_shape=[
             jax.ShapeDtypeStruct(queries.shape, BF16),
             jax.ShapeDtypeStruct(keys.shape, BF16),
             jax.ShapeDtypeStruct(values.shape, BF16),
-        ],
-        compiler_params=pltpu.CompilerParams(vmem_limit_bytes=48 * 2**20),
+        ]
+        + [jax.ShapeDtypeStruct(s[1:], BF16) for s in shapes],
+        scratch_shapes=scratch,
+        compiler_params=pltpu.CompilerParams(vmem_limit_bytes=60 * 2**20, **remote_params),
         cost_estimate=cost(25),
-    )(dp.reshape(1), starts, queries, keys, values, logs_in, grad, cosine, sine)
+    )(
+        starts,
+        queries,
+        keys,
+        values,
+        logs_in,
+        grad,
+        cosine,
+        sine,
+        *[v for v, _, _ in sums],
+        *[extra for _, _, extra in sums],
+    )
 
 
 def input_body(
@@ -938,7 +1082,7 @@
         in_specs=[VMEM] * 12,
         out_specs=[VMEM] * 5,
         scratch_shapes=[pltpu.VMEM(dk.shape, BF16)],
-        compiler_params=pltpu.CompilerParams(vmem_limit_bytes=48 * 2**20),
+        compiler_params=pltpu.CompilerParams(vmem_limit_bytes=60 * 2**20),
         cost_estimate=cost(10),
     )(normed, dq, dk, dv, cosine, sine, *weights, tokens, gain, grad_residual)
 
@@ -1023,7 +1167,7 @@
     )
     nb = bit_count(nd)
     orders = [order[:-1][::-1] for order in gather_orders(nd)]
-    mix, grad_in, pair_dots, kept_a, kept_b, landed_a, landed_b = experts(
+    mix, grad_in, pair_dots, *grads = experts(
         normed_all.reshape(ne * every, width),
         cots,
         probs_here,
@@ -1036,23 +1180,20 @@
         nd,
         6,
     )
+    kept, landed, last = grads[:2], grads[2:4], grads[4:]
     pair_dots = pair_dots.reshape(here, ne, every).transpose(1, 0, 2)
-
-    grads_a, grads_b, grad_back, dots_all = reduce(
+    head = (slice(None), slice(0, 1))
+    *grads, grad_back, dots_all = reduce(
         ne,
         nd,
-        [
-            (kept, order[1:], landed, False)
-            for kept, landed, order in (
-                (kept_a, landed_a, orders[0]),
-                (kept_b, landed_b, orders[1]),
-            )
-        ],
+        [(last[i], orders[i], None, None, False) for i in range(2)]
+        + [(kept[i], orders[i][1:], head, landed[i], False) for i in range(2)],
         (grad_in.reshape(ne, every, width),),
         (pair_dots,),
         2,
         40,
     )
+    grads_last, grads_head = grads[:2], grads[2:]
     pair_dot = dots_all.reshape(EXPERTS, every).T
     grad_logits = gate_probs * (
         pair_dot - jnp.sum(gate_probs * pair_dot, axis=1, keepdims=True)
@@ -1076,8 +1217,8 @@
     grad_attn = jnp.einsum("td,fd->tf", residual_low, w_out, preferred_element_type=F32).astype(
         BF16
     )
-    grad_query, grad_key_all, grad_value_all = attend_back(
-        dp,
+    more = kept[0].shape[1] > 1
+    grad_query, grad_key_all, grad_value_all, *grads_more = attend_back(
         starts,
         query_rot,
         key_all,
@@ -1086,22 +1227,43 @@
         grad_attn,
         cosine,
         sine,
+        [(kept[i], orders[i][1:], landed[i]) for i in range(2)] if more else [],
         micro,
         rows,
         nd,
-    )
-    whole = [[0] + order for order in orders]
-    grad_key, grad_value = reduce(
+        5,
+    )
+
+    def by_owner(grad):
+        share = grad.shape[0] // (ne * nd)
+        return grad.astype(BF16).reshape(ne, nd, share, grad.shape[1]).transpose(1, 0, 2, 3)
+
+    full = [[0] + order for order in orders]
+    grad_w_out = by_owner(grad_w_out)
+    columns = [(slice(None),) * 3 + (slice(i * kv_width, (i + 1) * kv_width),) for i in range(2)]
+    grad_key, grad_value, *d_out = reduce(
         ne,
         nd,
-        [(grad_key_all, whole[0], None, False), (grad_value_all, whole[1], None, False)],
+        [
+            (grad_key_all, full[0], None, None, False),
+            (grad_value_all, full[1], None, None, False),
+            (grad_w_out, full[0], columns[0], None, True),
+            (grad_w_out, full[1], columns[1], None, True),
+        ],
         (),
         (),
         3,
-        25,
-    )
-
-    grads = jnp.stack([grads_a, grads_b], axis=1)
+        35,
+    )
+    d_out = jnp.concatenate(d_out, axis=1).astype(F32)
+
+    per_path = [
+        jnp.concatenate(
+            [grads_head[i]] + ([grads_more[i]] if more else []) + [grads_last[i][None]], axis=0
+        )
+        for i in range(2)
+    ]
+    grads = jnp.stack(per_path, axis=1)
     grads = grads.reshape((here,) + grads.shape[2:]).astype(F32)
     share = width // nd
     grad_w_gate, grad_w_up = grads[:, :share], grads[:, share : 2 * share]
@@ -1137,30 +1299,24 @@
         axis=1,
     )
 
-    def by_owner(grad):
-        share = grad.shape[0] // (ne * nd)
-        return grad.astype(BF16).reshape(ne, nd, share, grad.shape[1]).transpose(1, 0, 2, 3)
-
     def blocks_of(grad):
         return grad.reshape(nd, ne, -1, grad.shape[2])
 
-    dense = [
-        blocks_of(grad_w_query),
-        by_owner(grad_w_out),
-        blocks_of(grad_w_key),
-        blocks_of(grad_w_value),
-        by_owner(small),
-    ]
     *dense, mix_own = reduce(
         ne,
         nd,
-        [(v, whole[i % 2], None, True) for i, v in enumerate(dense)],
+        [
+            (blocks_of(grad_w_query), full[0], None, None, True),
+            (blocks_of(grad_w_key), full[1], None, None, True),
+            (blocks_of(grad_w_value), full[1], None, None, True),
+            (by_owner(small), full[0], None, None, True),
+        ],
         (mix.reshape(ne, every, width),),
         (),
         4,
-        60,
-    )
-    d_query, d_out, d_key, d_value, d_small = (v.astype(F32) for v in dense)
+        50,
+    )
+    d_query, d_key, d_value, d_small = (v.astype(F32) for v in dense)
     output = (residual + mix_own.astype(F32)).astype(BF16).reshape(tokens.shape)
     return (
         output,

time: 394 us -> 384 us (0.975)
  local copies, waits for them, and re-layouts: 27 us -> 15.7 us
  Pallas kernels: 342 us -> 333 us
  matrix products: 4.95 us -> 8.96 us
    pallas_call x1, Pallas kernels: 101 us -> 84.2 us  [experts(): pl.pallas_call(functools.partial(expert_body, ne, nd, micro, rows), grid=...]
    unnamed x82 -> x50, local copies, waits for them, and re-layouts: 14.8 us -> 1.32 us
    pallas_call x1, Pallas kernels: 15.1 us -> 23.5 us  [attend_back(): pl.pallas_call(functools.partial(attend_back_body, nd // 2 + 1, nd, tuple...]
  transfers between devices with their start and end apart: 3 -> 3, of which waited for: 0 -> 0; matrix products, arithmetic and copies ran while one was open for 2% -> 3% of each run, Pallas kernels for 21% -> 22%
where the time goes in v6:
time: 384 us; the launch traced here: 379 us
  Pallas kernels  333 us (87%)
  local copies, waits for them, and re-layouts  15.7 us (4%)
  other arithmetic  15.2 us (4%)
  matrix products  8.96 us (2%)
  starting transfers between devices  5.57 us (1%)
    pallas_call x3, Pallas kernels, reduce(): pl.pallas_call(functools.partial(reduce_body, ne, nd, kinds, len(lines),...  136 us
    pallas_call x1, Pallas kernels, experts(): pl.pallas_call(functools.partial(expert_body, ne, nd, micro, rows), grid=...  84.2 us
    pallas_call x2, Pallas kernels, gather(): pl.pallas_call(functools.partial(gather_body, ne, nd, len(dp_arrays), len...  64.8 us
    pallas_call x1, Pallas kernels, attend_back(): pl.pallas_call(functools.partial(attend_back_body, nd // 2 + 1, nd, tuple...  23.5 us
    pallas_call x1, Pallas kernels, attend(): pl.pallas_call(functools.partial(attend_body, nd // 2 + 1), grid_spec=plt...  11.5 us
  transfers between devices with their start and end apart: 3, of which 0 were waited for; matrix products, arithmetic and copies ran while one was open for 3% of the time, Pallas kernels for 22%

profile of v6, /device:TPU:10, one launch (start us, length us, event | category | flops | bytes accessed | tf_op | source)
XLA Modules:
  0.0 379.2 jit_solution(6688251498125853807)
XLA Ops:
  1.2 2.6 collective-permute-start.1
  3.8 2.5 collective-permute-start
  10.2 5.4 %shard_map.229 = (bf16[256,1024]{1,0:T(8,128)(2,1)}, bf16[256,1024]{1,0:T(8,128)(2,1)}, bf16[256,512]{1,0:T(8,128)(2,1)}, bf16[256,512]{1,0:T(8,128)(2,1)}) custom-call(bf16[256,1024]{1,0:T(8,128)(2,1)} %bitcast.89, f32[1,1024]{1,0:T(1,128)} %bitcast.111, f32[256,128]{1,0:T(8,128)} %copy.40.cos_ref.refs_6_, ...), custom_call_target="tpu_custom_call" | custom-call | bytes 15000000 | tf_op jit(solution)/shard_map/pallas_call | solution.py:793
  15.6 23.0 %shard_map.230 = (bf16[8,256,512]{2,1,0:T(8,128)(2,1)}, bf16[8,256,512]{2,1,0:T(8,128)(2,1)}, f32[8,8,128]{2,1,0:T(8,128)}) custom-call(bf16[256,512]{1,0:T(8,128)(2,1)} %get-tuple-element.57.refs_0_, bf16[256,512]{1,0:T(8,128)(2,1)} %get-tuple-element.58.refs_1_, f32[8,128]{1,0:T(8,128)} %concatenate.29.refs_2_), custom_call_target="tpu_custom_call" | custom-call | bytes 75000000 | tf_op jit(solution)/shard_map/pallas_call | solution.py:166
  40.4 11.5 %shard_map.231 = (bf16[256,1024]{1,0:T(8,128)(2,1)}, f32[2,4,512,1]{3,2,1,0:T(8,128)}) custom-call(s32[1]{0:T(128)} %bitcast.1.dp_ref, s32[256,1]{1,0:T(8,128)} %copy.41.starts_ref.refs_0_, bf16[256,1024]{1,0:T(8,128)(2,1)} %get-tuple-element.60.q_ref.refs_1_, bf16[8,256,512]{2,1,0:T(8,128)(2,1)} %get-tuple-element.61.k_ref.refs_2_, ...), custom_call_target="tpu_custom_call" | custom-call | bytes 45000000 | tf_op jit(solution)/shard_map/pallas_call | solution.py:880
  51.9 1.9 multiply_reduce_fusion.2
  54.9 41.8 %shard_map.232 = (bf16[4,256,1024]{2,1,0:T(8,128)(2,1)}, f32[4,32,256]{2,1,0:T(8,128)}) custom-call(bf16[256,1024]{1,0:T(8,128)(2,1)} %copy-done.5, f32[32,256]{1,0:T(8,128)} %fusion.9.refs_1_), custom_call_target="tpu_custom_call" | custom-call | bytes 114000000 | tf_op jit(solution)/shard_map/pallas_call | solution.py:166
  98.2 84.2 %shard_map.233 = (bf16[1024,1024]{1,0:T(8,128)(2,1)}, bf16[1024,1024]{1,0:T(8,128)(2,1)}, f32[8,8,128]{2,1,0:T(8,128)}, bf16[2,3,384,512]{3,2,1,0:T(8,128)(2,1)}...) custom-call(bf16[256,1024]{1,0:T(8,128)(2,1)} %bitcast.95, ...), custom_call_target="tpu_custom_call" | custom-call | bytes 225000000 | tf_op jit(solution)/shard_map/pallas_call | solution.py:700
  183.8 44.3 %shard_map.234 = (bf16[384,512]{1,0:T(8,128)(2,1)}, bf16[384,512]{1,0:T(8,128)(2,1)}, bf16[1,384,512]{2,1,0:T(8,128)(2,1)}, bf16[1,384,512]{2,1,0:T(8,128)(2,1)}...) custom-call(bf16[4,384,512]{2,1,0:T(8,128)(2,1)} %get-tuple-element.68.refs_0_, ...), custom_call_target="tpu_custom_call" | custom-call | bytes 120000000 | tf_op jit(solution)/shard_map/pallas_call | solution.py:425
  229.1 1.1 convolution_convert_fusion.2
  230.2 2.0 multiply_reduce_fusion
  232.6 1.2 copy-done.4
  233.8 1.6 convolution_convert_fusion.1.refs_5_
  235.4 2.1 convolution_convert_fusion
  238.4 3.2 copy.57
  241.6 23.5 %shard_map.235 = (bf16[256,1024]{1,0:T(8,128)(2,1)}, bf16[8,256,512]{2,1,0:T(8,128)(2,1)}, bf16[8,256,512]{2,1,0:T(8,128)(2,1)}, bf16[2,384,512]{2,1,0:T(8,128)(2,1)}, bf16[2,384,512]{2,1,0:T(8,128)(2,1)}) custom-call(s32[256,1]{1,0:T(8,128)} %copy.41.starts_ref.refs_0_, bf16[256,1024]{1,0:T(8,128)(2,1)} %get-tuple-element.60.q_ref.refs_1_, ...), custom_call_target="tpu_custom_call" | custom-call | bytes 75000000 | tf_op jit(solution)/shard_map/pallas_call | solution.py:992
  265.1 39.0 %shard_map.236 = (bf16[256,512]{1,0:T(8,128)(2,1)}, bf16[256,512]{1,0:T(8,128)(2,1)}, bf16[32,512]{1,0:T(8,128)(2,1)}, bf16[32,512]{1,0:T(8,128)(2,1)}) custom-call(bf16[8,256,512]{2,1,0:T(8,128)(2,1)} %get-tuple-element.79.refs_0_, bf16[8,256,512]{2,1,0:T(8,128)(2,1)} %get-tuple-element.80.refs_1_, bf16[8,4,32,1024]{3,2,1,0:T(8,128)(2,1)} %bitcast.86, ...), custom_call_target="tpu_custom_call" | custom-call | bytes 105000000 | tf_op jit(solution)/shard_map/pallas_call | solution.py:425
  304.1 6.8 %shard_map.237 = (bf16[8,128,1024]{2,1,0:T(8,128)(2,1)}, bf16[8,128,512]{2,1,0:T(8,128)(2,1)}, bf16[8,128,512]{2,1,0:T(8,128)(2,1)}, f32[256,1024]{1,0:T(8,128)}, f32[1,1024]{1,0:T(1,128)}) custom-call(bf16[256,1024]{1,0:T(8,128)(2,1)} %get-tuple-element.64.n_ref, bf16[256,1024]{1,0:T(8,128)(2,1)} %get-tuple-element.78.dq_ref, ...), custom_call_target="tpu_custom_call" | custom-call | bytes 30000000 | tf_op jit(solution)/shard_map/pallas_call | solution.py:1075
  312.1 1.0 maximum_bitcast_fusion.2.refs_3_
  313.1 53.1 %shard_map.238 = (bf16[32,1024]{1,0:T(8,128)(2,1)}, bf16[32,512]{1,0:T(8,128)(2,1)}, bf16[32,512]{1,0:T(8,128)(2,1)}, bf16[32,128]{1,0:T(8,128)(2,1)}, bf16[256,1024]{1,0:T(8,128)(2,1)}) custom-call(bf16[8,4,32,1024]{3,2,1,0:T(8,128)(2,1)} %bitcast.98, bf16[8,4,32,512]{3,2,1,0:T(8,128)(2,1)} %bitcast.100, bf16[8,4,32,512]{3,2,1,0:T(8,128)(2,1)} %bitcast.101, ...), custom_call_target="tpu_custom_call" | custom-call | bytes 150000000 | tf_op jit(solution)/shard_map/pallas_call | solution.py:425
  366.2 1.3 slice.42
  368.2 1.4 maximum_bitcast_fusion
  370.9 2.5 fusion.19
  377.6 1.5 pad_maximum_fusion
  (100 shorter events, 19.8 us)
Async XLA Ops:
  0.6 53.3 %copy-start = (bf16[1024,32]{0,1:T(8,128)(2,1)S(1)}, bf16[1024,32]{0,1:T(8,128)(2,1)}, u32[]{:S(2)}) copy-start(bf16[1024,32]{0,1:T(8,128)(2,1)} %param.23) | copy-start | bytes 196612
  0.7 97.5 %collective-permute-start.2 = (bf16[256,1024]{1,0:T(8,128)(2,1)}, bf16[256,1024]{1,0:T(8,128)(2,1)}, u32[]{:S(2)}, u32[]{:S(2)}) collective-permute-start(bf16[256,1024]{1,0:T(8,128)(2,1)} %bitcast.92), channel_id=1, source_target_pairs={{0,24},{8,0},{16,8},{24,16},{1,25},{9,1},{17,9},{25,17},{2,26},{10... | collective-permute-start | bytes 1572872 | tf_op jit(solution)/shard_map/ppermute | solution.py:1137
  1.2 97.0 %collective-permute-start.1 = (bf16[256,1024]{1,0:T(8,128)(2,1)}, bf16[256,1024]{1,0:T(8,128)(2,1)}, u32[]{:S(2)}, u32[]{:S(2)}) collective-permute-start(bf16[256,1024]{1,0:T(8,128)(2,1)} %bitcast.93), channel_id=1, source_target_pairs={{0,16},{8,24},{16,0},{24,8},{1,17},{9,25},{17,1},{25,9},{2,18},{10... | collective-permute-start | bytes 1572872 | tf_op jit(solution)/shard_map/ppermute | solution.py:1137
  3.8 94.4 %collective-permute-start = (bf16[256,1024]{1,0:T(8,128)(2,1)}, bf16[256,1024]{1,0:T(8,128)(2,1)}, u32[]{:S(2)}, u32[]{:S(2)}) collective-permute-start(bf16[256,1024]{1,0:T(8,128)(2,1)} %bitcast.94), channel_id=1, source_target_pairs={{0,8},{8,16},{16,24},{24,0},{1,9},{9,17},{17,25},{25,1},{2,10},{10... | collective-permute-start | bytes 1572872 | tf_op jit(solution)/shard_map/ppermute | solution.py:1137
  10.2 29.2 %copy-start.23 = (s32[2,1,128]{2,1,0:T(1,128)S(1)}, s32[2,1,128]{2,1,0:T(1,128)}, u32[]{:S(2)}) copy-start(s32[2,1,128]{2,1,0:T(1,128)} %param.15) | copy-start | bytes 3076
  40.4 11.5 %copy-start.3 = (bf16[1024,1024]{1,0:T(8,128)(2,1)S(1)}, bf16[1024,1024]{1,0:T(8,128)(2,1)}, u32[]{:S(2)}) copy-start(bf16[1024,1024]{1,0:T(8,128)(2,1)} %param.21) | copy-start | bytes 6291460
  40.4 11.5 %copy-start.7 = (bf16[2,128,1024]{2,1,0:T(8,128)(2,1)S(1)}, bf16[2,128,1024]{2,1,0:T(8,128)(2,1)}, u32[]{:S(2)}) copy-start(bf16[2,128,1024]{2,1,0:T(8,128)(2,1)} %param.14) | copy-start | bytes 1572868
  51.8 1.9 copy-start.18
  183.8 45.2 %copy-start.6 = (bf16[256,1024]{1,0:T(8,128)(2,1)S(1)}, bf16[256,1024]{1,0:T(8,128)(2,1)}, u32[]{:S(2)}) copy-start(bf16[256,1024]{1,0:T(8,128)(2,1)} %copy-done.5) | copy-start | bytes 1572868
  228.2 4.1 %copy-start.8 = (bf16[2,128,1024]{2,1,0:T(8,128)(2,1)S(1)}, bf16[2,128,1024]{2,1,0:T(8,128)(2,1)}, u32[]{:S(2)}) copy-start(bf16[2,128,1024]{2,1,0:T(8,128)(2,1)} %param.27) | copy-start | bytes 1572868
  228.2 4.1 %copy-start.10 = (bf16[256,1024]{1,0:T(8,128)(2,1)S(1)}, bf16[256,1024]{1,0:T(8,128)(2,1)}, u32[]{:S(2)}) copy-start(bf16[256,1024]{1,0:T(8,128)(2,1)} %get-tuple-element.77) | copy-start | bytes 1572868
  232.2 1.6 copy-start.4
  233.8 3.7 copy-start.2
  313.0 55.2 %copy-start.11 = (bf16[2,384,512]{2,1,0:T(8,128)(2,1)S(1)}, bf16[2,384,512]{2,1,0:T(8,128)(2,1)}, u32[]{:S(2)}) copy-start(bf16[2,384,512]{2,1,0:T(8,128)(2,1)} %get-tuple-element.97) | copy-start | bytes 2359300
  313.0 55.2 %copy-start.12 = (bf16[2,384,512]{2,1,0:T(8,128)(2,1)S(1)}, bf16[2,384,512]{2,1,0:T(8,128)(2,1)}, u32[]{:S(2)}) copy-start(bf16[2,384,512]{2,1,0:T(8,128)(2,1)} %get-tuple-element.100) | copy-start | bytes 2359300
  313.0 55.2 %copy-start.14 = (bf16[384,512]{1,0:T(8,128)(2,1)S(1)}, bf16[384,512]{1,0:T(8,128)(2,1)}, u32[]{:S(2)}) copy-start(bf16[384,512]{1,0:T(8,128)(2,1)} %get-tuple-element.98) | copy-start | bytes 1179652
  313.0 55.2 %copy-start.15 = (bf16[384,512]{1,0:T(8,128)(2,1)S(1)}, bf16[384,512]{1,0:T(8,128)(2,1)}, u32[]{:S(2)}) copy-start(bf16[384,512]{1,0:T(8,128)(2,1)} %get-tuple-element.101) | copy-start | bytes 1179652
  313.0 55.2 %copy-start.16 = (bf16[1,384,512]{2,1,0:T(8,128)(2,1)S(1)}, bf16[1,384,512]{2,1,0:T(8,128)(2,1)}, u32[]{:S(2)}) copy-start(bf16[1,384,512]{2,1,0:T(8,128)(2,1)} %get-tuple-element.96) | copy-start | bytes 1179652
  370.9 2.5 copy-start.13
  373.4 1.7 copy-start.20
  373.4 2.3 copy-start.19
  373.4 2.9 copy-start.17
  373.4 3.6 copy-start.21
  373.4 3.6 copy-start.22
  (3 other events, 4.1 us)

commit v7 on v6

--- a/solution.py
+++ b/solution.py
@@ -196,14 +196,10 @@
 
 
 class PairSum:
-    def __init__(self, dp, order, sources, held, extra, landing, load_sem, send_sem, recv_sem):
+    def __init__(self, dp, order, loads, held, extra, landing, send_sem, recv_sem):
         self.dp, self.order, self.held, self.landing = dp, order, held, landing
         self.send_sem, self.recv_sem = send_sem, recv_sem
-        self.extra = extra
-        self.loads = [
-            pltpu.make_async_copy(src, dst, load_sem.at[i])
-            for i, (src, dst) in enumerate(zip(sources, (held, extra)))
-        ]
+        self.extra, self.loads = extra, loads
         self.index = 0
         for b in order:
             side = jnp.bitwise_and(lax.shift_right_logical(dp, b), 1)
@@ -239,7 +235,7 @@
         if t == 0:
             for copy in self.loads:
                 copy.wait()
-            if len(self.loads) > 1:
+            if self.extra is not None:
                 add_into(self.held, self.extra)
         elif t <= len(self.order):
             for m, k, copy in self.copies(t - 1):
@@ -312,13 +308,13 @@
     return tuple(len(range(*w.indices(n))) for w, n in zip(where, array.shape)) + array.shape[len(where) :]
 
 
-def reduce_body(ne, nd, pairs, n_line, n_swap, *refs):
+def reduce_body(ne, nd, pairs, line_parts, n_swap, *refs):
     refs = list(refs)
 
     def take(n):
         return [refs.pop(0) for _ in range(n)]
 
-    n_pair = len(pairs)
+    n_pair, n_line = len(pairs), len(line_parts)
     n_extra = sum(p[2] for p in pairs)
     n_both = sum(p[3] for p in pairs)
     n_sum = n_pair + n_line
@@ -330,23 +326,16 @@
     ep, dp = lax.axis_index("ep"), lax.axis_index("dp")
     sums, then = [], []
     for a, (order, where, has_extra, both) in enumerate(pairs):
-        sources = [ins[a].at[where] if where else ins[a]]
+        targets = [(ins[a], held[a])]
         extra = extras.pop(0) if has_extra else None
         if has_extra:
-            source = extra_ins.pop(0)
-            sources.append(source.at[where] if where else source)
+            targets.append((extra_ins.pop(0), extra))
+        loads = [
+            pltpu.make_async_copy(src.at[where] if where else src, dst, load_sem.at[a, i])
+            for i, (src, dst) in enumerate(targets)
+        ]
         sums.append(
-            PairSum(
-                dp,
-                order,
-                sources,
-                held[a],
-                extra,
-                pair_in[a],
-                load_sem.at[a],
-                dp_send.at[a],
-                dp_recv.at[a],
-            )
+            PairSum(dp, order, loads, held[a], extra, pair_in[a], dp_send.at[a], dp_recv.at[a])
         )
         if both:
             i = len(then)
@@ -356,7 +345,8 @@
     lines, line_loads = [], []
     for i in range(n_line):
         a = n_pair + i
-        line_loads.append(pltpu.make_async_copy(ins[a], held[a], load_sem.at[a, 0]))
+        src = ins[a].at[line_parts[i]] if line_parts[i] else ins[a]
+        line_loads.append(pltpu.make_async_copy(src, held[a], load_sem.at[a, 0]))
         lines.append(
             LineSum(
                 ep, ne, held[a], line_in[i], ep_send.at[n_both + i], ep_recv.at[n_both + i]
@@ -408,22 +398,25 @@
 
 
 def reduce(ne, nd, pairs, lines, swaps, collective, us):
+    line_parts = tuple(where for _, where in lines)
+    line_shapes = [shape_at(v, where) if where else v.shape for v, where in lines]
+    lines = [v for v, _ in lines]
     arrays = [p[0] for p in pairs] + list(lines)
     extras = [p[3] for p in pairs if p[3] is not None]
     kinds = tuple((tuple(p[1]), p[2], p[3] is not None, p[4]) for p in pairs)
     shapes = [shape_at(p[0], p[2]) if p[2] else p[0].shape for p in pairs]
     boths = [s for s, p in zip(shapes, pairs) if p[4]]
     results = [s[2:] if p[4] else s[1:] for s, p in zip(shapes, pairs)]
-    results += [v.shape[1:] for v in lines]
-    scratch = shapes + [v.shape for v in lines]
+    results += [s[1:] for s in line_shapes]
+    scratch = shapes + line_shapes
     scratch += [s for s, p in zip(shapes, pairs) if p[3] is not None]
     scratch += [(s[0] - 1,) + s[1:] for s in shapes]
-    scratch += [(2,) + s[1:] for s in boths] + [(2,) + v.shape for v in lines]
+    scratch += [(2,) + s[1:] for s in boths] + [(2,) + s for s in line_shapes]
     some = lambda n: max(n, 1)
     line_count = some(len(lines) + len(boths))
     deep = max([s[0] - 1 for s in shapes] + [1])
     return pl.pallas_call(
-        functools.partial(reduce_body, ne, nd, kinds, len(lines), len(swaps)),
+        functools.partial(reduce_body, ne, nd, kinds, line_parts, len(swaps)),
         out_shape=[jax.ShapeDtypeStruct(s, BF16) for s in results]
         + [jax.ShapeDtypeStruct(v.shape, v.dtype) for v in swaps],
         in_specs=[ANY] * (len(arrays) + len(extras) + len(swaps)),
@@ -891,53 +884,53 @@
     )(dp.reshape(1), starts, queries, keys, values)
 
 
-def attend_back_body(span, nd, orders, *refs):
-    starts_ref, q_ref, k_ref, v_ref, log_ref, g_ref, cos_ref, sin_ref = refs[:8]
+def attend_back_body(span, ne, nd, orders, *refs):
+    refs = list(refs)
+
+    def take(n):
+        return [refs.pop(0) for _ in range(n)]
+
+    starts_ref, q_ref, k_ref, v_ref, log_ref, g_ref, cos_ref, sin_ref = take(8)
     n = len(orders)
-    sources, extras = refs[8 : 8 + n], refs[8 + n : 8 + 2 * n]
-    dq_ref, dk_ref, dv_ref = refs[8 + 2 * n : 11 + 2 * n]
-    outs, rest = refs[11 + 2 * n : 11 + 3 * n], refs[11 + 3 * n :]
-    dp = lax.axis_index("dp")
+    sources, extras, (mix_ref,) = take(n), take(n), take(1)
+    dq_ref, dk_ref, dv_ref = take(3)
+    outs, (mix_out,) = take(n), take(1)
+    held, more, landing, (mix_held, mix_in) = take(n), take(n), take(n), take(2)
+    load_sem, out_sem, send_sem, recv_sem, mix_sem, line_send, line_recv = refs
+    ep, dp = lax.axis_index("ep"), lax.axis_index("dp")
     step = pl.program_id(0) * pl.num_programs(1) + pl.program_id(1)
     final = pl.num_programs(0) * pl.num_programs(1) - 1
-    if n:
-        held, more, landing, (load_sem, out_sem, send_sem, recv_sem) = (
-            rest[:n],
-            rest[n : 2 * n],
-            rest[2 * n : 3 * n],
-            rest[3 * n :],
+    sums = []
+    for a in range(n):
+        part = pl.ds(1, sources[a].shape[1] - 1)
+        loads = [
+            pltpu.make_async_copy(src.at[:, part], dst, load_sem.at[a, i])
+            for i, (src, dst) in enumerate(((sources[a], held[a]), (extras[a], more[a])))
+        ]
+        sums.append(
+            PairSum(
+                dp, orders[a], loads, held[a], more[a], landing[a], send_sem.at[a], recv_sem.at[a]
+            )
         )
-        sums = [
-            PairSum(
-                dp,
-                orders[a],
-                (sources[a].at[:, 1:], extras[a].at[:, 1:]),
-                held[a],
-                more[a],
-                landing[a],
-                load_sem.at[a],
-                send_sem.at[a],
-                recv_sem.at[a],
-            )
-            for a in range(n)
-        ]
-
-        @pl.when(step == 0)
-        def _():
-            for each in sums:
-                each.load()
-            barrier = pltpu.get_barrier_semaphore()
-            met = sorted(set(b for order in orders for b in order))
-            for bit in met:
-                pl.semaphore_signal(
-                    barrier,
-                    inc=1,
-                    device_id={"dp": jnp.bitwise_xor(dp, 1 << bit)},
-                    device_id_type=MESH,
-                )
-            pl.semaphore_wait(barrier, len(met))
-            for each in sums:
-                each.step(0)
+    line = LineSum(ep, ne, mix_held, mix_in, line_send, line_recv)
+    mix_load = pltpu.make_async_copy(
+        mix_ref.at[:, pl.ds(0, mix_held.shape[1])], mix_held, mix_sem.at[0]
+    )
+
+    @pl.when(step == 0)
+    def _():
+        mix_load.start()
+        for each in sums:
+            each.load()
+        greet(ep, dp, ne, nd)
+        mix_load.wait()
+        line.step(0)
+        for each in sums:
+            each.step(0)
+
+    @pl.when(step == final // 2 + 1)
+    def _():
+        line.step(1)
 
     rows = q_ref.shape[0]
     q = spread(q_ref[...].astype(F32) * SCALE).astype(BF16)
@@ -960,50 +953,64 @@
     dv = dot(probs.astype(BF16), g, ((0,), (0,))).astype(BF16)
     dv_ref[here] = dv.reshape(span, rows, dv.shape[1])
 
-    if n:
-
-        @pl.when(step == final)
-        def _():
-            copies = []
-            for t in range(1, max(len(order) for order in orders) + 1):
-                for each in sums:
-                    each.step(t)
-            for a, each in enumerate(sums):
-                copies.append(pltpu.make_async_copy(each.own(), outs[a], out_sem.at[a]))
-                copies[a].start()
+    @pl.when(step == final)
+    def _():
+        for t in range(2, ne):
+            line.step(t)
+        for t in range(1, max([len(order) for order in orders] + [0]) + 1):
             for each in sums:
-                each.wait_sends()
-            for copy in copies:
-                copy.wait()
+                each.step(t)
+        copies = [pltpu.make_async_copy(line.own(), mix_out, mix_sem.at[1])]
+        for a, each in enumerate(sums):
+            copies.append(pltpu.make_async_copy(each.own(), outs[a], out_sem.at[a]))
+        for copy in copies:
+            copy.start()
+        for each in sums + [line]:
+            each.wait_sends()
+        for copy in copies:
+            copy.wait()
 
 
 def attend_back(
-    starts, queries, keys, values, logs_in, grad, cosine, sine, sums, micro, rows, nd, collective
+    starts, queries, keys, values, logs_in, grad, cosine, sine, sums, mix, micro, rows, collective
 ):
+    nd, ne = keys.shape[0], mix.shape[0]
     grid, mine, theirs, column, logs, _ = attention_specs(micro, rows, nd)
     table = pl.BlockSpec((rows, 128), lambda m, h, *_: (0, 0))
     n = len(sums)
     shapes = [(v.shape[0], v.shape[1] - 1) + v.shape[2:] for v, _, _ in sums]
     deep = max([s[0] - 1 for s in shapes] + [1])
-    scratch = [pltpu.VMEM(s, BF16) for s in shapes] * 2
-    scratch += [pltpu.VMEM((s[0] - 1,) + s[1:], BF16) for s in shapes]
-    scratch += [DMA((n, 2)), DMA((n,)), DMA((n, deep)), DMA((n, deep))] if n else []
-    remote_params = dict(collective_id=collective, has_side_effects=True) if n else {}
+    some = max(n, 1)
+    line = (ne, rows, mix.shape[2])
     return pl.pallas_call(
         functools.partial(
-            attend_back_body, nd // 2 + 1, nd, tuple(tuple(order) for _, order, _ in sums)
+            attend_back_body, nd // 2 + 1, ne, nd, tuple(tuple(order) for _, order, _ in sums)
         ),
         grid=grid,
-        in_specs=[column, mine, theirs, theirs, logs, mine, table, table] + [ANY] * (2 * n),
-        out_specs=[mine, theirs, theirs] + [ANY] * n,
+        in_specs=[column, mine, theirs, theirs, logs, mine, table, table] + [ANY] * (2 * n + 1),
+        out_specs=[mine, theirs, theirs] + [ANY] * (n + 1),
         out_shape=[
             jax.ShapeDtypeStruct(queries.shape, BF16),
             jax.ShapeDtypeStruct(keys.shape, BF16),
             jax.ShapeDtypeStruct(values.shape, BF16),
         ]
-        + [jax.ShapeDtypeStruct(s[1:], BF16) for s in shapes],
-        scratch_shapes=scratch,
-        compiler_params=pltpu.CompilerParams(vmem_limit_bytes=60 * 2**20, **remote_params),
+        + [jax.ShapeDtypeStruct(s[1:], BF16) for s in shapes]
+        + [jax.ShapeDtypeStruct(line[1:], BF16)],
+        scratch_shapes=[pltpu.VMEM(s, BF16) for s in shapes] * 2
+        + [pltpu.VMEM((s[0] - 1,) + s[1:], BF16) for s in shapes]
+        + [pltpu.VMEM(line, BF16), pltpu.VMEM((2,) + line, BF16)]
+        + [
+            DMA((some, 2)),
+            DMA((some,)),
+            DMA((some, deep)),
+            DMA((some, deep)),
+            DMA((2,)),
+            DMA((2, ne)),
+            DMA((2, ne)),
+        ],
+        compiler_params=pltpu.CompilerParams(
+            vmem_limit_bytes=60 * 2**20, collective_id=collective, has_side_effects=True
+        ),
         cost_estimate=cost(25),
     )(
         starts,
@@ -1016,75 +1023,186 @@
         sine,
         *[v for v, _, _ in sums],
         *[extra for _, _, extra in sums],
-    )
-
-
-def input_body(
-    ne,
-    nd,
-    n_ref,
-    dq_ref,
-    dk_ref,
-    dv_ref,
-    cos_ref,
-    sin_ref,
-    wq_ref,
-    wk_ref,
-    wv_ref,
-    tokens_ref,
-    gain_ref,
-    res_ref,
-    wq_out,
-    wk_out,
-    wv_out,
-    tok_out,
-    gain_out,
-    dk_turned,
-):
+        mix,
+    )
+
+
+def finish_body(ne, nd, orders, n_out, *refs):
+    refs = list(refs)
+
+    def take(n):
+        return [refs.pop(0) for _ in range(n)]
+
+    n_ref, dq_ref, dk_ref, dv_ref, cos_ref, sin_ref, tokens_ref, gain_ref = take(8)
+    res_ref, wq_ref, wk_ref, wv_ref, wo_ref, small_ref = take(6)
+    (tok_out,) = take(1)
+    count = 2 * n_out + 3
+    outs, held, pair_in, line_in = take(count), take(count), take(count), take(count)
+    dk_turned, wq, wk, wv, res = take(5)
+    load_sem, own_sem, out_sem, dp_send, dp_recv, ep_send, ep_recv = refs
+    ep, dp = lax.axis_index("ep"), lax.axis_index("dp")
+    columns = held[0].shape[3]
+    own = [
+        pltpu.make_async_copy(src, dst, own_sem.at[i])
+        for i, (src, dst) in enumerate(
+            ((wq_ref, wq), (wk_ref, wk), (wv_ref, wv), (res_ref, res))
+        )
+    ]
+    sums = []
+    for a in range(count):
+        loads = []
+        if a < n_out or a == count - 1:
+            src = wo_ref if a < n_out else small_ref
+            at = pl.ds(a * columns if a < n_out else 0, held[a].shape[3])
+            loads = [
+                pltpu.make_async_copy(src.at[e, :, :, at], held[a].at[:, e], load_sem.at[a, e])
+                for e in range(ne)
+            ]
+        sums.append(
+            PairSum(
+                dp, orders[a % 2], loads, held[a], None, pair_in[a], dp_send.at[a], dp_recv.at[a]
+            )
+        )
+    lines = [
+        LineSum(ep, ne, sums[a].own(), line_in[a], ep_send.at[a], ep_recv.at[a])
+        for a in range(count)
+    ]
+    early, made, small = sums[:n_out], sums[n_out:-1], sums[-1]
+    for each in early + [small]:
+        each.load()
+    for copy in own:
+        copy.start()
+    greet(ep, dp, ne, nd)
+    for each in early:
+        each.step(0)
+
     normed = n_ref[...]
     cosine, sine = cos_ref[...], -sin_ref[...]
     for i in range(0, dk_ref.shape[1], 128):
         part = dk_ref[:, i : i + 128].astype(F32)
         dk_turned[:, i : i + 128] = turn(part, cosine, sine).astype(BF16)
     tile = 256
-    for grad, out in ((dq_ref, wq_out), (dk_turned, wk_out), (dv_ref, wv_out)):
-        share = out.shape[1] // ne
-        for c in range(0, grad.shape[1], tile):
-            y = dot(normed, grad[:, c : c + tile], ((0,), (0,))).astype(BF16)
+
+    def product(grad, first, each):
+        share = each.held.shape[2]
+        for c in range(0, each.held.shape[3], tile):
+            y = dot(normed, grad[:, first + c : first + c + tile], ((0,), (0,))).astype(BF16)
             for e in range(ne):
                 for d in range(nd):
                     r = (e * nd + d) * share
-                    out[d, e * share : (e + 1) * share, c : c + tile] = y[r : r + share]
+                    each.held[d, e, :, c : c + tile] = y[r : r + share]
+        each.step(0)
+
+    turns = bit_count(nd)
+    for i, each in enumerate(made):
+        if i < n_out:
+            product(dq_ref, i * columns, each)
+        else:
+            product((dk_turned, dv_ref)[i - n_out], 0, each)
+        if i == 1:
+            for first in early:
+                first.step(1)
+    for copy in own:
+        copy.wait()
     back = (
-        dot(dq_ref[...], wq_ref[...], ((1,), (1,)))
-        + dot(dk_turned[...], wk_ref[...], ((1,), (1,)))
-        + dot(dv_ref[...], wv_ref[...], ((1,), (1,)))
-    )
+        dot(dq_ref[...], wq[...], ((1,), (1,)))
+        + dot(dk_turned[...], wk[...], ((1,), (1,)))
+        + dot(dv_ref[...], wv[...], ((1,), (1,)))
+    )
+    for each in made:
+        each.step(1)
+    for each in early:
+        each.step(2)
     x = tokens_ref[...].astype(F32)
     r = rms_scale(x)
     scaled = back * gain_ref[...]
-    gain_out[...] = jnp.sum(back * x * r, axis=0, keepdims=True)
     tok_out[...] = (
-        res_ref[...] + r * scaled - x * (r * r * r) * jnp.mean(scaled * x, axis=1, keepdims=True)
-    )
-
-
-def input_grads(ne, nd, normed, dq, dk, dv, cosine, sine, weights, tokens, gain, grad_residual):
+        res[...] + r * scaled - x * (r * r * r) * jnp.mean(scaled * x, axis=1, keepdims=True)
+    )
+    term = back * x * r
+    high = term.astype(BF16)
+    low = (term - high.astype(F32)).astype(BF16)
+    ones = jnp.ones((x.shape[0], 128), BF16)
+    column = dot(high, ones, ((0,), (0,))) + dot(low, ones, ((0,), (0,)))
+    lane = lax.broadcasted_iota(jnp.int32, column.shape, 1)
+    column = jnp.where(lane == EXPERTS, column, 0.0)
+    for copy in small.loads:
+        copy.wait()
+    share = held[-1].shape[2]
+    for e in range(ne):
+        for d in range(nd):
+            i = (e * nd + d) * share
+            held[-1][d, e] = (held[-1][d, e].astype(F32) + column[i : i + share]).astype(BF16)
+    small.loads = []
+    small.step(0)
+    small.step(1)
+    for t in range(2, turns + 1):
+        for each in early:
+            if t > 2:
+                each.step(t)
+        for each in made + [small]:
+            each.step(t)
+    order = list(range(count))
+    for t in range(ne):
+        for a in order:
+            lines[a].step(t)
+    copies = []
+    for a in order:
+        copies.append(pltpu.make_async_copy(lines[a].own(), outs[a], out_sem.at[a]))
+        copies[-1].start()
+    for each in sums + lines:
+        each.wait_sends()
+    for copy in copies:
+        copy.wait()
+
+
+def finish(
+    ne, nd, orders, normed, grads, cosine, sine, tokens, gain, grad_residual, weights, w_out, small
+):
     rows, width = tokens.shape
     share = width // (ne * nd)
+    columns = weights[1].shape[1]
+    n_out = width // columns
+    count = 2 * n_out + 3
+    wide = [columns] * (count - 1) + [128]
+    split = lambda v: v.reshape(ne, nd, share, v.shape[1])
     return pl.pallas_call(
-        functools.partial(input_body, ne, nd),
-        out_shape=[jax.ShapeDtypeStruct((nd, ne * share, w.shape[1]), BF16) for w in weights]
+        functools.partial(finish_body, ne, nd, tuple(map(tuple, orders)), n_out),
+        out_shape=[jax.ShapeDtypeStruct((rows, width), F32)]
+        + [jax.ShapeDtypeStruct((share, c), BF16) for c in wide],
+        in_specs=[VMEM] * 8 + [ANY] * 6,
+        out_specs=[VMEM] + [ANY] * count,
+        scratch_shapes=[pltpu.VMEM((nd, ne, share, c), BF16) for c in wide]
+        + [pltpu.VMEM((nd - 1, ne, share, c), BF16) for c in wide]
+        + [pltpu.VMEM((2, ne, share, c), BF16) for c in wide]
+        + [pltpu.VMEM(grads[1].shape, BF16)]
+        + [pltpu.VMEM(w.shape, BF16) for w in weights]
+        + [pltpu.VMEM((rows, width), F32)]
         + [
-            jax.ShapeDtypeStruct((rows, width), F32),
-            jax.ShapeDtypeStruct((1, width), F32),
+            DMA((count, ne)),
+            DMA((4,)),
+            DMA((count,)),
+            DMA((count, nd - 1)),
+            DMA((count, nd - 1)),
+            DMA((count, 2, ne)),
+            DMA((count, 2, ne)),
         ],
-        in_specs=[VMEM] * 12,
-        out_specs=[VMEM] * 5,
-        scratch_shapes=[pltpu.VMEM(dk.shape, BF16)],
-        compiler_params=pltpu.CompilerParams(vmem_limit_bytes=60 * 2**20),
-        cost_estimate=cost(10),
-    )(normed, dq, dk, dv, cosine, sine, *weights, tokens, gain, grad_residual)
+        compiler_params=pltpu.CompilerParams(
+            vmem_limit_bytes=60 * 2**20, collective_id=4, has_side_effects=True
+        ),
+        cost_estimate=cost(45),
+    )(
+        normed,
+        *grads,
+        cosine,
+        sine,
+        tokens,
+        gain,
+        grad_residual,
+        *weights,
+        split(w_out),
+        split(small),
+    )
 
 
 def per_device(
@@ -1188,7 +1306,7 @@
         nd,
         [(last[i], orders[i], None, None, False) for i in range(2)]
         + [(kept[i], orders[i][1:], head, landed[i], False) for i in range(2)],
-        (grad_in.reshape(ne, every, width),),
+        ((grad_in.reshape(ne, every, width), None),),
         (pair_dots,),
         2,
         40,
@@ -1218,7 +1336,8 @@
         BF16
     )
     more = kept[0].shape[1] > 1
-    grad_query, grad_key_all, grad_value_all, *grads_more = attend_back(
+    mix = mix.reshape(ne, every, width)
+    grad_query, grad_key_all, grad_value_all, *grads_more, mix_first = attend_back(
         starts,
         query_rot,
         key_all,
@@ -1228,34 +1347,25 @@
         cosine,
         sine,
         [(kept[i], orders[i][1:], landed[i]) for i in range(2)] if more else [],
+        mix,
         micro,
         rows,
-        nd,
         5,
     )
-
-    def by_owner(grad):
-        share = grad.shape[0] // (ne * nd)
-        return grad.astype(BF16).reshape(ne, nd, share, grad.shape[1]).transpose(1, 0, 2, 3)
-
     full = [[0] + order for order in orders]
-    grad_w_out = by_owner(grad_w_out)
-    columns = [(slice(None),) * 3 + (slice(i * kv_width, (i + 1) * kv_width),) for i in range(2)]
-    grad_key, grad_value, *d_out = reduce(
+    grad_key, grad_value, mix_rest = reduce(
         ne,
         nd,
         [
             (grad_key_all, full[0], None, None, False),
             (grad_value_all, full[1], None, None, False),
-            (grad_w_out, full[0], columns[0], None, True),
-            (grad_w_out, full[1], columns[1], None, True),
         ],
-        (),
+        ((mix, (slice(None), slice(rows, every))),),
         (),
         3,
-        35,
-    )
-    d_out = jnp.concatenate(d_out, axis=1).astype(F32)
+        30,
+    )
+    mix_own = jnp.concatenate([mix_first, mix_rest], axis=0)
 
     per_path = [
         jnp.concatenate(
@@ -1274,49 +1384,34 @@
         ],
         axis=2,
     )
-    grad_w_query, grad_w_key, grad_w_value, grad_tokens, grad_gain_one = input_grads(
-        ne,
-        nd,
-        normed_one,
-        grad_query,
-        grad_key,
-        grad_value,
-        cosine,
-        sine,
-        (w_query, w_key, w_value),
-        tokens_flat,
-        gain_one,
-        grad_residual,
-    )
-
     small = jnp.concatenate(
         [
             grad_w_router,
-            grad_gain_one.reshape(width, 1),
+            jnp.zeros((width, 1), F32),
             grad_gain_two[:, None],
             jnp.zeros((width, 128 - EXPERTS - 2), F32),
         ],
         axis=1,
-    )
-
-    def blocks_of(grad):
-        return grad.reshape(nd, ne, -1, grad.shape[2])
-
-    *dense, mix_own = reduce(
+    ).astype(BF16)
+    grad_tokens, *dense = finish(
         ne,
         nd,
-        [
-            (blocks_of(grad_w_query), full[0], None, None, True),
-            (blocks_of(grad_w_key), full[1], None, None, True),
-            (blocks_of(grad_w_value), full[1], None, None, True),
-            (by_owner(small), full[0], None, None, True),
-        ],
-        (mix.reshape(ne, every, width),),
-        (),
-        4,
-        50,
-    )
-    d_query, d_key, d_value, d_small = (v.astype(F32) for v in dense)
+        full,
+        normed_one,
+        (grad_query, grad_key, grad_value),
+        cosine,
+        sine,
+        tokens_flat,
+        gain_one,
+        grad_residual,
+        (w_query, w_key, w_value),
+        grad_w_out.astype(BF16),
+        small,
+    )
+    n_out = width // kv_width
+    d_out = jnp.concatenate(dense[:n_out], axis=1).astype(F32)
+    d_query = jnp.concatenate(dense[n_out : 2 * n_out], axis=1).astype(F32)
+    d_key, d_value, d_small = (v.astype(F32) for v in dense[2 * n_out :])
     output = (residual + mix_own.astype(F32)).astype(BF16).reshape(tokens.shape)
     return (
         output,

time: 384 us -> 364 us (0.948)
  Pallas kernels: 333 us -> 321 us
    pallas_call x5 -> x4, Pallas kernels: 167 us -> 155 us  [the longest x2 73.5 us: reduce(): pl.pallas_call(functools.partial(reduce_body, ne, nd, kinds, line_parts,...]
  transfers between devices with their start and end apart: 3 -> 3, of which waited for: 0 -> 0; matrix products, arithmetic and copies ran while one was open for 3% -> 3% of each run, Pallas kernels for 22% -> 23%
where the time goes in v7:
time: 364 us; the launch traced here: 363 us
  Pallas kernels  321 us (88%)
  other arithmetic  13.8 us (4%)
  local copies, waits for them, and re-layouts  12.9 us (4%)
  matrix products  8.98 us (2%)
  starting transfers between devices  5.57 us (2%)
    pallas_call x1, Pallas kernels, experts(): pl.pallas_call(functools.partial(expert_body, ne, nd, micro, rows), grid=...  84.2 us
    pallas_call x2, Pallas kernels, reduce(): pl.pallas_call(functools.partial(reduce_body, ne, nd, kinds, line_parts,...  73.5 us
    pallas_call x2, Pallas kernels, gather(): pl.pallas_call(functools.partial(gather_body, ne, nd, len(dp_arrays), len...  64.8 us
    pallas_call x1, Pallas kernels, finish(): pl.pallas_call(functools.partial(finish_body, ne, nd, tuple(map(tuple, or...  54.5 us
    pallas_call x1, Pallas kernels, attend_back(): pl.pallas_call(functools.partial(attend_back_body, nd // 2 + 1, ne, nd, t...  26.7 us
    pallas_call x1, Pallas kernels, attend(): pl.pallas_call(functools.partial(attend_body, nd // 2 + 1), grid_spec=plt...  11.5 us
  transfers between devices with their start and end apart: 3, of which 0 were waited for; matrix products, arithmetic and copies ran while one was open for 3% of the time, Pallas kernels for 23%

profile of v7, /device:TPU:10, one launch (start us, length us, event | category | flops | bytes accessed | tf_op | source)
XLA Modules:
  0.0 362.9 jit_solution(15402367751304054454)
XLA Ops:
  1.2 2.6 collective-permute-start.1
  3.8 2.5 collective-permute-start
  10.3 5.4 %shard_map.229 = (bf16[256,1024]{1,0:T(8,128)(2,1)}, bf16[256,1024]{1,0:T(8,128)(2,1)}, bf16[256,512]{1,0:T(8,128)(2,1)}, bf16[256,512]{1,0:T(8,128)(2,1)}) custom-call(bf16[256,1024]{1,0:T(8,128)(2,1)} %bitcast.81, f32[1,1024]{1,0:T(1,128)} %bitcast.101, f32[256,128]{1,0:T(8,128)} %copy.39.cos_ref.refs_6_.refs_4_, ...), custom_call_target="tpu_custom_call" | custom-call | bytes 15000000 | tf_op jit(solution)/shard_map/pallas_call | solution.py:786
  15.7 23.0 %shard_map.230 = (bf16[8,256,512]{2,1,0:T(8,128)(2,1)}, bf16[8,256,512]{2,1,0:T(8,128)(2,1)}, f32[8,8,128]{2,1,0:T(8,128)}) custom-call(bf16[256,512]{1,0:T(8,128)(2,1)} %get-tuple-element.55.refs_0_, bf16[256,512]{1,0:T(8,128)(2,1)} %get-tuple-element.56.refs_1_, f32[8,128]{1,0:T(8,128)} %concatenate.33.refs_2_), custom_call_target="tpu_custom_call" | custom-call | bytes 75000000 | tf_op jit(solution)/shard_map/pallas_call | solution.py:166
  40.5 11.5 %shard_map.231 = (bf16[256,1024]{1,0:T(8,128)(2,1)}, f32[2,4,512,1]{3,2,1,0:T(8,128)}) custom-call(s32[1]{0:T(128)} %bitcast.1.dp_ref, s32[256,1]{1,0:T(8,128)} %copy.40.starts_ref.refs_0_, bf16[256,1024]{1,0:T(8,128)(2,1)} %get-tuple-element.58.q_ref.refs_1_, bf16[8,256,512]{2,1,0:T(8,128)(2,1)} %get-tuple-element.59.k_ref.refs_2_, ...), custom_call_target="tpu_custom_call" | custom-call | bytes 45000000 | tf_op jit(solution)/shard_map/pallas_call | solution.py:873
  52.0 1.9 multiply_reduce_fusion.2
  55.0 41.8 %shard_map.232 = (bf16[4,256,1024]{2,1,0:T(8,128)(2,1)}, f32[4,32,256]{2,1,0:T(8,128)}) custom-call(bf16[256,1024]{1,0:T(8,128)(2,1)} %copy-done.5, f32[32,256]{1,0:T(8,128)} %fusion.9.refs_1_), custom_call_target="tpu_custom_call" | custom-call | bytes 114000000 | tf_op jit(solution)/shard_map/pallas_call | solution.py:166
  98.2 84.2 %shard_map.233 = (bf16[1024,1024]{1,0:T(8,128)(2,1)}, bf16[1024,1024]{1,0:T(8,128)(2,1)}, f32[8,8,128]{2,1,0:T(8,128)}, bf16[2,3,384,512]{3,2,1,0:T(8,128)(2,1)}...) custom-call(bf16[256,1024]{1,0:T(8,128)(2,1)} %bitcast.87, ...), custom_call_target="tpu_custom_call" | custom-call | bytes 225000000 | tf_op jit(solution)/shard_map/pallas_call | solution.py:693
  183.9 44.4 %shard_map.234 = (bf16[384,512]{1,0:T(8,128)(2,1)}, bf16[384,512]{1,0:T(8,128)(2,1)}, bf16[1,384,512]{2,1,0:T(8,128)(2,1)}, bf16[1,384,512]{2,1,0:T(8,128)(2,1)}...) custom-call(bf16[4,384,512]{2,1,0:T(8,128)(2,1)} %get-tuple-element.65.refs_0_, ...), custom_call_target="tpu_custom_call" | custom-call | bytes 120000000 | tf_op jit(solution)/shard_map/pallas_call | solution.py:418
  229.2 1.1 convolution_convert_fusion.2
  230.3 2.0 multiply_reduce_fusion
  232.8 1.2 copy-done.4
  233.9 1.6 convolution_convert_fusion.1.refs_5_
  235.6 2.1 convolution_convert_fusion
  238.3 26.7 %shard_map.235 = (bf16[256,1024]{1,0:T(8,128)(2,1)}, bf16[8,256,512]{2,1,0:T(8,128)(2,1)}, bf16[8,256,512]{2,1,0:T(8,128)(2,1)}, bf16[2,384,512]{2,1,0:T(8,128)(...) custom-call(s32[256,1]{1,0:T(8,128)} %copy.40.starts_ref.refs_0_, ...), custom_call_target="tpu_custom_call" | custom-call | bytes 75000000 | tf_op jit(solution)/shard_map/pallas_call | solution.py:985
  265.0 29.1 %shard_map.236 = (bf16[256,512]{1,0:T(8,128)(2,1)}, bf16[256,512]{1,0:T(8,128)(2,1)}, bf16[128,1024]{1,0:T(8,128)(2,1)}) custom-call(bf16[8,256,512]{2,1,0:T(8,128)(2,1)} %get-tuple-element.77.refs_0_, bf16[8,256,512]{2,1,0:T(8,128)(2,1)} %get-tuple-element.78.refs_1_, bf16[4,256,1024]{2,1,0:T(8,128)(2,1)} %bitcast.79), custom_call_target="tpu_custom_call" | custom-call | bytes 90000000 | tf_op jit(solution)/shard_map/pallas_call | solution.py:418
  294.1 0.9 maximum_maximum_fusion.refs_13_
  295.0 54.5 %shard_map.237 = (f32[256,1024]{1,0:T(8,128)}, bf16[32,512]{1,0:T(8,128)(2,1)}, bf16[32,512]{1,0:T(8,128)(2,1)}, bf16[32,512]{1,0:T(8,128)(2,1)}, bf16[32,512]{1...) custom-call(bf16[256,1024]{1,0:T(8,128)(2,1)} %get-tuple-element.80.refs_0_, ...), custom_call_target="tpu_custom_call" | custom-call | bytes 135000000 | tf_op jit(solution)/shard_map/pallas_call | solution.py:1169
  349.5 1.3 slice.42
  351.6 1.4 maximum_bitcast_fusion
  354.3 2.5 fusion.19
  358.7 0.9 add_convert_fusion
  359.7 1.5 pad_maximum_fusion
  361.9 1.0 copy.57
  (100 shorter events, 16.9 us)
Async XLA Ops:
  0.6 53.4 %copy-start = (bf16[1024,32]{0,1:T(8,128)(2,1)S(1)}, bf16[1024,32]{0,1:T(8,128)(2,1)}, u32[]{:S(2)}) copy-start(bf16[1024,32]{0,1:T(8,128)(2,1)} %param.23) | copy-start | bytes 196612
  0.7 97.5 %collective-permute-start.2 = (bf16[256,1024]{1,0:T(8,128)(2,1)}, bf16[256,1024]{1,0:T(8,128)(2,1)}, u32[]{:S(2)}, u32[]{:S(2)}) collective-permute-start(bf16[256,1024]{1,0:T(8,128)(2,1)} %bitcast.84), channel_id=1, source_target_pairs={{0,24},{8,0},{16,8},{24,16},{1,25},{9,1},{17,9},{25,17},{2,26},{10... | collective-permute-start | bytes 1572872 | tf_op jit(solution)/shard_map/ppermute | solution.py:1255
  1.2 97.0 %collective-permute-start.1 = (bf16[256,1024]{1,0:T(8,128)(2,1)}, bf16[256,1024]{1,0:T(8,128)(2,1)}, u32[]{:S(2)}, u32[]{:S(2)}) collective-permute-start(bf16[256,1024]{1,0:T(8,128)(2,1)} %bitcast.85), channel_id=1, source_target_pairs={{0,16},{8,24},{16,0},{24,8},{1,17},{9,25},{17,1},{25,9},{2,18},{10... | collective-permute-start | bytes 1572872 | tf_op jit(solution)/shard_map/ppermute | solution.py:1255
  3.8 94.5 %collective-permute-start = (bf16[256,1024]{1,0:T(8,128)(2,1)}, bf16[256,1024]{1,0:T(8,128)(2,1)}, u32[]{:S(2)}, u32[]{:S(2)}) collective-permute-start(bf16[256,1024]{1,0:T(8,128)(2,1)} %bitcast.86), channel_id=1, source_target_pairs={{0,8},{8,16},{16,24},{24,0},{1,9},{9,17},{17,25},{25,1},{2,10},{10... | collective-permute-start | bytes 1572872 | tf_op jit(solution)/shard_map/ppermute | solution.py:1255
  10.3 29.2 %copy-start.26 = (s32[2,1,128]{2,1,0:T(1,128)S(1)}, s32[2,1,128]{2,1,0:T(1,128)}, u32[]{:S(2)}) copy-start(s32[2,1,128]{2,1,0:T(1,128)} %param.15) | copy-start | bytes 3076
  40.5 11.5 %copy-start.3 = (bf16[1024,1024]{1,0:T(8,128)(2,1)S(1)}, bf16[1024,1024]{1,0:T(8,128)(2,1)}, u32[]{:S(2)}) copy-start(bf16[1024,1024]{1,0:T(8,128)(2,1)} %param.21) | copy-start | bytes 6291460
  40.5 11.5 %copy-start.7 = (bf16[2,128,1024]{2,1,0:T(8,128)(2,1)S(1)}, bf16[2,128,1024]{2,1,0:T(8,128)(2,1)}, u32[]{:S(2)}) copy-start(bf16[2,128,1024]{2,1,0:T(8,128)(2,1)} %param.14) | copy-start | bytes 1572868
  52.0 1.9 copy-start.19
  183.9 45.3 %copy-start.6 = (bf16[256,1024]{1,0:T(8,128)(2,1)S(1)}, bf16[256,1024]{1,0:T(8,128)(2,1)}, u32[]{:S(2)}) copy-start(bf16[256,1024]{1,0:T(8,128)(2,1)} %copy-done.5) | copy-start | bytes 1572868
  228.3 4.1 %copy-start.8 = (bf16[2,128,1024]{2,1,0:T(8,128)(2,1)S(1)}, bf16[2,128,1024]{2,1,0:T(8,128)(2,1)}, u32[]{:S(2)}) copy-start(bf16[2,128,1024]{2,1,0:T(8,128)(2,1)} %param.27) | copy-start | bytes 1572868
  228.3 4.1 %copy-start.10 = (bf16[256,1024]{1,0:T(8,128)(2,1)S(1)}, bf16[256,1024]{1,0:T(8,128)(2,1)}, u32[]{:S(2)}) copy-start(bf16[256,1024]{1,0:T(8,128)(2,1)} %get-tuple-element.74) | copy-start | bytes 1572868
  233.9 3.7 %copy-start.2 = (f32[256,1024]{1,0:T(8,128)}, f32[256,1024]{1,0:T(8,128)S(1)}, u32[]{:S(2)}) copy-start(f32[256,1024]{1,0:T(8,128)S(1)} %multiply_subtract_fusion.refs_8_) | copy-start | bytes 3145732
  233.9 1.6 copy-start.9
  295.0 56.5 %copy-start.12 = (bf16[2,384,512]{2,1,0:T(8,128)(2,1)S(1)}, bf16[2,384,512]{2,1,0:T(8,128)(2,1)}, u32[]{:S(2)}) copy-start(bf16[2,384,512]{2,1,0:T(8,128)(2,1)} %get-tuple-element.93) | copy-start | bytes 2359300
  295.0 56.5 %copy-start.13 = (bf16[2,384,512]{2,1,0:T(8,128)(2,1)S(1)}, bf16[2,384,512]{2,1,0:T(8,128)(2,1)}, u32[]{:S(2)}) copy-start(bf16[2,384,512]{2,1,0:T(8,128)(2,1)} %get-tuple-element.96) | copy-start | bytes 2359300
  295.0 56.5 %copy-start.14 = (bf16[384,512]{1,0:T(8,128)(2,1)S(1)}, bf16[384,512]{1,0:T(8,128)(2,1)}, u32[]{:S(2)}) copy-start(bf16[384,512]{1,0:T(8,128)(2,1)} %get-tuple-element.94) | copy-start | bytes 1179652
  295.0 56.5 %copy-start.15 = (bf16[384,512]{1,0:T(8,128)(2,1)S(1)}, bf16[384,512]{1,0:T(8,128)(2,1)}, u32[]{:S(2)}) copy-start(bf16[384,512]{1,0:T(8,128)(2,1)} %get-tuple-element.97) | copy-start | bytes 1179652
  295.0 56.6 %copy-start.16 = (bf16[1,384,512]{2,1,0:T(8,128)(2,1)S(1)}, bf16[1,384,512]{2,1,0:T(8,128)(2,1)}, u32[]{:S(2)}) copy-start(bf16[1,384,512]{2,1,0:T(8,128)(2,1)} %get-tuple-element.92) | copy-start | bytes 1179652
  354.2 3.2 copy-start.25
  354.2 3.8 %copy-start.24 = (bf16[32,512]{1,0:T(8,128)(2,1)S(1)}, bf16[32,512]{1,0:T(8,128)(2,1)}, u32[]{:S(2)}) copy-start(bf16[32,512]{1,0:T(8,128)(2,1)} %get-tuple-element.89) | copy-start | bytes 98308
  354.3 4.5 %copy-start.17 = (bf16[128,1024]{1,0:T(8,128)(2,1)S(1)}, bf16[128,1024]{1,0:T(8,128)(2,1)}, u32[]{:S(2)}) copy-start(bf16[128,1024]{1,0:T(8,128)(2,1)} %get-tuple-element.76) | copy-start | bytes 786436
  354.3 4.4 %copy-start.18 = (bf16[128,1024]{1,0:T(8,128)(2,1)S(1)}, bf16[128,1024]{1,0:T(8,128)(2,1)}, u32[]{:S(2)}) copy-start(bf16[128,1024]{1,0:T(8,128)(2,1)} %get-tuple-element.79) | copy-start | bytes 786436
  359.7 2.3 copy-start.11
  359.7 3.2 copy-start.1
  (6 other events, 8.7 us)

commit v8 on v7

--- a/solution.py
+++ b/solution.py
@@ -892,11 +892,11 @@
 
     starts_ref, q_ref, k_ref, v_ref, log_ref, g_ref, cos_ref, sin_ref = take(8)
     n = len(orders)
-    sources, extras, (mix_ref,) = take(n), take(n), take(1)
+    sources, extras = take(n), take(n)
     dq_ref, dk_ref, dv_ref = take(3)
-    outs, (mix_out,) = take(n), take(1)
-    held, more, landing, (mix_held, mix_in) = take(n), take(n), take(n), take(2)
-    load_sem, out_sem, send_sem, recv_sem, mix_sem, line_send, line_recv = refs
+    outs = take(n)
+    held, more, landing = take(n), take(n), take(n)
+    load_sem, out_sem, send_sem, recv_sem = refs
     ep, dp = lax.axis_index("ep"), lax.axis_index("dp")
     step = pl.program_id(0) * pl.num_programs(1) + pl.program_id(1)
     final = pl.num_programs(0) * pl.num_programs(1) - 1
@@ -912,25 +912,13 @@
                 dp, orders[a], loads, held[a], more[a], landing[a], send_sem.at[a], recv_sem.at[a]
             )
         )
-    line = LineSum(ep, ne, mix_held, mix_in, line_send, line_recv)
-    mix_load = pltpu.make_async_copy(
-        mix_ref.at[:, pl.ds(0, mix_held.shape[1])], mix_held, mix_sem.at[0]
-    )
-
     @pl.when(step == 0)
     def _():
-        mix_load.start()
         for each in sums:
             each.load()
         greet(ep, dp, ne, nd)
-        mix_load.wait()
-        line.step(0)
         for each in sums:
             each.step(0)
-
-    @pl.when(step == final // 2 + 1)
-    def _():
-        line.step(1)
 
     rows = q_ref.shape[0]
     q = spread(q_ref[...].astype(F32) * SCALE).astype(BF16)
@@ -955,59 +943,46 @@
 
     @pl.when(step == final)
     def _():
-        for t in range(2, ne):
-            line.step(t)
         for t in range(1, max([len(order) for order in orders] + [0]) + 1):
             for each in sums:
                 each.step(t)
-        copies = [pltpu.make_async_copy(line.own(), mix_out, mix_sem.at[1])]
-        for a, each in enumerate(sums):
-            copies.append(pltpu.make_async_copy(each.own(), outs[a], out_sem.at[a]))
+        copies = [
+            pltpu.make_async_copy(each.own(), outs[a], out_sem.at[a]) for a, each in enumerate(sums)
+        ]
         for copy in copies:
             copy.start()
-        for each in sums + [line]:
+        for each in sums:
             each.wait_sends()
         for copy in copies:
             copy.wait()
 
 
 def attend_back(
-    starts, queries, keys, values, logs_in, grad, cosine, sine, sums, mix, micro, rows, collective
+    starts, queries, keys, values, logs_in, grad, cosine, sine, sums, micro, rows, ne, collective
 ):
-    nd, ne = keys.shape[0], mix.shape[0]
+    nd = keys.shape[0]
     grid, mine, theirs, column, logs, _ = attention_specs(micro, rows, nd)
     table = pl.BlockSpec((rows, 128), lambda m, h, *_: (0, 0))
     n = len(sums)
     shapes = [(v.shape[0], v.shape[1] - 1) + v.shape[2:] for v, _, _ in sums]
     deep = max([s[0] - 1 for s in shapes] + [1])
     some = max(n, 1)
-    line = (ne, rows, mix.shape[2])
     return pl.pallas_call(
         functools.partial(
             attend_back_body, nd // 2 + 1, ne, nd, tuple(tuple(order) for _, order, _ in sums)
         ),
         grid=grid,
-        in_specs=[column, mine, theirs, theirs, logs, mine, table, table] + [ANY] * (2 * n + 1),
-        out_specs=[mine, theirs, theirs] + [ANY] * (n + 1),
+        in_specs=[column, mine, theirs, theirs, logs, mine, table, table] + [ANY] * (2 * n),
+        out_specs=[mine, theirs, theirs] + [ANY] * n,
         out_shape=[
             jax.ShapeDtypeStruct(queries.shape, BF16),
             jax.ShapeDtypeStruct(keys.shape, BF16),
             jax.ShapeDtypeStruct(values.shape, BF16),
         ]
-        + [jax.ShapeDtypeStruct(s[1:], BF16) for s in shapes]
-        + [jax.ShapeDtypeStruct(line[1:], BF16)],
+        + [jax.ShapeDtypeStruct(s[1:], BF16) for s in shapes],
         scratch_shapes=[pltpu.VMEM(s, BF16) for s in shapes] * 2
         + [pltpu.VMEM((s[0] - 1,) + s[1:], BF16) for s in shapes]
-        + [pltpu.VMEM(line, BF16), pltpu.VMEM((2,) + line, BF16)]
-        + [
-            DMA((some, 2)),
-            DMA((some,)),
-            DMA((some, deep)),
-            DMA((some, deep)),
-            DMA((2,)),
-            DMA((2, ne)),
-            DMA((2, ne)),
-        ],
+        + [DMA((some, 2)), DMA((some,)), DMA((some, deep)), DMA((some, deep))],
         compiler_params=pltpu.CompilerParams(
             vmem_limit_bytes=60 * 2**20, collective_id=collective, has_side_effects=True
         ),
@@ -1023,7 +998,6 @@
         sine,
         *[v for v, _, _ in sums],
         *[extra for _, _, extra in sums],
-        mix,
     )
 
 
@@ -1034,11 +1008,12 @@
         return [refs.pop(0) for _ in range(n)]
 
     n_ref, dq_ref, dk_ref, dv_ref, cos_ref, sin_ref, tokens_ref, gain_ref = take(8)
-    res_ref, wq_ref, wk_ref, wv_ref, wo_ref, small_ref = take(6)
+    res_ref, wq_ref, wk_ref, wv_ref, wo_ref, small_ref, mix_ref = take(7)
     (tok_out,) = take(1)
     count = 2 * n_out + 3
-    outs, held, pair_in, line_in = take(count), take(count), take(count), take(count)
-    dk_turned, wq, wk, wv, res = take(5)
+    outs, (mix_out,) = take(count), take(1)
+    held, pair_in, line_in = take(count), take(count), take(count)
+    dk_turned, wq, wk, wv, res, mix_held, mix_in = take(7)
     load_sem, own_sem, out_sem, dp_send, dp_recv, ep_send, ep_recv = refs
     ep, dp = lax.axis_index("ep"), lax.axis_index("dp")
     columns = held[0].shape[3]
@@ -1068,13 +1043,35 @@
         for a in range(count)
     ]
     early, made, small = sums[:n_out], sums[n_out:-1], sums[-1]
-    for each in early + [small]:
+    queries, others = made[:n_out], made[n_out:]
+    mix = LineSum(ep, ne, mix_held, mix_in, ep_send.at[count], ep_recv.at[count])
+    mix_load = pltpu.make_async_copy(
+        mix_ref.at[:, pl.ds(mix_ref.shape[1] - mix_held.shape[1], mix_held.shape[1])],
+        mix_held,
+        own_sem.at[4],
+    )
+    for each in early:
         each.load()
+    mix_load.start()
     for copy in own:
         copy.start()
+    small.load()
     greet(ep, dp, ne, nd)
-    for each in early:
-        each.step(0)
+    turns = bit_count(nd)
+
+    def steps(group, t):
+        for each in group:
+            if t <= turns:
+                each.step(t)
+
+    def line_steps(group, t):
+        for each in group:
+            if t < ne:
+                lines[sums.index(each)].step(t)
+
+    steps(early, 0)
+    mix_load.wait()
+    mix.step(0)
 
     normed = n_ref[...]
     cosine, sine = cos_ref[...], -sin_ref[...]
@@ -1093,26 +1090,23 @@
                     each.held[d, e, :, c : c + tile] = y[r : r + share]
         each.step(0)
 
-    turns = bit_count(nd)
     for i, each in enumerate(made):
         if i < n_out:
             product(dq_ref, i * columns, each)
         else:
             product((dk_turned, dv_ref)[i - n_out], 0, each)
-        if i == 1:
-            for first in early:
-                first.step(1)
+        if i == 0:
+            steps(early, 1)
+        else:
+            made[i - 1].step(1)
     for copy in own:
         copy.wait()
-    back = (
-        dot(dq_ref[...], wq[...], ((1,), (1,)))
-        + dot(dk_turned[...], wk[...], ((1,), (1,)))
-        + dot(dv_ref[...], wv[...], ((1,), (1,)))
-    )
-    for each in made:
-        each.step(1)
-    for each in early:
-        each.step(2)
+    back = dot(dq_ref[...], wq[...], ((1,), (1,)))
+    steps(made[-1:], 1)
+    mix.step(1)
+    back = back + dot(dk_turned[...], wk[...], ((1,), (1,)))
+    back = back + dot(dv_ref[...], wv[...], ((1,), (1,)))
+    steps(early, 2)
     x = tokens_ref[...].astype(F32)
     r = rms_scale(x)
     scaled = back * gain_ref[...]
@@ -1134,32 +1128,61 @@
             i = (e * nd + d) * share
             held[-1][d, e] = (held[-1][d, e].astype(F32) + column[i : i + share]).astype(BF16)
     small.loads = []
-    small.step(0)
-    small.step(1)
-    for t in range(2, turns + 1):
-        for each in early:
-            if t > 2:
-                each.step(t)
-        for each in made + [small]:
-            each.step(t)
+    steps([small], 0)
+    steps(queries, 2)
+    steps([small], 1)
+    mix.step(2)
+    for t in range(3, turns + 1):
+        steps(early, t)
+    line_steps(early, 0)
+    steps(others, 2)
+    for t in range(3, turns + 1):
+        steps(queries, t)
+    for t in range(3, ne):
+        mix.step(t)
+    line_steps(early, 1)
+    line_steps(queries, 0)
+    steps([small], 2)
+    for t in range(3, turns + 1):
+        steps(others, t)
+        steps([small], t)
+    tail = others + [small]
+    for t in range(ne):
+        line_steps(early, t + 2)
+        line_steps(queries, t + 1)
+        line_steps(tail, t)
     order = list(range(count))
-    for t in range(ne):
-        for a in order:
-            lines[a].step(t)
     copies = []
     for a in order:
         copies.append(pltpu.make_async_copy(lines[a].own(), outs[a], out_sem.at[a]))
         copies[-1].start()
-    for each in sums + lines:
+    copies.append(pltpu.make_async_copy(mix.own(), mix_out, out_sem.at[count]))
+    copies[-1].start()
+    for each in sums + lines + [mix]:
         each.wait_sends()
     for copy in copies:
         copy.wait()
 
 
 def finish(
-    ne, nd, orders, normed, grads, cosine, sine, tokens, gain, grad_residual, weights, w_out, small
+    ne,
+    nd,
+    orders,
+    normed,
+    grads,
+    cosine,
+    sine,
+    tokens,
+    gain,
+    grad_residual,
+    weights,
+    w_out,
+    small,
+    mix,
+    mix_rows,
 ):
     rows, width = tokens.shape
+    line = (ne, mix_rows, width)
     share = width // (ne * nd)
     columns = weights[1].shape[1]
     n_out = width // columns
@@ -1169,23 +1192,25 @@
     return pl.pallas_call(
         functools.partial(finish_body, ne, nd, tuple(map(tuple, orders)), n_out),
         out_shape=[jax.ShapeDtypeStruct((rows, width), F32)]
-        + [jax.ShapeDtypeStruct((share, c), BF16) for c in wide],
-        in_specs=[VMEM] * 8 + [ANY] * 6,
-        out_specs=[VMEM] + [ANY] * count,
+        + [jax.ShapeDtypeStruct((share, c), BF16) for c in wide]
+        + [jax.ShapeDtypeStruct(line[1:], BF16)],
+        in_specs=[VMEM] * 8 + [ANY] * 7,
+        out_specs=[VMEM] + [ANY] * (count + 1),
         scratch_shapes=[pltpu.VMEM((nd, ne, share, c), BF16) for c in wide]
         + [pltpu.VMEM((nd - 1, ne, share, c), BF16) for c in wide]
         + [pltpu.VMEM((2, ne, share, c), BF16) for c in wide]
         + [pltpu.VMEM(grads[1].shape, BF16)]
         + [pltpu.VMEM(w.shape, BF16) for w in weights]
         + [pltpu.VMEM((rows, width), F32)]
+        + [pltpu.VMEM(line, BF16), pltpu.VMEM((2,) + line, BF16)]
         + [
             DMA((count, ne)),
-            DMA((4,)),
-            DMA((count,)),
+            DMA((5,)),
+            DMA((count + 1,)),
             DMA((count, nd - 1)),
             DMA((count, nd - 1)),
-            DMA((count, 2, ne)),
-            DMA((count, 2, ne)),
+            DMA((count + 1, 2, ne)),
+            DMA((count + 1, 2, ne)),
         ],
         compiler_params=pltpu.CompilerParams(
             vmem_limit_bytes=60 * 2**20, collective_id=4, has_side_effects=True
@@ -1202,7 +1227,88 @@
         *weights,
         split(w_out),
         split(small),
-    )
+        mix,
+    )
+
+
+def results_body(share, n_out, per_path, *refs):
+    refs = list(refs)
+
+    def take(n):
+        return [refs.pop(0) for _ in range(n)]
+
+    residual_ref, mix_first, mix_rest = take(3)
+    paths = [take(per_path) for _ in range(2)]
+    dense = take(2 * n_out + 3)
+    out_ref, d_out, d_query, d_key, d_value, router, gain_one, gain_two = take(8)
+    gate, up, down = refs
+    e = pl.program_id(0)
+
+    @pl.when(e == 0)
+    def _():
+        rows = mix_first.shape[0]
+        for i, mix in enumerate((mix_first, mix_rest)):
+            at = slice(i * rows, i * rows + mix.shape[0])
+            out_ref[at, :] = (residual_ref[at, :] + mix[...].astype(F32)).astype(BF16)
+        width = dense[0].shape[1]
+        for i in range(n_out):
+            d_out[:, i * width : (i + 1) * width] = dense[i][...].astype(F32)
+            d_query[:, i * width : (i + 1) * width] = dense[n_out + i][...].astype(F32)
+        d_key[...] = dense[2 * n_out][...].astype(F32)
+        d_value[...] = dense[2 * n_out + 1][...].astype(F32)
+        small = dense[-1][...].astype(F32)
+        router[...] = small[:, :EXPERTS]
+        turned = small.T
+        gain_one[...] = turned[EXPERTS : EXPERTS + 1]
+        gain_two[...] = turned[EXPERTS + 1 : EXPERTS + 2]
+
+    k = 0
+    for n in range(per_path):
+        for m in range(paths[0][n].shape[0]):
+            for i in range(2):
+
+                @pl.when(e == k)
+                def _(src=paths[i][n], m=m):
+                    gate[0] = src[m, :share].astype(F32)
+                    up[0] = src[m, share : 2 * share].astype(F32)
+                    piece, columns = down.shape[1], src.shape[2]
+                    for j in range(down.shape[2] // columns):
+                        at = 2 * share + j * piece
+                        down[0, :, j * columns : (j + 1) * columns] = src[
+                            m, at : at + piece
+                        ].astype(F32)
+
+                k += 1
+
+
+def results(residual, mix, grads, dense, n_out, share, w_gate, w_down, nd, rows_share):
+    rows, width = residual.shape
+    n_exp, _, inner = w_gate.shape
+    piece = w_down.shape[1] // nd
+    ins = [residual, *mix, *grads[0], *grads[1], *dense]
+    kv = dense[-2].shape[1]
+    same = lambda v: pl.BlockSpec(v, lambda e: (0,) * len(v))
+    outs = [
+        ((rows, width), BF16),
+        ((rows_share, width), F32),
+        ((rows_share, width), F32),
+        ((rows_share, kv), F32),
+        ((rows_share, kv), F32),
+        ((rows_share, EXPERTS), F32),
+        ((1, rows_share), F32),
+        ((1, rows_share), F32),
+    ]
+    experts_out = [((n_exp, share, inner), F32)] * 2 + [((n_exp, piece, width), F32)]
+    return pl.pallas_call(
+        functools.partial(results_body, share, n_out, len(grads[0])),
+        grid=(n_exp,),
+        out_shape=[jax.ShapeDtypeStruct(*v) for v in outs + experts_out],
+        in_specs=[same(v.shape) for v in ins],
+        out_specs=[same(v[0]) for v in outs]
+        + [pl.BlockSpec((1,) + v[0][1:], lambda e: (e, 0, 0)) for v in experts_out],
+        compiler_params=pltpu.CompilerParams(vmem_limit_bytes=60 * 2**20),
+        cost_estimate=cost(6),
+    )(*ins)
 
 
 def per_device(
@@ -1337,7 +1443,7 @@
     )
     more = kept[0].shape[1] > 1
     mix = mix.reshape(ne, every, width)
-    grad_query, grad_key_all, grad_value_all, *grads_more, mix_first = attend_back(
+    grad_query, grad_key_all, grad_value_all, *grads_more = attend_back(
         starts,
         query_rot,
         key_all,
@@ -1347,42 +1453,23 @@
         cosine,
         sine,
         [(kept[i], orders[i][1:], landed[i]) for i in range(2)] if more else [],
-        mix,
         micro,
         rows,
+        ne,
         5,
     )
     full = [[0] + order for order in orders]
-    grad_key, grad_value, mix_rest = reduce(
+    grad_key, grad_value, mix_first = reduce(
         ne,
         nd,
         [
             (grad_key_all, full[0], None, None, False),
             (grad_value_all, full[1], None, None, False),
         ],
-        ((mix, (slice(None), slice(rows, every))),),
+        ((mix, (slice(None), slice(0, rows))),),
         (),
         3,
         30,
-    )
-    mix_own = jnp.concatenate([mix_first, mix_rest], axis=0)
-
-    per_path = [
-        jnp.concatenate(
-            [grads_head[i]] + ([grads_more[i]] if more else []) + [grads_last[i][None]], axis=0
-        )
-        for i in range(2)
-    ]
-    grads = jnp.stack(per_path, axis=1)
-    grads = grads.reshape((here,) + grads.shape[2:]).astype(F32)
-    share = width // nd
-    grad_w_gate, grad_w_up = grads[:, :share], grads[:, share : 2 * share]
-    grad_w_down = jnp.concatenate(
-        [
-            grads[:, at : at + w_down.shape[1] // nd]
-            for at in range(2 * share, grads.shape[1], w_down.shape[1] // nd)
-        ],
-        axis=2,
     )
     small = jnp.concatenate(
         [
@@ -1393,7 +1480,7 @@
         ],
         axis=1,
     ).astype(BF16)
-    grad_tokens, *dense = finish(
+    grad_tokens, *dense, mix_rest = finish(
         ne,
         nd,
         full,
@@ -1407,25 +1494,49 @@
         (w_query, w_key, w_value),
         grad_w_out.astype(BF16),
         small,
-    )
-    n_out = width // kv_width
-    d_out = jnp.concatenate(dense[:n_out], axis=1).astype(F32)
-    d_query = jnp.concatenate(dense[n_out : 2 * n_out], axis=1).astype(F32)
-    d_key, d_value, d_small = (v.astype(F32) for v in dense[2 * n_out :])
-    output = (residual + mix_own.astype(F32)).astype(BF16).reshape(tokens.shape)
+        mix,
+        every - rows,
+    )
+    (
+        output,
+        d_out,
+        d_query,
+        d_key,
+        d_value,
+        d_router,
+        d_gain_one,
+        d_gain_two,
+        d_gate,
+        d_up,
+        d_down,
+    ) = results(
+        residual,
+        (mix_first, mix_rest),
+        [
+            [grads_head[i]] + ([grads_more[i]] if more else []) + [grads_last[i][None]]
+            for i in range(2)
+        ],
+        dense,
+        width // kv_width,
+        width // nd,
+        w_gate,
+        w_down,
+        nd,
+        width // (ne * nd),
+    )
     return (
-        output,
+        output.reshape(tokens.shape),
         grad_tokens.reshape(tokens.shape),
-        d_small[:, EXPERTS],
+        d_gain_one.reshape(-1),
         d_query,
         d_key,
         d_value,
         d_out,
-        d_small[:, EXPERTS + 1],
-        d_small[:, :EXPERTS],
-        grad_w_gate,
-        grad_w_up,
-        grad_w_down,
+        d_gain_two.reshape(-1),
+        d_router,
+        d_gate,
+        d_up,
+        d_down,
     )
 
 

time: 364 us -> 354 us (0.973)
  other arithmetic: 13.8 us -> 6.92 us
  local copies, waits for them, and re-layouts: 12.9 us -> 7.49 us
    pallas_call x0 -> x1, Pallas kernels: none -> 7 us  [results(): pl.pallas_call(functools.partial(results_body, share, n_out, len(grads[0]...]
    slice x5 -> x1, local copies, waits for them, and re-layouts: 5.38 us -> 0.75 us  [the longest x1 2.46 us: per_device(): grad_w_gate, grad_w_up = (grads[:, :share], grads[:, share:2 * share])]
    pallas_call x1, Pallas kernels: 54.5 us -> 50.2 us  [finish(): pl.pallas_call(functools.partial(finish_body, ne, nd, tuple(map(tuple, or...]
    convert_element_type x6 -> x0, other arithmetic: 4.04 us -> none  [the longest x3 1.97 us: per_device(): d_key, d_value, d_small = (v.astype(F32) for v in dense[2 * n_out:])]
where the time goes in v8:
time: 354 us; the launch traced here: 351 us
  Pallas kernels  321 us (91%)
  matrix products  8.96 us (3%)
  local copies, waits for them, and re-layouts  7.49 us (2%)
  other arithmetic  6.92 us (2%)
  starting transfers between devices  5.57 us (2%)
    pallas_call x1, Pallas kernels, experts(): pl.pallas_call(functools.partial(expert_body, ne, nd, micro, rows), grid=...  84.2 us
    pallas_call x2, Pallas kernels, reduce(): pl.pallas_call(functools.partial(reduce_body, ne, nd, kinds, line_parts,...  73.4 us
    pallas_call x2, Pallas kernels, gather(): pl.pallas_call(functools.partial(gather_body, ne, nd, len(dp_arrays), len...  64.8 us
    pallas_call x1, Pallas kernels, finish(): pl.pallas_call(functools.partial(finish_body, ne, nd, tuple(map(tuple, or...  50.2 us
    pallas_call x1, Pallas kernels, attend_back(): pl.pallas_call(functools.partial(attend_back_body, nd // 2 + 1, ne, nd, t...  24.5 us
    pallas_call x1, Pallas kernels, attend(): pl.pallas_call(functools.partial(attend_body, nd // 2 + 1), grid_spec=plt...  11.5 us
  transfers between devices with their start and end apart: 3, of which 0 were waited for; matrix products, arithmetic and copies ran while one was open for 3% of the time, Pallas kernels for 23%

profile of v8, /device:TPU:10, one launch (start us, length us, event | category | flops | bytes accessed | tf_op | source)
XLA Modules:
  0.0 350.9 jit_solution(1352186680499762411)
XLA Ops:
  1.2 2.6 collective-permute-start.1
  3.8 2.5 collective-permute-start
  6.4 0.8 convert_reduce_fusion
  10.3 5.4 %shard_map.229 = (bf16[256,1024]{1,0:T(8,128)(2,1)}, bf16[256,1024]{1,0:T(8,128)(2,1)}, bf16[256,512]{1,0:T(8,128)(2,1)}, bf16[256,512]{1,0:T(8,128)(2,1)}) custom-call(bf16[256,1024]{1,0:T(8,128)(2,1)} %bitcast.76, f32[1,1024]{1,0:T(1,128)} %bitcast.95, f32[256,128]{1,0:T(8,128)} %copy.38.cos_ref.refs_6_.refs_4_, ...), custom_call_target="tpu_custom_call" | custom-call | bytes 15000000 | tf_op jit(solution)/shard_map/pallas_call | solution.py:786
  15.7 23.0 %shard_map.230 = (bf16[8,256,512]{2,1,0:T(8,128)(2,1)}, bf16[8,256,512]{2,1,0:T(8,128)(2,1)}, f32[8,8,128]{2,1,0:T(8,128)}) custom-call(bf16[256,512]{1,0:T(8,128)(2,1)} %get-tuple-element.66.refs_0_, bf16[256,512]{1,0:T(8,128)(2,1)} %get-tuple-element.67.refs_1_, f32[8,128]{1,0:T(8,128)} %concatenate.15.refs_2_), custom_call_target="tpu_custom_call" | custom-call | bytes 75000000 | tf_op jit(solution)/shard_map/pallas_call | solution.py:166
  38.7 0.8 slice_reduce_fusion
  39.7 0.8 copy.39.starts_ref.refs_0_
  40.5 11.5 %shard_map.231 = (bf16[256,1024]{1,0:T(8,128)(2,1)}, f32[2,4,512,1]{3,2,1,0:T(8,128)}) custom-call(s32[1]{0:T(128)} %bitcast.1.dp_ref, s32[256,1]{1,0:T(8,128)} %copy.39.starts_ref.refs_0_, bf16[256,1024]{1,0:T(8,128)(2,1)} %get-tuple-element.69.q_ref.refs_1_, bf16[8,256,512]{2,1,0:T(8,128)(2,1)} %get-tuple-element.70.k_ref.refs_2_, ...), custom_call_target="tpu_custom_call" | custom-call | bytes 45000000 | tf_op jit(solution)/shard_map/pallas_call | solution.py:873
  52.0 1.9 multiply_reduce_fusion.2
  55.0 41.8 %shard_map.232 = (bf16[4,256,1024]{2,1,0:T(8,128)(2,1)}, f32[4,32,256]{2,1,0:T(8,128)}) custom-call(bf16[256,1024]{1,0:T(8,128)(2,1)} %copy-done.6, f32[32,256]{1,0:T(8,128)} %fusion.9.refs_1_), custom_call_target="tpu_custom_call" | custom-call | bytes 114000000 | tf_op jit(solution)/shard_map/pallas_call | solution.py:166
  98.2 84.2 %shard_map.233 = (bf16[1024,1024]{1,0:T(8,128)(2,1)}, bf16[1024,1024]{1,0:T(8,128)(2,1)}, f32[8,8,128]{2,1,0:T(8,128)}, bf16[2,3,384,512]{3,2,1,0:T(8,128)(2,1)}...) custom-call(bf16[256,1024]{1,0:T(8,128)(2,1)} %bitcast.82, ...), custom_call_target="tpu_custom_call" | custom-call | bytes 225000000 | tf_op jit(solution)/shard_map/pallas_call | solution.py:693
  183.9 44.3 %shard_map.234 = (bf16[384,512]{1,0:T(8,128)(2,1)}, bf16[384,512]{1,0:T(8,128)(2,1)}, bf16[1,384,512]{2,1,0:T(8,128)(2,1)}, bf16[1,384,512]{2,1,0:T(8,128)(2,1)}...) custom-call(bf16[4,384,512]{2,1,0:T(8,128)(2,1)} %get-tuple-element.76.refs_0_, ...), custom_call_target="tpu_custom_call" | custom-call | bytes 120000000 | tf_op jit(solution)/shard_map/pallas_call | solution.py:418
  228.2 0.9 fusion.3
  229.1 1.1 convolution_convert_fusion.2
  230.2 2.0 multiply_reduce_fusion
  232.7 1.2 copy-done.5
  233.9 1.6 convolution_convert_fusion.1.refs_5_
  235.5 2.1 convolution_convert_fusion
  238.2 24.5 %shard_map.235 = (bf16[256,1024]{1,0:T(8,128)(2,1)}, bf16[8,256,512]{2,1,0:T(8,128)(2,1)}, bf16[8,256,512]{2,1,0:T(8,128)(2,1)}, bf16[2,384,512]{2,1,0:T(8,128)(2,1)}, bf16[2,384,512]{2,1,0:T(8,128)(2,1)}) custom-call(s32[256,1]{1,0:T(8,128)} %copy.39.starts_ref.refs_0_, bf16[256,1024]{1,0:T(8,128)(2,1)} %get-tuple-element.69.q_ref.refs_1_, ...), custom_call_target="tpu_custom_call" | custom-call | bytes 75000000 | tf_op jit(solution)/shard_map/pallas_call | solution.py:970
  262.7 29.1 %shard_map.236 = (bf16[256,512]{1,0:T(8,128)(2,1)}, bf16[256,512]{1,0:T(8,128)(2,1)}, bf16[128,1024]{1,0:T(8,128)(2,1)}) custom-call(bf16[8,256,512]{2,1,0:T(8,128)(2,1)} %get-tuple-element.86.refs_0_, bf16[8,256,512]{2,1,0:T(8,128)(2,1)} %get-tuple-element.87.refs_1_, bf16[4,256,1024]{2,1,0:T(8,128)(2,1)} %bitcast.73), custom_call_target="tpu_custom_call" | custom-call | bytes 90000000 | tf_op jit(solution)/shard_map/pallas_call | solution.py:418
  291.8 0.9 maximum_maximum_fusion.refs_13_
  292.7 50.2 %shard_map.237 = (f32[256,1024]{1,0:T(8,128)}, bf16[32,512]{1,0:T(8,128)(2,1)}, bf16[32,512]{1,0:T(8,128)(2,1)}, bf16[32,512]{1,0:T(8,128)(2,1)}, bf16[32,512]{1...) custom-call(bf16[256,1024]{1,0:T(8,128)(2,1)} %get-tuple-element.90., ...), custom_call_target="tpu_custom_call" | custom-call | bytes 135000000 | tf_op jit(solution)/shard_map/pallas_call | solution.py:1192
  342.9 7.0 %shard_map.238 = (bf16[256,1024]{1,0:T(8,128)(2,1)}, f32[32,1024]{1,0:T(8,128)}, f32[32,1024]{1,0:T(8,128)}, f32[32,512]{1,0:T(8,128)}, f32[32,512]{1,0:T(8,128)...) custom-call(f32[256,1024]{1,0:T(8,128)} %copy-done.2, ...), custom_call_target="tpu_custom_call" | custom-call | bytes 18000000 | tf_op jit(solution)/shard_map/pallas_call | solution.py:1302
  349.9 1.0 copy.55
  (64 shorter events, 8.9 us)
Async XLA Ops:
  0.6 53.4 %copy-start = (bf16[1024,32]{0,1:T(8,128)(2,1)S(1)}, bf16[1024,32]{0,1:T(8,128)(2,1)}, u32[]{:S(2)}) copy-start(bf16[1024,32]{0,1:T(8,128)(2,1)} %param.23) | copy-start | bytes 196612
  0.7 97.6 %collective-permute-start.2 = (bf16[256,1024]{1,0:T(8,128)(2,1)}, bf16[256,1024]{1,0:T(8,128)(2,1)}, u32[]{:S(2)}, u32[]{:S(2)}) collective-permute-start(bf16[256,1024]{1,0:T(8,128)(2,1)} %bitcast.79), channel_id=1, source_target_pairs={{0,24},{8,0},{16,8},{24,16},{1,25},{9,1},{17,9},{25,17},{2,26},{10... | collective-permute-start | bytes 1572872 | tf_op jit(solution)/shard_map/ppermute | solution.py:1361
  1.2 97.1 %collective-permute-start.1 = (bf16[256,1024]{1,0:T(8,128)(2,1)}, bf16[256,1024]{1,0:T(8,128)(2,1)}, u32[]{:S(2)}, u32[]{:S(2)}) collective-permute-start(bf16[256,1024]{1,0:T(8,128)(2,1)} %bitcast.80), channel_id=1, source_target_pairs={{0,16},{8,24},{16,0},{24,8},{1,17},{9,25},{17,1},{25,9},{2,18},{10... | collective-permute-start | bytes 1572872 | tf_op jit(solution)/shard_map/ppermute | solution.py:1361
  3.8 94.5 %collective-permute-start = (bf16[256,1024]{1,0:T(8,128)(2,1)}, bf16[256,1024]{1,0:T(8,128)(2,1)}, u32[]{:S(2)}, u32[]{:S(2)}) collective-permute-start(bf16[256,1024]{1,0:T(8,128)(2,1)} %bitcast.81), channel_id=1, source_target_pairs={{0,8},{8,16},{16,24},{24,0},{1,9},{9,17},{17,25},{25,1},{2,10},{10... | collective-permute-start | bytes 1572872 | tf_op jit(solution)/shard_map/ppermute | solution.py:1361
  10.3 29.2 %copy-start.14 = (s32[2,1,128]{2,1,0:T(1,128)S(1)}, s32[2,1,128]{2,1,0:T(1,128)}, u32[]{:S(2)}) copy-start(s32[2,1,128]{2,1,0:T(1,128)} %param.15) | copy-start | bytes 3076
  40.5 11.5 %copy-start.4 = (bf16[1024,1024]{1,0:T(8,128)(2,1)S(1)}, bf16[1024,1024]{1,0:T(8,128)(2,1)}, u32[]{:S(2)}) copy-start(bf16[1024,1024]{1,0:T(8,128)(2,1)} %param.21) | copy-start | bytes 6291460
  40.5 11.5 %copy-start.8 = (bf16[2,128,1024]{2,1,0:T(8,128)(2,1)S(1)}, bf16[2,128,1024]{2,1,0:T(8,128)(2,1)}, u32[]{:S(2)}) copy-start(bf16[2,128,1024]{2,1,0:T(8,128)(2,1)} %param.14) | copy-start | bytes 1572868
  52.0 1.9 copy-start.13
  53.9 178.4 %copy-start.2 = (f32[256,1024]{1,0:T(8,128)}, f32[256,1024]{1,0:T(8,128)S(1)}, u32[]{:S(2)}) copy-start(f32[256,1024]{1,0:T(8,128)S(1)} %get-tuple-element.129.refs_0_) | copy-start | bytes 3145732
  54.1 1.0 copy-start.6
  183.9 45.2 %copy-start.7 = (bf16[256,1024]{1,0:T(8,128)(2,1)S(1)}, bf16[256,1024]{1,0:T(8,128)(2,1)}, u32[]{:S(2)}) copy-start(bf16[256,1024]{1,0:T(8,128)(2,1)} %copy-done.6) | copy-start | bytes 1572868
  228.2 4.1 %copy-start.9 = (bf16[2,128,1024]{2,1,0:T(8,128)(2,1)S(1)}, bf16[2,128,1024]{2,1,0:T(8,128)(2,1)}, u32[]{:S(2)}) copy-start(bf16[2,128,1024]{2,1,0:T(8,128)(2,1)} %param.27) | copy-start | bytes 1572868
  228.2 4.1 %copy-start.11 = (bf16[256,1024]{1,0:T(8,128)(2,1)S(1)}, bf16[256,1024]{1,0:T(8,128)(2,1)}, u32[]{:S(2)}) copy-start(bf16[256,1024]{1,0:T(8,128)(2,1)} %get-tuple-element.85) | copy-start | bytes 1572868
  232.3 1.6 copy-start.5
  233.9 3.7 %copy-start.3 = (f32[256,1024]{1,0:T(8,128)}, f32[256,1024]{1,0:T(8,128)S(1)}, u32[]{:S(2)}) copy-start(f32[256,1024]{1,0:T(8,128)S(1)} %multiply_subtract_fusion.refs_8_) | copy-start | bytes 3145732
  233.9 1.6 copy-start.10
  342.9 7.0 %copy-start.12 = (f32[256,1024]{1,0:T(8,128)S(1)}, f32[256,1024]{1,0:T(8,128)}, u32[]{:S(2)}) copy-start(f32[256,1024]{1,0:T(8,128)} %get-tuple-element.109) | copy-start | bytes 3145732
  342.9 8.0 %copy-start.1 = (bf16[1024,32]{0,1:T(8,128)(2,1)S(1)}, bf16[1024,32]{0,1:T(8,128)(2,1)}, u32[]{:S(2)}) copy-start(bf16[1024,32]{0,1:T(8,128)(2,1)} %param.23) | copy-start | bytes 196612

commit v9 on v8

--- a/solution.py
+++ b/solution.py
@@ -2,6 +2,7 @@
 
 import jax
 import jax.numpy as jnp
+import numpy as np
 from jax import lax
 from jax.experimental import pallas as pl
 from jax.experimental.pallas import tpu as pltpu
@@ -448,8 +449,8 @@
     normed_ref, probs_ref, gate_ref, up_ref, down_ref = refs[:5]
     mix_ref, grad_ref, dots_ref = refs[5:8]
     kept, landed, whole = refs[8:10], refs[10:12], refs[12:14]
-    rows_in, cots_in, picks, first, second, keep, send, arrived, leaving = refs[14:23]
-    load_sem, store_sem, send_sem, recv_sem, free_sem, far_send, far_recv = refs[23:]
+    rows_in, cots_in, picks, first, second, sides, arrived, leaving = refs[14:22]
+    load_sem, store_sem, send_sem, recv_sem, free_sem, far_send, far_recv = refs[22:]
     e = pl.program_id(0)
     last = pl.num_programs(0) - 1
     ep, dp = lax.axis_index("ep"), lax.axis_index("dp")
@@ -458,6 +459,9 @@
     blocks = ne * micro
     width = first.shape[1]
     n_exp = rows_in.shape[1]
+
+    core = jnp.bitwise_and(dp, 1)
+    keep, send = sides.at[core], sides.at[1 - core]
 
     def exchange():
         return remote(send, arrived, send_sem, recv_sem, other)
@@ -491,9 +495,9 @@
 
     def far(i, n):
         return remote(
-            leaving.at[i],
+            leaving.at[i, lax.rem(n, leaving.shape[1])],
             landed[i].at[:, n],
-            far_send.at[i],
+            far_send.at[i, lax.rem(n, leaving.shape[1])],
             far_recv.at[i, n],
             {"dp": jnp.bitwise_xor(dp, 1 << first_bits(nd)[i])},
         )
@@ -503,36 +507,29 @@
 
     def collect():
         exchange().wait_recv()
-        pieces = keep.shape[0]
+        pieces = sides.shape[1]
         n = (e - 1) // 2
         for i, bit in enumerate(first_bits(nd)):
-
-            def put(side, i=i, bit=bit):
-                for j in range(pieces):
-                    value = (keep[j].astype(F32) + arrived[j].astype(F32)).astype(BF16)
-                    at = (j >> bit << (bit - 1)) | (j & ((1 << (bit - 1)) - 1))
-                    if (j >> (bit - 1)) & 1 == side:
-                        kept[i][at, 0] = value
-                    else:
-                        leaving[i, at] = value
+            mine = jnp.bitwise_and(lax.shift_right_logical(dp, bit), 1)
+
+            def piece(at, side, bit=bit):
+                low = (1 << (bit - 1)) - 1
+                j = ((at & ~low) << 1 | (at & low)) + (side << (bit - 1))
+                return (keep[j].astype(F32) + arrived[j].astype(F32)).astype(BF16)
 
             @pl.when((lax.rem(e - 1, 2) == i) & (n < n_exp // 2 - 1))
-            def _(i=i, bit=bit, put=put):
-                @pl.when(n > 0)
+            def _(i=i, mine=mine, piece=piece):
+                slots = leaving.shape[1]
+
+                @pl.when(n >= slots)
                 def _():
-                    far(i, n - 1).wait_send()
-
-                mine = jnp.bitwise_and(lax.shift_right_logical(dp, bit), 1)
-
-                @pl.when(mine == 0)
-                def _():
-                    put(0)
-
-                @pl.when(mine == 1)
-                def _():
-                    put(1)
-
+                    far(i, n - slots).wait_send()
+
+                for at in range(pieces // 2):
+                    leaving[i, lax.rem(n, slots), at] = piece(at, 1 - mine)
                 far(i, n).start()
+                for at in range(pieces // 2):
+                    kept[i][at, 0] = piece(at, mine)
 
             @pl.when((lax.rem(e - 1, 2) == i) & (n == n_exp // 2 - 1))
             def _(i=i):
@@ -611,24 +608,14 @@
 
         def split(value, offset):
             value = value.astype(BF16)
-            piece, columns = value.shape[0] // nd, keep.shape[2]
-
-            def put(even, odd):
-                for i in range(nd):
-                    ref = odd if i % 2 else even
-                    for j in range(value.shape[1] // columns):
-                        at = offset + j * piece
-                        ref[i // 2, at : at + piece] = value[
-                            i * piece : (i + 1) * piece, j * columns : (j + 1) * columns
-                        ]
-
-            @pl.when(jnp.bitwise_and(dp, 1) == 0)
-            def _():
-                put(keep, send)
-
-            @pl.when(jnp.bitwise_and(dp, 1) == 1)
-            def _():
-                put(send, keep)
+            piece, columns = value.shape[0] // nd, sides.shape[3]
+
+            for i in range(nd):
+                for j in range(value.shape[1] // columns):
+                    at = offset + j * piece
+                    sides[i % 2, i // 2, at : at + piece] = value[
+                        i * piece : (i + 1) * piece, j * columns : (j + 1) * columns
+                    ]
 
         share = width // nd
         split(dot(scaled, c, ((0,), (0,))), 2 * share)
@@ -664,7 +651,8 @@
 
         last_copy().wait()
         for i in range(2):
-            far(i, n_exp // 2 - 2).wait_send()
+            for n in range(max(n_exp // 2 - 1 - leaving.shape[1], 0), n_exp // 2 - 1):
+                far(i, n).wait_send()
 
             @pl.loop(0, n_exp // 2 - 1)
             def _(n, i=i):
@@ -708,16 +696,15 @@
             pltpu.VMEM((blocks, n_exp * CAP, rows), BF16),
             pltpu.VMEM(full, BF16),
             pltpu.VMEM(full, BF16),
+            pltpu.VMEM((2, half, packed, inner), BF16),
             pltpu.VMEM((half, packed, inner), BF16),
-            pltpu.VMEM((half, packed, inner), BF16),
-            pltpu.VMEM((half, packed, inner), BF16),
-            pltpu.VMEM((2, half // 2, packed, inner), BF16),
+            pltpu.VMEM((2, min(early, 2), half // 2, packed, inner), BF16),
             DMA((ne + 1,)),
             DMA((2, blocks)),
             DMA,
             DMA,
             pltpu.SemaphoreType.REGULAR,
-            DMA((2,)),
+            DMA((2, 2)),
             DMA((2, early)),
         ],
         out_shape=[
@@ -752,8 +739,12 @@
     return x * cosine + partner(x) * sine
 
 
+def repeated(table, rows):
+    return jnp.concatenate([table] * (rows // table.shape[0]), axis=0)
+
+
 def project_body(
-    tokens_ref, gain_ref, cos_ref, sin_ref, wq_ref, wk_ref, wv_ref, n_ref, q_ref, k_ref, v_ref, *rest
+    tokens_ref, gain_ref, tables_ref, wq_ref, wk_ref, wv_ref, n_ref, q_ref, k_ref, v_ref, *rest
 ):
     wq, wk, wv, sem = rest
     loads = [
@@ -765,7 +756,7 @@
     x = tokens_ref[...].astype(F32)
     n_ref[...] = (x * rms_scale(x) * gain_ref[...]).astype(BF16)
     normed = n_ref[...]
-    cosine, sine = cos_ref[...], sin_ref[...]
+    cosine, sine = (repeated(tables_ref[i], x.shape[0]) for i in range(2))
     tile = 256
     for copy, (w, out, turned) in zip(
         loads, ((wk, k_ref, True), (wv, v_ref, False), (wq, q_ref, True))
@@ -780,18 +771,18 @@
                 out[:, c : c + tile] = y.astype(BF16)
 
 
-def project(tokens, gain, cosine, sine, w_query, w_key, w_value):
+def project(tokens, gain, tables, w_query, w_key, w_value):
     rows, width = tokens.shape
     shapes = [width, w_query.shape[1], w_key.shape[1], w_value.shape[1]]
     return pl.pallas_call(
         project_body,
         out_shape=[jax.ShapeDtypeStruct((rows, n), BF16) for n in shapes],
-        in_specs=[VMEM] * 4 + [ANY] * 3,
+        in_specs=[VMEM] * 3 + [ANY] * 3,
         out_specs=[VMEM] * 4,
         scratch_shapes=[pltpu.VMEM(w.shape, BF16) for w in (w_query, w_key, w_value)] + [DMA((3,))],
         compiler_params=pltpu.CompilerParams(vmem_limit_bytes=60 * 2**20),
         cost_estimate=cost(5),
-    )(tokens, gain, cosine, sine, w_query, w_key, w_value)
+    )(tokens, gain, tables, w_query, w_key, w_value)
 
 
 def spread(x):
@@ -844,9 +835,73 @@
 SCALE = HEAD_DIM ** (-0.5)
 
 
-def attend_body(span, dp_ref, starts_ref, q_ref, k_ref, v_ref, out_ref, log_ref):
-    dp = dp_ref[0]
+class LineGather:
+    def __init__(self, ep, ne, own, whole, send_sem, recv_sem):
+        self.ep, self.ne, self.own, self.whole = ep, ne, own, whole
+        self.send_sem, self.recv_sem = send_sem, recv_sem
+
+    def copy(self, m, s, way):
+        shard = lax.rem(self.ep - way * s + self.ne, self.ne)
+        k = 0 if way == 1 else 1
+        return remote(
+            self.own.at[m] if s == 0 else self.whole.at[shard, m],
+            self.whole.at[shard, m],
+            self.send_sem.at[m, k, s],
+            self.recv_sem.at[m, k, s],
+            {"ep": lax.rem(self.ep + way + self.ne, self.ne)},
+        )
+
+    def sends(self, s, way):
+        ep, ne = self.ep, self.ne
+        return (ep >= s) & (ep < ne - 1) if way == 1 else (ep + s <= ne - 1) & (ep >= 1)
+
+    def receives(self, s, way):
+        return self.ep >= 1 + s if way == 1 else self.ep + 1 + s <= self.ne - 1
+
+    def step(self, m, s):
+        for way in (1, -1):
+            if s > 0:
+
+                @pl.when(self.receives(s - 1, way))
+                def _(way=way):
+                    self.copy(m, s - 1, way).wait_recv()
+
+            if s < self.ne - 1:
+
+                @pl.when(self.sends(s, way))
+                def _(way=way):
+                    self.copy(m, s, way).start()
+
+    def wait_sends(self, m):
+        for s in range(self.ne - 1):
+            for way in (1, -1):
+
+                @pl.when(self.sends(s, way))
+                def _(s=s, way=way):
+                    self.copy(m, s, way).wait_send()
+
+
+def attend_body(span, ne, nd, micro, *refs):
+    starts_ref, q_ref, k_ref, v_ref, tokens_ref, wo_ref, gain_ref, router_ref, hit_ref = refs[:9]
+    out_ref, log_ref, res_ref, normed_ref, probs_ref, normed_all, marked_all = refs[9:16]
+    attn, normed_own, marked_own, own_sem, send_sem, recv_sem = refs[16:]
+    ep, dp = lax.axis_index("ep"), lax.axis_index("dp")
+    m, h = pl.program_id(0), pl.program_id(1)
+    final = pl.num_programs(1) - 1
     rows = q_ref.shape[0]
+    lines = [
+        LineGather(ep, ne, own, whole, send_sem.at[i], recv_sem.at[i])
+        for i, (own, whole) in enumerate(((normed_own, normed_all), (marked_own, marked_all)))
+    ]
+
+    def hop(batch, s):
+        for line in lines:
+            line.step(batch, s)
+
+    @pl.when((m == 0) & (h == 0))
+    def _():
+        greet(ep, dp, ne, nd)
+
     q = spread(q_ref[...].astype(F32) * SCALE).astype(BF16)
     scores = window_scores(dp, span, rows, starts_ref, q, in_window(k_ref, dp, span))
     top = jnp.max(scores, axis=1, keepdims=True)
@@ -854,8 +909,48 @@
     total = jnp.sum(terms, axis=1, keepdims=True)
     log_ref[0, 0] = top + jnp.log(total)
     weights = (terms * (1.0 / total)).astype(BF16)
-    out = dot(weights, in_window(v_ref, dp, span))
-    out_ref[...] = gathered(out, rows).astype(BF16)
+    out = gathered(dot(weights, in_window(v_ref, dp, span)), rows).astype(BF16)
+    out_ref[...] = out
+    attn[:, pl.ds(pl.multiple_of(h * out.shape[1], out.shape[1]), out.shape[1])] = out
+
+    def own_copies(batch):
+        return [
+            pltpu.make_async_copy(line.own.at[batch], line.whole.at[ep, batch], own_sem.at[i, batch])
+            for i, line in enumerate(lines)
+        ]
+
+    for batch in range(micro):
+
+        @pl.when((m == batch) & (h == final))
+        def _(batch=batch):
+            for earlier in range(batch):
+                hop(earlier, batch - earlier)
+            residual = tokens_ref[...].astype(F32) + dot(attn[...], wo_ref[...])
+            res_ref[...] = residual
+            normed = (residual * rms_scale(residual) * gain_ref[...]).astype(BF16)
+            normed_ref[...] = normed
+            normed_own[batch] = normed
+            hit = hit_ref[...] > 0.0
+            logits = jnp.where(hit, dot(router_ref[...], normed, ((1,), (1,))), MASKED)
+            terms = jnp.exp(logits - jnp.max(logits, axis=0, keepdims=True))
+            terms = jnp.where(hit, terms, 0.0)
+            probs = terms / jnp.sum(terms, axis=0, keepdims=True)
+            probs_ref[...] = probs
+            marked_own[batch] = jnp.where(hit, probs, -1.0)
+            hop(batch, 0)
+            for copy in own_copies(batch):
+                copy.start()
+            if batch == micro - 1:
+                for t in range(1, ne + micro - 1):
+                    for each in range(micro):
+                        s = t + micro - 1 - each
+                        if s < ne:
+                            hop(each, s)
+                for each in range(micro):
+                    for line in lines:
+                        line.wait_sends(each)
+                    for copy in own_copies(each):
+                        copy.wait()
 
 
 def attention_specs(micro, rows, nd):
@@ -868,20 +963,44 @@
     return (micro, pairs), mine, theirs, column, logs, log_shape
 
 
-def attend(dp, starts, queries, keys, values, micro, rows, nd):
+def attend(
+    starts, queries, keys, values, tokens, w_out, gain, router, hit, micro, rows, ne, collective
+):
+    nd, width = keys.shape[0], tokens.shape[1]
     grid, mine, theirs, column, logs, log_shape = attention_specs(micro, rows, nd)
+    one = pl.Buffered(1)
+    whole = lambda v: pl.BlockSpec(v.shape, lambda m, h: (0, 0), pipeline_mode=one)
+    wide = pl.BlockSpec((rows, width), lambda m, h: (m, 0))
+    chosen = pl.BlockSpec((hit.shape[0], rows), lambda m, h: (0, m))
+    every = micro * rows
     return pl.pallas_call(
-        functools.partial(attend_body, nd // 2 + 1),
-        grid_spec=pltpu.PrefetchScalarGridSpec(
-            num_scalar_prefetch=1,
-            grid=grid,
-            in_specs=[column, mine, theirs, theirs],
-            out_specs=[mine, logs],
+        functools.partial(attend_body, nd // 2 + 1, ne, nd, micro),
+        grid=grid,
+        in_specs=[column, mine, theirs, theirs, wide, whole(w_out), whole(gain), whole(router)]
+        + [chosen],
+        out_specs=[mine, logs, wide, wide, chosen, ANY, ANY],
+        out_shape=[
+            jax.ShapeDtypeStruct(queries.shape, BF16),
+            log_shape,
+            jax.ShapeDtypeStruct((every, width), F32),
+            jax.ShapeDtypeStruct((every, width), BF16),
+            jax.ShapeDtypeStruct(hit.shape, F32),
+            jax.ShapeDtypeStruct((ne, micro, rows, width), BF16),
+            jax.ShapeDtypeStruct((ne, micro, hit.shape[0], rows), F32),
+        ],
+        scratch_shapes=[
+            pltpu.VMEM((rows, width), BF16),
+            pltpu.VMEM((micro, rows, width), BF16),
+            pltpu.VMEM((micro, hit.shape[0], rows), F32),
+            DMA((2, micro)),
+            DMA((2, micro, 2, ne - 1)),
+            DMA((2, micro, 2, ne - 1)),
+        ],
+        compiler_params=pltpu.CompilerParams(
+            vmem_limit_bytes=60 * 2**20, collective_id=collective, has_side_effects=True
         ),
-        out_shape=[jax.ShapeDtypeStruct(queries.shape, BF16), log_shape],
-        compiler_params=pltpu.CompilerParams(vmem_limit_bytes=60 * 2**20),
-        cost_estimate=cost(15),
-    )(dp.reshape(1), starts, queries, keys, values)
+        cost_estimate=cost(50),
+    )(starts, queries, keys, values, tokens, w_out, gain, router, hit)
 
 
 def attend_back_body(span, ne, nd, orders, *refs):
@@ -890,7 +1009,7 @@
     def take(n):
         return [refs.pop(0) for _ in range(n)]
 
-    starts_ref, q_ref, k_ref, v_ref, log_ref, g_ref, cos_ref, sin_ref = take(8)
+    starts_ref, q_ref, k_ref, v_ref, log_ref, g_ref, tables_ref = take(7)
     n = len(orders)
     sources, extras = take(n), take(n)
     dq_ref, dk_ref, dv_ref = take(3)
@@ -930,7 +1049,7 @@
     total = jnp.sum(probs * grad_probs, axis=1, keepdims=True)
     grad_scores = (probs * (grad_probs - total)).astype(BF16)
     dq = gathered(dot(grad_scores, k) * SCALE, rows)
-    cosine, sine = cos_ref[...], -sin_ref[...]
+    cosine, sine = tables_ref[0], -tables_ref[1]
     for i in range(0, dq.shape[1], 128):
         dq_ref[:, i : i + 128] = turn(dq[:, i : i + 128], cosine, sine).astype(BF16)
     dk_ref[...] = jnp.zeros_like(dk_ref)
@@ -958,11 +1077,11 @@
 
 
 def attend_back(
-    starts, queries, keys, values, logs_in, grad, cosine, sine, sums, micro, rows, ne, collective
+    starts, queries, keys, values, logs_in, grad, tables, sums, micro, rows, ne, collective
 ):
     nd = keys.shape[0]
     grid, mine, theirs, column, logs, _ = attention_specs(micro, rows, nd)
-    table = pl.BlockSpec((rows, 128), lambda m, h, *_: (0, 0))
+    table = pl.BlockSpec(tables.shape, lambda m, h: (0, 0, 0))
     n = len(sums)
     shapes = [(v.shape[0], v.shape[1] - 1) + v.shape[2:] for v, _, _ in sums]
     deep = max([s[0] - 1 for s in shapes] + [1])
@@ -972,7 +1091,7 @@
             attend_back_body, nd // 2 + 1, ne, nd, tuple(tuple(order) for _, order, _ in sums)
         ),
         grid=grid,
-        in_specs=[column, mine, theirs, theirs, logs, mine, table, table] + [ANY] * (2 * n),
+        in_specs=[column, mine, theirs, theirs, logs, mine, table] + [ANY] * (2 * n),
         out_specs=[mine, theirs, theirs] + [ANY] * n,
         out_shape=[
             jax.ShapeDtypeStruct(queries.shape, BF16),
@@ -994,8 +1113,7 @@
         values,
         logs_in,
         grad,
-        cosine,
-        sine,
+        tables,
         *[v for v, _, _ in sums],
         *[extra for _, _, extra in sums],
     )
@@ -1007,7 +1125,7 @@
     def take(n):
         return [refs.pop(0) for _ in range(n)]
 
-    n_ref, dq_ref, dk_ref, dv_ref, cos_ref, sin_ref, tokens_ref, gain_ref = take(8)
+    n_ref, dq_ref, dk_ref, dv_ref, tables_ref, tokens_ref, gain_ref = take(7)
     res_ref, wq_ref, wk_ref, wv_ref, wo_ref, small_ref, mix_ref = take(7)
     (tok_out,) = take(1)
     count = 2 * n_out + 3
@@ -1074,7 +1192,8 @@
     mix.step(0)
 
     normed = n_ref[...]
-    cosine, sine = cos_ref[...], -sin_ref[...]
+    cosine, sine = (repeated(tables_ref[i], normed.shape[0]) for i in range(2))
+    sine = -sine
     for i in range(0, dk_ref.shape[1], 128):
         part = dk_ref[:, i : i + 128].astype(F32)
         dk_turned[:, i : i + 128] = turn(part, cosine, sine).astype(BF16)
@@ -1170,8 +1289,7 @@
     orders,
     normed,
     grads,
-    cosine,
-    sine,
+    tables,
     tokens,
     gain,
     grad_residual,
@@ -1194,7 +1312,7 @@
         out_shape=[jax.ShapeDtypeStruct((rows, width), F32)]
         + [jax.ShapeDtypeStruct((share, c), BF16) for c in wide]
         + [jax.ShapeDtypeStruct(line[1:], BF16)],
-        in_specs=[VMEM] * 8 + [ANY] * 7,
+        in_specs=[VMEM] * 7 + [ANY] * 7,
         out_specs=[VMEM] + [ANY] * (count + 1),
         scratch_shapes=[pltpu.VMEM((nd, ne, share, c), BF16) for c in wide]
         + [pltpu.VMEM((nd - 1, ne, share, c), BF16) for c in wide]
@@ -1219,8 +1337,7 @@
     )(
         normed,
         *grads,
-        cosine,
-        sine,
+        tables,
         tokens,
         gain,
         grad_residual,
@@ -1336,19 +1453,18 @@
     inputs = tokens.reshape(every, width).astype(F32)
     grad_output = cotangent.reshape(every, width).astype(F32)
 
-    query_pos = dp * rows + jnp.arange(rows, dtype=jnp.int32)
     halfway = HEAD_DIM // 2
-    frequency = ROPE_BASE ** (-(jnp.arange(halfway, dtype=F32) * 2.0 / HEAD_DIM))
-    angles = query_pos.astype(F32)[:, None] * frequency[None, :]
+    frequency = ROPE_BASE ** (-(np.arange(halfway) * 2.0 / HEAD_DIM))
+    angles = np.arange(nd * rows)[:, None] * frequency[None, :]
     lanes = 2 * HEAD_DIM // halfway
-    sign = jnp.where(jnp.arange(2 * HEAD_DIM) % HEAD_DIM < halfway, -1.0, 1.0).astype(F32)
-    cosine = jnp.tile(jnp.cos(angles), (micro, lanes))
-    sine = jnp.tile(jnp.sin(angles), (micro, lanes)) * sign
+    sign = np.where(np.arange(2 * HEAD_DIM) % HEAD_DIM < halfway, -1.0, 1.0)
+    tables = np.stack([np.tile(np.cos(angles), lanes), np.tile(np.sin(angles), lanes) * sign])
+    tables = lax.dynamic_slice_in_dim(jnp.asarray(tables, F32), dp * rows, rows, axis=1)
 
     tokens_flat = tokens.reshape(every, width)
     gain_one = first_gain.reshape(1, width)
     normed_one, query_rot, key_rot, value_own = project(
-        tokens_flat, gain_one, cosine, sine, w_query, w_key, w_value
+        tokens_flat, gain_one, tables, w_query, w_key, w_value
     )
 
     ids = jnp.arange(128, dtype=jnp.int32)
@@ -1367,28 +1483,29 @@
     lower = (ids[None, None, :] < segments[:, 0, :, None]).astype(F32)
     starts = jnp.sum(lower * totals[:, None, :], axis=2).astype(jnp.int32)
     starts = starts.reshape(every, 1)
-    attn_low, logs = attend(dp, starts, query_rot, key_all, value_all, micro, rows, nd)
-    residual = inputs + jnp.dot(attn_low, w_out, preferred_element_type=F32)
+    routing = routes.reshape(every, routes.shape[2])
+    hit = jnp.any(
+        jnp.arange(EXPERTS, dtype=jnp.int32)[:, None, None] == routing[None], axis=2
+    ).astype(F32)
+    attn_low, logs, residual, normed_two, gate_probs, normed_all, marked_all = attend(
+        starts,
+        query_rot,
+        key_all,
+        value_all,
+        tokens_flat,
+        w_out,
+        second_gain.reshape(1, width),
+        w_router.T,
+        hit,
+        micro,
+        rows,
+        ne,
+        1,
+    )
     inv_two = rms_scale(residual)
-    normed_two = (residual * inv_two * second_gain).astype(BF16)
-    logits = jnp.dot(normed_two, w_router, preferred_element_type=F32)
-    routing = routes.reshape(every, routes.shape[2])
-    chosen = jnp.any(
-        routing[:, :, None] == jnp.arange(EXPERTS, dtype=jnp.int32)[None, None, :], axis=1
-    )
-    masked = jnp.where(chosen, logits, MASKED)
-    terms = jnp.where(chosen, jnp.exp(masked - jnp.max(masked, axis=1, keepdims=True)), 0.0)
-    gate_probs = terms / jnp.sum(terms, axis=1, keepdims=True)
-    marked = jnp.where(chosen, gate_probs, -1.0).T
-
-    normed_all, marked_all = gather(ne, nd, (), (normed_two, marked), 1, 38)
     here = EXPERTS // ne
-    probs_here = lax.dynamic_slice_in_dim(marked_all, ep * here, here, axis=1)
-    probs_here = (
-        probs_here.reshape(ne, here, micro, rows)
-        .transpose(0, 2, 1, 3)
-        .reshape(ne * micro, here, rows)
-    )
+    probs_here = lax.dynamic_slice_in_dim(marked_all, ep * here, here, axis=2)
+    probs_here = probs_here.reshape(ne * micro, here, rows)
     nb = bit_count(nd)
     orders = [order[:-1][::-1] for order in gather_orders(nd)]
     mix, grad_in, pair_dots, *grads = experts(
@@ -1418,15 +1535,15 @@
         40,
     )
     grads_last, grads_head = grads[:2], grads[2:]
-    pair_dot = dots_all.reshape(EXPERTS, every).T
+    pair_dot = dots_all.reshape(EXPERTS, every)
     grad_logits = gate_probs * (
-        pair_dot - jnp.sum(gate_probs * pair_dot, axis=1, keepdims=True)
+        pair_dot - jnp.sum(gate_probs * pair_dot, axis=0, keepdims=True)
     )
     grad_w_router = jnp.einsum(
-        "td,te->de", normed_two.astype(F32), grad_logits, precision=HIGHEST
+        "td,et->de", normed_two.astype(F32), grad_logits, precision=HIGHEST
     )
     grad_normed_two = (
-        jnp.einsum("te,de->td", grad_logits, w_router.astype(F32), precision=HIGHEST)
+        jnp.einsum("et,de->td", grad_logits, w_router.astype(F32), precision=HIGHEST)
         + grad_back.astype(F32)
     )
     scaled_two = grad_normed_two * second_gain
@@ -1450,8 +1567,7 @@
         value_all,
         logs,
         grad_attn,
-        cosine,
-        sine,
+        tables,
         [(kept[i], orders[i][1:], landed[i]) for i in range(2)] if more else [],
         micro,
         rows,
@@ -1486,8 +1602,7 @@
         full,
         normed_one,
         (grad_query, grad_key, grad_value),
-        cosine,
-        sine,
+        tables,
         tokens_flat,
         gain_one,
         grad_residual,

time: 354 us -> 348 us (0.983)
  Pallas kernels: 321 us -> 315 us
    pallas_call x2 -> x1, Pallas kernels: 64.8 us -> 23 us  [gather(): pl.pallas_call(functools.partial(gather_body, ne, nd, len(dp_arrays), len...]
    pallas_call x1, Pallas kernels: 11.5 us -> 48.8 us  [attend(): pl.pallas_call(functools.partial(attend_body, nd // 2 + 1, ne, nd, micro)...]
  transfers between devices with their start and end apart: 3 -> 3, of which waited for: 0 -> 0; matrix products, arithmetic and copies ran while one was open for 3% -> 2% of each run, Pallas kernels for 23% -> 22%
where the time goes in v9:
time: 348 us; the launch traced here: 344 us
  Pallas kernels  315 us (91%)
  local copies, waits for them, and re-layouts  10.6 us (3%)
  matrix products  6.71 us (2%)
  other arithmetic  5.96 us (2%)
  starting transfers between devices  5.57 us (2%)
    pallas_call x1, Pallas kernels, experts(): pl.pallas_call(functools.partial(expert_body, ne, nd, micro, rows), grid=...  81.7 us
    pallas_call x2, Pallas kernels, reduce(): pl.pallas_call(functools.partial(reduce_body, ne, nd, kinds, line_parts,...  75.5 us
    pallas_call x1, Pallas kernels, finish(): pl.pallas_call(functools.partial(finish_body, ne, nd, tuple(map(tuple, or...  50.3 us
    pallas_call x1, Pallas kernels, attend(): pl.pallas_call(functools.partial(attend_body, nd // 2 + 1, ne, nd, micro)...  48.8 us
    pallas_call x1, Pallas kernels, attend_back(): pl.pallas_call(functools.partial(attend_back_body, nd // 2 + 1, ne, nd, t...  23.1 us
    pallas_call x1, Pallas kernels, gather(): pl.pallas_call(functools.partial(gather_body, ne, nd, len(dp_arrays), len...  23 us
    pallas_call x1, Pallas kernels, results(): pl.pallas_call(functools.partial(results_body, share, n_out, len(grads[0]...  7 us
  transfers between devices with their start and end apart: 3, of which 0 were waited for; matrix products, arithmetic and copies ran while one was open for 2% of the time, Pallas kernels for 22%

profile of v9, /device:TPU:10, one launch (start us, length us, event | category | flops | bytes accessed | tf_op | source)
XLA Modules:
  0.0 344.4 jit_solution(16966078972117569721)
XLA Ops:
  1.1 2.6 collective-permute-start.1
  3.7 2.5 collective-permute-start
  7.6 1.6 constant_dynamic-slice_fusion.1.tables_ref.refs_6_.refs_4_
  9.2 5.4 %shard_map.238 = (bf16[256,1024]{1,0:T(8,128)(2,1)}, bf16[256,1024]{1,0:T(8,128)(2,1)}, bf16[256,512]{1,0:T(8,128)(2,1)}, bf16[256,512]{1,0:T(8,128)(2,1)}) custom-call(bf16[256,1024]{1,0:T(8,128)(2,1)} %bitcast.43, f32[1,1024]{1,0:T(1,128)} %bitcast.60, f32[2,128,128]{2,1,0:T(8,128)} %constant_dynamic-slice_fusion.1.tables_ref.refs_6_.refs_4_, ...), custom_call_target="tpu_custom_call" | custom-call | bytes 15000000 | tf_op jit(solution)/shard_map/pallas_call | solution.py:777
  14.6 23.0 %shard_map.239 = (bf16[8,256,512]{2,1,0:T(8,128)(2,1)}, bf16[8,256,512]{2,1,0:T(8,128)(2,1)}, f32[8,8,128]{2,1,0:T(8,128)}) custom-call(bf16[256,512]{1,0:T(8,128)(2,1)} %get-tuple-element.69.refs_0_, bf16[256,512]{1,0:T(8,128)(2,1)} %get-tuple-element.70.refs_1_, f32[8,128]{1,0:T(8,128)} %concatenate.12.refs_2_), custom_call_target="tpu_custom_call" | custom-call | bytes 75000000 | tf_op jit(solution)/shard_map/pallas_call | solution.py:167
  39.4 0.8 copy.34.refs_0_
  40.2 48.8 %shard_map.240 = (bf16[256,1024]{1,0:T(8,128)(2,1)}, f32[2,4,512,1]{3,2,1,0:T(8,128)}, f32[256,1024]{1,0:T(8,128)}, bf16[256,1024]{1,0:T(8,128)(2,1)}, f32[32,25...) custom-call(s32[256,1]{1,0:T(8,128)} %copy.34.refs_0_, ...), custom_call_target="tpu_custom_call" | custom-call | bytes 150000000 | tf_op jit(solution)/shard_map/pallas_call | solution.py:976
  89.1 1.4 constant_dynamic-slice_fusion
  90.4 1.4 multiply_reduce_fusion.2
  93.0 81.7 %shard_map.241 = (bf16[1024,1024]{1,0:T(8,128)(2,1)}, bf16[1024,1024]{1,0:T(8,128)(2,1)}, f32[8,8,128]{2,1,0:T(8,128)}, bf16[2,3,384,512]{3,2,1,0:T(8,128)(2,1)}...) custom-call(bf16[256,1024]{1,0:T(8,128)(2,1)} %bitcast.49, ...), custom_call_target="tpu_custom_call" | custom-call | bytes 225000000 | tf_op jit(solution)/shard_map/pallas_call | solution.py:681
  176.1 46.5 %shard_map.242 = (bf16[384,512]{1,0:T(8,128)(2,1)}, bf16[384,512]{1,0:T(8,128)(2,1)}, bf16[1,384,512]{2,1,0:T(8,128)(2,1)}, bf16[1,384,512]{2,1,0:T(8,128)(2,1)}...) custom-call(bf16[4,384,512]{2,1,0:T(8,128)(2,1)} %get-tuple-element.80.refs_0_, ...), custom_call_target="tpu_custom_call" | custom-call | bytes 120000000 | tf_op jit(solution)/shard_map/pallas_call | solution.py:419
  222.7 0.9 fusion.3
  223.6 1.1 convolution_convert_fusion.2
  224.9 2.0 multiply_reduce_fusion
  226.9 1.1 concatenate.16
  228.4 1.2 copy-done.2
  229.6 1.5 convolution_convert_fusion.1.refs_5_
  231.2 2.1 convolution_convert_fusion
  233.2 23.1 %shard_map.243 = (bf16[256,1024]{1,0:T(8,128)(2,1)}, bf16[8,256,512]{2,1,0:T(8,128)(2,1)}, bf16[8,256,512]{2,1,0:T(8,128)(2,1)}, bf16[2,384,512]{2,1,0:T(8,128)(2,1)}, bf16[2,384,512]{2,1,0:T(8,128)(2,1)}) custom-call(s32[256,1]{1,0:T(8,128)} %copy.34.refs_0_, bf16[256,1024]{1,0:T(8,128)(2,1)} %get-tuple-element.72.refs_1_, ...), custom_call_target="tpu_custom_call" | custom-call | bytes 75000000 | tf_op jit(solution)/shard_map/pallas_call | solution.py:1089
  256.3 28.9 %shard_map.244 = (bf16[256,512]{1,0:T(8,128)(2,1)}, bf16[256,512]{1,0:T(8,128)(2,1)}, bf16[128,1024]{1,0:T(8,128)(2,1)}) custom-call(bf16[8,256,512]{2,1,0:T(8,128)(2,1)} %get-tuple-element.90.refs_0_, bf16[8,256,512]{2,1,0:T(8,128)(2,1)} %get-tuple-element.91.refs_1_, bf16[4,256,1024]{2,1,0:T(8,128)(2,1)} %bitcast.40), custom_call_target="tpu_custom_call" | custom-call | bytes 90000000 | tf_op jit(solution)/shard_map/pallas_call | solution.py:419
  285.3 0.9 maximum_maximum_fusion.refs_12_
  286.2 50.3 %shard_map.245 = (f32[256,1024]{1,0:T(8,128)}, bf16[32,512]{1,0:T(8,128)(2,1)}, bf16[32,512]{1,0:T(8,128)(2,1)}, bf16[32,512]{1,0:T(8,128)(2,1)}, bf16[32,512]{1...) custom-call(bf16[256,1024]{1,0:T(8,128)(2,1)} %get-tuple-element.94., ...), custom_call_target="tpu_custom_call" | custom-call | bytes 135000000 | tf_op jit(solution)/shard_map/pallas_call | solution.py:1310
  336.4 7.0 %shard_map.246 = (bf16[256,1024]{1,0:T(8,128)(2,1)}, f32[32,1024]{1,0:T(8,128)}, f32[32,1024]{1,0:T(8,128)}, f32[32,512]{1,0:T(8,128)}, f32[32,512]{1,0:T(8,128)...) custom-call(f32[256,1024]{1,0:T(8,128)} %get-tuple-element.75.refs_0, ...), custom_call_target="tpu_custom_call" | custom-call | bytes 18000000 | tf_op jit(solution)/shard_map/pallas_call | solution.py:1419
  343.5 1.0 copy.42
  (53 shorter events, 6.8 us)
Async XLA Ops:
  0.6 91.2 %collective-permute-start.2 = (bf16[256,1024]{1,0:T(8,128)(2,1)}, bf16[256,1024]{1,0:T(8,128)(2,1)S(1)}, u32[]{:S(2)}, u32[]{:S(2)}) collective-permute-start(bf16[256,1024]{1,0:T(8,128)(2,1)} %bitcast.46), channel_id=1, source_target_pairs={{0,24},{8,0},{16,8},{24,16},{1,25},{9,1},{17,9},{25,17},{2,26},{10... | collective-permute-start | bytes 1572872 | tf_op jit(solution)/shard_map/ppermute | solution.py:1477
  1.1 90.7 %collective-permute-start.1 = (bf16[256,1024]{1,0:T(8,128)(2,1)}, bf16[256,1024]{1,0:T(8,128)(2,1)S(1)}, u32[]{:S(2)}, u32[]{:S(2)}) collective-permute-start(bf16[256,1024]{1,0:T(8,128)(2,1)} %bitcast.47), channel_id=1, source_target_pairs={{0,16},{8,24},{16,0},{24,8},{1,17},{9,25},{17,1},{25,9},{2,18},{10... | collective-permute-start | bytes 1572872 | tf_op jit(solution)/shard_map/ppermute | solution.py:1477
  3.7 88.1 %collective-permute-start = (bf16[256,1024]{1,0:T(8,128)(2,1)}, bf16[256,1024]{1,0:T(8,128)(2,1)S(1)}, u32[]{:S(2)}, u32[]{:S(2)}) collective-permute-start(bf16[256,1024]{1,0:T(8,128)(2,1)} %bitcast.48), channel_id=1, source_target_pairs={{0,8},{8,16},{16,24},{24,0},{1,9},{9,17},{17,25},{25,1},{2,10},{10... | collective-permute-start | bytes 1572872 | tf_op jit(solution)/shard_map/ppermute | solution.py:1477
  9.2 29.2 %copy-start.16 = (s32[2,1,128]{2,1,0:T(1,128)S(1)}, s32[2,1,128]{2,1,0:T(1,128)}, u32[]{:S(2)}) copy-start(s32[2,1,128]{2,1,0:T(1,128)} %param.16) | copy-start | bytes 3076
  9.2 29.3 %copy-start.15 = (s32[2,128,8]{1,2,0:T(8,128)S(1)}, s32[2,128,8]{1,2,0:T(8,128)}, u32[]{:S(2)}) copy-start(s32[2,128,8]{1,2,0:T(8,128)} %param.17) | copy-start | bytes 24580
  91.8 0.8 copy-start.7
  91.9 0.9 copy-start.8
  91.9 1.1 copy-start.9
  176.1 46.6 %copy-start.12 = (f32[32,256]{1,0:T(8,128)S(1)}, f32[32,256]{1,0:T(8,128)}, u32[]{:S(2)}) copy-start(f32[32,256]{1,0:T(8,128)} %get-tuple-element.77) | copy-start | bytes 98308
  176.1 47.5 %copy-start.11 = (bf16[256,1024]{1,0:T(8,128)(2,1)S(1)}, bf16[256,1024]{1,0:T(8,128)(2,1)}, u32[]{:S(2)}) copy-start(bf16[256,1024]{1,0:T(8,128)(2,1)} %get-tuple-element.99) | copy-start | bytes 1572868
  176.1 48.8 %copy-start = (f32[256,1024]{1,0:T(8,128)S(1)}, f32[256,1024]{1,0:T(8,128)}, u32[]{:S(2)}) copy-start(f32[256,1024]{1,0:T(8,128)} %get-tuple-element.75.refs_0_) | copy-start | bytes 3145732
  176.1 48.8 %copy-start.13 = (bf16[1024,32]{0,1:T(8,128)(2,1)S(1)}, bf16[1024,32]{0,1:T(8,128)(2,1)}, u32[]{:S(2)}) copy-start(bf16[1024,32]{0,1:T(8,128)(2,1)} %param.24) | copy-start | bytes 196612
  176.1 48.8 %copy-start.14 = (f32[1024]{0:T(1024)S(1)}, f32[1024]{0:T(1024)}, u32[]{:S(2)}) copy-start(f32[1024]{0:T(1024)} %param.23) | copy-start | bytes 12292
  222.7 5.4 %copy-start.3 = (bf16[2,128,1024]{2,1,0:T(8,128)(2,1)S(1)}, bf16[2,128,1024]{2,1,0:T(8,128)(2,1)}, u32[]{:S(2)}) copy-start(bf16[2,128,1024]{2,1,0:T(8,128)(2,1)} %param.28) | copy-start | bytes 1572868
  222.7 5.4 %copy-start.4 = (bf16[256,1024]{1,0:T(8,128)(2,1)S(1)}, bf16[256,1024]{1,0:T(8,128)(2,1)}, u32[]{:S(2)}) copy-start(bf16[256,1024]{1,0:T(8,128)(2,1)} %get-tuple-element.89) | copy-start | bytes 1572868
  228.0 1.6 copy-start.2
  229.6 3.6 %copy-start.1 = (f32[256,1024]{1,0:T(8,128)}, f32[256,1024]{1,0:T(8,128)S(1)}, u32[]{:S(2)}) copy-start(f32[256,1024]{1,0:T(8,128)S(1)} %multiply_subtract_fusion.refs_7_) | copy-start | bytes 3145732
  229.6 1.6 copy-start.10
  256.3 29.0 %copy-start.6 = (bf16[4,8,32,1]{3,2,1,0:T(8,128)(2,1)S(1)}, bf16[4,8,32,1]{3,2,1,0:T(8,128)(2,1)}, u32[]{:S(2)}) copy-start(bf16[4,8,32,1]{3,2,1,0:T(8,128)(2,1)} %concatenate.16) | copy-start | bytes 6148
  336.4 7.0 %copy-start.5 = (f32[256,1024]{1,0:T(8,128)S(1)}, f32[256,1024]{1,0:T(8,128)}, u32[]{:S(2)}) copy-start(f32[256,1024]{1,0:T(8,128)} %get-tuple-element.115) | copy-start | bytes 3145732

commit v10 on v9

--- a/solution.py
+++ b/solution.py
@@ -449,8 +449,8 @@
     normed_ref, probs_ref, gate_ref, up_ref, down_ref = refs[:5]
     mix_ref, grad_ref, dots_ref = refs[5:8]
     kept, landed, whole = refs[8:10], refs[10:12], refs[12:14]
-    rows_in, cots_in, picks, first, second, sides, arrived, leaving = refs[14:22]
-    load_sem, store_sem, send_sem, recv_sem, free_sem, far_send, far_recv = refs[22:]
+    rows_in, cots_in, picks, first, second, chances, sides, arrived, leaving = refs[14:23]
+    load_sem, store_sem, send_sem, recv_sem, free_sem, far_send, far_recv = refs[23:]
     e = pl.program_id(0)
     last = pl.num_programs(0) - 1
     ep, dp = lax.axis_index("ep"), lax.axis_index("dp")
@@ -467,7 +467,14 @@
         return remote(send, arrived, send_sem, recv_sem, other)
 
     def loads():
-        out = [pltpu.make_async_copy(normed_ref, first, load_sem.at[ne])]
+        out = [
+            pltpu.make_async_copy(normed_ref, first, load_sem.at[ne]),
+            pltpu.make_async_copy(
+                probs_ref.at[:, pl.ds(pl.multiple_of(ep * n_exp, n_exp), n_exp)],
+                chances,
+                load_sem.at[ne + 1],
+            ),
+        ]
         for k in range(ne):
             at = pl.multiple_of(lax.rem(ep - k + ne, ne) * every, every)
             out.append(
@@ -502,42 +509,45 @@
             {"dp": jnp.bitwise_xor(dp, 1 << first_bits(nd)[i])},
         )
 
-    def last_copy():
-        return pltpu.make_async_copy(keep, whole[1], load_sem.at[0])
+    def last_copy(k):
+        return pltpu.make_async_copy(keep, whole[k], load_sem.at[k])
 
     def collect():
         exchange().wait_recv()
-        pieces = sides.shape[1]
-        n = (e - 1) // 2
-        for i, bit in enumerate(first_bits(nd)):
-            mine = jnp.bitwise_and(lax.shift_right_logical(dp, bit), 1)
-
-            def piece(at, side, bit=bit):
+        pieces, height, slots = sides.shape[1], leaving.shape[3], leaving.shape[1]
+        n = e - 1
+        early = n_exp - 2
+
+        @pl.when(n < early)
+        def _():
+            @pl.when(n >= slots)
+            def _():
+                for i in range(2):
+                    far(i, n - slots).wait_send()
+
+            def piece(i, at, other_side):
+                bit = first_bits(nd)[i]
+                mine = jnp.bitwise_and(lax.shift_right_logical(dp, bit), 1)
+                side = 1 - mine if other_side else mine
                 low = (1 << (bit - 1)) - 1
                 j = ((at & ~low) << 1 | (at & low)) + (side << (bit - 1))
-                return (keep[j].astype(F32) + arrived[j].astype(F32)).astype(BF16)
-
-            @pl.when((lax.rem(e - 1, 2) == i) & (n < n_exp // 2 - 1))
-            def _(i=i, mine=mine, piece=piece):
-                slots = leaving.shape[1]
-
-                @pl.when(n >= slots)
-                def _():
-                    far(i, n - slots).wait_send()
-
+                part = slice(i * height, (i + 1) * height)
+                return (keep[j, part].astype(F32) + arrived[j, part].astype(F32)).astype(BF16)
+
+            for i in range(2):
                 for at in range(pieces // 2):
-                    leaving[i, lax.rem(n, slots), at] = piece(at, 1 - mine)
+                    leaving[i, lax.rem(n, slots), at] = piece(i, at, True)
                 far(i, n).start()
+            for i in range(2):
                 for at in range(pieces // 2):
-                    kept[i][at, 0] = piece(at, mine)
-
-            @pl.when((lax.rem(e - 1, 2) == i) & (n == n_exp // 2 - 1))
-            def _(i=i):
+                    kept[i][at, 0] = piece(i, at, False)
+
+        for k in range(2):
+
+            @pl.when(n == early + k)
+            def _(k=k):
                 add_into(keep, arrived)
-                if i == 0:
-                    whole[0][...] = keep[...]
-                else:
-                    last_copy().start()
+                last_copy(k).start()
 
     @pl.when(e == 0)
     def _():
@@ -563,7 +573,7 @@
         @pl.loop(0, blocks)
         def _(s):
             at = block_at(s)
-            probs = probs_ref[s]
+            probs = chances[s]
             hit = probs >= 0.0
             rank = dot(hit.astype(BF16), earlier)
             rank = jnp.where(hit, rank, -1.0).astype(jnp.int32)
@@ -579,16 +589,22 @@
         x = rows_in[:, e].reshape(blocks * CAP, width)
         c = cots_in[:, e].reshape(blocks * CAP, width)
         flat = picks[:, pl.ds(pl.multiple_of(e * CAP, CAP), CAP), :].astype(F32)
-        p = jnp.sum(flat * probs_ref[:, pl.ds(e, 1), :], axis=2, keepdims=True)
+        p = jnp.sum(flat * chances[:, pl.ds(e, 1), :], axis=2, keepdims=True)
         p = p.reshape(blocks * CAP, 1)
         w_gate, w_up, w_down = gate_ref[0], up_ref[0], down_ref[0]
         gate_pre = dot(x, w_gate)
         up_pre = dot(x, w_up)
+        back = dot(c, w_down, ((1,), (1,)))
+
+        @pl.when(e > 0)
+        def _():
+            collect()
+            pl.semaphore_signal(free_sem, inc=1, device_id=other, device_id_type=MESH)
+
         sigma = jax.nn.sigmoid(gate_pre)
         silu = gate_pre * sigma
         hidden = (silu * up_pre).astype(BF16)
         out = dot(hidden, w_down) * p
-        back = dot(c, w_down, ((1,), (1,)))
         wide = hidden.astype(F32)
         pair = jnp.sum(wide * back, axis=1, keepdims=True)
         back = back * p
@@ -596,15 +612,17 @@
         grad_gate = (back * up_pre * (sigma * (1.0 + gate_pre * (1.0 - sigma)))).astype(BF16)
         scaled = (wide * p).astype(BF16)
         grad_x = dot(grad_gate, w_gate, ((1,), (1,))) + dot(grad_up, w_up, ((1,), (1,)))
-
-        dots_ref[0] = jnp.sum(flat * pair.reshape(blocks, CAP, 1), axis=1)
+        pair = jnp.sum(flat * pair.reshape(blocks, CAP, 1), axis=1)
+        dots_ref[:, 0] = pair.reshape(ne, micro, rows)
 
         @pl.when(e > 0)
         def _():
-            collect()
-            pl.semaphore_signal(free_sem, inc=1, device_id=other, device_id_type=MESH)
             exchange().wait_send()
             pl.semaphore_wait(free_sem, 1)
+
+        @pl.when(e == n_exp - 1)
+        def _():
+            last_copy(0).wait()
 
         def split(value, offset):
             value = value.astype(BF16)
@@ -649,12 +667,13 @@
             for copy in stores(t):
                 copy.wait()
 
-        last_copy().wait()
+        last_copy(1).wait()
+        early, slots = n_exp - 2, leaving.shape[1]
         for i in range(2):
-            for n in range(max(n_exp // 2 - 1 - leaving.shape[1], 0), n_exp // 2 - 1):
+            for n in range(max(early - slots, 0), early):
                 far(i, n).wait_send()
 
-            @pl.loop(0, n_exp // 2 - 1)
+            @pl.loop(0, early)
             def _(n, i=i):
                 far(i, n).wait_recv()
 
@@ -669,37 +688,44 @@
     half = nd // 2
     packed = 2 * width // nd + (inner // nd) * (width // inner)
     full = (blocks * rows, width)
-    one = pl.Buffered(1)
     weight = lambda e: (jnp.minimum(e, n_exp - 1), 0, 0)
-    early = n_exp // 2 - 1
-    part = (half // 2, early, packed, inner)
+    early = n_exp - 2
+    part = (half // 2, early, packed // 2, inner)
     kept = pl.BlockSpec(
-        (half // 2, 1, packed, inner),
-        lambda e: (0, jnp.minimum(jnp.maximum(e - 1, 0) // 2, early - 1), 0, 0),
+        (half // 2, 1, packed // 2, inner), lambda e: (0, jnp.clip(e - 1, 0, early - 1), 0, 0)
     )
     last = (half, packed, inner)
     return pl.pallas_call(
         functools.partial(expert_body, ne, nd, micro, rows),
         grid=(n_exp + 1,),
-        in_specs=[ANY] * (ne + 1)
+        in_specs=[ANY] * (ne + 2)
         + [
-            pl.BlockSpec(probs.shape, lambda e: (0, 0, 0), pipeline_mode=one),
             pl.BlockSpec((1, width, inner), weight),
             pl.BlockSpec((1, width, inner), weight),
             pl.BlockSpec((1, inner, width), weight),
         ],
-        out_specs=[ANY, ANY, pl.BlockSpec((1, blocks, rows), weight), kept, kept, ANY, ANY]
-        + [pl.BlockSpec(last, lambda e: (0, 0, 0), pipeline_mode=one), ANY],
+        out_specs=[
+            ANY,
+            ANY,
+            pl.BlockSpec((ne, 1, micro, rows), lambda e: (0, jnp.minimum(e, n_exp - 1), 0, 0)),
+            kept,
+            kept,
+            ANY,
+            ANY,
+            ANY,
+            ANY,
+        ],
         scratch_shapes=[
             pltpu.VMEM((blocks, n_exp, CAP, width), BF16),
             pltpu.VMEM((blocks, n_exp, CAP, width), BF16),
             pltpu.VMEM((blocks, n_exp * CAP, rows), BF16),
             pltpu.VMEM(full, BF16),
             pltpu.VMEM(full, BF16),
+            pltpu.VMEM((blocks, n_exp, rows), F32),
             pltpu.VMEM((2, half, packed, inner), BF16),
             pltpu.VMEM((half, packed, inner), BF16),
-            pltpu.VMEM((2, min(early, 2), half // 2, packed, inner), BF16),
-            DMA((ne + 1,)),
+            pltpu.VMEM((2, 2 if early > 2 else 1, half // 2, packed // 2, inner), BF16),
+            DMA((ne + 2,)),
             DMA((2, blocks)),
             DMA,
             DMA,
@@ -710,12 +736,12 @@
         out_shape=[
             jax.ShapeDtypeStruct(full, BF16),
             jax.ShapeDtypeStruct(full, BF16),
-            jax.ShapeDtypeStruct((n_exp, blocks, rows), F32),
+            jax.ShapeDtypeStruct((ne, n_exp, micro, rows), F32),
         ]
         + [jax.ShapeDtypeStruct(part, BF16)] * 4
         + [jax.ShapeDtypeStruct(last, BF16)] * 2,
         compiler_params=pltpu.CompilerParams(
-            vmem_limit_bytes=62 * 2**20,
+            vmem_limit_bytes=63 * 2**20,
             dimension_semantics=("arbitrary",),
             collective_id=collective,
             has_side_effects=True,
@@ -1003,17 +1029,20 @@
     )(starts, queries, keys, values, tokens, w_out, gain, router, hit)
 
 
-def attend_back_body(span, ne, nd, orders, *refs):
+def attend_back_body(span, ne, nd, micro, skip, orders, *refs):
     refs = list(refs)
 
     def take(n):
         return [refs.pop(0) for _ in range(n)]
 
-    starts_ref, q_ref, k_ref, v_ref, log_ref, g_ref, tables_ref = take(7)
+    starts_ref, q_ref, k_ref, v_ref, log_ref, tables_ref = take(6)
+    cot_ref, dots_ref, probs_ref, grad_ref, residual_ref, gain_ref, normed_ref, attn_ref = take(8)
+    wo_ref, router_ref = take(2)
     n = len(orders)
     sources, extras = take(n), take(n)
-    dq_ref, dk_ref, dv_ref = take(3)
+    dq_ref, dk_ref, dv_ref, res_out, wo_out, router_out, gain_out = take(7)
     outs = take(n)
+    (grads,) = take(1)
     held, more, landing = take(n), take(n), take(n)
     load_sem, out_sem, send_sem, recv_sem = refs
     ep, dp = lax.axis_index("ep"), lax.axis_index("dp")
@@ -1021,7 +1050,7 @@
     final = pl.num_programs(0) * pl.num_programs(1) - 1
     sums = []
     for a in range(n):
-        part = pl.ds(1, sources[a].shape[1] - 1)
+        part = pl.ds(skip, sources[a].shape[1] - skip)
         loads = [
             pltpu.make_async_copy(src.at[:, part], dst, load_sem.at[a, i])
             for i, (src, dst) in enumerate(((sources[a], held[a]), (extras[a], more[a])))
@@ -1038,10 +1067,41 @@
         greet(ep, dp, ne, nd)
         for each in sums:
             each.step(0)
+        rows = q_ref.shape[0]
+        pairs = [dots_ref[:, :, m, :].reshape(-1, rows) for m in range(micro)]
+        pair = jnp.concatenate(pairs, axis=1)
+        probs = probs_ref[...]
+        grad_logits = probs * (pair - jnp.sum(probs * pair, axis=0, keepdims=True))
+        high = grad_logits.astype(BF16)
+        low = (grad_logits - high.astype(F32)).astype(BF16)
+        normed = normed_ref[...]
+        router_out[...] = dot(high, normed) + dot(low, normed)
+        router = router_ref[...]
+        grad_normed = (
+            grad_ref[...].astype(F32)
+            + dot(high, router, ((0,), (0,)))
+            + dot(low, router, ((0,), (0,)))
+        )
+        residual = residual_ref[...]
+        r = rms_scale(residual)
+        gain_out[...] = jnp.sum(grad_normed * residual * r, axis=0, keepdims=True)
+        scaled = grad_normed * gain_ref[...]
+        mean = jnp.mean(scaled * residual, axis=1, keepdims=True)
+        grad_residual = cot_ref[...].astype(F32) + r * scaled - residual * (r * r * r) * mean
+        res_out[...] = grad_residual
+        low_res = grad_residual.astype(BF16)
+        tile = 256
+        for c in range(0, wo_out.shape[1], tile):
+            wo_out[:, c : c + tile] = dot(
+                attn_ref[...], low_res[:, c : c + tile], ((0,), (0,))
+            ).astype(BF16)
+        for c in range(0, wo_ref.shape[0], tile):
+            grads[c // tile] = dot(low_res, wo_ref[c : c + tile, :], ((1,), (1,))).astype(BF16)
 
     rows = q_ref.shape[0]
     q = spread(q_ref[...].astype(F32) * SCALE).astype(BF16)
-    g = spread(g_ref[...].astype(F32)).astype(BF16)
+    mine = pl.ds(pl.multiple_of(pl.program_id(0) * rows, rows), rows)
+    g = spread(grads[pl.program_id(1), mine, :].astype(F32)).astype(BF16)
     k, v = in_window(k_ref, dp, span), in_window(v_ref, dp, span)
     scores = window_scores(dp, span, rows, starts_ref, q, k)
     probs = jnp.exp(scores - log_ref[0, 0])
@@ -1077,43 +1137,81 @@
 
 
 def attend_back(
-    starts, queries, keys, values, logs_in, grad, tables, sums, micro, rows, ne, collective
+    starts,
+    queries,
+    keys,
+    values,
+    logs_in,
+    tables,
+    cot,
+    dots,
+    probs,
+    grad_normed,
+    residual,
+    gain,
+    normed,
+    attn,
+    w_out,
+    router,
+    sums,
+    skip,
+    collective,
 ):
-    nd = keys.shape[0]
+    nd, ne, micro, rows = keys.shape[0], dots.shape[0], dots.shape[2], dots.shape[3]
+    every, width = residual.shape
     grid, mine, theirs, column, logs, _ = attention_specs(micro, rows, nd)
-    table = pl.BlockSpec(tables.shape, lambda m, h: (0, 0, 0))
+    one = pl.Buffered(1)
+    whole = lambda v: pl.BlockSpec(v.shape, lambda m, h: (0,) * len(v.shape), pipeline_mode=one)
     n = len(sums)
-    shapes = [(v.shape[0], v.shape[1] - 1) + v.shape[2:] for v, _, _ in sums]
+    shapes = [(v.shape[0], v.shape[1] - skip) + v.shape[2:] for v, _, _ in sums]
     deep = max([s[0] - 1 for s in shapes] + [1])
     some = max(n, 1)
+    before = [cot, dots, probs, grad_normed, residual, gain, normed, attn, w_out, router]
+    after = [
+        jax.ShapeDtypeStruct((every, width), F32),
+        jax.ShapeDtypeStruct(w_out.shape, BF16),
+        jax.ShapeDtypeStruct(router.shape, F32),
+        jax.ShapeDtypeStruct((1, width), F32),
+    ]
+    tile = 4 * HEAD_DIM
     return pl.pallas_call(
         functools.partial(
-            attend_back_body, nd // 2 + 1, ne, nd, tuple(tuple(order) for _, order, _ in sums)
+            attend_back_body,
+            nd // 2 + 1,
+            ne,
+            nd,
+            micro,
+            skip,
+            tuple(tuple(order) for _, order, _ in sums),
         ),
         grid=grid,
-        in_specs=[column, mine, theirs, theirs, logs, mine, table] + [ANY] * (2 * n),
-        out_specs=[mine, theirs, theirs] + [ANY] * n,
+        in_specs=[column, mine, theirs, theirs, logs, whole(tables)]
+        + [whole(v) for v in before]
+        + [ANY] * (2 * n),
+        out_specs=[mine, theirs, theirs] + [whole(v) for v in after] + [ANY] * n,
         out_shape=[
             jax.ShapeDtypeStruct(queries.shape, BF16),
             jax.ShapeDtypeStruct(keys.shape, BF16),
             jax.ShapeDtypeStruct(values.shape, BF16),
         ]
+        + after
         + [jax.ShapeDtypeStruct(s[1:], BF16) for s in shapes],
-        scratch_shapes=[pltpu.VMEM(s, BF16) for s in shapes] * 2
+        scratch_shapes=[pltpu.VMEM((w_out.shape[0] // tile, every, tile), BF16)]
+        + [pltpu.VMEM(s, BF16) for s in shapes] * 2
         + [pltpu.VMEM((s[0] - 1,) + s[1:], BF16) for s in shapes]
         + [DMA((some, 2)), DMA((some,)), DMA((some, deep)), DMA((some, deep))],
         compiler_params=pltpu.CompilerParams(
             vmem_limit_bytes=60 * 2**20, collective_id=collective, has_side_effects=True
         ),
-        cost_estimate=cost(25),
+        cost_estimate=cost(28),
     )(
         starts,
         queries,
         keys,
         values,
         logs_in,
-        grad,
         tables,
+        *before,
         *[v for v, _, _ in sums],
         *[extra for _, _, extra in sums],
     )
@@ -1125,8 +1223,8 @@
     def take(n):
         return [refs.pop(0) for _ in range(n)]
 
-    n_ref, dq_ref, dk_ref, dv_ref, tables_ref, tokens_ref, gain_ref = take(7)
-    res_ref, wq_ref, wk_ref, wv_ref, wo_ref, small_ref, mix_ref = take(7)
+    n_ref, dq_ref, dk_ref, dv_ref, tables_ref, tokens_ref, gain_ref, router_ref, gain_two = take(9)
+    res_ref, wq_ref, wk_ref, wv_ref, wo_ref, mix_ref = take(6)
     (tok_out,) = take(1)
     count = 2 * n_out + 3
     outs, (mix_out,) = take(count), take(1)
@@ -1144,11 +1242,10 @@
     sums = []
     for a in range(count):
         loads = []
-        if a < n_out or a == count - 1:
-            src = wo_ref if a < n_out else small_ref
-            at = pl.ds(a * columns if a < n_out else 0, held[a].shape[3])
+        if a < n_out:
+            at = pl.ds(a * columns, columns)
             loads = [
-                pltpu.make_async_copy(src.at[e, :, :, at], held[a].at[:, e], load_sem.at[a, e])
+                pltpu.make_async_copy(wo_ref.at[e, :, :, at], held[a].at[:, e], load_sem.at[a, e])
                 for e in range(ne)
             ]
         sums.append(
@@ -1173,7 +1270,6 @@
     mix_load.start()
     for copy in own:
         copy.start()
-    small.load()
     greet(ep, dp, ne, nd)
     turns = bit_count(nd)
 
@@ -1232,21 +1328,14 @@
     tok_out[...] = (
         res[...] + r * scaled - x * (r * r * r) * jnp.mean(scaled * x, axis=1, keepdims=True)
     )
-    term = back * x * r
-    high = term.astype(BF16)
-    low = (term - high.astype(F32)).astype(BF16)
-    ones = jnp.ones((x.shape[0], 128), BF16)
-    column = dot(high, ones, ((0,), (0,))) + dot(low, ones, ((0,), (0,)))
-    lane = lax.broadcasted_iota(jnp.int32, column.shape, 1)
-    column = jnp.where(lane == EXPERTS, column, 0.0)
-    for copy in small.loads:
-        copy.wait()
+    one_row = jnp.sum(back * x * r, axis=0, keepdims=True)
+    blank = jnp.zeros((held[-1].shape[3] - EXPERTS - 2, x.shape[1]), F32)
+    column = jnp.concatenate([router_ref[...], one_row, gain_two[...], blank], axis=0).T
     share = held[-1].shape[2]
     for e in range(ne):
         for d in range(nd):
             i = (e * nd + d) * share
-            held[-1][d, e] = (held[-1][d, e].astype(F32) + column[i : i + share]).astype(BF16)
-    small.loads = []
+            held[-1][d, e] = column[i : i + share].astype(BF16)
     steps([small], 0)
     steps(queries, 2)
     steps([small], 1)
@@ -1295,7 +1384,8 @@
     grad_residual,
     weights,
     w_out,
-    small,
+    router_grad,
+    gain_two_grad,
     mix,
     mix_rows,
 ):
@@ -1312,7 +1402,7 @@
         out_shape=[jax.ShapeDtypeStruct((rows, width), F32)]
         + [jax.ShapeDtypeStruct((share, c), BF16) for c in wide]
         + [jax.ShapeDtypeStruct(line[1:], BF16)],
-        in_specs=[VMEM] * 7 + [ANY] * 7,
+        in_specs=[VMEM] * 9 + [ANY] * 6,
         out_specs=[VMEM] + [ANY] * (count + 1),
         scratch_shapes=[pltpu.VMEM((nd, ne, share, c), BF16) for c in wide]
         + [pltpu.VMEM((nd - 1, ne, share, c), BF16) for c in wide]
@@ -1340,22 +1430,23 @@
         tables,
         tokens,
         gain,
+        router_grad,
+        gain_two_grad,
         grad_residual,
         *weights,
         split(w_out),
-        split(small),
         mix,
     )
 
 
-def results_body(share, n_out, per_path, *refs):
+def results_body(share, n_out, groups, *refs):
     refs = list(refs)
 
     def take(n):
         return [refs.pop(0) for _ in range(n)]
 
     residual_ref, mix_first, mix_rest = take(3)
-    paths = [take(per_path) for _ in range(2)]
+    halves = [take(groups) for _ in range(2)]
     dense = take(2 * n_out + 3)
     out_ref, d_out, d_query, d_key, d_value, router, gain_one, gain_two = take(8)
     gate, up, down = refs
@@ -1380,22 +1471,23 @@
         gain_two[...] = turned[EXPERTS + 1 : EXPERTS + 2]
 
     k = 0
-    for n in range(per_path):
-        for m in range(paths[0][n].shape[0]):
-            for i in range(2):
-
-                @pl.when(e == k)
-                def _(src=paths[i][n], m=m):
-                    gate[0] = src[m, :share].astype(F32)
-                    up[0] = src[m, share : 2 * share].astype(F32)
-                    piece, columns = down.shape[1], src.shape[2]
-                    for j in range(down.shape[2] // columns):
-                        at = 2 * share + j * piece
-                        down[0, :, j * columns : (j + 1) * columns] = src[
-                            m, at : at + piece
-                        ].astype(F32)
-
-                k += 1
+    for first, second in zip(*halves):
+        for m in range(first.shape[0]):
+
+            @pl.when(e == k)
+            def _(first=first, second=second, m=m):
+                over = first.shape[1] - share
+                gate[0] = first[m, :share].astype(F32)
+                up[0, :over] = first[m, share:].astype(F32)
+                up[0, over:] = second[m, : share - over].astype(F32)
+                piece, columns = down.shape[1], second.shape[2]
+                for j in range(down.shape[2] // columns):
+                    at = share - over + j * piece
+                    down[0, :, j * columns : (j + 1) * columns] = second[
+                        m, at : at + piece
+                    ].astype(F32)
+
+            k += 1
 
 
 def results(residual, mix, grads, dense, n_out, share, w_gate, w_down, nd, rows_share):
@@ -1446,12 +1538,9 @@
 ):
     micro, rows, width = tokens.shape
     ne, nd = lax.axis_size("ep"), lax.axis_size("dp")
-    ep, dp = lax.axis_index("ep"), lax.axis_index("dp")
-    groups = HEADS // KV_HEADS
+    dp = lax.axis_index("dp")
     kv_width = KV_HEADS * HEAD_DIM
     every = micro * rows
-    inputs = tokens.reshape(every, width).astype(F32)
-    grad_output = cotangent.reshape(every, width).astype(F32)
 
     halfway = HEAD_DIM // 2
     frequency = ROPE_BASE ** (-(np.arange(halfway) * 2.0 / HEAD_DIM))
@@ -1487,6 +1576,7 @@
     hit = jnp.any(
         jnp.arange(EXPERTS, dtype=jnp.int32)[:, None, None] == routing[None], axis=2
     ).astype(F32)
+    router = w_router.T
     attn_low, logs, residual, normed_two, gate_probs, normed_all, marked_all = attend(
         starts,
         query_rot,
@@ -1495,23 +1585,18 @@
         tokens_flat,
         w_out,
         second_gain.reshape(1, width),
-        w_router.T,
+        router,
         hit,
         micro,
         rows,
         ne,
         1,
     )
-    inv_two = rms_scale(residual)
-    here = EXPERTS // ne
-    probs_here = lax.dynamic_slice_in_dim(marked_all, ep * here, here, axis=2)
-    probs_here = probs_here.reshape(ne * micro, here, rows)
-    nb = bit_count(nd)
     orders = [order[:-1][::-1] for order in gather_orders(nd)]
     mix, grad_in, pair_dots, *grads = experts(
         normed_all.reshape(ne * every, width),
         cots,
-        probs_here,
+        marked_all.reshape(ne * micro, EXPERTS, rows),
         w_gate,
         w_up,
         w_down,
@@ -1522,56 +1607,51 @@
         6,
     )
     kept, landed, last = grads[:2], grads[2:4], grads[4:]
-    pair_dots = pair_dots.reshape(here, ne, every).transpose(1, 0, 2)
-    head = (slice(None), slice(0, 1))
+    height = kept[0].shape[2]
+    halves = [(slice(None), slice(i * height, (i + 1) * height)) for i in range(2)]
+    skip = min(2, kept[0].shape[1])
+    more = kept[0].shape[1] > skip
+    head = (slice(None), slice(0, skip))
     *grads, grad_back, dots_all = reduce(
         ne,
         nd,
-        [(last[i], orders[i], None, None, False) for i in range(2)]
+        [(last[k], orders[i], halves[i], None, False) for k in range(2) for i in range(2)]
         + [(kept[i], orders[i][1:], head, landed[i], False) for i in range(2)],
         ((grad_in.reshape(ne, every, width), None),),
         (pair_dots,),
         2,
         40,
     )
-    grads_last, grads_head = grads[:2], grads[2:]
-    pair_dot = dots_all.reshape(EXPERTS, every)
-    grad_logits = gate_probs * (
-        pair_dot - jnp.sum(gate_probs * pair_dot, axis=0, keepdims=True)
-    )
-    grad_w_router = jnp.einsum(
-        "td,et->de", normed_two.astype(F32), grad_logits, precision=HIGHEST
-    )
-    grad_normed_two = (
-        jnp.einsum("et,de->td", grad_logits, w_router.astype(F32), precision=HIGHEST)
-        + grad_back.astype(F32)
-    )
-    scaled_two = grad_normed_two * second_gain
-    grad_gain_two = jnp.sum(grad_normed_two * residual * inv_two, axis=0)
-    grad_residual = (
-        grad_output
-        + inv_two * scaled_two
-        - residual * inv_two**3 * jnp.mean(scaled_two * residual, axis=-1, keepdims=True)
-    )
-    residual_low = grad_residual.astype(BF16)
-    grad_w_out = jnp.einsum("tf,td->fd", attn_low, residual_low, preferred_element_type=F32)
-    grad_attn = jnp.einsum("td,fd->tf", residual_low, w_out, preferred_element_type=F32).astype(
-        BF16
-    )
-    more = kept[0].shape[1] > 1
+    grads_last, grads_head = grads[:4], grads[4:]
     mix = mix.reshape(ne, every, width)
-    grad_query, grad_key_all, grad_value_all, *grads_more = attend_back(
+    (
+        grad_query,
+        grad_key_all,
+        grad_value_all,
+        grad_residual,
+        grad_w_out,
+        grad_router,
+        grad_gain_two,
+        *grads_more,
+    ) = attend_back(
         starts,
         query_rot,
         key_all,
         value_all,
         logs,
-        grad_attn,
         tables,
+        cot_own,
+        dots_all,
+        gate_probs,
+        grad_back,
+        residual,
+        second_gain.reshape(1, width),
+        normed_two,
+        attn_low,
+        w_out,
+        router,
         [(kept[i], orders[i][1:], landed[i]) for i in range(2)] if more else [],
-        micro,
-        rows,
-        ne,
+        skip,
         5,
     )
     full = [[0] + order for order in orders]
@@ -1587,15 +1667,6 @@
         3,
         30,
     )
-    small = jnp.concatenate(
-        [
-            grad_w_router,
-            jnp.zeros((width, 1), F32),
-            grad_gain_two[:, None],
-            jnp.zeros((width, 128 - EXPERTS - 2), F32),
-        ],
-        axis=1,
-    ).astype(BF16)
     grad_tokens, *dense, mix_rest = finish(
         ne,
         nd,
@@ -1607,8 +1678,9 @@
         gain_one,
         grad_residual,
         (w_query, w_key, w_value),
-        grad_w_out.astype(BF16),
-        small,
+        grad_w_out,
+        grad_router,
+        grad_gain_two,
         mix,
         every - rows,
     )
@@ -1628,7 +1700,9 @@
         residual,
         (mix_first, mix_rest),
         [
-            [grads_head[i]] + ([grads_more[i]] if more else []) + [grads_last[i][None]]
+            [grads_head[i]]
+            + ([grads_more[i]] if more else [])
+            + [grads_last[i][None], grads_last[2 + i][None]]
             for i in range(2)
         ],
         dense,

time: 348 us -> 326 us (0.937)
  matrix products: 6.71 us -> 0 us
  Pallas kernels: 315 us -> 309 us
  local copies, waits for them, and re-layouts: 10.6 us -> 4.73 us
    dot_general x4 -> x0, matrix products: 6.71 us -> none  [the longest x1 2.07 us: per_device(): jnp.einsum('tf,td->fd', attn_low, residual_low, preferred_element_type=F32)]
    pallas_call x1, Pallas kernels: 81.7 us -> 75.3 us  [experts(): pl.pallas_call(functools.partial(expert_body, ne, nd, micro, rows), grid=...]
    pallas_call x1, Pallas kernels: 23.1 us -> 26.6 us  [attend_back(): pl.pallas_call(functools.partial(attend_back_body, nd // 2 + 1, ne, nd, m...]
  transfers between devices with their start and end apart: 3 -> 3, of which waited for: 0 -> 0; matrix products, arithmetic and copies ran while one was open for 2% -> 2% of each run, Pallas kernels for 22% -> 24%
where the time goes in v10:
time: 326 us; the launch traced here: 324 us
  Pallas kernels  309 us (95%)
  starting transfers between devices  5.57 us (2%)
  local copies, waits for them, and re-layouts  4.73 us (1%)
    pallas_call x1, Pallas kernels, experts(): pl.pallas_call(functools.partial(expert_body, ne, nd, micro, rows), grid=...  75.3 us
    pallas_call x2, Pallas kernels, reduce(): pl.pallas_call(functools.partial(reduce_body, ne, nd, kinds, line_parts,...  74 us
    pallas_call x1, Pallas kernels, finish(): pl.pallas_call(functools.partial(finish_body, ne, nd, tuple(map(tuple, or...  49.5 us
    pallas_call x1, Pallas kernels, attend(): pl.pallas_call(functools.partial(attend_body, nd // 2 + 1, ne, nd, micro)...  48.7 us
    pallas_call x1, Pallas kernels, attend_back(): pl.pallas_call(functools.partial(attend_back_body, nd // 2 + 1, ne, nd, m...  26.6 us
    pallas_call x1, Pallas kernels, gather(): pl.pallas_call(functools.partial(gather_body, ne, nd, len(dp_arrays), len...  23 us
    pallas_call x1, Pallas kernels, results(): pl.pallas_call(functools.partial(results_body, share, n_out, len(grads[0]...  6.98 us
  transfers between devices with their start and end apart: 3, of which 0 were waited for; matrix products, arithmetic and copies ran while one was open for 2% of the time, Pallas kernels for 24%

profile of v10, /device:TPU:10, one launch (start us, length us, event | category | flops | bytes accessed | tf_op | source)
XLA Modules:
  0.0 323.6 jit_solution(14322781824093890335)
XLA Ops:
  0.6 0.5 collective-permute-start.2
  1.1 2.6 collective-permute-start.1
  3.7 2.5 collective-permute-start
  6.2 0.8 fusion
  7.0 0.6 convert_element_type.23.refs_8_
  7.6 0.8 convert_reduce_fusion
  8.4 0.6 concatenate.3.refs_2_
  9.0 1.6 constant_dynamic-slice_fusion.tables_ref.refs_5_.refs_4_
  10.6 5.4 %shard_map.238 = (bf16[256,1024]{1,0:T(8,128)(2,1)}, bf16[256,1024]{1,0:T(8,128)(2,1)}, bf16[256,512]{1,0:T(8,128)(2,1)}, bf16[256,512]{1,0:T(8,128)(2,1)}) custom-call(bf16[256,1024]{1,0:T(8,128)(2,1)} %bitcast.23, f32[1,1024]{1,0:T(1,128)} %bitcast.44, f32[2,128,128]{2,1,0:T(8,128)} %constant_dynamic-slice_fusion.tables_ref.refs_5_.refs_4_, ...), custom_call_target="tpu_custom_call" | custom-call | bytes 15000000 | tf_op jit(solution)/shard_map/pallas_call | solution.py:803
  15.9 23.0 %shard_map.239 = (bf16[8,256,512]{2,1,0:T(8,128)(2,1)}, bf16[8,256,512]{2,1,0:T(8,128)(2,1)}, f32[8,8,128]{2,1,0:T(8,128)}) custom-call(bf16[256,512]{1,0:T(8,128)(2,1)} %get-tuple-element.75.refs_0_, bf16[256,512]{1,0:T(8,128)(2,1)} %get-tuple-element.76.refs_1_, f32[8,128]{1,0:T(8,128)} %concatenate.3.refs_2_), custom_call_target="tpu_custom_call" | custom-call | bytes 75000000 | tf_op jit(solution)/shard_map/pallas_call | solution.py:167
  38.9 0.8 slice_reduce_fusion
  39.7 0.2 select_reduce_fusion
  39.9 0.8 copy.30.refs_0_
  40.7 48.7 %shard_map.240 = (bf16[256,1024]{1,0:T(8,128)(2,1)}, f32[2,4,512,1]{3,2,1,0:T(8,128)}, f32[256,1024]{1,0:T(8,128)}, bf16[256,1024]{1,0:T(8,128)(2,1)}, f32[32,25...) custom-call(s32[256,1]{1,0:T(8,128)} %copy.30.refs_0_, ...), custom_call_target="tpu_custom_call" | custom-call | bytes 150000000 | tf_op jit(solution)/shard_map/pallas_call | solution.py:1002
  89.4 0.0 collective-permute-done.2.refs_3_
  89.4 0.0 copy-start.1
  89.4 0.8 copy-done.1
  90.2 75.3 %shard_map.241 = (bf16[1024,1024]{1,0:T(8,128)(2,1)}, bf16[1024,1024]{1,0:T(8,128)(2,1)}, f32[4,8,2,128]{3,2,1,0:T(2,128)}, bf16[2,6,192,512]{3,2,1,0:T(8,128)(2...) custom-call(bf16[256,1024]{1,0:T(8,128)(2,1)} %bitcast.29, ...), custom_call_target="tpu_custom_call" | custom-call | bytes 225000000 | tf_op jit(solution)/shard_map/pallas_call | solution.py:698
  165.5 44.8 %shard_map.242 = (bf16[192,512]{1,0:T(8,128)(2,1)}, bf16[192,512]{1,0:T(8,128)(2,1)}, bf16[192,512]{1,0:T(8,128)(2,1)}, bf16[192,512]{1,0:T(8,128)(2,1)}, bf16[2...) custom-call(bf16[4,384,512]{2,1,0:T(8,128)(2,1)} %get-tuple-element., ...), custom_call_target="tpu_custom_call" | custom-call | bytes 120000000 | tf_op jit(solution)/shard_map/pallas_call | solution.py:419
  210.3 26.6 %shard_map.243 = (bf16[256,1024]{1,0:T(8,128)(2,1)}, bf16[8,256,512]{2,1,0:T(8,128)(2,1)}, bf16[8,256,512]{2,1,0:T(8,128)(2,1)}, f32[256,1024]{1,0:T(8,128)}, bf...) custom-call(s32[256,1]{1,0:T(8,128)} %copy.30.refs_0_, ...), custom_call_target="tpu_custom_call" | custom-call | bytes 84000000 | tf_op jit(solution)/shard_map/pallas_call | solution.py:1177
  236.9 29.1 %shard_map.244 = (bf16[256,512]{1,0:T(8,128)(2,1)}, bf16[256,512]{1,0:T(8,128)(2,1)}, bf16[128,1024]{1,0:T(8,128)(2,1)}) custom-call(bf16[8,256,512]{2,1,0:T(8,128)(2,1)} %get-tuple-element.98.refs_0_, bf16[8,256,512]{2,1,0:T(8,128)(2,1)} %get-tuple-element.99.refs_1_, bf16[4,256,1024]{2,1,0:T(8,128)(2,1)} %bitcast.21), custom_call_target="tpu_custom_call" | custom-call | bytes 90000000 | tf_op jit(solution)/shard_map/pallas_call | solution.py:419
  266.1 49.5 %shard_map.245 = (f32[256,1024]{1,0:T(8,128)}, bf16[32,512]{1,0:T(8,128)(2,1)}, bf16[32,512]{1,0:T(8,128)(2,1)}, bf16[32,512]{1,0:T(8,128)(2,1)}, bf16[32,512]{1...) custom-call(bf16[256,1024]{1,0:T(8,128)(2,1)} %get-tuple-element.102, ...), custom_call_target="tpu_custom_call" | custom-call | bytes 135000000 | tf_op jit(solution)/shard_map/pallas_call | solution.py:1400
  315.6 7.0 %shard_map.246 = (bf16[256,1024]{1,0:T(8,128)(2,1)}, f32[32,1024]{1,0:T(8,128)}, f32[32,1024]{1,0:T(8,128)}, f32[32,512]{1,0:T(8,128)}, f32[32,512]{1,0:T(8,128)...) custom-call(f32[256,1024]{1,0:T(8,128)} %get-tuple-element.81.refs_1, ...), custom_call_target="tpu_custom_call" | custom-call | bytes 18000000 | tf_op jit(solution)/shard_map/pallas_call | solution.py:1511
  322.6 1.0 copy.33
  (7 shorter events, 0.0 us)
Async XLA Ops:
  0.6 88.8 %collective-permute-start.2 = (bf16[256,1024]{1,0:T(8,128)(2,1)}, bf16[256,1024]{1,0:T(8,128)(2,1)S(1)}, u32[]{:S(2)}, u32[]{:S(2)}) collective-permute-start(bf16[256,1024]{1,0:T(8,128)(2,1)} %bitcast.26), channel_id=1, source_target_pairs={{0,24},{8,0},{16,8},{24,16},{1,25},{9,1},{17,9},{25,17},{2,26},{10... | collective-permute-start | bytes 1572872 | tf_op jit(solution)/shard_map/ppermute | solution.py:1566
  1.1 88.3 %collective-permute-start.1 = (bf16[256,1024]{1,0:T(8,128)(2,1)}, bf16[256,1024]{1,0:T(8,128)(2,1)}, u32[]{:S(2)}, u32[]{:S(2)}) collective-permute-start(bf16[256,1024]{1,0:T(8,128)(2,1)} %bitcast.27), channel_id=1, source_target_pairs={{0,16},{8,24},{16,0},{24,8},{1,17},{9,25},{17,1},{25,9},{2,18},{10... | collective-permute-start | bytes 1572872 | tf_op jit(solution)/shard_map/ppermute | solution.py:1566
  3.7 85.7 %collective-permute-start = (bf16[256,1024]{1,0:T(8,128)(2,1)}, bf16[256,1024]{1,0:T(8,128)(2,1)}, u32[]{:S(2)}, u32[]{:S(2)}) collective-permute-start(bf16[256,1024]{1,0:T(8,128)(2,1)} %bitcast.28), channel_id=1, source_target_pairs={{0,8},{8,16},{16,24},{24,0},{1,9},{9,17},{17,25},{25,1},{2,10},{10... | collective-permute-start | bytes 1572872 | tf_op jit(solution)/shard_map/ppermute | solution.py:1566
  10.6 29.1 %copy-start.2 = (s32[2,1,128]{2,1,0:T(1,128)S(1)}, s32[2,1,128]{2,1,0:T(1,128)}, u32[]{:S(2)}) copy-start(s32[2,1,128]{2,1,0:T(1,128)} %param.16) | copy-start | bytes 3076
  89.4 0.8 copy-start.1
  315.6 7.0 %copy-start = (f32[256,1024]{1,0:T(8,128)S(1)}, f32[256,1024]{1,0:T(8,128)}, u32[]{:S(2)}) copy-start(f32[256,1024]{1,0:T(8,128)} %get-tuple-element.127) | copy-start | bytes 3145732

commit v11 on v10

--- a/solution.py
+++ b/solution.py
@@ -1029,7 +1029,7 @@
     )(starts, queries, keys, values, tokens, w_out, gain, router, hit)
 
 
-def attend_back_body(span, ne, nd, micro, skip, orders, *refs):
+def attend_back_body(span, ne, nd, micro, skip, full, orders, *refs):
     refs = list(refs)
 
     def take(n):
@@ -1037,14 +1037,15 @@
 
     starts_ref, q_ref, k_ref, v_ref, log_ref, tables_ref = take(6)
     cot_ref, dots_ref, probs_ref, grad_ref, residual_ref, gain_ref, normed_ref, attn_ref = take(8)
-    wo_ref, router_ref = take(2)
+    wo_ref, router_ref, mix_ref = take(3)
     n = len(orders)
     sources, extras = take(n), take(n)
-    dq_ref, dk_ref, dv_ref, res_out, wo_out, router_out, gain_out = take(7)
+    dq_ref, res_out, wo_out, router_out, gain_out, dk_out, dv_out, mix_out = take(8)
     outs = take(n)
-    (grads,) = take(1)
+    grads, mix_held, mix_in = take(3)
+    kv_held, kv_in = take(2), take(2)
     held, more, landing = take(n), take(n), take(n)
-    load_sem, out_sem, send_sem, recv_sem = refs
+    load_sem, out_sem, send_sem, recv_sem, kv_send, kv_recv, kv_out, mix_sem, line_send, line_recv = refs
     ep, dp = lax.axis_index("ep"), lax.axis_index("dp")
     step = pl.program_id(0) * pl.num_programs(1) + pl.program_id(1)
     final = pl.num_programs(0) * pl.num_programs(1) - 1
@@ -1060,13 +1061,58 @@
                 dp, orders[a], loads, held[a], more[a], landing[a], send_sem.at[a], recv_sem.at[a]
             )
         )
+    batch_sums = [
+        [
+            PairSum(
+                dp,
+                full[i],
+                [],
+                kv_held[i].at[m],
+                None,
+                kv_in[i].at[m],
+                kv_send.at[i, m],
+                kv_recv.at[i, m],
+            )
+            for i in range(2)
+        ]
+        for m in range(micro)
+    ]
+    lines = [
+        LineSum(ep, ne, mix_held.at[m], mix_in.at[m], line_send.at[m], line_recv.at[m])
+        for m in range(micro)
+    ]
+    count = q_ref.shape[0]
+    line_loads = [
+        pltpu.make_async_copy(
+            mix_ref.at[:, pl.ds(m * count, count)], mix_held.at[m], mix_sem.at[0, m]
+        )
+        for m in range(micro)
+    ]
+    turns = bit_count(nd)
+
+    def batch_step(m, t):
+        if t <= turns:
+            for each in batch_sums[m]:
+                each.step(t)
+
+    def line_step(m, t):
+        if t < ne:
+            lines[m].step(t)
+
     @pl.when(step == 0)
     def _():
+        for copy in line_loads:
+            copy.start()
         for each in sums:
             each.load()
         greet(ep, dp, ne, nd)
+        for m in range(micro):
+            line_loads[m].wait()
+            line_step(m, 0)
         for each in sums:
             each.step(0)
+        for i in range(2):
+            kv_held[i][...] = jnp.zeros_like(kv_held[i])
         rows = q_ref.shape[0]
         pairs = [dots_ref[:, :, m, :].reshape(-1, rows) for m in range(micro)]
         pair = jnp.concatenate(pairs, axis=1)
@@ -1112,25 +1158,68 @@
     cosine, sine = tables_ref[0], -tables_ref[1]
     for i in range(0, dq.shape[1], 128):
         dq_ref[:, i : i + 128] = turn(dq[:, i : i + 128], cosine, sine).astype(BF16)
-    dk_ref[...] = jnp.zeros_like(dk_ref)
-    dv_ref[...] = jnp.zeros_like(dv_ref)
     here = pl.ds(window_of(dp, span), span)
+    head = pl.program_id(1)
+    at = pl.ds(pl.multiple_of(head * 2 * HEAD_DIM, 2 * HEAD_DIM), 2 * HEAD_DIM)
+    batch = pl.program_id(0)
     dk = dot(grad_scores, q, ((0,), (0,))).astype(BF16)
-    dk_ref[here] = dk.reshape(span, rows, dk.shape[1])
+    kv_held[0][batch, here, :, at] = dk.reshape(span, rows, dk.shape[1])
     dv = dot(probs.astype(BF16), g, ((0,), (0,))).astype(BF16)
-    dv_ref[here] = dv.reshape(span, rows, dv.shape[1])
+    kv_held[1][batch, here, :, at] = dv.reshape(span, rows, dv.shape[1])
+
+    heads = pl.num_programs(1)
+    for m in range(micro):
+
+        @pl.when((batch == m) & (head == heads - 1))
+        def _(m=m):
+            batch_step(m, 0)
+
+        if m > 0:
+
+            @pl.when((batch == m) & (head == 0))
+            def _(m=m):
+                batch_step(m - 1, 1)
+
+    @pl.when(step == final // 4 + 1)
+    def _():
+        line_step(0, 1)
+
+    @pl.when(step == final // 2 + 2)
+    def _():
+        line_step(1, 1)
 
     @pl.when(step == final)
     def _():
+        copies = []
+
+        def leave(copy):
+            copy.start()
+            copies.append(copy)
+
+        line_step(0, 2)
+        last = micro - 1
+        batch_step(last - 1, 2)
         for t in range(1, max([len(order) for order in orders] + [0]) + 1):
             for each in sums:
                 each.step(t)
-        copies = [
-            pltpu.make_async_copy(each.own(), outs[a], out_sem.at[a]) for a, each in enumerate(sums)
-        ]
-        for copy in copies:
-            copy.start()
-        for each in sums:
+        for a, each in enumerate(sums):
+            leave(pltpu.make_async_copy(each.own(), outs[a], out_sem.at[a]))
+        batch_step(last, 1)
+        line_step(1, 2)
+        for t in range(3, turns + 1):
+            batch_step(last - 1, t)
+        batch_step(last, 2)
+        for t in range(3, ne):
+            line_step(0, t)
+            line_step(1, t)
+        for t in range(3, turns + 1):
+            batch_step(last, t)
+        for m in range(micro):
+            own = pl.ds(m * rows, rows)
+            for i, out in enumerate((dk_out, dv_out)):
+                leave(pltpu.make_async_copy(batch_sums[m][i].own(), out.at[own], kv_out.at[i, m]))
+            leave(pltpu.make_async_copy(lines[m].own(), mix_out.at[own], mix_sem.at[1, m]))
+        for each in sums + lines + sum(batch_sums, []):
             each.wait_sends()
         for copy in copies:
             copy.wait()
@@ -1153,7 +1242,9 @@
     attn,
     w_out,
     router,
+    mix,
     sums,
+    full,
     skip,
     collective,
 ):
@@ -1182,28 +1273,44 @@
             nd,
             micro,
             skip,
+            tuple(map(tuple, full)),
             tuple(tuple(order) for _, order, _ in sums),
         ),
         grid=grid,
         in_specs=[column, mine, theirs, theirs, logs, whole(tables)]
         + [whole(v) for v in before]
-        + [ANY] * (2 * n),
-        out_specs=[mine, theirs, theirs] + [whole(v) for v in after] + [ANY] * n,
-        out_shape=[
-            jax.ShapeDtypeStruct(queries.shape, BF16),
-            jax.ShapeDtypeStruct(keys.shape, BF16),
-            jax.ShapeDtypeStruct(values.shape, BF16),
+        + [ANY] * (2 * n + 1),
+        out_specs=[mine] + [whole(v) for v in after] + [ANY] * (n + 3),
+        out_shape=[jax.ShapeDtypeStruct(queries.shape, BF16)]
+        + after
+        + [jax.ShapeDtypeStruct((every, keys.shape[2]), BF16)] * 2
+        + [jax.ShapeDtypeStruct((every, width), BF16)]
+        + [jax.ShapeDtypeStruct(s[1:], BF16) for s in shapes],
+        scratch_shapes=[
+            pltpu.VMEM((w_out.shape[0] // tile, every, tile), BF16),
+            pltpu.VMEM((micro, ne, rows, width), BF16),
+            pltpu.VMEM((micro, 2, ne, rows, width), BF16),
         ]
-        + after
-        + [jax.ShapeDtypeStruct(s[1:], BF16) for s in shapes],
-        scratch_shapes=[pltpu.VMEM((w_out.shape[0] // tile, every, tile), BF16)]
+        + [pltpu.VMEM((micro, nd, rows, keys.shape[2]), BF16)] * 2
+        + [pltpu.VMEM((micro, nd - 1, rows, keys.shape[2]), BF16)] * 2
         + [pltpu.VMEM(s, BF16) for s in shapes] * 2
         + [pltpu.VMEM((s[0] - 1,) + s[1:], BF16) for s in shapes]
-        + [DMA((some, 2)), DMA((some,)), DMA((some, deep)), DMA((some, deep))],
+        + [
+            DMA((some, 2)),
+            DMA((some,)),
+            DMA((some, deep)),
+            DMA((some, deep)),
+            DMA((2, micro, nd - 1)),
+            DMA((2, micro, nd - 1)),
+            DMA((2, micro)),
+            DMA((2, micro)),
+            DMA((micro, 2, ne)),
+            DMA((micro, 2, ne)),
+        ],
         compiler_params=pltpu.CompilerParams(
-            vmem_limit_bytes=60 * 2**20, collective_id=collective, has_side_effects=True
+            vmem_limit_bytes=63 * 2**20, collective_id=collective, has_side_effects=True
         ),
-        cost_estimate=cost(28),
+        cost_estimate=cost(40),
     )(
         starts,
         queries,
@@ -1212,6 +1319,7 @@
         logs_in,
         tables,
         *before,
+        mix,
         *[v for v, _, _ in sums],
         *[extra for _, _, extra in sums],
     )
@@ -1224,12 +1332,11 @@
         return [refs.pop(0) for _ in range(n)]
 
     n_ref, dq_ref, dk_ref, dv_ref, tables_ref, tokens_ref, gain_ref, router_ref, gain_two = take(9)
-    res_ref, wq_ref, wk_ref, wv_ref, wo_ref, mix_ref = take(6)
+    res_ref, wq_ref, wk_ref, wv_ref, wo_ref = take(5)
     (tok_out,) = take(1)
     count = 2 * n_out + 3
-    outs, (mix_out,) = take(count), take(1)
-    held, pair_in, line_in = take(count), take(count), take(count)
-    dk_turned, wq, wk, wv, res, mix_held, mix_in = take(7)
+    outs, held, pair_in, line_in = take(count), take(count), take(count), take(count)
+    dk_turned, wq, wk, wv, res = take(5)
     load_sem, own_sem, out_sem, dp_send, dp_recv, ep_send, ep_recv = refs
     ep, dp = lax.axis_index("ep"), lax.axis_index("dp")
     columns = held[0].shape[3]
@@ -1259,15 +1366,8 @@
     ]
     early, made, small = sums[:n_out], sums[n_out:-1], sums[-1]
     queries, others = made[:n_out], made[n_out:]
-    mix = LineSum(ep, ne, mix_held, mix_in, ep_send.at[count], ep_recv.at[count])
-    mix_load = pltpu.make_async_copy(
-        mix_ref.at[:, pl.ds(mix_ref.shape[1] - mix_held.shape[1], mix_held.shape[1])],
-        mix_held,
-        own_sem.at[4],
-    )
     for each in early:
         each.load()
-    mix_load.start()
     for copy in own:
         copy.start()
     greet(ep, dp, ne, nd)
@@ -1284,8 +1384,6 @@
                 lines[sums.index(each)].step(t)
 
     steps(early, 0)
-    mix_load.wait()
-    mix.step(0)
 
     normed = n_ref[...]
     cosine, sine = (repeated(tables_ref[i], normed.shape[0]) for i in range(2))
@@ -1318,7 +1416,6 @@
         copy.wait()
     back = dot(dq_ref[...], wq[...], ((1,), (1,)))
     steps(made[-1:], 1)
-    mix.step(1)
     back = back + dot(dk_turned[...], wk[...], ((1,), (1,)))
     back = back + dot(dv_ref[...], wv[...], ((1,), (1,)))
     steps(early, 2)
@@ -1339,15 +1436,12 @@
     steps([small], 0)
     steps(queries, 2)
     steps([small], 1)
-    mix.step(2)
     for t in range(3, turns + 1):
         steps(early, t)
     line_steps(early, 0)
     steps(others, 2)
     for t in range(3, turns + 1):
         steps(queries, t)
-    for t in range(3, ne):
-        mix.step(t)
     line_steps(early, 1)
     line_steps(queries, 0)
     steps([small], 2)
@@ -1364,9 +1458,7 @@
     for a in order:
         copies.append(pltpu.make_async_copy(lines[a].own(), outs[a], out_sem.at[a]))
         copies[-1].start()
-    copies.append(pltpu.make_async_copy(mix.own(), mix_out, out_sem.at[count]))
-    copies[-1].start()
-    for each in sums + lines + [mix]:
+    for each in sums + lines:
         each.wait_sends()
     for copy in copies:
         copy.wait()
@@ -1386,11 +1478,8 @@
     w_out,
     router_grad,
     gain_two_grad,
-    mix,
-    mix_rows,
 ):
     rows, width = tokens.shape
-    line = (ne, mix_rows, width)
     share = width // (ne * nd)
     columns = weights[1].shape[1]
     n_out = width // columns
@@ -1400,25 +1489,23 @@
     return pl.pallas_call(
         functools.partial(finish_body, ne, nd, tuple(map(tuple, orders)), n_out),
         out_shape=[jax.ShapeDtypeStruct((rows, width), F32)]
-        + [jax.ShapeDtypeStruct((share, c), BF16) for c in wide]
-        + [jax.ShapeDtypeStruct(line[1:], BF16)],
-        in_specs=[VMEM] * 9 + [ANY] * 6,
-        out_specs=[VMEM] + [ANY] * (count + 1),
+        + [jax.ShapeDtypeStruct((share, c), BF16) for c in wide],
+        in_specs=[VMEM] * 9 + [ANY] * 5,
+        out_specs=[VMEM] + [ANY] * count,
         scratch_shapes=[pltpu.VMEM((nd, ne, share, c), BF16) for c in wide]
         + [pltpu.VMEM((nd - 1, ne, share, c), BF16) for c in wide]
         + [pltpu.VMEM((2, ne, share, c), BF16) for c in wide]
         + [pltpu.VMEM(grads[1].shape, BF16)]
         + [pltpu.VMEM(w.shape, BF16) for w in weights]
         + [pltpu.VMEM((rows, width), F32)]
-        + [pltpu.VMEM(line, BF16), pltpu.VMEM((2,) + line, BF16)]
         + [
             DMA((count, ne)),
-            DMA((5,)),
-            DMA((count + 1,)),
+            DMA((4,)),
+            DMA((count,)),
             DMA((count, nd - 1)),
             DMA((count, nd - 1)),
-            DMA((count + 1, 2, ne)),
-            DMA((count + 1, 2, ne)),
+            DMA((count, 2, ne)),
+            DMA((count, 2, ne)),
         ],
         compiler_params=pltpu.CompilerParams(
             vmem_limit_bytes=60 * 2**20, collective_id=4, has_side_effects=True
@@ -1435,7 +1522,6 @@
         grad_residual,
         *weights,
         split(w_out),
-        mix,
     )
 
 
@@ -1445,7 +1531,7 @@
     def take(n):
         return [refs.pop(0) for _ in range(n)]
 
-    residual_ref, mix_first, mix_rest = take(3)
+    residual_ref, mix_ref = take(2)
     halves = [take(groups) for _ in range(2)]
     dense = take(2 * n_out + 3)
     out_ref, d_out, d_query, d_key, d_value, router, gain_one, gain_two = take(8)
@@ -1454,10 +1540,7 @@
 
     @pl.when(e == 0)
     def _():
-        rows = mix_first.shape[0]
-        for i, mix in enumerate((mix_first, mix_rest)):
-            at = slice(i * rows, i * rows + mix.shape[0])
-            out_ref[at, :] = (residual_ref[at, :] + mix[...].astype(F32)).astype(BF16)
+        out_ref[...] = (residual_ref[...] + mix_ref[...].astype(F32)).astype(BF16)
         width = dense[0].shape[1]
         for i in range(n_out):
             d_out[:, i * width : (i + 1) * width] = dense[i][...].astype(F32)
@@ -1624,14 +1707,16 @@
     )
     grads_last, grads_head = grads[:4], grads[4:]
     mix = mix.reshape(ne, every, width)
+    full = [[0] + order for order in orders]
     (
         grad_query,
-        grad_key_all,
-        grad_value_all,
         grad_residual,
         grad_w_out,
         grad_router,
         grad_gain_two,
+        grad_key,
+        grad_value,
+        mix_own,
         *grads_more,
     ) = attend_back(
         starts,
@@ -1650,24 +1735,13 @@
         attn_low,
         w_out,
         router,
+        mix,
         [(kept[i], orders[i][1:], landed[i]) for i in range(2)] if more else [],
+        full,
         skip,
         5,
     )
-    full = [[0] + order for order in orders]
-    grad_key, grad_value, mix_first = reduce(
-        ne,
-        nd,
-        [
-            (grad_key_all, full[0], None, None, False),
-            (grad_value_all, full[1], None, None, False),
-        ],
-        ((mix, (slice(None), slice(0, rows))),),
-        (),
-        3,
-        30,
-    )
-    grad_tokens, *dense, mix_rest = finish(
+    grad_tokens, *dense = finish(
         ne,
         nd,
         full,
@@ -1681,8 +1755,6 @@
         grad_w_out,
         grad_router,
         grad_gain_two,
-        mix,
-        every - rows,
     )
     (
         output,
@@ -1698,7 +1770,7 @@
         d_down,
     ) = results(
         residual,
-        (mix_first, mix_rest),
+        (mix_own,),
         [
             [grads_head[i]]
             + ([grads_more[i]] if more else [])

time: 326 us -> 317 us (0.972)
  Pallas kernels: 309 us -> 300 us
    pallas_call x2 -> x1, Pallas kernels: 74 us -> 44.9 us  [reduce(): pl.pallas_call(functools.partial(reduce_body, ne, nd, kinds, line_parts,...]
    pallas_call x1, Pallas kernels: 26.6 us -> 45.3 us  [attend_back(): pl.pallas_call(functools.partial(attend_back_body, nd // 2 + 1, ne, nd, m...]
  transfers between devices with their start and end apart: 3 -> 3, of which waited for: 0 -> 0; matrix products, arithmetic and copies ran while one was open for 2% -> 2% of each run, Pallas kernels for 24% -> 25%
where the time goes in v11:
time: 317 us; the launch traced here: 315 us
  Pallas kernels  300 us (95%)
  starting transfers between devices  5.57 us (2%)
  local copies, waits for them, and re-layouts  4.73 us (1%)
    pallas_call x1, Pallas kernels, experts(): pl.pallas_call(functools.partial(expert_body, ne, nd, micro, rows), grid=...  75.3 us
    pallas_call x1, Pallas kernels, finish(): pl.pallas_call(functools.partial(finish_body, ne, nd, tuple(map(tuple, or...  50.7 us
    pallas_call x1, Pallas kernels, attend(): pl.pallas_call(functools.partial(attend_body, nd // 2 + 1, ne, nd, micro)...  48.7 us
    pallas_call x1, Pallas kernels, attend_back(): pl.pallas_call(functools.partial(attend_back_body, nd // 2 + 1, ne, nd, m...  45.3 us
    pallas_call x1, Pallas kernels, reduce(): pl.pallas_call(functools.partial(reduce_body, ne, nd, kinds, line_parts,...  44.9 us
    pallas_call x1, Pallas kernels, gather(): pl.pallas_call(functools.partial(gather_body, ne, nd, len(dp_arrays), len...  23 us
    pallas_call x1, Pallas kernels, results(): pl.pallas_call(functools.partial(results_body, share, n_out, len(grads[0]...  7.03 us
  transfers between devices with their start and end apart: 3, of which 0 were waited for; matrix products, arithmetic and copies ran while one was open for 2% of the time, Pallas kernels for 25%

profile of v11, /device:TPU:10, one launch (start us, length us, event | category | flops | bytes accessed | tf_op | source)
XLA Modules:
  0.0 314.5 jit_solution(13477312097566761595)
XLA Ops:
  0.6 0.5 collective-permute-start.2
  1.1 2.6 collective-permute-start.1
  3.7 2.5 collective-permute-start
  6.2 0.8 fusion
  7.0 0.6 convert_element_type.23.refs_8_
  7.6 0.8 convert_reduce_fusion
  8.4 0.6 concatenate.3.refs_2_
  9.0 1.6 constant_dynamic-slice_fusion.tables_ref.refs_5_.refs_4_
  10.6 5.4 %shard_map.238 = (bf16[256,1024]{1,0:T(8,128)(2,1)}, bf16[256,1024]{1,0:T(8,128)(2,1)}, bf16[256,512]{1,0:T(8,128)(2,1)}, bf16[256,512]{1,0:T(8,128)(2,1)}) custom-call(bf16[256,1024]{1,0:T(8,128)(2,1)} %bitcast.21, f32[1,1024]{1,0:T(1,128)} %bitcast.43, f32[2,128,128]{2,1,0:T(8,128)} %constant_dynamic-slice_fusion.tables_ref.refs_5_.refs_4_, ...), custom_call_target="tpu_custom_call" | custom-call | bytes 15000000 | tf_op jit(solution)/shard_map/pallas_call | solution.py:803
  15.9 23.0 %shard_map.239 = (bf16[8,256,512]{2,1,0:T(8,128)(2,1)}, bf16[8,256,512]{2,1,0:T(8,128)(2,1)}, f32[8,8,128]{2,1,0:T(8,128)}) custom-call(bf16[256,512]{1,0:T(8,128)(2,1)} %get-tuple-element.72.refs_0_, bf16[256,512]{1,0:T(8,128)(2,1)} %get-tuple-element.73.refs_1_, f32[8,128]{1,0:T(8,128)} %concatenate.3.refs_2_), custom_call_target="tpu_custom_call" | custom-call | bytes 75000000 | tf_op jit(solution)/shard_map/pallas_call | solution.py:167
  38.9 0.8 slice_reduce_fusion
  39.7 0.2 select_reduce_fusion
  39.9 0.8 copy.30.refs_0_
  40.7 48.7 %shard_map.240 = (bf16[256,1024]{1,0:T(8,128)(2,1)}, f32[2,4,512,1]{3,2,1,0:T(8,128)}, f32[256,1024]{1,0:T(8,128)}, bf16[256,1024]{1,0:T(8,128)(2,1)}, f32[32,25...) custom-call(s32[256,1]{1,0:T(8,128)} %copy.30.refs_0_, ...), custom_call_target="tpu_custom_call" | custom-call | bytes 150000000 | tf_op jit(solution)/shard_map/pallas_call | solution.py:1002
  89.5 0.0 collective-permute-done.2.refs_3_
  89.5 0.0 copy-start.1
  89.5 0.0 collective-permute-done.1.refs_2_
  89.5 0.8 copy-done.1
  90.3 75.3 %shard_map.241 = (bf16[1024,1024]{1,0:T(8,128)(2,1)}, bf16[1024,1024]{1,0:T(8,128)(2,1)}, f32[4,8,2,128]{3,2,1,0:T(2,128)}, bf16[2,6,192,512]{3,2,1,0:T(8,128)(2...) custom-call(bf16[256,1024]{1,0:T(8,128)(2,1)} %bitcast.27, ...), custom_call_target="tpu_custom_call" | custom-call | bytes 225000000 | tf_op jit(solution)/shard_map/pallas_call | solution.py:698
  165.6 44.9 %shard_map.242 = (bf16[192,512]{1,0:T(8,128)(2,1)}, bf16[192,512]{1,0:T(8,128)(2,1)}, bf16[192,512]{1,0:T(8,128)(2,1)}, bf16[192,512]{1,0:T(8,128)(2,1)}, bf16[2...) custom-call(bf16[4,384,512]{2,1,0:T(8,128)(2,1)} %get-tuple-element., ...), custom_call_target="tpu_custom_call" | custom-call | bytes 120000000 | tf_op jit(solution)/shard_map/pallas_call | solution.py:419
  210.5 45.3 %shard_map.243 = (bf16[256,1024]{1,0:T(8,128)(2,1)}, f32[256,1024]{1,0:T(8,128)}, bf16[1024,1024]{1,0:T(8,128)(2,1)}, f32[32,1024]{1,0:T(8,128)}, f32[1,1024]{1,...) custom-call(s32[256,1]{1,0:T(8,128)} %copy.30.refs_0_, ...), custom_call_target="tpu_custom_call" | custom-call | bytes 120000000 | tf_op jit(solution)/shard_map/pallas_call | solution.py:1268
  255.8 50.7 %shard_map.244 = (f32[256,1024]{1,0:T(8,128)}, bf16[32,512]{1,0:T(8,128)(2,1)}, bf16[32,512]{1,0:T(8,128)(2,1)}, bf16[32,512]{1,0:T(8,128)(2,1)}, bf16[32,512]{1...) custom-call(bf16[256,1024]{1,0:T(8,128)(2,1)} %get-tuple-element.105.refs_0_, ...), custom_call_target="tpu_custom_call" | custom-call | bytes 135000000 | tf_op jit(solution)/shard_map/pallas_call | solution.py:1489
  306.5 7.0 %shard_map.245 = (bf16[256,1024]{1,0:T(8,128)(2,1)}, f32[32,1024]{1,0:T(8,128)}, f32[32,1024]{1,0:T(8,128)}, f32[32,512]{1,0:T(8,128)}, f32[32,512]{1,0:T(8,128)...) custom-call(f32[256,1024]{1,0:T(8,128)} %get-tuple-element.78.refs_1, ...), custom_call_target="tpu_custom_call" | custom-call | bytes 18000000 | tf_op jit(solution)/shard_map/pallas_call | solution.py:1594
  313.6 1.0 copy.33
  (6 shorter events, 0.0 us)
Async XLA Ops:
  0.6 88.8 %collective-permute-start.2 = (bf16[256,1024]{1,0:T(8,128)(2,1)}, bf16[256,1024]{1,0:T(8,128)(2,1)S(1)}, u32[]{:S(2)}, u32[]{:S(2)}) collective-permute-start(bf16[256,1024]{1,0:T(8,128)(2,1)} %bitcast.24), channel_id=1, source_target_pairs={{0,24},{8,0},{16,8},{24,16},{1,25},{9,1},{17,9},{25,17},{2,26},{10... | collective-permute-start | bytes 1572872 | tf_op jit(solution)/shard_map/ppermute | solution.py:1649
  1.1 88.3 %collective-permute-start.1 = (bf16[256,1024]{1,0:T(8,128)(2,1)}, bf16[256,1024]{1,0:T(8,128)(2,1)}, u32[]{:S(2)}, u32[]{:S(2)}) collective-permute-start(bf16[256,1024]{1,0:T(8,128)(2,1)} %bitcast.25), channel_id=1, source_target_pairs={{0,16},{8,24},{16,0},{24,8},{1,17},{9,25},{17,1},{25,9},{2,18},{10... | collective-permute-start | bytes 1572872 | tf_op jit(solution)/shard_map/ppermute | solution.py:1649
  3.7 85.8 %collective-permute-start = (bf16[256,1024]{1,0:T(8,128)(2,1)}, bf16[256,1024]{1,0:T(8,128)(2,1)}, u32[]{:S(2)}, u32[]{:S(2)}) collective-permute-start(bf16[256,1024]{1,0:T(8,128)(2,1)} %bitcast.26), channel_id=1, source_target_pairs={{0,8},{8,16},{16,24},{24,0},{1,9},{9,17},{17,25},{25,1},{2,10},{10... | collective-permute-start | bytes 1572872 | tf_op jit(solution)/shard_map/ppermute | solution.py:1649
  10.6 29.1 %copy-start.2 = (s32[2,1,128]{2,1,0:T(1,128)S(1)}, s32[2,1,128]{2,1,0:T(1,128)}, u32[]{:S(2)}) copy-start(s32[2,1,128]{2,1,0:T(1,128)} %param.16) | copy-start | bytes 3076
  89.5 0.8 copy-start.1
  306.5 7.0 %copy-start = (f32[256,1024]{1,0:T(8,128)S(1)}, f32[256,1024]{1,0:T(8,128)}, u32[]{:S(2)}) copy-start(f32[256,1024]{1,0:T(8,128)} %get-tuple-element.121) | copy-start | bytes 3145732

commit v12 on v11

--- a/solution.py
+++ b/solution.py
@@ -13,6 +13,7 @@
 HEAD_DIM = 64
 EXPERTS = 32
 CAP = 64
+SEGMENT_IDS = 4
 EPSILON = 1e-06
 ROPE_BASE = 10000.0
 MASKED = -1e30
@@ -60,129 +61,40 @@
     )
 
 
-def gather_body(ne, nd, n_dp, n_ep, *refs):
-    n_in = n_dp + n_ep
-    ins, outs, sems = refs[:n_in], refs[n_in : 2 * n_in], refs[2 * n_in :]
-    ep, dp = lax.axis_index("ep"), lax.axis_index("dp")
-    own_sem, dp_send, dp_recv, ep_send, ep_recv = sems
-    greet(ep, dp, ne, nd)
-    own = []
-    for a in range(n_in):
-        me = dp if a < n_dp else ep
-        copy = pltpu.make_async_copy(ins[a], outs[a].at[me], own_sem.at[a])
-        copy.start()
-        own.append(copy)
-
-    def dp_copy(a, t, m):
-        order = gather_orders(nd)[a % 2]
-        block = jnp.bitwise_xor(dp, m)
-        k = (1 << t) - 1 + masks(order[:t]).index(m)
+class PairGather:
+    def __init__(self, dp, nd, order, own, whole, send_sem, recv_sem):
+        self.dp, self.order, self.own, self.whole = dp, order, own, whole
+        self.send_sem, self.recv_sem = send_sem, recv_sem
+
+    def copy(self, t, m):
+        block = jnp.bitwise_xor(self.dp, m)
+        k = (1 << t) - 1 + masks(self.order[:t]).index(m)
         return remote(
-            ins[a] if m == 0 else outs[a].at[block],
-            outs[a].at[block],
-            dp_send.at[a, k],
-            dp_recv.at[a, k],
-            {"dp": jnp.bitwise_xor(dp, 1 << order[t])},
+            self.own if m == 0 else self.whole.at[block],
+            self.whole.at[block],
+            self.send_sem.at[k],
+            self.recv_sem.at[k],
+            {"dp": jnp.bitwise_xor(self.dp, 1 << self.order[t])},
         )
 
-    def ep_copy(a, s, way):
-        shard = lax.rem(ep - way * s + ne, ne)
-        src = ins[n_dp + a] if s == 0 else outs[n_dp + a].at[shard]
-        k = 0 if way == 1 else 1
-        return remote(
-            src,
-            outs[n_dp + a].at[shard],
-            ep_send.at[a, k, s],
-            ep_recv.at[a, k, s],
-            {"ep": lax.rem(ep + way + ne, ne)},
-        )
-
-    def sends(s, way):
-        if way == 1:
-            return (ep >= s) & (ep < ne - 1)
-        return (ep + s <= ne - 1) & (ep >= 1)
-
-    def receives(s, way):
-        if way == 1:
-            return ep >= 1 + s
-        return ep + 1 + s <= ne - 1
-
-    def ep_start(s):
-        for a in range(n_ep):
-            for way in (1, -1):
-
-                @pl.when(sends(s, way))
-                def _(a=a, way=way):
-                    ep_copy(a, s, way).start()
-
-    def ep_wait(s):
-        for a in range(n_ep):
-            for way in (1, -1):
-
-                @pl.when(receives(s, way))
-                def _(a=a, way=way):
-                    ep_copy(a, s, way).wait_recv()
-
-    dp_steps = bit_count(nd) if n_dp else 0
-    ep_steps = ne - 1 if n_ep else 0
-    for t in range(dp_steps):
-        for a in range(n_dp):
-            dp_copy(a, t, 0).start()
-    for t in range(max(dp_steps, ep_steps) + 1):
-        if 0 < t <= dp_steps:
-            for a in range(n_dp):
-                order = gather_orders(nd)[a % 2]
-                for m in masks(order[: t - 1]):
-                    dp_copy(a, t - 1, m).wait_recv()
-                    for later in range(t, dp_steps):
-                        dp_copy(a, later, m | (1 << order[t - 1])).start()
-        if 0 < t <= ep_steps:
-            ep_wait(t - 1)
-        if t < ep_steps:
-            ep_start(t)
-    for t in range(dp_steps):
-        for a in range(n_dp):
-            for m in masks(gather_orders(nd)[a % 2][:t]):
-                dp_copy(a, t, m).wait_send()
-    for s in range(ep_steps):
-        for a in range(n_ep):
-            for way in (1, -1):
-
-                @pl.when(sends(s, way))
-                def _(a=a, s=s, way=way):
-                    ep_copy(a, s, way).wait_send()
-
-    for c in own:
-        c.wait()
+    def start(self):
+        for t in range(len(self.order)):
+            self.copy(t, 0).start()
+
+    def step(self, t):
+        for m in masks(self.order[:t]):
+            self.copy(t, m).wait_recv()
+            for later in range(t + 1, len(self.order)):
+                self.copy(later, m | (1 << self.order[t])).start()
+
+    def wait_sends(self):
+        for t in range(len(self.order)):
+            for m in masks(self.order[:t]):
+                self.copy(t, m).wait_send()
 
 
 def cost(us):
     return pl.CostEstimate(flops=0, bytes_accessed=int(us * 3.0e6), transcendentals=0)
-
-
-def gather(ne, nd, dp_arrays, ep_arrays, collective, us):
-    arrays = list(dp_arrays) + list(ep_arrays)
-    counts = [nd] * len(dp_arrays) + [ne] * len(ep_arrays)
-    a, b = max(len(dp_arrays), 1), max(len(ep_arrays), 1)
-    return pl.pallas_call(
-        functools.partial(gather_body, ne, nd, len(dp_arrays), len(ep_arrays)),
-        out_shape=[
-            jax.ShapeDtypeStruct((n,) + v.shape, v.dtype) for n, v in zip(counts, arrays)
-        ],
-        in_specs=[ANY] * len(arrays),
-        out_specs=[ANY] * len(arrays),
-        scratch_shapes=[
-            DMA((len(arrays),)),
-            DMA((a, nd - 1)),
-            DMA((a, nd - 1)),
-            DMA((b, 2, ne - 1)),
-            DMA((b, 2, ne - 1)),
-        ],
-        compiler_params=pltpu.CompilerParams(
-            collective_id=collective, has_side_effects=True, vmem_limit_bytes=60 * 2**20
-        ),
-        cost_estimate=cost(us),
-    )(*arrays)
 
 
 def add_into(ref, arrived):
@@ -303,6 +215,41 @@
                 @pl.when(has)
                 def _(way=way, dest=dest):
                     self.copy(dest, way).wait_send()
+
+
+class SpreadSum:
+    def __init__(self, ep, ne, blocks, landing, send_sem, recv_sem):
+        self.ep, self.blocks, self.landing = ep, blocks, landing
+        self.copies = []
+        for k in range(1, ne):
+            to = lax.rem(ep + k, ne)
+            self.copies.append(
+                remote(
+                    blocks.at[to],
+                    landing.at[k - 1],
+                    send_sem.at[k - 1],
+                    recv_sem.at[k - 1],
+                    {"ep": to},
+                )
+            )
+
+    def step(self, t):
+        if t == 0:
+            for copy in self.copies:
+                copy.start()
+        elif t == 1:
+            total = self.blocks[self.ep].astype(F32)
+            for k, copy in enumerate(self.copies):
+                copy.wait_recv()
+                total = total + self.landing[k].astype(F32)
+            self.blocks[self.ep] = total.astype(BF16)
+
+    def own(self):
+        return self.blocks.at[self.ep]
+
+    def wait_sends(self):
+        for copy in self.copies:
+            copy.wait_send()
 
 
 def shape_at(array, where):
@@ -769,24 +716,65 @@
     return jnp.concatenate([table] * (rows // table.shape[0]), axis=0)
 
 
-def project_body(
-    tokens_ref, gain_ref, tables_ref, wq_ref, wk_ref, wv_ref, n_ref, q_ref, k_ref, v_ref, *rest
-):
-    wq, wk, wv, sem = rest
+def project_body(ne, nd, *refs):
+    tokens_ref, gain_ref, segments_ref, tables_all, wq_ref, wk_ref, wv_ref = refs[:7]
+    n_ref, q_ref, tables_ref, starts_ref, key_all, value_all = refs[7:13]
+    wq, wk, wv, key_own, value_own, count_own, count_all = refs[13:20]
+    sem, own_sem, send_sem, recv_sem = refs[20:]
+    ep, dp = lax.axis_index("ep"), lax.axis_index("dp")
+    micro, rows = segments_ref.shape
     loads = [
         pltpu.make_async_copy(src, dst, sem.at[i])
-        for i, (src, dst) in enumerate(((wk_ref, wk), (wv_ref, wv), (wq_ref, wq)))
+        for i, (src, dst) in enumerate(
+            (
+                (tables_all.at[:, pl.ds(pl.multiple_of(dp * rows, rows), rows)], tables_ref),
+                (wk_ref, wk),
+                (wv_ref, wv),
+                (wq_ref, wq),
+            )
+        )
     ]
     for copy in loads:
         copy.start()
+    arrays = ((count_own, count_all), (key_own, key_all), (value_own, value_all))
+    gathers = [
+        PairGather(
+            dp, nd, gather_orders(nd)[i // 2], own, whole, send_sem.at[i], recv_sem.at[i]
+        )
+        for i, (own, whole) in enumerate(arrays)
+    ]
+    own_copies = [
+        pltpu.make_async_copy(own, whole.at[dp], own_sem.at[i])
+        for i, (own, whole) in enumerate(arrays)
+    ]
+
+    def leave(i):
+        gathers[i].start()
+        own_copies[i].start()
+
+    segments = segments_ref[...]
+    lane = lax.broadcasted_iota(jnp.int32, (micro, count_own.shape[1]), 1)
+    counts = jnp.zeros(lane.shape, F32)
+    for i in range(SEGMENT_IDS):
+        held = jnp.sum((segments == i).astype(F32), axis=1, keepdims=True)
+        counts = counts + jnp.where(lane == i, held, 0.0)
+    count_own[...] = jnp.zeros_like(count_own)
+    count_own[:micro] = counts
+    greet(ep, dp, ne, nd)
+    leave(0)
+
     x = tokens_ref[...].astype(F32)
     n_ref[...] = (x * rms_scale(x) * gain_ref[...]).astype(BF16)
     normed = n_ref[...]
+    loads[0].wait()
     cosine, sine = (repeated(tables_ref[i], x.shape[0]) for i in range(2))
     tile = 256
-    for copy, (w, out, turned) in zip(
-        loads, ((wk, k_ref, True), (wv, v_ref, False), (wq, q_ref, True))
-    ):
+    steps = (
+        (wk, key_own, True, 1),
+        (wv, value_own, False, 2),
+        (wq, q_ref, True, None),
+    )
+    for copy, (w, out, turned, array) in zip(loads[1:], steps):
         copy.wait()
         for c in range(0, w.shape[1], tile):
             y = dot(normed, w[:, c : c + tile])
@@ -795,20 +783,51 @@
                     out[:, c + i : c + i + 128] = turn(y[:, i : i + 128], cosine, sine).astype(BF16)
             else:
                 out[:, c : c + tile] = y.astype(BF16)
-
-
-def project(tokens, gain, tables, w_query, w_key, w_value):
+        if array is not None:
+            leave(array)
+    for t in range(bit_count(nd)):
+        for each in gathers:
+            each.step(t)
+    for copy in own_copies:
+        copy.wait()
+    totals = jnp.sum(count_all[...], axis=0)
+    padded = jnp.concatenate([segments, jnp.zeros((8 - micro, rows), jnp.int32)], axis=0)
+    column = padded.astype(F32).T
+    ids = lax.broadcasted_iota(jnp.int32, (rows, totals.shape[1]), 1).astype(F32)
+    for m in range(micro):
+        lower = jnp.where(ids < column[:, m : m + 1], totals[m : m + 1], 0.0)
+        starts_ref[m * rows : (m + 1) * rows] = jnp.sum(lower, axis=1, keepdims=True).astype(
+            jnp.int32
+        )
+    for each in gathers:
+        each.wait_sends()
+
+
+def project(tokens, gain, segments, tables, w_query, w_key, w_value, ne, nd, collective):
     rows, width = tokens.shape
-    shapes = [width, w_query.shape[1], w_key.shape[1], w_value.shape[1]]
+    micro, count = segments.shape
+    keys = jax.ShapeDtypeStruct((nd, rows, w_key.shape[1]), BF16)
     return pl.pallas_call(
-        project_body,
-        out_shape=[jax.ShapeDtypeStruct((rows, n), BF16) for n in shapes],
-        in_specs=[VMEM] * 3 + [ANY] * 3,
-        out_specs=[VMEM] * 4,
-        scratch_shapes=[pltpu.VMEM(w.shape, BF16) for w in (w_query, w_key, w_value)] + [DMA((3,))],
-        compiler_params=pltpu.CompilerParams(vmem_limit_bytes=60 * 2**20),
-        cost_estimate=cost(5),
-    )(tokens, gain, tables, w_query, w_key, w_value)
+        functools.partial(project_body, ne, nd),
+        out_shape=[
+            jax.ShapeDtypeStruct((rows, width), BF16),
+            jax.ShapeDtypeStruct((rows, w_query.shape[1]), BF16),
+            jax.ShapeDtypeStruct((2, count, tables.shape[2]), F32),
+            jax.ShapeDtypeStruct((rows, 1), jnp.int32),
+            keys,
+            keys,
+        ],
+        in_specs=[VMEM] * 3 + [ANY] * 4,
+        out_specs=[VMEM] * 4 + [ANY] * 2,
+        scratch_shapes=[pltpu.VMEM(w.shape, BF16) for w in (w_query, w_key, w_value)]
+        + [pltpu.VMEM(keys.shape[1:], BF16)] * 2
+        + [pltpu.VMEM((8, 128), F32), pltpu.VMEM((nd, 8, 128), F32)]
+        + [DMA((4,)), DMA((3,)), DMA((3, nd - 1)), DMA((3, nd - 1))],
+        compiler_params=pltpu.CompilerParams(
+            vmem_limit_bytes=60 * 2**20, collective_id=collective, has_side_effects=True
+        ),
+        cost_estimate=cost(26),
+    )(tokens, gain, segments, tables, w_query, w_key, w_value)
 
 
 def spread(x):
@@ -1360,8 +1379,8 @@
                 dp, orders[a % 2], loads, held[a], None, pair_in[a], dp_send.at[a], dp_recv.at[a]
             )
         )
-    lines = [
-        LineSum(ep, ne, sums[a].own(), line_in[a], ep_send.at[a], ep_recv.at[a])
+    spreads = [
+        SpreadSum(ep, ne, sums[a].own(), line_in[a], ep_send.at[a], ep_recv.at[a])
         for a in range(count)
     ]
     early, made, small = sums[:n_out], sums[n_out:-1], sums[-1]
@@ -1378,10 +1397,9 @@
             if t <= turns:
                 each.step(t)
 
-    def line_steps(group, t):
+    def spread_steps(group, t):
         for each in group:
-            if t < ne:
-                lines[sums.index(each)].step(t)
+            spreads[sums.index(each)].step(t)
 
     steps(early, 0)
 
@@ -1438,27 +1456,24 @@
     steps([small], 1)
     for t in range(3, turns + 1):
         steps(early, t)
-    line_steps(early, 0)
+    spread_steps(early, 0)
     steps(others, 2)
     for t in range(3, turns + 1):
         steps(queries, t)
-    line_steps(early, 1)
-    line_steps(queries, 0)
+    spread_steps(queries, 0)
     steps([small], 2)
     for t in range(3, turns + 1):
         steps(others, t)
         steps([small], t)
-    tail = others + [small]
-    for t in range(ne):
-        line_steps(early, t + 2)
-        line_steps(queries, t + 1)
-        line_steps(tail, t)
-    order = list(range(count))
+    spread_steps(others + [small], 0)
+    spread_steps(early, 1)
+    spread_steps(queries, 1)
+    spread_steps(others + [small], 1)
     copies = []
-    for a in order:
-        copies.append(pltpu.make_async_copy(lines[a].own(), outs[a], out_sem.at[a]))
+    for a in range(count):
+        copies.append(pltpu.make_async_copy(spreads[a].own(), outs[a], out_sem.at[a]))
         copies[-1].start()
-    for each in sums + lines:
+    for each in sums + spreads:
         each.wait_sends()
     for copy in copies:
         copy.wait()
@@ -1494,7 +1509,7 @@
         out_specs=[VMEM] + [ANY] * count,
         scratch_shapes=[pltpu.VMEM((nd, ne, share, c), BF16) for c in wide]
         + [pltpu.VMEM((nd - 1, ne, share, c), BF16) for c in wide]
-        + [pltpu.VMEM((2, ne, share, c), BF16) for c in wide]
+        + [pltpu.VMEM((ne - 1, share, c), BF16) for c in wide]
         + [pltpu.VMEM(grads[1].shape, BF16)]
         + [pltpu.VMEM(w.shape, BF16) for w in weights]
         + [pltpu.VMEM((rows, width), F32)]
@@ -1504,8 +1519,8 @@
             DMA((count,)),
             DMA((count, nd - 1)),
             DMA((count, nd - 1)),
-            DMA((count, 2, ne)),
-            DMA((count, 2, ne)),
+            DMA((count, ne - 1)),
+            DMA((count, ne - 1)),
         ],
         compiler_params=pltpu.CompilerParams(
             vmem_limit_bytes=60 * 2**20, collective_id=4, has_side_effects=True
@@ -1621,7 +1636,6 @@
 ):
     micro, rows, width = tokens.shape
     ne, nd = lax.axis_size("ep"), lax.axis_size("dp")
-    dp = lax.axis_index("dp")
     kv_width = KV_HEADS * HEAD_DIM
     every = micro * rows
 
@@ -1631,30 +1645,26 @@
     lanes = 2 * HEAD_DIM // halfway
     sign = np.where(np.arange(2 * HEAD_DIM) % HEAD_DIM < halfway, -1.0, 1.0)
     tables = np.stack([np.tile(np.cos(angles), lanes), np.tile(np.sin(angles), lanes) * sign])
-    tables = lax.dynamic_slice_in_dim(jnp.asarray(tables, F32), dp * rows, rows, axis=1)
-
     tokens_flat = tokens.reshape(every, width)
     gain_one = first_gain.reshape(1, width)
-    normed_one, query_rot, key_rot, value_own = project(
-        tokens_flat, gain_one, tables, w_query, w_key, w_value
+    normed_one, query_rot, tables, starts, key_all, value_all = project(
+        tokens_flat,
+        gain_one,
+        segments.reshape(micro, rows),
+        jnp.asarray(tables, F32),
+        w_query,
+        w_key,
+        w_value,
+        ne,
+        nd,
+        0,
     )
-
-    ids = jnp.arange(128, dtype=jnp.int32)
-    counts = jnp.sum((segments[:, 0, :, None] == ids).astype(F32), axis=1)
-    counts = jnp.concatenate([counts, jnp.zeros((8 - micro, 128), F32)], axis=0)
-
     cot_own = cotangent.reshape(every, width)
 
     def around(value, k):
         return lax.ppermute(value, "ep", [(i, (i + k) % ne) for i in range(ne)])
 
     cots = [cot_own] + [around(cot_own, k) for k in range(1, ne)]
-    key_all, value_all, count_all = gather(ne, nd, (key_rot, value_own, counts), (), 0, 25)
-
-    totals = jnp.sum(count_all[:, :micro], axis=0)
-    lower = (ids[None, None, :] < segments[:, 0, :, None]).astype(F32)
-    starts = jnp.sum(lower * totals[:, None, :], axis=2).astype(jnp.int32)
-    starts = starts.reshape(every, 1)
     routing = routes.reshape(every, routes.shape[2])
     hit = jnp.any(
         jnp.arange(EXPERTS, dtype=jnp.int32)[:, None, None] == routing[None], axis=2

time: 317 us -> 315 us (level)
    pallas_call x2 -> x1, Pallas kernels: 28.3 us -> 26.3 us  [project(): pl.pallas_call(functools.partial(project_body, ne, nd), out_shape=[jax.Sh...]
  transfers between devices with their start and end apart: 3 -> 3, of which waited for: 0 -> 0; matrix products, arithmetic and copies ran while one was open for 2% -> 0% of each run, Pallas kernels for 25% -> 25%
where the time goes in v12:
time: 315 us; the launch traced here: 311 us
  Pallas kernels  301 us (96%)
  starting transfers between devices  5.57 us (2%)
    pallas_call x1, Pallas kernels, experts(): pl.pallas_call(functools.partial(expert_body, ne, nd, micro, rows), grid=...  75.3 us
    pallas_call x1, Pallas kernels, attend(): pl.pallas_call(functools.partial(attend_body, nd // 2 + 1, ne, nd, micro)...  51 us
    pallas_call x1, Pallas kernels, finish(): pl.pallas_call(functools.partial(finish_body, ne, nd, tuple(map(tuple, or...  48.4 us
    pallas_call x1, Pallas kernels, reduce(): pl.pallas_call(functools.partial(reduce_body, ne, nd, kinds, line_parts,...  47 us
    pallas_call x1, Pallas kernels, attend_back(): pl.pallas_call(functools.partial(attend_back_body, nd // 2 + 1, ne, nd, m...  46.2 us
    pallas_call x1, Pallas kernels, project(): pl.pallas_call(functools.partial(project_body, ne, nd), out_shape=[jax.Sh...  26.3 us
    pallas_call x1, Pallas kernels, results(): pl.pallas_call(functools.partial(results_body, share, n_out, len(grads[0]...  7.03 us
  transfers between devices with their start and end apart: 3, of which 0 were waited for; matrix products, arithmetic and copies ran while one was open for 0% of the time, Pallas kernels for 25%

profile of v12, /device:TPU:10, one launch (start us, length us, event | category | flops | bytes accessed | tf_op | source)
XLA Modules:
  0.0 310.8 jit_solution(4593028860766533989)
XLA Ops:
  0.6 0.5 collective-permute-start.2
  1.1 2.6 collective-permute-start.1
  3.7 2.5 collective-permute-start
  6.2 0.8 fusion
  7.0 0.6 convert_element_type.3.refs_8_
  7.6 26.3 %shard_map.238 = (bf16[256,1024]{1,0:T(8,128)(2,1)}, bf16[256,1024]{1,0:T(8,128)(2,1)}, f32[2,128,128]{2,1,0:T(8,128)}, s32[256,1]{1,0:T(8,128)}, bf16[8,256,512...) custom-call(bf16[256,1024]{1,0:T(8,128)(2,1)} %bitcast.20, f32[1,1024]{1,0:T(1,128)} %bitcast.42, s32[2,128]{1,0:T(2,128)} %bitcast.45, ...), custom_call_target="tpu_custom_call" | custom-call | bytes 78000000 | tf_op jit(solution)/shard_map/pallas_call | solution.py:810
  33.9 51.0 %shard_map.239 = (bf16[256,1024]{1,0:T(8,128)(2,1)}, f32[2,4,512,1]{3,2,1,0:T(8,128)}, f32[256,1024]{1,0:T(8,128)}, bf16[256,1024]{1,0:T(8,128)(2,1)}, f32[32,25...) custom-call(s32[256,1]{1,0:T(8,128)} %get-tuple-element.71.refs_0_, ...), custom_call_target="tpu_custom_call" | custom-call | bytes 150000000 | tf_op jit(solution)/shard_map/pallas_call | solution.py:1021
  85.0 0.0 collective-permute-done.2.refs_3_
  85.0 0.0 copy-start.1
  85.0 0.0 collective-permute-done.1.refs_2_
  85.0 0.0 collective-permute-done.refs_1_
  85.0 0.8 copy-done.1
  85.8 75.3 %shard_map.240 = (bf16[1024,1024]{1,0:T(8,128)(2,1)}, bf16[1024,1024]{1,0:T(8,128)(2,1)}, f32[4,8,2,128]{3,2,1,0:T(2,128)}, bf16[2,6,192,512]{3,2,1,0:T(8,128)(2...) custom-call(bf16[256,1024]{1,0:T(8,128)(2,1)} %bitcast.26, ...), custom_call_target="tpu_custom_call" | custom-call | bytes 225000000 | tf_op jit(solution)/shard_map/pallas_call | solution.py:645
  161.1 47.0 %shard_map.241 = (bf16[192,512]{1,0:T(8,128)(2,1)}, bf16[192,512]{1,0:T(8,128)(2,1)}, bf16[192,512]{1,0:T(8,128)(2,1)}, bf16[192,512]{1,0:T(8,128)(2,1)}, bf16[2...) custom-call(bf16[4,384,512]{2,1,0:T(8,128)(2,1)} %get-tuple-element., ...), custom_call_target="tpu_custom_call" | custom-call | bytes 120000000 | tf_op jit(solution)/shard_map/pallas_call | solution.py:366
  208.1 46.2 %shard_map.242 = (bf16[256,1024]{1,0:T(8,128)(2,1)}, f32[256,1024]{1,0:T(8,128)}, bf16[1024,1024]{1,0:T(8,128)(2,1)}, f32[32,1024]{1,0:T(8,128)}, f32[1,1024]{1,...) custom-call(s32[256,1]{1,0:T(8,128)} %get-tuple-element.71.refs_0_, ...), custom_call_target="tpu_custom_call" | custom-call | bytes 120000000 | tf_op jit(solution)/shard_map/pallas_call | solution.py:1287
  254.3 48.4 %shard_map.243 = (f32[256,1024]{1,0:T(8,128)}, bf16[32,512]{1,0:T(8,128)(2,1)}, bf16[32,512]{1,0:T(8,128)(2,1)}, bf16[32,512]{1,0:T(8,128)(2,1)}, bf16[32,512]{1...) custom-call(bf16[256,1024]{1,0:T(8,128)(2,1)} %get-tuple-element.103.refs_0_, ...), custom_call_target="tpu_custom_call" | custom-call | bytes 135000000 | tf_op jit(solution)/shard_map/pallas_call | solution.py:1504
  302.8 0.0 copy-start
  302.8 7.0 %shard_map.244 = (bf16[256,1024]{1,0:T(8,128)(2,1)}, f32[32,1024]{1,0:T(8,128)}, f32[32,1024]{1,0:T(8,128)}, f32[32,512]{1,0:T(8,128)}, f32[32,512]{1,0:T(8,128)...) custom-call(f32[256,1024]{1,0:T(8,128)} %get-tuple-element.75.refs_1, ...), custom_call_target="tpu_custom_call" | custom-call | bytes 18000000 | tf_op jit(solution)/shard_map/pallas_call | solution.py:1609
  309.8 0.0 copy-done
  309.8 1.0 copy.29
Async XLA Ops:
  0.6 84.3 %collective-permute-start.2 = (bf16[256,1024]{1,0:T(8,128)(2,1)}, bf16[256,1024]{1,0:T(8,128)(2,1)S(1)}, u32[]{:S(2)}, u32[]{:S(2)}) collective-permute-start(bf16[256,1024]{1,0:T(8,128)(2,1)} %bitcast.23), channel_id=1, source_target_pairs={{0,24},{8,0},{16,8},{24,16},{1,25},{9,1},{17,9},{25,17},{2,26},{10... | collective-permute-start | bytes 1572872 | tf_op jit(solution)/shard_map/ppermute | solution.py:1665
  1.1 83.8 %collective-permute-start.1 = (bf16[256,1024]{1,0:T(8,128)(2,1)}, bf16[256,1024]{1,0:T(8,128)(2,1)}, u32[]{:S(2)}, u32[]{:S(2)}) collective-permute-start(bf16[256,1024]{1,0:T(8,128)(2,1)} %bitcast.24), channel_id=1, source_target_pairs={{0,16},{8,24},{16,0},{24,8},{1,17},{9,25},{17,1},{25,9},{2,18},{10... | collective-permute-start | bytes 1572872 | tf_op jit(solution)/shard_map/ppermute | solution.py:1665
  3.7 81.3 %collective-permute-start = (bf16[256,1024]{1,0:T(8,128)(2,1)}, bf16[256,1024]{1,0:T(8,128)(2,1)}, u32[]{:S(2)}, u32[]{:S(2)}) collective-permute-start(bf16[256,1024]{1,0:T(8,128)(2,1)} %bitcast.25), channel_id=1, source_target_pairs={{0,8},{8,16},{16,24},{24,0},{1,9},{9,17},{17,25},{25,1},{2,10},{10... | collective-permute-start | bytes 1572872 | tf_op jit(solution)/shard_map/ppermute | solution.py:1665
  85.0 0.8 copy-start.1
  302.8 7.0 %copy-start = (f32[256,1024]{1,0:T(8,128)S(1)}, f32[256,1024]{1,0:T(8,128)}, u32[]{:S(2)}) copy-start(f32[256,1024]{1,0:T(8,128)} %get-tuple-element.119) | copy-start | bytes 3145732

commit v13 on v12

--- a/solution.py
+++ b/solution.py
@@ -109,20 +109,34 @@
 
 
 class PairSum:
-    def __init__(self, dp, order, loads, held, extra, landing, send_sem, recv_sem):
+    def __init__(self, dp, order, loads, held, extra, landing, send_sem, recv_sem, major=False):
         self.dp, self.order, self.held, self.landing = dp, order, held, landing
         self.send_sem, self.recv_sem = send_sem, recv_sem
-        self.extra, self.loads = extra, loads
+        self.extra, self.loads, self.major = extra, loads, major
         self.index = 0
         for b in order:
             side = jnp.bitwise_and(lax.shift_right_logical(dp, b), 1)
             self.index = self.index + (side << self.place(b))
 
     def place(self, bit):
+        if self.major:
+            return len(self.order) - 1 - self.order.index(bit)
         return sorted(self.order).index(bit)
 
     def copies(self, t):
         order = self.order
+        if self.major:
+            count = 1 << (len(order) - 1 - t)
+            first = sum(1 << (len(order) - 1 - i) for i in range(t))
+            mine = self.index - lax.rem(self.index, count)
+            copy = remote(
+                self.held.at[pl.ds(jnp.bitwise_xor(mine, count), count)],
+                self.landing.at[pl.ds(first, count)],
+                self.send_sem.at[t],
+                self.recv_sem.at[t],
+                {"dp": jnp.bitwise_xor(self.dp, 1 << order[t])},
+            )
+            return [(pl.ds(mine, count), pl.ds(first, count), copy)]
         partner = jnp.bitwise_xor(self.index, 1 << self.place(order[t]))
         first = sum(1 << (len(order) - 1 - i) for i in range(t))
         return [
@@ -153,7 +167,8 @@
         elif t <= len(self.order):
             for m, k, copy in self.copies(t - 1):
                 copy.wait_recv()
-                add_into(self.held.at[jnp.bitwise_xor(self.index, m)], self.landing.at[k])
+                mine = m if self.major else jnp.bitwise_xor(self.index, m)
+                add_into(self.held.at[mine], self.landing.at[k])
         if t < len(self.order):
             for m, k, copy in self.copies(t):
                 copy.start()
@@ -165,6 +180,10 @@
         for t in range(len(self.order)):
             for m, k, copy in self.copies(t):
                 copy.wait_send()
+
+
+def slot_of(order, d):
+    return sum(((d >> b) & 1) << (len(order) - 1 - i) for i, b in enumerate(order))
 
 
 class LineSum:
@@ -392,7 +411,7 @@
 
 
 def expert_body(ne, nd, micro, rows, *refs):
-    cots, refs = refs[:ne], refs[ne:]
+    cot_first, cots, refs = refs[0], refs[1 : ne + 1], refs[ne + 1 :]
     normed_ref, probs_ref, gate_ref, up_ref, down_ref = refs[:5]
     mix_ref, grad_ref, dots_ref = refs[5:8]
     kept, landed, whole = refs[8:10], refs[10:12], refs[12:14]
@@ -422,10 +441,16 @@
                 load_sem.at[ne + 1],
             ),
         ]
+        held = every - rows
         for k in range(ne):
-            at = pl.multiple_of(lax.rem(ep - k + ne, ne) * every, every)
+            at = pl.multiple_of(lax.rem(ep - k + ne, ne) * every + rows, rows)
             out.append(
-                pltpu.make_async_copy(cots[k], second.at[pl.ds(at, every)], load_sem.at[k])
+                pltpu.make_async_copy(cots[k], second.at[pl.ds(at, held)], load_sem.at[k])
+            )
+            out.append(
+                pltpu.make_async_copy(
+                    cot_first.at[k], second.at[pl.ds(k * every, rows)], load_sem.at[ne + 2 + k]
+                )
             )
         return out
 
@@ -645,7 +670,7 @@
     return pl.pallas_call(
         functools.partial(expert_body, ne, nd, micro, rows),
         grid=(n_exp + 1,),
-        in_specs=[ANY] * (ne + 2)
+        in_specs=[ANY] * (ne + 3)
         + [
             pl.BlockSpec((1, width, inner), weight),
             pl.BlockSpec((1, width, inner), weight),
@@ -672,7 +697,7 @@
             pltpu.VMEM((2, half, packed, inner), BF16),
             pltpu.VMEM((half, packed, inner), BF16),
             pltpu.VMEM((2, 2 if early > 2 else 1, half // 2, packed // 2, inner), BF16),
-            DMA((ne + 2,)),
+            DMA((2 * ne + 2,)),
             DMA((2, blocks)),
             DMA,
             DMA,
@@ -717,10 +742,10 @@
 
 
 def project_body(ne, nd, *refs):
-    tokens_ref, gain_ref, segments_ref, tables_all, wq_ref, wk_ref, wv_ref = refs[:7]
-    n_ref, q_ref, tables_ref, starts_ref, key_all, value_all = refs[7:13]
-    wq, wk, wv, key_own, value_own, count_own, count_all = refs[13:20]
-    sem, own_sem, send_sem, recv_sem = refs[20:]
+    tokens_ref, gain_ref, segments_ref, tables_all, wq_ref, wk_ref, wv_ref, cot_ref = refs[:8]
+    n_ref, q_ref, tables_ref, starts_ref, key_all, value_all, cot_all = refs[8:15]
+    wq, wk, wv, key_own, value_own, count_own, count_all = refs[15:22]
+    sem, own_sem, send_sem, recv_sem, line_send, line_recv = refs[22:]
     ep, dp = lax.axis_index("ep"), lax.axis_index("dp")
     micro, rows = segments_ref.shape
     loads = [
@@ -748,6 +773,9 @@
         for i, (own, whole) in enumerate(arrays)
     ]
 
+    line = LineGather(ep, ne, cot_ref, cot_all, line_send, line_recv)
+    own_copies.append(pltpu.make_async_copy(cot_ref.at[0], cot_all.at[ep, 0], own_sem.at[3]))
+
     def leave(i):
         gathers[i].start()
         own_copies[i].start()
@@ -762,10 +790,12 @@
     count_own[:micro] = counts
     greet(ep, dp, ne, nd)
     leave(0)
+    line.step(0, 0)
+    own_copies[3].start()
 
     x = tokens_ref[...].astype(F32)
-    n_ref[...] = (x * rms_scale(x) * gain_ref[...]).astype(BF16)
-    normed = n_ref[...]
+    rounded = (x * rms_scale(x) * gain_ref[...]).astype(BF16)
+    normed = rounded
     loads[0].wait()
     cosine, sine = (repeated(tables_ref[i], x.shape[0]) for i in range(2))
     tile = 256
@@ -785,9 +815,16 @@
                 out[:, c : c + tile] = y.astype(BF16)
         if array is not None:
             leave(array)
+    n_ref[...] = rounded.astype(F32).T.astype(BF16)
+    hops = iter(range(1, ne))
     for t in range(bit_count(nd)):
         for each in gathers:
             each.step(t)
+        for s in hops:
+            line.step(0, s)
+            break
+    for s in hops:
+        line.step(0, s)
     for copy in own_copies:
         copy.wait()
     totals = jnp.sum(count_all[...], axis=0)
@@ -801,33 +838,36 @@
         )
     for each in gathers:
         each.wait_sends()
-
-
-def project(tokens, gain, segments, tables, w_query, w_key, w_value, ne, nd, collective):
+    line.wait_sends(0)
+
+
+def project(tokens, gain, segments, tables, w_query, w_key, w_value, cot, ne, nd, collective):
     rows, width = tokens.shape
     micro, count = segments.shape
     keys = jax.ShapeDtypeStruct((nd, rows, w_key.shape[1]), BF16)
     return pl.pallas_call(
         functools.partial(project_body, ne, nd),
         out_shape=[
-            jax.ShapeDtypeStruct((rows, width), BF16),
+            jax.ShapeDtypeStruct((width, rows), BF16),
             jax.ShapeDtypeStruct((rows, w_query.shape[1]), BF16),
             jax.ShapeDtypeStruct((2, count, tables.shape[2]), F32),
             jax.ShapeDtypeStruct((rows, 1), jnp.int32),
             keys,
             keys,
+            jax.ShapeDtypeStruct((ne, 1) + cot.shape[1:], BF16),
         ],
-        in_specs=[VMEM] * 3 + [ANY] * 4,
-        out_specs=[VMEM] * 4 + [ANY] * 2,
+        in_specs=[VMEM] * 3 + [ANY] * 5,
+        out_specs=[VMEM] * 4 + [ANY] * 3,
         scratch_shapes=[pltpu.VMEM(w.shape, BF16) for w in (w_query, w_key, w_value)]
         + [pltpu.VMEM(keys.shape[1:], BF16)] * 2
         + [pltpu.VMEM((8, 128), F32), pltpu.VMEM((nd, 8, 128), F32)]
-        + [DMA((4,)), DMA((3,)), DMA((3, nd - 1)), DMA((3, nd - 1))],
+        + [DMA((4,)), DMA((4,)), DMA((3, nd - 1)), DMA((3, nd - 1))]
+        + [DMA((1, 2, ne - 1)), DMA((1, 2, ne - 1))],
         compiler_params=pltpu.CompilerParams(
             vmem_limit_bytes=60 * 2**20, collective_id=collective, has_side_effects=True
         ),
         cost_estimate=cost(26),
-    )(tokens, gain, segments, tables, w_query, w_key, w_value)
+    )(tokens, gain, segments, tables, w_query, w_key, w_value, cot)
 
 
 def spread(x):
@@ -1156,10 +1196,15 @@
         res_out[...] = grad_residual
         low_res = grad_residual.astype(BF16)
         tile = 256
-        for c in range(0, wo_out.shape[1], tile):
-            wo_out[:, c : c + tile] = dot(
-                attn_ref[...], low_res[:, c : c + tile], ((0,), (0,))
-            ).astype(BF16)
+        for c in range(0, wo_ref.shape[1], tile):
+            y = dot(attn_ref[...], low_res[:, c : c + tile], ((0,), (0,))).astype(BF16)
+            a, at = c // wo_out.shape[4], c % wo_out.shape[4]
+            share = wo_out.shape[3]
+            for e in range(ne):
+                for d in range(nd):
+                    i = (e * nd + d) * share
+                    slot = slot_of(full[a % 2], d)
+                    wo_out[a, slot, e, :, at : at + tile] = y[i : i + share]
         for c in range(0, wo_ref.shape[0], tile):
             grads[c // tile] = dot(low_res, wo_ref[c : c + tile, :], ((1,), (1,))).astype(BF16)
 
@@ -1276,10 +1321,12 @@
     shapes = [(v.shape[0], v.shape[1] - skip) + v.shape[2:] for v, _, _ in sums]
     deep = max([s[0] - 1 for s in shapes] + [1])
     some = max(n, 1)
+    kv_width = keys.shape[2]
+    wo_shape = (width // kv_width, nd, ne, w_out.shape[0] // (ne * nd), kv_width)
     before = [cot, dots, probs, grad_normed, residual, gain, normed, attn, w_out, router]
     after = [
         jax.ShapeDtypeStruct((every, width), F32),
-        jax.ShapeDtypeStruct(w_out.shape, BF16),
+        jax.ShapeDtypeStruct(wo_shape, BF16),
         jax.ShapeDtypeStruct(router.shape, F32),
         jax.ShapeDtypeStruct((1, width), F32),
     ]
@@ -1369,14 +1416,18 @@
     for a in range(count):
         loads = []
         if a < n_out:
-            at = pl.ds(a * columns, columns)
-            loads = [
-                pltpu.make_async_copy(wo_ref.at[e, :, :, at], held[a].at[:, e], load_sem.at[a, e])
-                for e in range(ne)
-            ]
+            loads = [pltpu.make_async_copy(wo_ref.at[a], held[a], load_sem.at[a])]
         sums.append(
             PairSum(
-                dp, orders[a % 2], loads, held[a], None, pair_in[a], dp_send.at[a], dp_recv.at[a]
+                dp,
+                orders[a % 2],
+                loads,
+                held[a],
+                None,
+                pair_in[a],
+                dp_send.at[a],
+                dp_recv.at[a],
+                major=True,
             )
         )
     spreads = [
@@ -1404,7 +1455,7 @@
     steps(early, 0)
 
     normed = n_ref[...]
-    cosine, sine = (repeated(tables_ref[i], normed.shape[0]) for i in range(2))
+    cosine, sine = (repeated(tables_ref[i], normed.shape[1]) for i in range(2))
     sine = -sine
     for i in range(0, dk_ref.shape[1], 128):
         part = dk_ref[:, i : i + 128].astype(F32)
@@ -1414,11 +1465,11 @@
     def product(grad, first, each):
         share = each.held.shape[2]
         for c in range(0, each.held.shape[3], tile):
-            y = dot(normed, grad[:, first + c : first + c + tile], ((0,), (0,))).astype(BF16)
+            y = dot(normed, grad[:, first + c : first + c + tile]).astype(BF16)
             for e in range(ne):
                 for d in range(nd):
                     r = (e * nd + d) * share
-                    each.held[d, e, :, c : c + tile] = y[r : r + share]
+                    each.held[slot_of(each.order, d), e, :, c : c + tile] = y[r : r + share]
         each.step(0)
 
     for i, each in enumerate(made):
@@ -1428,21 +1479,24 @@
             product((dk_turned, dv_ref)[i - n_out], 0, each)
         if i == 0:
             steps(early, 1)
-        else:
-            made[i - 1].step(1)
+        if i == 2:
+            steps(queries, 1)
     for copy in own:
         copy.wait()
     back = dot(dq_ref[...], wq[...], ((1,), (1,)))
-    steps(made[-1:], 1)
+    steps(early, 2)
+    steps(others, 1)
     back = back + dot(dk_turned[...], wk[...], ((1,), (1,)))
     back = back + dot(dv_ref[...], wv[...], ((1,), (1,)))
-    steps(early, 2)
     x = tokens_ref[...].astype(F32)
     r = rms_scale(x)
     scaled = back * gain_ref[...]
     tok_out[...] = (
         res[...] + r * scaled - x * (r * r * r) * jnp.mean(scaled * x, axis=1, keepdims=True)
     )
+    for t in range(3, turns + 1):
+        steps(early, t)
+    spread_steps(early, 0)
     one_row = jnp.sum(back * x * r, axis=0, keepdims=True)
     blank = jnp.zeros((held[-1].shape[3] - EXPERTS - 2, x.shape[1]), F32)
     column = jnp.concatenate([router_ref[...], one_row, gain_two[...], blank], axis=0).T
@@ -1450,21 +1504,16 @@
     for e in range(ne):
         for d in range(nd):
             i = (e * nd + d) * share
-            held[-1][d, e] = column[i : i + share].astype(BF16)
+            held[-1][slot_of(small.order, d), e] = column[i : i + share].astype(BF16)
     steps([small], 0)
     steps(queries, 2)
     steps([small], 1)
     for t in range(3, turns + 1):
-        steps(early, t)
-    spread_steps(early, 0)
-    steps(others, 2)
-    for t in range(3, turns + 1):
         steps(queries, t)
     spread_steps(queries, 0)
-    steps([small], 2)
+    steps(others + [small], 2)
     for t in range(3, turns + 1):
-        steps(others, t)
-        steps([small], t)
+        steps(others + [small], t)
     spread_steps(others + [small], 0)
     spread_steps(early, 1)
     spread_steps(queries, 1)
@@ -1500,7 +1549,6 @@
     n_out = width // columns
     count = 2 * n_out + 3
     wide = [columns] * (count - 1) + [128]
-    split = lambda v: v.reshape(ne, nd, share, v.shape[1])
     return pl.pallas_call(
         functools.partial(finish_body, ne, nd, tuple(map(tuple, orders)), n_out),
         out_shape=[jax.ShapeDtypeStruct((rows, width), F32)]
@@ -1514,11 +1562,11 @@
         + [pltpu.VMEM(w.shape, BF16) for w in weights]
         + [pltpu.VMEM((rows, width), F32)]
         + [
-            DMA((count, ne)),
+            DMA((count,)),
             DMA((4,)),
             DMA((count,)),
-            DMA((count, nd - 1)),
-            DMA((count, nd - 1)),
+            DMA((count, bit_count(nd))),
+            DMA((count, bit_count(nd))),
             DMA((count, ne - 1)),
             DMA((count, ne - 1)),
         ],
@@ -1536,7 +1584,7 @@
         gain_two_grad,
         grad_residual,
         *weights,
-        split(w_out),
+        w_out,
     )
 
 
@@ -1647,7 +1695,7 @@
     tables = np.stack([np.tile(np.cos(angles), lanes), np.tile(np.sin(angles), lanes) * sign])
     tokens_flat = tokens.reshape(every, width)
     gain_one = first_gain.reshape(1, width)
-    normed_one, query_rot, tables, starts, key_all, value_all = project(
+    normed_one, query_rot, tables, starts, key_all, value_all, cot_first = project(
         tokens_flat,
         gain_one,
         segments.reshape(micro, rows),
@@ -1655,6 +1703,7 @@
         w_query,
         w_key,
         w_value,
+        cotangent,
         ne,
         nd,
         0,
@@ -1664,7 +1713,8 @@
     def around(value, k):
         return lax.ppermute(value, "ep", [(i, (i + k) % ne) for i in range(ne)])
 
-    cots = [cot_own] + [around(cot_own, k) for k in range(1, ne)]
+    rest = cot_own[rows:]
+    cots = [cot_first.reshape(ne, rows, width), rest] + [around(rest, k) for k in range(1, ne)]
     routing = routes.reshape(every, routes.shape[2])
     hit = jnp.any(
         jnp.arange(EXPERTS, dtype=jnp.int32)[:, None, None] == routing[None], axis=2

time: 315 us -> 320 us (1.016)
  Pallas kernels: 301 us -> 306 us
    pallas_call x1, Pallas kernels: 26.3 us -> 38.4 us  [project(): pl.pallas_call(functools.partial(project_body, ne, nd), out_shape=[jax.Sh...]
    pallas_call x1, Pallas kernels: 51 us -> 47.6 us  [attend(): pl.pallas_call(functools.partial(attend_body, nd // 2 + 1, ne, nd, micro)...]
  transfers between devices with their start and end apart: 3 -> 3, of which waited for: 0 -> 0; matrix products, arithmetic and copies ran while one was open for 0% -> 0% of each run, Pallas kernels for 25% -> 27%
where the time goes in v13:
time: 320 us; the launch traced here: 317 us
  Pallas kernels  306 us (96%)
  starting transfers between devices  5.57 us (2%)
    pallas_call x1, Pallas kernels, experts(): pl.pallas_call(functools.partial(expert_body, ne, nd, micro, rows), grid=...  75.3 us
    pallas_call x1, Pallas kernels, attend(): pl.pallas_call(functools.partial(attend_body, nd // 2 + 1, ne, nd, micro)...  47.6 us
    pallas_call x1, Pallas kernels, attend_back(): pl.pallas_call(functools.partial(attend_back_body, nd // 2 + 1, ne, nd, m...  46.8 us
    pallas_call x1, Pallas kernels, finish(): pl.pallas_call(functools.partial(finish_body, ne, nd, tuple(map(tuple, or...  45.7 us
    pallas_call x1, Pallas kernels, reduce(): pl.pallas_call(functools.partial(reduce_body, ne, nd, kinds, line_parts,...  45.4 us
    pallas_call x1, Pallas kernels, project(): pl.pallas_call(functools.partial(project_body, ne, nd), out_shape=[jax.Sh...  38.4 us
    pallas_call x1, Pallas kernels, results(): pl.pallas_call(functools.partial(results_body, share, n_out, len(grads[0]...  7.03 us
  transfers between devices with their start and end apart: 3, of which 0 were waited for; matrix products, arithmetic and copies ran while one was open for 0% of the time, Pallas kernels for 27%

profile of v13, /device:TPU:10, one launch (start us, length us, event | category | flops | bytes accessed | tf_op | source)
XLA Modules:
  0.0 316.9 jit_solution(6898469186035824888)
XLA Ops:
  0.6 1.0 slice_bitcast_fusion.refs_1_
  1.6 0.0 copy-start
  1.6 0.5 collective-permute-start.2
  2.1 2.6 collective-permute-start.1
  4.7 2.5 collective-permute-start
  7.2 0.8 fusion
  8.0 0.6 convert_element_type.3.refs_8_
  8.6 38.4 %shard_map.238 = (bf16[1024,256]{1,0:T(8,128)(2,1)}, bf16[256,1024]{1,0:T(8,128)(2,1)}, f32[2,128,128]{2,1,0:T(8,128)}, s32[256,1]{1,0:T(8,128)}, bf16[8,256,512...) custom-call(bf16[256,1024]{1,0:T(8,128)(2,1)} %bitcast.22, f32[1,1024]{1,0:T(1,128)} %bitcast.40, ...), custom_call_target="tpu_custom_call" | custom-call | bytes 78000000 | tf_op jit(solution)/shard_map/pallas_call | solution.py:848
  47.1 47.6 %shard_map.239 = (bf16[256,1024]{1,0:T(8,128)(2,1)}, f32[2,4,512,1]{3,2,1,0:T(8,128)}, f32[256,1024]{1,0:T(8,128)}, bf16[256,1024]{1,0:T(8,128)(2,1)}, f32[32,25...) custom-call(s32[256,1]{1,0:T(8,128)} %get-tuple-element.72.refs_0_, ...), custom_call_target="tpu_custom_call" | custom-call | bytes 150000000 | tf_op jit(solution)/shard_map/pallas_call | solution.py:1061
  94.7 0.0 collective-permute-done.2.refs_4_
  94.7 0.0 copy-start.2
  94.7 0.0 collective-permute-done.1.refs_3_
  94.7 0.0 copy-start.3
  94.7 0.0 collective-permute-done.refs_2_
  94.8 0.0 copy-start.4
  94.8 0.8 copy-done.4
  95.5 0.1 copy-done.3
  95.6 75.3 %shard_map.240 = (bf16[1024,1024]{1,0:T(8,128)(2,1)}, bf16[1024,1024]{1,0:T(8,128)(2,1)}, f32[4,8,2,128]{3,2,1,0:T(2,128)}, bf16[2,6,192,512]{3,2,1,0:T(8,128)(2...) custom-call(bf16[4,128,1024]{2,1,0:T(8,128)(2,1)} %bitcast.29, ...), custom_call_target="tpu_custom_call" | custom-call | bytes 225000000 | tf_op jit(solution)/shard_map/pallas_call | solution.py:670
  170.9 45.4 %shard_map.241 = (bf16[192,512]{1,0:T(8,128)(2,1)}, bf16[192,512]{1,0:T(8,128)(2,1)}, bf16[192,512]{1,0:T(8,128)(2,1)}, bf16[192,512]{1,0:T(8,128)(2,1)}, bf16[2...) custom-call(bf16[4,384,512]{2,1,0:T(8,128)(2,1)} %get-tuple-element., ...), custom_call_target="tpu_custom_call" | custom-call | bytes 120000000 | tf_op jit(solution)/shard_map/pallas_call | solution.py:385
  216.3 46.8 %shard_map.242 = (bf16[256,1024]{1,0:T(8,128)(2,1)}, f32[256,1024]{1,0:T(8,128)}, bf16[2,8,4,32,512]{4,3,2,1,0:T(8,128)(2,1)}, f32[32,1024]{1,0:T(8,128)}, f32[1...) custom-call(s32[256,1]{1,0:T(8,128)} %get-tuple-element.72.refs_0_, ...), custom_call_target="tpu_custom_call" | custom-call | bytes 120000000 | tf_op jit(solution)/shard_map/pallas_call | solution.py:1334
  263.1 45.7 %shard_map.243 = (f32[256,1024]{1,0:T(8,128)}, bf16[32,512]{1,0:T(8,128)(2,1)}, bf16[32,512]{1,0:T(8,128)(2,1)}, bf16[32,512]{1,0:T(8,128)(2,1)}, bf16[32,512]{1...) custom-call(bf16[1024,256]{1,0:T(8,128)(2,1)} %get-tuple-element.105.refs_0_, ...), custom_call_target="tpu_custom_call" | custom-call | bytes 135000000 | tf_op jit(solution)/shard_map/pallas_call | solution.py:1552
  308.9 7.0 %shard_map.244 = (bf16[256,1024]{1,0:T(8,128)(2,1)}, f32[32,1024]{1,0:T(8,128)}, f32[32,1024]{1,0:T(8,128)}, f32[32,512]{1,0:T(8,128)}, f32[32,512]{1,0:T(8,128)...) custom-call(f32[256,1024]{1,0:T(8,128)} %get-tuple-element.76.refs_1, ...), custom_call_target="tpu_custom_call" | custom-call | bytes 18000000 | tf_op jit(solution)/shard_map/pallas_call | solution.py:1657
  315.9 0.0 copy-done.1
  315.9 1.0 copy.29
  (3 shorter events, 0.0 us)
Async XLA Ops:
  1.6 45.4 %copy-start = (bf16[128,1024]{1,0:T(8,128)(2,1)}, bf16[128,1024]{1,0:T(8,128)(2,1)S(1)}, u32[]{:S(2)}) copy-start(bf16[128,1024]{1,0:T(8,128)(2,1)S(1)} %slice_bitcast_fusion.refs_1_) | copy-start | bytes 786436
  1.6 93.1 %collective-permute-start.2 = (bf16[128,1024]{1,0:T(8,128)(2,1)S(1)}, bf16[128,1024]{1,0:T(8,128)(2,1)S(1)}, u32[]{:S(2)}, u32[]{:S(2)}) collective-permute-start(bf16[128,1024]{1,0:T(8,128)(2,1)S(1)} %slice_bitcast_fusion.refs_1_), channel_id=1, source_target_pairs={{0,24},{8,0},{16,8},{24,16},{1,25},{9,1},{17,9},{25,17},{2,26},{10... | collective-permute-start | bytes 786440 | tf_op jit(solution)/shard_map/ppermute | solution.py:1714
  2.1 92.6 %collective-permute-start.1 = (bf16[128,1024]{1,0:T(8,128)(2,1)S(1)}, bf16[128,1024]{1,0:T(8,128)(2,1)S(1)}, u32[]{:S(2)}, u32[]{:S(2)}) collective-permute-start(bf16[128,1024]{1,0:T(8,128)(2,1)S(1)} %slice_bitcast_fusion.refs_1_), channel_id=1, source_target_pairs={{0,16},{8,24},{16,0},{24,8},{1,17},{9,25},{17,1},{25,9},{2,18},{10... | collective-permute-start | bytes 786440 | tf_op jit(solution)/shard_map/ppermute | solution.py:1714
  4.7 90.0 %collective-permute-start = (bf16[128,1024]{1,0:T(8,128)(2,1)S(1)}, bf16[128,1024]{1,0:T(8,128)(2,1)S(1)}, u32[]{:S(2)}, u32[]{:S(2)}) collective-permute-start(bf16[128,1024]{1,0:T(8,128)(2,1)S(1)} %slice_bitcast_fusion.refs_1_), channel_id=1, source_target_pairs={{0,8},{8,16},{16,24},{24,0},{1,9},{9,17},{17,25},{25,1},{2,10},{10... | collective-permute-start | bytes 786440 | tf_op jit(solution)/shard_map/ppermute | solution.py:1714
  94.7 0.8 copy-start.2
  94.7 0.9 copy-start.3
  94.8 0.8 copy-start.4
  308.9 7.0 %copy-start.1 = (f32[256,1024]{1,0:T(8,128)S(1)}, f32[256,1024]{1,0:T(8,128)}, u32[]{:S(2)}) copy-start(f32[256,1024]{1,0:T(8,128)} %get-tuple-element.121) | copy-start | bytes 3145732

commit v14 on v13

--- a/solution.py
+++ b/solution.py
@@ -81,8 +81,8 @@
         for t in range(len(self.order)):
             self.copy(t, 0).start()
 
-    def step(self, t):
-        for m in masks(self.order[:t]):
+    def step(self, t, first=0, last=None):
+        for m in masks(self.order[:t])[first:last]:
             self.copy(t, m).wait_recv()
             for later in range(t + 1, len(self.order)):
                 self.copy(later, m | (1 << self.order[t])).start()
@@ -411,7 +411,7 @@
 
 
 def expert_body(ne, nd, micro, rows, *refs):
-    cot_first, cots, refs = refs[0], refs[1 : ne + 1], refs[ne + 1 :]
+    cots, refs = refs[:2], refs[2:]
     normed_ref, probs_ref, gate_ref, up_ref, down_ref = refs[:5]
     mix_ref, grad_ref, dots_ref = refs[5:8]
     kept, landed, whole = refs[8:10], refs[10:12], refs[12:14]
@@ -441,17 +441,17 @@
                 load_sem.at[ne + 1],
             ),
         ]
-        held = every - rows
         for k in range(ne):
-            at = pl.multiple_of(lax.rem(ep - k + ne, ne) * every + rows, rows)
-            out.append(
-                pltpu.make_async_copy(cots[k], second.at[pl.ds(at, held)], load_sem.at[k])
-            )
-            out.append(
-                pltpu.make_async_copy(
-                    cot_first.at[k], second.at[pl.ds(k * every, rows)], load_sem.at[ne + 2 + k]
+            at = k * every
+            for i, part in enumerate(cots):
+                out.append(
+                    pltpu.make_async_copy(
+                        part.at[k],
+                        second.at[pl.ds(at, part.shape[1])],
+                        load_sem.at[k if i == 0 else ne + 2 + k],
+                    )
                 )
-            )
+                at += part.shape[1]
         return out
 
     def block_at(s):
@@ -670,7 +670,7 @@
     return pl.pallas_call(
         functools.partial(expert_body, ne, nd, micro, rows),
         grid=(n_exp + 1,),
-        in_specs=[ANY] * (ne + 3)
+        in_specs=[ANY] * 4
         + [
             pl.BlockSpec((1, width, inner), weight),
             pl.BlockSpec((1, width, inner), weight),
@@ -773,8 +773,9 @@
         for i, (own, whole) in enumerate(arrays)
     ]
 
-    line = LineGather(ep, ne, cot_ref, cot_all, line_send, line_recv)
-    own_copies.append(pltpu.make_async_copy(cot_ref.at[0], cot_all.at[ep, 0], own_sem.at[3]))
+    cot_own = cot_ref.at[:, pl.ds(0, cot_all.shape[2])]
+    line = LineGather(ep, ne, cot_own, cot_all, line_send, line_recv)
+    own_copies.append(pltpu.make_async_copy(cot_own.at[0], cot_all.at[ep, 0], own_sem.at[3]))
 
     def leave(i):
         gathers[i].start()
@@ -819,10 +820,12 @@
     hops = iter(range(1, ne))
     for t in range(bit_count(nd)):
         for each in gathers:
-            each.step(t)
+            each.step(t, 0, 1)
         for s in hops:
             line.step(0, s)
             break
+        for each in gathers:
+            each.step(t, 1)
     for s in hops:
         line.step(0, s)
     for copy in own_copies:
@@ -841,7 +844,9 @@
     line.wait_sends(0)
 
 
-def project(tokens, gain, segments, tables, w_query, w_key, w_value, cot, ne, nd, collective):
+def project(
+    tokens, gain, segments, tables, w_query, w_key, w_value, cot, early, ne, nd, collective
+):
     rows, width = tokens.shape
     micro, count = segments.shape
     keys = jax.ShapeDtypeStruct((nd, rows, w_key.shape[1]), BF16)
@@ -854,7 +859,7 @@
             jax.ShapeDtypeStruct((rows, 1), jnp.int32),
             keys,
             keys,
-            jax.ShapeDtypeStruct((ne, 1) + cot.shape[1:], BF16),
+            jax.ShapeDtypeStruct((ne, 1, early, width), BF16),
         ],
         in_specs=[VMEM] * 3 + [ANY] * 5,
         out_specs=[VMEM] * 4 + [ANY] * 3,
@@ -968,11 +973,13 @@
 
 def attend_body(span, ne, nd, micro, *refs):
     starts_ref, q_ref, k_ref, v_ref, tokens_ref, wo_ref, gain_ref, router_ref, hit_ref = refs[:9]
-    out_ref, log_ref, res_ref, normed_ref, probs_ref, normed_all, marked_all = refs[9:16]
-    attn, normed_own, marked_own, own_sem, send_sem, recv_sem = refs[16:]
+    cot_ref = refs[9]
+    out_ref, log_ref, res_ref, normed_ref, probs_ref, normed_all, marked_all, cot_all = refs[10:18]
+    attn, normed_own, marked_own, own_sem, send_sem, recv_sem, cot_sem, cot_send, cot_recv = refs[18:]
     ep, dp = lax.axis_index("ep"), lax.axis_index("dp")
     m, h = pl.program_id(0), pl.program_id(1)
     final = pl.num_programs(1) - 1
+    final_step = micro * (KV_HEADS // 2) - 1
     rows = q_ref.shape[0]
     lines = [
         LineGather(ep, ne, own, whole, send_sem.at[i], recv_sem.at[i])
@@ -983,9 +990,23 @@
         for line in lines:
             line.step(batch, s)
 
+    count = cot_all.shape[2]
+    cot_own = cot_ref.at[:, pl.ds(cot_ref.shape[1] - count, count)]
+    cot_line = LineGather(ep, ne, cot_own, cot_all, cot_send, cot_recv)
+    cot_copy = pltpu.make_async_copy(cot_own.at[0], cot_all.at[ep, 0], cot_sem)
+
     @pl.when((m == 0) & (h == 0))
     def _():
         greet(ep, dp, ne, nd)
+        cot_line.step(0, 0)
+        cot_copy.start()
+
+    for s in range(1, ne):
+        at = min(1 + 2 * s, final_step)
+
+        @pl.when(m * pl.num_programs(1) + h == at)
+        def _(s=s):
+            cot_line.step(0, s)
 
     q = spread(q_ref[...].astype(F32) * SCALE).astype(BF16)
     scores = window_scores(dp, span, rows, starts_ref, q, in_window(k_ref, dp, span))
@@ -1036,6 +1057,8 @@
                         line.wait_sends(each)
                     for copy in own_copies(each):
                         copy.wait()
+                cot_line.wait_sends(0)
+                cot_copy.wait()
 
 
 def attention_specs(micro, rows, nd):
@@ -1049,7 +1072,7 @@
 
 
 def attend(
-    starts, queries, keys, values, tokens, w_out, gain, router, hit, micro, rows, ne, collective
+    starts, queries, keys, values, tokens, w_out, gain, router, hit, cot, late, micro, rows, ne, collective
 ):
     nd, width = keys.shape[0], tokens.shape[1]
     grid, mine, theirs, column, logs, log_shape = attention_specs(micro, rows, nd)
@@ -1062,8 +1085,8 @@
         functools.partial(attend_body, nd // 2 + 1, ne, nd, micro),
         grid=grid,
         in_specs=[column, mine, theirs, theirs, wide, whole(w_out), whole(gain), whole(router)]
-        + [chosen],
-        out_specs=[mine, logs, wide, wide, chosen, ANY, ANY],
+        + [chosen, ANY],
+        out_specs=[mine, logs, wide, wide, chosen, ANY, ANY, ANY],
         out_shape=[
             jax.ShapeDtypeStruct(queries.shape, BF16),
             log_shape,
@@ -1072,6 +1095,7 @@
             jax.ShapeDtypeStruct(hit.shape, F32),
             jax.ShapeDtypeStruct((ne, micro, rows, width), BF16),
             jax.ShapeDtypeStruct((ne, micro, hit.shape[0], rows), F32),
+            jax.ShapeDtypeStruct((ne, 1, late, width), BF16),
         ],
         scratch_shapes=[
             pltpu.VMEM((rows, width), BF16),
@@ -1080,12 +1104,15 @@
             DMA((2, micro)),
             DMA((2, micro, 2, ne - 1)),
             DMA((2, micro, 2, ne - 1)),
+            DMA,
+            DMA((1, 2, ne - 1)),
+            DMA((1, 2, ne - 1)),
         ],
         compiler_params=pltpu.CompilerParams(
             vmem_limit_bytes=60 * 2**20, collective_id=collective, has_side_effects=True
         ),
         cost_estimate=cost(50),
-    )(starts, queries, keys, values, tokens, w_out, gain, router, hit)
+    )(starts, queries, keys, values, tokens, w_out, gain, router, hit, cot)
 
 
 def attend_back_body(span, ne, nd, micro, skip, full, orders, *refs):
@@ -1695,6 +1722,8 @@
     tables = np.stack([np.tile(np.cos(angles), lanes), np.tile(np.sin(angles), lanes) * sign])
     tokens_flat = tokens.reshape(every, width)
     gain_one = first_gain.reshape(1, width)
+    cot_own = cotangent.reshape(every, width)
+    late = rows // 2
     normed_one, query_rot, tables, starts, key_all, value_all, cot_first = project(
         tokens_flat,
         gain_one,
@@ -1703,24 +1732,18 @@
         w_query,
         w_key,
         w_value,
-        cotangent,
+        cot_own[None],
+        every - late,
         ne,
         nd,
         0,
     )
-    cot_own = cotangent.reshape(every, width)
-
-    def around(value, k):
-        return lax.ppermute(value, "ep", [(i, (i + k) % ne) for i in range(ne)])
-
-    rest = cot_own[rows:]
-    cots = [cot_first.reshape(ne, rows, width), rest] + [around(rest, k) for k in range(1, ne)]
     routing = routes.reshape(every, routes.shape[2])
     hit = jnp.any(
         jnp.arange(EXPERTS, dtype=jnp.int32)[:, None, None] == routing[None], axis=2
     ).astype(F32)
     router = w_router.T
-    attn_low, logs, residual, normed_two, gate_probs, normed_all, marked_all = attend(
+    attn_low, logs, residual, normed_two, gate_probs, normed_all, marked_all, cot_last = attend(
         starts,
         query_rot,
         key_all,
@@ -1730,6 +1753,8 @@
         second_gain.reshape(1, width),
         router,
         hit,
+        cot_own[None],
+        late,
         micro,
         rows,
         ne,
@@ -1738,7 +1763,7 @@
     orders = [order[:-1][::-1] for order in gather_orders(nd)]
     mix, grad_in, pair_dots, *grads = experts(
         normed_all.reshape(ne * every, width),
-        cots,
+        [cot.reshape(ne, -1, width) for cot in (cot_first, cot_last)],
         marked_all.reshape(ne * micro, EXPERTS, rows),
         w_gate,
         w_up,

time: 320 us -> 314 us (0.981)
  starting transfers between devices: 5.57 us -> 0 us
    ppermute x3 -> x0, starting transfers between devices: 5.57 us -> none  [around(): return lax.ppermute(value, 'ep', [(i, (i + k) % ne) for i in range(ne)])]
    pallas_call x1, Pallas kernels: 47.6 us -> 51.8 us  [attend(): pl.pallas_call(functools.partial(attend_body, nd // 2 + 1, ne, nd, micro)...]
  transfers between devices with their start and end apart: 3 -> 0, of which waited for: 0 -> 0; matrix products, arithmetic and copies ran while one was open for 0% -> 0% of each run, Pallas kernels for 27% -> 0%
where the time goes in v14:
time: 314 us; the launch traced here: 311 us
  Pallas kernels  308 us (98%)
    pallas_call x1, Pallas kernels, experts(): pl.pallas_call(functools.partial(expert_body, ne, nd, micro, rows), grid=...  75.3 us
    pallas_call x1, Pallas kernels, attend(): pl.pallas_call(functools.partial(attend_body, nd // 2 + 1, ne, nd, micro)...  51.8 us
    pallas_call x1, Pallas kernels, finish(): pl.pallas_call(functools.partial(finish_body, ne, nd, tuple(map(tuple, or...  47.2 us
    pallas_call x1, Pallas kernels, attend_back(): pl.pallas_call(functools.partial(attend_back_body, nd // 2 + 1, ne, nd, m...  45.4 us
    pallas_call x1, Pallas kernels, reduce(): pl.pallas_call(functools.partial(reduce_body, ne, nd, kinds, line_parts,...  44.8 us
    pallas_call x1, Pallas kernels, project(): pl.pallas_call(functools.partial(project_body, ne, nd), out_shape=[jax.Sh...  36.3 us
    pallas_call x1, Pallas kernels, results(): pl.pallas_call(functools.partial(results_body, share, n_out, len(grads[0]...  7.03 us

profile of v14, /device:TPU:10, one launch (start us, length us, event | category | flops | bytes accessed | tf_op | source)
XLA Modules:
  0.0 310.9 jit_solution(261410971492651170)
XLA Ops:
  0.6 0.8 fusion
  1.4 0.6 convert_element_type.3.refs_8_
  2.1 36.3 %shard_map.238 = (bf16[1024,256]{1,0:T(8,128)(2,1)}, bf16[256,1024]{1,0:T(8,128)(2,1)}, f32[2,128,128]{2,1,0:T(8,128)}, s32[256,1]{1,0:T(8,128)}, bf16[8,256,512...) custom-call(bf16[256,1024]{1,0:T(8,128)(2,1)} %bitcast.25, f32[1,1024]{1,0:T(1,128)} %bitcast.43, ...), custom_call_target="tpu_custom_call" | custom-call | bytes 78000000 | tf_op jit(solution)/shard_map/pallas_call | solution.py:853
  38.3 51.8 %shard_map.239 = (bf16[256,1024]{1,0:T(8,128)(2,1)}, f32[2,4,512,1]{3,2,1,0:T(8,128)}, f32[256,1024]{1,0:T(8,128)}, bf16[256,1024]{1,0:T(8,128)(2,1)}, f32[32,25...) custom-call(s32[256,1]{1,0:T(8,128)} %get-tuple-element.73.refs_0_, ...), custom_call_target="tpu_custom_call" | custom-call | bytes 150000000 | tf_op jit(solution)/shard_map/pallas_call | solution.py:1084
  90.1 75.3 %shard_map.240 = (bf16[1024,1024]{1,0:T(8,128)(2,1)}, bf16[1024,1024]{1,0:T(8,128)(2,1)}, f32[4,8,2,128]{3,2,1,0:T(2,128)}, bf16[2,6,192,512]{3,2,1,0:T(8,128)(2...) custom-call(bf16[4,192,1024]{2,1,0:T(8,128)(2,1)} %bitcast.31, ...), custom_call_target="tpu_custom_call" | custom-call | bytes 225000000 | tf_op jit(solution)/shard_map/pallas_call | solution.py:670
  165.4 44.8 %shard_map.241 = (bf16[192,512]{1,0:T(8,128)(2,1)}, bf16[192,512]{1,0:T(8,128)(2,1)}, bf16[192,512]{1,0:T(8,128)(2,1)}, bf16[192,512]{1,0:T(8,128)(2,1)}, bf16[2...) custom-call(bf16[4,384,512]{2,1,0:T(8,128)(2,1)} %get-tuple-element., ...), custom_call_target="tpu_custom_call" | custom-call | bytes 120000000 | tf_op jit(solution)/shard_map/pallas_call | solution.py:385
  210.2 45.4 %shard_map.242 = (bf16[256,1024]{1,0:T(8,128)(2,1)}, f32[256,1024]{1,0:T(8,128)}, bf16[2,8,4,32,512]{4,3,2,1,0:T(8,128)(2,1)}, f32[32,1024]{1,0:T(8,128)}, f32[1...) custom-call(s32[256,1]{1,0:T(8,128)} %get-tuple-element.73.refs_0_, ...), custom_call_target="tpu_custom_call" | custom-call | bytes 120000000 | tf_op jit(solution)/shard_map/pallas_call | solution.py:1361
  255.6 47.2 %shard_map.243 = (f32[256,1024]{1,0:T(8,128)}, bf16[32,512]{1,0:T(8,128)(2,1)}, bf16[32,512]{1,0:T(8,128)(2,1)}, bf16[32,512]{1,0:T(8,128)(2,1)}, bf16[32,512]{1...) custom-call(bf16[1024,256]{1,0:T(8,128)(2,1)} %get-tuple-element.107.refs_0_, ...), custom_call_target="tpu_custom_call" | custom-call | bytes 135000000 | tf_op jit(solution)/shard_map/pallas_call | solution.py:1579
  302.9 0.0 copy-start
  302.9 7.0 %shard_map.244 = (bf16[256,1024]{1,0:T(8,128)(2,1)}, f32[32,1024]{1,0:T(8,128)}, f32[32,1024]{1,0:T(8,128)}, f32[32,512]{1,0:T(8,128)}, f32[32,512]{1,0:T(8,128)...) custom-call(f32[256,1024]{1,0:T(8,128)} %get-tuple-element.77.refs_1, ...), custom_call_target="tpu_custom_call" | custom-call | bytes 18000000 | tf_op jit(solution)/shard_map/pallas_call | solution.py:1684
  309.9 0.0 copy-done
  310.0 1.0 copy.29
Async XLA Ops:
  302.9 7.0 %copy-start = (f32[256,1024]{1,0:T(8,128)S(1)}, f32[256,1024]{1,0:T(8,128)}, u32[]{:S(2)}) copy-start(f32[256,1024]{1,0:T(8,128)} %get-tuple-element.123) | copy-start | bytes 3145732

commit v15 on v14

--- a/solution.py
+++ b/solution.py
@@ -583,7 +583,6 @@
         grad_up = (back * silu).astype(BF16)
         grad_gate = (back * up_pre * (sigma * (1.0 + gate_pre * (1.0 - sigma)))).astype(BF16)
         scaled = (wide * p).astype(BF16)
-        grad_x = dot(grad_gate, w_gate, ((1,), (1,))) + dot(grad_up, w_up, ((1,), (1,)))
         pair = jnp.sum(flat * pair.reshape(blocks, CAP, 1), axis=1)
         dots_ref[:, 0] = pair.reshape(ne, micro, rows)
 
@@ -613,6 +612,7 @@
         split(dot(x, grad_up, ((0,), (0,))), share)
         exchange().start()
 
+        grad_x = dot(grad_gate, w_gate, ((1,), (1,))) + dot(grad_up, w_up, ((1,), (1,)))
         rows_in[:, e] = grad_x.astype(BF16).reshape(blocks, CAP, width)
         cots_in[:, e] = out.astype(BF16).reshape(blocks, CAP, width)
 
@@ -1723,7 +1723,7 @@
     tokens_flat = tokens.reshape(every, width)
     gain_one = first_gain.reshape(1, width)
     cot_own = cotangent.reshape(every, width)
-    late = rows // 2
+    late = rows // 4
     normed_one, query_rot, tables, starts, key_all, value_all, cot_first = project(
         tokens_flat,
         gain_one,

time: 314 us -> 312 us (level)
  no operation moved by 1% of the time
where the time goes in v15:
time: 312 us; the launch traced here: 309 us
  Pallas kernels  306 us (98%)
    pallas_call x1, Pallas kernels, experts(): pl.pallas_call(functools.partial(expert_body, ne, nd, micro, rows), grid=...  73.7 us
    pallas_call x1, Pallas kernels, attend(): pl.pallas_call(functools.partial(attend_body, nd // 2 + 1, ne, nd, micro)...  49 us
    pallas_call x1, Pallas kernels, attend_back(): pl.pallas_call(functools.partial(attend_back_body, nd // 2 + 1, ne, nd, m...  46.5 us
    pallas_call x1, Pallas kernels, finish(): pl.pallas_call(functools.partial(finish_body, ne, nd, tuple(map(tuple, or...  45.8 us
    pallas_call x1, Pallas kernels, reduce(): pl.pallas_call(functools.partial(reduce_body, ne, nd, kinds, line_parts,...  45 us
    pallas_call x1, Pallas kernels, project(): pl.pallas_call(functools.partial(project_body, ne, nd), out_shape=[jax.Sh...  39 us
    pallas_call x1, Pallas kernels, results(): pl.pallas_call(functools.partial(results_body, share, n_out, len(grads[0]...  7.03 us

profile of v15, /device:TPU:10, one launch (start us, length us, event | category | flops | bytes accessed | tf_op | source)
XLA Modules:
  0.0 309.1 jit_solution(3923816855085307075)
XLA Ops:
  0.6 0.8 fusion
  1.4 0.6 convert_element_type.3.refs_8_
  2.1 39.0 %shard_map.238 = (bf16[1024,256]{1,0:T(8,128)(2,1)}, bf16[256,1024]{1,0:T(8,128)(2,1)}, f32[2,128,128]{2,1,0:T(8,128)}, s32[256,1]{1,0:T(8,128)}, bf16[8,256,512...) custom-call(bf16[256,1024]{1,0:T(8,128)(2,1)} %bitcast.25, f32[1,1024]{1,0:T(1,128)} %bitcast.43, ...), custom_call_target="tpu_custom_call" | custom-call | bytes 78000000 | tf_op jit(solution)/shard_map/pallas_call | solution.py:853
  41.0 49.0 %shard_map.239 = (bf16[256,1024]{1,0:T(8,128)(2,1)}, f32[2,4,512,1]{3,2,1,0:T(8,128)}, f32[256,1024]{1,0:T(8,128)}, bf16[256,1024]{1,0:T(8,128)(2,1)}, f32[32,25...) custom-call(s32[256,1]{1,0:T(8,128)} %get-tuple-element.73.refs_0_, ...), custom_call_target="tpu_custom_call" | custom-call | bytes 150000000 | tf_op jit(solution)/shard_map/pallas_call | solution.py:1084
  90.0 73.7 %shard_map.240 = (bf16[1024,1024]{1,0:T(8,128)(2,1)}, bf16[1024,1024]{1,0:T(8,128)(2,1)}, f32[4,8,2,128]{3,2,1,0:T(2,128)}, bf16[2,6,192,512]{3,2,1,0:T(8,128)(2...) custom-call(bf16[4,224,1024]{2,1,0:T(8,128)(2,1)} %bitcast.31, ...), custom_call_target="tpu_custom_call" | custom-call | bytes 225000000 | tf_op jit(solution)/shard_map/pallas_call | solution.py:670
  163.7 45.0 %shard_map.241 = (bf16[192,512]{1,0:T(8,128)(2,1)}, bf16[192,512]{1,0:T(8,128)(2,1)}, bf16[192,512]{1,0:T(8,128)(2,1)}, bf16[192,512]{1,0:T(8,128)(2,1)}, bf16[2...) custom-call(bf16[4,384,512]{2,1,0:T(8,128)(2,1)} %get-tuple-element., ...), custom_call_target="tpu_custom_call" | custom-call | bytes 120000000 | tf_op jit(solution)/shard_map/pallas_call | solution.py:385
  208.7 46.5 %shard_map.242 = (bf16[256,1024]{1,0:T(8,128)(2,1)}, f32[256,1024]{1,0:T(8,128)}, bf16[2,8,4,32,512]{4,3,2,1,0:T(8,128)(2,1)}, f32[32,1024]{1,0:T(8,128)}, f32[1...) custom-call(s32[256,1]{1,0:T(8,128)} %get-tuple-element.73.refs_0_, ...), custom_call_target="tpu_custom_call" | custom-call | bytes 120000000 | tf_op jit(solution)/shard_map/pallas_call | solution.py:1361
  255.3 45.8 %shard_map.243 = (f32[256,1024]{1,0:T(8,128)}, bf16[32,512]{1,0:T(8,128)(2,1)}, bf16[32,512]{1,0:T(8,128)(2,1)}, bf16[32,512]{1,0:T(8,128)(2,1)}, bf16[32,512]{1...) custom-call(bf16[1024,256]{1,0:T(8,128)(2,1)} %get-tuple-element.107.refs_0_, ...), custom_call_target="tpu_custom_call" | custom-call | bytes 135000000 | tf_op jit(solution)/shard_map/pallas_call | solution.py:1579
  301.1 0.0 copy-start
  301.1 7.0 %shard_map.244 = (bf16[256,1024]{1,0:T(8,128)(2,1)}, f32[32,1024]{1,0:T(8,128)}, f32[32,1024]{1,0:T(8,128)}, f32[32,512]{1,0:T(8,128)}, f32[32,512]{1,0:T(8,128)...) custom-call(f32[256,1024]{1,0:T(8,128)} %get-tuple-element.77.refs_1, ...), custom_call_target="tpu_custom_call" | custom-call | bytes 18000000 | tf_op jit(solution)/shard_map/pallas_call | solution.py:1684
  308.1 0.0 copy-done
  308.1 1.0 copy.29
Async XLA Ops:
  301.1 7.0 %copy-start = (f32[256,1024]{1,0:T(8,128)S(1)}, f32[256,1024]{1,0:T(8,128)}, u32[]{:S(2)}) copy-start(f32[256,1024]{1,0:T(8,128)} %get-tuple-element.123) | copy-start | bytes 3145732
